TPU v7x, 32 devices: a whole 2x2x4 slice. The times are simulated.
32 devices in a mesh: groups: 2 (over y), batch: 4 (over z), tensor: 4 (over x, core).
Axes of the slice: x: 2, y: 2, z: 4, core: 2. Of those that a mesh axis runs over, the one named last changes fastest.
Arguments:
- tokens: bfloat16 [6144, 8192], P(('groups', 'batch'), 'tensor'), parts along dimension 0, may hold values from -6 to 6
- request_adapter: int32 [6144], P(('groups', 'batch')), parts along dimension 0, may hold values from 0 to 31, as said below
- adapter_entry: int32 [32], replicated, may hold values from 0 to 31, each once
- key_value_weight: bfloat16 [8192, 1024], P('tensor'), may hold values from -0.0625 to 0.0625
- adapter_down: bfloat16 [32, 8192, 128], P('batch', 'tensor'), may hold values from -0.0625 to 0.0625
- adapter_up: bfloat16 [32, 64, 1024], P('batch', None, 'tensor'), may hold values from -0.75 to 0.75
Outputs:
- projected: bfloat16 [6144, 1024], P(('groups', 'batch'), 'tensor'), parts along dimension 0
There are 2 independent parts, one for each index of `groups`. A program takes and returns all parts, laid end to end along the dimension named above; an argument that names none is the same for every part. Nothing has to cross between parts.
Inputs may be any that keep to these rules, and one draw needn't show every extreme that they name: `request_adapter`: on the rows of one device (aligned blocks of 768), one adapter appears exactly 48 times and every other at most 24 times; the adapter that appears 48 times is the same on every device of a group, and so is another one that appears exactly 24 times. `adapter_entry`: every entry once.
All inputs are finite; a program needn't handle non-finite values.
Results may differ from a plain program's by a relative error of at most 0.001.
Values may be sent and summed in bfloat16 or wider, within the bound.
No kernel may reach another device: no remote copies, remote signals or barrier semaphores. Data moves between devices by JAX's collectives and lax.ppermute only.
A program may use at most 64 MiB of HBM per device.

v0:
```python
import jax
import jax.numpy as jnp
from jax import lax
from jax.sharding import PartitionSpec as P

adapter_scale = 0.5


def pick_half(down_product, rank_columns, column_start, value_start):
    offset = jnp.where(column_start >= value_start, rank_columns, 0).astype(jnp.int32)
    return lax.dynamic_slice_in_dim(down_product, offset, rank_columns, down_product.ndim - 1)


def on_device(tokens, request_adapter, adapter_entry, key_value_weight, adapter_down, adapter_up):
    row_count, feat_width = tokens.shape
    total_adapters = adapter_entry.shape[0]
    adapters_held = adapter_down.shape[0]
    rank_columns = adapter_up.shape[1]
    output_width = adapter_up.shape[2]
    value_start = key_value_weight.shape[1] // 2
    home_count = lax.axis_size("batch")
    column_start = lax.axis_index("tensor") * output_width
    light_cap = row_count // total_adapters
    heavy_cap = 2 * light_cap
    partial_value = jnp.dot(tokens, key_value_weight, preferred_element_type=jnp.float32)
    base_product = lax.psum_scatter(partial_value, "tensor", scatter_dimension=1, tiled=True)
    adapter_range = jnp.arange(total_adapters, dtype=jnp.int32)
    onehot = (request_adapter[:, None] == adapter_range[None, :]).astype(jnp.int32)
    before = jnp.cumsum(onehot, axis=0) - onehot
    position = jnp.sum(before * onehot, axis=1)
    row_slot = jnp.sum(onehot * adapter_entry[None, :], axis=1)
    local_up_factor = adapter_up.astype(jnp.float32)
    send_mask = jnp.ones(request_adapter.shape, jnp.bool_)
    entry_total = total_adapters * heavy_cap
    entry_index = jnp.where(send_mask, row_slot * heavy_cap + position, entry_total)
    outgoing = (
        jnp.zeros((entry_total, feat_width), tokens.dtype).at[entry_index].set(tokens, mode="drop")
    )
    outgoing = outgoing.reshape(home_count, adapters_held, heavy_cap, feat_width)
    down_product = jnp.einsum(
        "sjcd,jdr->sjcr",
        lax.all_to_all(outgoing, "batch", split_axis=0, concat_axis=0, tiled=True),
        adapter_down,
        preferred_element_type=jnp.float32,
    )
    down_product = lax.psum(down_product, "tensor")
    picked_rows = pick_half(down_product, rank_columns, column_start, value_start)
    adapter_delta = jnp.einsum(
        "zpia,pab->zpib", picked_rows, local_up_factor, precision=lax.Precision.HIGHEST
    )
    restored_rows = lax.all_to_all(adapter_delta, "batch", split_axis=0, concat_axis=0, tiled=True)
    sorted_inputs = restored_rows.reshape(entry_total, output_width)
    adapter_delta = jnp.take(sorted_inputs, jnp.minimum(entry_index, entry_total - 1), axis=0)
    return (base_product + adapter_scale * adapter_delta).astype(jnp.bfloat16)


def solution(mesh):
    in_specs = (
        P(("groups", "batch"), "tensor"),
        P(("groups", "batch")),
        P(),
        P("tensor", None),
        P("batch", "tensor", None),
        P("batch", None, "tensor"),
    )
    out_specs = P(("groups", "batch"), "tensor")
    return jax.shard_map(
        on_device, mesh=mesh, in_specs=in_specs, out_specs=out_specs, check_vma=False
    )
```

profile of v0, /device:TPU:0, one launch (start us, length us, event | category | flops | bytes accessed | tf_op | source)
XLA Modules:
  0.0 258.4 jit_solution(12790789017316501572)
XLA Ops:
  6.5 0.0 copy-start
  6.5 0.0 all-reduce.2.cloned.1.call-start
  6.5 0.7 fusion.15
  7.3 1.7 reduce-window.6
  9.0 0.3 slice_reduce_fusion
  9.3 0.8 select_reduce_fusion
  10.2 11.6 %scatter_custom_fusion = bf16[1536,2048]{1,0:T(8,128)(2,1)} fusion(s32[768]{0:T(1024)S(1)} %get-tuple-element.6, bf16[768,2048]{1,0:T(8,128)(2,1)} %param.6, bf16[]{:T(256)} %constant.17.clone.1), kind=kCustom, calls=%fused_computation.5 | custom fusion | bytes 6291968 | tf_op jit(solution)/shard_map/scatter | solution.py:37
  21.8 0.0 copy-start.1
  21.8 144.7 %all_to_all.10 = bf16[4,8,48,2048]{3,2,1,0:T(8,128)(2,1)S(1)} all-to-all(bf16[4,8,48,2048]{3,2,1,0:T(8,128)(2,1)} %bitcast.42), channel_id=1, replica_groups=mesh['groups'=2,'batch'=4,'tensor'=4] {'batch'}, dimensions={0} | all-to-all | bytes 12582912 | tf_op jit(solution)/shard_map/all_to_all | solution.py:42
  166.5 0.0 copy-done.1
  166.5 0.0 copy-start.2
  166.5 2.7 %fusion.5 = f32[4,8,48,128]{3,2,0,1:T(8,128)} fusion(bf16[8,2048,128]{2,1,0:T(8,128)(2,1)S(1)} %copy-done.1, bf16[4,8,48,2048]{3,2,1,0:T(8,128)(2,1)S(1)} %all_to_all.10), kind=kOutput, calls=%fused_computation.8 | convolution fusion | flops 805306368 | bytes 11272192 | tf_op jit(solution)/shard_map/sjcd,jdr->sjcr/dot_general | solution.py:40
  169.1 0.0 all-reduce.2.cloned.1.call-update
  169.2 0.2 reduce-scatter.2.cloned.1.call-start
  169.4 0.0 copy-done.2
  169.4 7.3 %fusion.19 = f32[768,1024]{1,0:T(8,128)} fusion(bf16[768,2048]{1,0:T(8,128)(2,1)S(1)} %copy-done.2, bf16[2048,1024]{1,0:T(8,128)(2,1)} %param.9), kind=kOutput, calls=%fused_computation.31 | convolution fusion | flops 3221225472 | bytes 10485760 | tf_op jit(solution)/shard_map/dot_general | solution.py:25
  176.7 0.0 reduce-scatter.2.cloned.1.call-update
  176.7 26.7 %all-reduce.2.cloned.1.call-done = f32[4,8,48,128]{3,2,0,1:T(8,128)} async-done(((f32[4,8,48,128]{3,2,0,1:T(8,128)}), f32[4,8,48,128]{3,2,0,1:T(8,128)}) %all-reduce.2.cloned.1.call-update) | async-done | bytes 786448 | tf_op jit(solution)/shard_map/psum | solution.py:46
  203.4 0.0 copy-done
  203.4 2.0 convolution_bitcast_fusion
  205.4 1.3 copy.16
  206.7 4.6 %all-to-all-start.1 = ((f32[4,8,48,256]{3,2,1,0:T(8,128)}), f32[4,8,48,256]{3,2,1,0:T(8,128)S(1)}, u32[]{:S(2)}, u32[]{:S(2)}) async-start(f32[4,8,48,256]{3,2,1,0:T(8,128)} %copy.16), calls=%async_computation.2 | async-start | bytes 3145728 | tf_op jit(solution)/shard_map/all_to_all | solution.py:51
  211.3 36.1 %all-to-all-done.1 = f32[4,8,48,256]{3,2,1,0:T(8,128)S(1)} async-done(((f32[4,8,48,256]{3,2,1,0:T(8,128)}), f32[4,8,48,256]{3,2,1,0:T(8,128)S(1)}, u32[]{:S(2)}, u32[]{:S(2)}) %all-to-all-start.1) | async-done | bytes 1572896 | tf_op jit(solution)/shard_map/all_to_all | solution.py:51
  247.4 2.1 gather_fusion
  249.5 0.0 reduce-scatter.2.cloned.1.call-done
  249.5 2.1 add_convert_fusion
  (4 shorter events, 0.1 us)
Async XLA Ops:
  6.5 196.9 %copy-start = (bf16[8,64,256]{2,1,0:T(8,128)(2,1)S(1)}, bf16[8,64,256]{2,1,0:T(8,128)(2,1)}, u32[]{:S(2)}) copy-start(bf16[8,64,256]{2,1,0:T(8,128)(2,1)} %param.11) | copy-start | bytes 786436
  6.5 196.9 %all-reduce.2.cloned.1.call-start = ((), (), s32[]{:S(2)}) async-start(), calls=%async_computation.4 | async-start | bytes 1572864 | tf_op jit(solution)/shard_map/psum | solution.py:46
  21.8 144.7 %copy-start.1 = (bf16[8,2048,128]{2,1,0:T(8,128)(2,1)S(1)}, bf16[8,2048,128]{2,1,0:T(8,128)(2,1)}, u32[]{:S(2)}) copy-start(bf16[8,2048,128]{2,1,0:T(8,128)(2,1)} %param.10) | copy-start | bytes 12582916
  166.5 2.9 %copy-start.2 = (bf16[768,2048]{1,0:T(8,128)(2,1)S(1)}, bf16[768,2048]{1,0:T(8,128)(2,1)}, u32[]{:S(2)}) copy-start(bf16[768,2048]{1,0:T(8,128)(2,1)} %param.6) | copy-start | bytes 9437188
  169.2 80.3 %reduce-scatter.2.cloned.1.call-start = ((), (), s32[]{:S(2)}) async-start(), calls=%async_computation.3 | async-start | bytes 3932160 | tf_op jit(solution)/shard_map/reduce_scatter | solution.py:26
  206.7 40.7 %all-to-all-start.1 = ((f32[4,8,48,256]{3,2,1,0:T(8,128)}), f32[4,8,48,256]{3,2,1,0:T(8,128)S(1)}, u32[]{:S(2)}, u32[]{:S(2)}) async-start(f32[4,8,48,256]{3,2,1,0:T(8,128)} %copy.16), calls=%async_computation.2 | async-start | bytes 3145728 | tf_op jit(solution)/shard_map/all_to_all | solution.py:51
Sparse Core Ops, SparseCore 0:
  169.3 34.0 all-reduce.1
  205.9 37.9 reduce-scatter.1
where the time goes:
time: 259 us; the launch traced here: 258 us
  blocking collectives  145 us (56%)
  waiting for transfers between devices  62.8 us (24%)
  local copies, waits for them, and re-layouts  15.2 us (6%)
  between operations  13.5 us (5%)
  matrix products  11.9 us (5%)
  other arithmetic  5.45 us (2%)
  starting transfers between devices  4.82 us (2%)
    all_to_all x1, blocking collectives, on_device(): lax.all_to_all(outgoing, 'batch', split_axis=0, concat_axis=0, tiled=True)  145 us
    all_to_all x1, waiting for transfers between devices, on_device(): lax.all_to_all(adapter_delta, 'batch', split_axis=0, concat_axis=0, tiled...  36.1 us
    psum x1, waiting for transfers between devices, on_device(): down_product = lax.psum(down_product, 'tensor')  26.7 us
    scatter x1, local copies, waits for them, and re-layouts, on_device(): jnp.zeros((entry_total, feat_width), tokens.dtype).at[entry_index]  11.6 us
    dot_general x1, matrix products, on_device(): jnp.dot(tokens, key_value_weight, preferred_element_type=jnp.float32)  7.29 us
  transfers between devices with their start and end apart: 3, of which 2 were waited for; matrix products, arithmetic and copies ran while one was open for 5% of the time, Pallas kernels for 0%

commit v1 on v0

v1 whole, which is shorter than its diff:
```python
import functools

import jax
import jax.numpy as jnp
from jax import lax
from jax.experimental import pallas as pl
from jax.experimental.pallas import tpu as pltpu
from jax.sharding import PartitionSpec as P

adapter_scale = 0.5
VMEM_BYTES = 48 * 1024 * 1024


def pack_kernel(homes, held, light, place_ref, request_ref, entry_ref, tokens_ref, *out_refs):
    index_ref, heavy_ref, block_refs = out_refs[0], out_refs[1], out_refs[2:]
    rows = tokens_ref.shape[0]
    adapters = entry_ref.shape[0]
    span = (held + 1) * light
    request = request_ref[...]
    onehot = lax.broadcasted_iota(jnp.int32, (adapters, rows), 0) == request
    earlier = lax.broadcasted_iota(jnp.int32, (rows, rows), 0) < lax.broadcasted_iota(
        jnp.int32, (rows, rows), 1
    )
    before = jnp.dot(
        onehot.astype(jnp.bfloat16), earlier.astype(jnp.bfloat16), preferred_element_type=jnp.float32
    )
    position = jnp.sum(jnp.where(onehot, before, 0.0), axis=0, keepdims=True).astype(jnp.int32)
    slot = jnp.sum(jnp.where(onehot, entry_ref[...], 0), axis=0, keepdims=True)
    home = slot // held
    relative = lax.rem(home - place_ref[0] + homes, homes)
    inside = jnp.where(
        position < light, (slot - home * held) * light + position, held * light + position - light
    )
    index = relative * span + inside
    index_ref[...] = index
    heavy = jnp.max(jnp.where(position >= light, slot, 0), axis=1, keepdims=True)
    heavy_ref[...] = jnp.broadcast_to(heavy, heavy_ref.shape)
    local = lax.broadcasted_iota(jnp.int32, (span, rows), 0)
    for r in range(homes):
        choose = (local + r * span == index).astype(jnp.bfloat16)
        block_refs[r][...] = jnp.dot(
            choose, tokens_ref[...], preferred_element_type=jnp.float32
        ).astype(jnp.bfloat16)


def pack(tokens, request_adapter, adapter_entry, place, homes, held, light):
    rows, width = tokens.shape
    span = (held + 1) * light
    vmem = pl.BlockSpec(memory_space=pltpu.VMEM)
    out = pl.pallas_call(
        functools.partial(pack_kernel, homes, held, light),
        out_shape=[
            jax.ShapeDtypeStruct((1, rows), jnp.int32),
            jax.ShapeDtypeStruct((8, 128), jnp.int32),
        ]
        + [jax.ShapeDtypeStruct((span, width), jnp.bfloat16)] * homes,
        in_specs=[pl.BlockSpec(memory_space=pltpu.SMEM), vmem, vmem, vmem],
        out_specs=[vmem] * (homes + 2),
        compiler_params=pltpu.CompilerParams(vmem_limit_bytes=VMEM_BYTES),
        name="pack",
    )(place.reshape(1), request_adapter.reshape(1, rows), adapter_entry.reshape(-1, 1), tokens)
    return out[0], out[1][0, 0], out[2:]


def split_pair(value):
    high = value.astype(jnp.bfloat16)
    low = (value - high.astype(jnp.float32)).astype(jnp.bfloat16)
    return high, low


def finish_kernel(homes, held, light, place_ref, index_ref, base_ref, up_ref, *refs):
    shrink_refs, out_ref, high_ref, low_ref = refs[:homes], refs[homes], refs[homes + 1], refs[homes + 2]
    span = (held + 1) * light
    rows = base_ref.shape[0]

    def expand(shrink, entry, start):
        high, low = split_pair(shrink)
        factor = up_ref[entry]
        delta = jnp.dot(high, factor, preferred_element_type=jnp.float32) + jnp.dot(
            low, factor, preferred_element_type=jnp.float32
        )
        high, low = split_pair(delta)
        high_ref[pl.ds(start, light), :] = high
        low_ref[pl.ds(start, light), :] = low

    heavy = place_ref[1]
    for r in range(homes):
        home = lax.rem(place_ref[0] + r, homes)
        for k in range(held):
            expand(shrink_refs[r][k * light : (k + 1) * light, :], home * held + k, r * span + k * light)
        expand(shrink_refs[r][held * light :, :], heavy, r * span + held * light)
    choose = (
        lax.broadcasted_iota(jnp.int32, (rows, homes * span), 1) == index_ref[...]
    ).astype(jnp.bfloat16)
    delta = jnp.dot(choose, high_ref[...], preferred_element_type=jnp.float32) + jnp.dot(
        choose, low_ref[...], preferred_element_type=jnp.float32
    )
    out_ref[...] = (base_ref[...] + adapter_scale * delta).astype(jnp.bfloat16)


def finish(place, heavy, index, base, up, shrinks, homes, held, light):
    rows, columns = base.shape
    span = (held + 1) * light
    vmem = pl.BlockSpec(memory_space=pltpu.VMEM)
    return pl.pallas_call(
        functools.partial(finish_kernel, homes, held, light),
        out_shape=jax.ShapeDtypeStruct((rows, columns), jnp.bfloat16),
        in_specs=[pl.BlockSpec(memory_space=pltpu.SMEM)] + [vmem] * (3 + homes),
        out_specs=vmem,
        scratch_shapes=[pltpu.VMEM((homes * span, columns), jnp.bfloat16)] * 2,
        compiler_params=pltpu.CompilerParams(vmem_limit_bytes=VMEM_BYTES),
        name="finish",
    )(jnp.stack([place, heavy]), index.reshape(rows, 1), base, up, *shrinks)


def on_device(tokens, request_adapter, adapter_entry, key_value_weight, adapter_down, adapter_up):
    rows, width = tokens.shape
    adapters = adapter_entry.shape[0]
    held, rank, columns = adapter_up.shape
    value_start = key_value_weight.shape[1] // 2
    homes = lax.axis_size("batch")
    pieces = lax.axis_size("tensor")
    place = lax.axis_index("batch").astype(jnp.int32)
    piece = lax.axis_index("tensor").astype(jnp.int32)
    light = rows // adapters

    index, heavy, blocks = pack(tokens, request_adapter, adapter_entry, place, homes, held, light)
    arrived = [blocks[0]] + [
        lax.ppermute(blocks[r], "batch", [(i, (i + r) % homes) for i in range(homes)])
        for r in range(1, homes)
    ]
    up = lax.all_gather(adapter_up, "batch", axis=0, tiled=True)
    partial = jnp.dot(tokens, key_value_weight, preferred_element_type=jnp.float32)
    base = lax.psum_scatter(partial, "tensor", scatter_dimension=1, tiled=True)

    heavy_here = heavy // held == place
    heavy_factor = lax.dynamic_index_in_dim(
        adapter_down, lax.rem(heavy, held), axis=0, keepdims=False
    )

    def half_of(value, other):
        return jnp.where(other * columns >= value_start, value[:, rank:], value[:, :rank])

    shrinks = []
    for r in range(homes):
        block = arrived[r]
        ordinary = jnp.einsum(
            "jcd,jdr->jcr",
            block[: held * light].reshape(held, light, width),
            adapter_down,
            preferred_element_type=jnp.float32,
        ).reshape(held * light, 2 * rank)
        extra = jnp.dot(block[held * light :], heavy_factor, preferred_element_type=jnp.float32)
        value = jnp.concatenate([ordinary, jnp.where(heavy_here, extra, 0.0)], axis=0)
        total = half_of(value, piece)
        for o in range(1, pieces):
            total = total + lax.ppermute(
                half_of(value, piece ^ o), "tensor", [(i, i ^ o) for i in range(pieces)]
            )
        if r:
            total = lax.ppermute(total, "batch", [(i, (i - r) % homes) for i in range(homes)])
        shrinks.append(total)
    return finish(place, heavy, index, base, up, shrinks, homes, held, light)


def solution(mesh):
    in_specs = (
        P(("groups", "batch"), "tensor"),
        P(("groups", "batch")),
        P(),
        P("tensor", None),
        P("batch", "tensor", None),
        P("batch", None, "tensor"),
    )
    out_specs = P(("groups", "batch"), "tensor")
    return jax.shard_map(
        on_device, mesh=mesh, in_specs=in_specs, out_specs=out_specs, check_vma=False
    )
```

time: 259 us -> 161 us (0.62)
  blocking collectives: 145 us -> 0 us
  waiting for transfers between devices: 62.8 us -> 85.9 us
  starting transfers between devices: 4.82 us -> 18.8 us
  matrix products: 11.9 us -> 20.9 us
  Pallas kernels: 0 us -> 8.79 us
  local copies, waits for them, and re-layouts: 15.2 us -> 7.73 us
  other arithmetic: 5.45 us -> 1.31 us
  between operations: 13.5 us -> 17.4 us
    all_to_all x1 -> x0, blocking collectives: 145 us -> none  [on_device(): lax.all_to_all(outgoing, 'batch', split_axis=0, concat_axis=0, tiled=True)]
    ppermute x0 -> x18, waiting for transfers between devices: none -> 85.2 us  [the longest x3 69.7 us: on_device(): lax.ppermute(blocks[r], 'batch', [(i, (i + r) % homes) for i in range(hom...]
    all_to_all x1 -> x0, waiting for transfers between devices: 36.1 us -> none  [on_device(): lax.all_to_all(adapter_delta, 'batch', split_axis=0, concat_axis=0, tiled...]
    psum x1 -> x0, waiting for transfers between devices: 26.7 us -> none  [on_device(): down_product = lax.psum(down_product, 'tensor')]
    ppermute x0 -> x18, starting transfers between devices: none -> 18.8 us  [the longest x12 8.79 us: on_device(): lax.ppermute(half_of(value, piece ^ o), 'tensor', [(i, i ^ o) for i in ra...]
    scatter x1 -> x0, local copies, waits for them, and re-layouts: 11.6 us -> none  [on_device(): jnp.zeros((entry_total, feat_width), tokens.dtype).at[entry_index]]
    pallas_call x0 -> x2, Pallas kernels: none -> 8.79 us  [the longest x1 6.07 us: pack(): pl.pallas_call(functools.partial(pack_kernel, homes, held, light), out_sh...]
    dot_general x2 -> x8, matrix products: 4.64 us -> 12.7 us  [the longest x4 7.99 us: on_device(): jnp.einsum('jcd,jdr->jcr', block[:held * light].reshape(held, light, widt...]
  transfers between devices with their start and end apart: 3 -> 20, of which waited for: 2 -> 7; matrix products, arithmetic and copies ran while one was open for 5% -> 17% of each run, Pallas kernels for 0% -> 4%
where the time goes in v1:
time: 161 us
  waiting for transfers between devices  85.9 us (53%)
  matrix products  20.9 us (13%)
  starting transfers between devices  18.8 us (12%)
  between operations  17.4 us (11%)
  Pallas kernels  8.79 us (5%)
  local copies, waits for them, and re-layouts  7.73 us (5%)
    ppermute x3, waiting for transfers between devices, on_device(): lax.ppermute(blocks[r], 'batch', [(i, (i + r) % homes) for i in range(hom...  69.7 us
    ppermute x12, starting transfers between devices, on_device(): lax.ppermute(half_of(value, piece ^ o), 'tensor', [(i, i ^ o) for i in ra...  8.79 us
    dot_general x1, matrix products, on_device(): jnp.dot(tokens, key_value_weight, preferred_element_type=jnp.float32)  8.19 us
    dot_general x4, matrix products, on_device(): jnp.einsum('jcd,jdr->jcr', block[:held * light].reshape(held, light, widt...  7.99 us
    ppermute x12, waiting for transfers between devices, on_device(): lax.ppermute(half_of(value, piece ^ o), 'tensor', [(i, i ^ o) for i in ra...  7.71 us
    ppermute x3, waiting for transfers between devices, on_device(): lax.ppermute(total, 'batch', [(i, (i - r) % homes) for i in range(homes)])  7.71 us
    ppermute x3, starting transfers between devices, on_device(): lax.ppermute(blocks[r], 'batch', [(i, (i + r) % homes) for i in range(hom...  6.12 us
    pallas_call x1, Pallas kernels, pack(): pl.pallas_call(functools.partial(pack_kernel, homes, held, light), out_sh...  6.07 us
  transfers between devices with their start and end apart: 20, of which 7 were waited for; matrix products, arithmetic and copies ran while one was open for 17% of the time, Pallas kernels for 4%

profile of v1, /device:TPU:0, one launch (start us, length us, event | category | flops | bytes accessed | tf_op | source)
XLA Modules:
  0.0 160.9 jit_solution(3994640566876451131)
XLA Ops:
  7.4 0.7 all-gather.2.cloned.1.call-update
  8.2 8.2 %fusion.16 = f32[768,1024]{1,0:T(8,128)} fusion(bf16[768,2048]{1,0:T(8,128)(2,1)} %tokens_ref.1, bf16[2048,1024]{1,0:T(8,128)(2,1)} %param.9), kind=kOutput, calls=%fused_computation.45 | convolution fusion | flops 3221225472 | bytes 10485760 | tf_op jit(solution)/shard_map/dot_general | solution.py:133
  16.4 0.1 copy.10.entry_ref
  16.5 6.1 %pack.1 = (s32[1,768]{1,0:T(1,128)S(1)}, s32[8,128]{1,0:T(8,128)S(1)}, bf16[216,2048]{1,0:T(8,128)(2,1)S(1)}, bf16[216,2048]{1,0:T(8,128)(2,1)S(1)}, bf16[216,20...) custom-call(s32[1]{0:T(128)} %bitcast.place_ref, s32[1,768]{1,0:T(1,128)S(1)} %reshape.34.request_ref, ...), custom_call_target="tpu_custom_call" | custom-call | tf_op jit(solution)/shard_map/pack/pallas_call | solution.py:50
  22.5 5.1 %collective-permute-start.13 = (bf16[216,2048]{1,0:T(8,128)(2,1)}, bf16[216,2048]{1,0:T(8,128)(2,1)}, u32[]{:S(2)}, u32[]{:S(2)}) collective-permute-start(bf16[216,2048]{1,0:T(8,128)(2,1)} %get-tuple-element.16), channel_id=1, source_target_pairs={{0,12},{4,0},{8,4},{12,8},{1,13},{5,1},{9,5},{13,9},{2,14},{6,2},{... | collective-permute-start | bytes 2654216 | tf_op jit(solution)/shard_map/ppermute | solution.py:129
  27.7 1.0 collective-permute-start.3
  28.7 0.5 slice.34
  31.5 1.2 convolution_select_fusion.3
  32.8 1.0 slice.35
  33.7 3.2 %fusion.17 = f32[8,24,128]{2,1,0:T(8,128)S(1)} fusion(bf16[8,24,2048]{2,1,0:T(8,128)(2,1)} %bitcast.33, bf16[8,2048,128]{2,1,0:T(8,128)(2,1)} %param.10), kind=kOutput, calls=%fused_computation.46 | convolution fusion | flops 100663296 | bytes 5079040 | tf_op jit(solution)/shard_map/jcd,jdr->jcr/dot_general | solution.py:147
  37.0 0.1 broadcast_select_fusion.11
  37.1 1.6 collective-permute-start.1
  38.7 0.2 copy.11.index_ref
  38.9 0.7 pad_add_fusion.place_ref
  39.5 19.2 %collective-permute-done.13 = bf16[216,2048]{1,0:T(8,128)(2,1)} collective-permute-done((bf16[216,2048]{1,0:T(8,128)(2,1)}, bf16[216,2048]{1,0:T(8,128)(2,1)}, u32[]{:S(2)}, u32[]{:S(2)}) %collective-permute-start.13) | collective-permute-done | bytes 884768 | tf_op jit(solution)/shard_map/ppermute | solution.py:129
  58.7 1.2 slice.102
  59.9 1.3 convolution_select_fusion
  61.2 3.2 %fusion.20 = f32[8,24,128]{2,1,0:T(8,128)S(1)} fusion(bf16[8,24,2048]{2,1,0:T(8,128)(2,1)S(1)} %bitcast.36, bf16[8,2048,128]{2,1,0:T(8,128)(2,1)} %param.10), kind=kOutput, calls=%fused_computation.49 | convolution fusion | flops 100663296 | bytes 5079040 | tf_op jit(solution)/shard_map/jcd,jdr->jcr/dot_general | solution.py:147
  64.4 0.1 broadcast_select_fusion.8
  64.5 1.5 collective-permute-start.15
  66.1 50.6 %collective-permute-done.8 = bf16[216,2048]{1,0:T(8,128)(2,1)} collective-permute-done((bf16[216,2048]{1,0:T(8,128)(2,1)S(1)}, bf16[216,2048]{1,0:T(8,128)(2,1)}, u32[]{:S(2)}, u32[]{:S(2)}) %collective-permute-start.8) | collective-permute-done | bytes 884768 | tf_op jit(solution)/shard_map/ppermute | solution.py:129
  116.6 1.0 collective-permute-start.16
  117.6 1.2 slice.98
  118.8 0.7 collective-permute-start.14
  119.5 1.2 slice.94
  120.7 1.1 convolution_select_fusion.1
  121.8 0.8 fusion.19
  122.6 0.1 broadcast_select_fusion.9
  122.7 1.1 convolution_select_fusion.2
  123.8 0.8 fusion.18
  124.6 0.1 broadcast_select_fusion.10
  124.8 0.6 collective-permute-start.10
  125.4 0.8 collective-permute-start.11
  126.2 0.8 collective-permute-start.9
  127.0 0.1 add_add_fusion
  127.1 3.7 %collective-permute-done.10 = f32[216,64]{1,0:T(8,128)S(1)} collective-permute-done((f32[216,64]{1,0:T(8,128)S(1)}, f32[216,64]{1,0:T(8,128)S(1)}, u32[]{:S(2)}, u32[]{:S(2)}) %collective-permute-start.10) | collective-permute-done | bytes 55328 | tf_op jit(solution)/shard_map/ppermute | solution.py:157
  130.8 0.1 collective-permute-start.5
  130.9 0.3 collective-permute-done.11
  131.3 1.5 collective-permute-start.6
  132.7 0.2 collective-permute-start.4
  133.0 3.6 %collective-permute-done.5 = f32[216,64]{1,0:T(8,128)S(1)} collective-permute-done((f32[216,64]{1,0:T(8,128)S(1)}, f32[216,64]{1,0:T(8,128)S(1)}, u32[]{:S(2)}, u32[]{:S(2)}) %collective-permute-start.5) | collective-permute-done | bytes 55328 | tf_op jit(solution)/shard_map/ppermute | solution.py:157
  136.6 0.1 collective-permute-start.12
  136.8 3.8 %collective-permute-start.7 = (f32[216,64]{1,0:T(8,128)S(1)}, f32[216,64]{1,0:T(8,128)S(1)}, u32[]{:S(2)}, u32[]{:S(2)}) collective-permute-start(f32[216,64]{1,0:T(8,128)S(1)} %add_add_fusion.2), channel_id=1, source_target_pairs={{0,12},{4,0},{8,4},{12,8},{1,13},{5,1},{9,5},{13,9},{2,14},{6,2},{... | collective-permute-start | bytes 165896 | tf_op jit(solution)/shard_map/ppermute | solution.py:161
  140.6 3.9 %collective-permute-done.17.refs_3_ = f32[216,64]{1,0:T(8,128)S(1)} collective-permute-done((f32[216,64]{1,0:T(8,128)S(1)}, f32[216,64]{1,0:T(8,128)S(1)}, u32[]{:S(2)}, u32[]{:S(2)}) %collective-permute-start.17) | collective-permute-done | bytes 55328 | tf_op jit(solution)/shard_map/ppermute | solution.py:161
  144.5 3.8 %collective-permute-done.12.refs_2_ = f32[216,64]{1,0:T(8,128)S(1)} collective-permute-done((f32[216,64]{1,0:T(8,128)S(1)}, f32[216,64]{1,0:T(8,128)S(1)}, u32[]{:S(2)}, u32[]{:S(2)}) %collective-permute-start.12) | collective-permute-done | bytes 55328 | tf_op jit(solution)/shard_map/ppermute | solution.py:161
  148.3 1.2 copy-done
  149.6 1.1 copy-done.1
  150.7 2.7 %finish.1 = bf16[768,256]{1,0:T(8,128)(2,1)} custom-call(s32[2]{0:T(128)S(1)} %pad_add_fusion.place_ref, s32[768,1]{1,0:T(8,128)S(1)} %copy.11.index_ref, f32[768,256]{1,0:T(8,128)S(1)} %copy-done.1, bf16[32,64,256]{2,1,0:T(8,128)(2,1)S(1)} %copy-done, f32[216,64]{1,0:T(8,128)S(1)} %add_add_fusion.3.refs_0_, f32[216,64]{1,0:T(8,128)S(1)} %collective-permute-done.7.refs_1_, ...), custom_call_target="tpu_custom_call" | custom-call | tf_op jit(solution)/shard_map/finish/pallas_call | solution.py:105
  (36 shorter events, 0.3 us)
Async XLA Ops:
  7.4 141.0 %all-gather.2.cloned.1.call-start = ((), (), s32[]{:S(2)}) async-start(), calls=%async_computation.2 | async-start | bytes 1310720 | tf_op jit(solution)/shard_map/all_gather | solution.py:132
  8.1 8.3 %copy-start.4 = (s32[32]{0:T(128)S(1)}, s32[32]{0:T(128)}, u32[]{:S(2)}) copy-start(s32[32]{0:T(128)} %param.8) | copy-start | bytes 388
  8.1 8.4 %copy-start.3 = (s32[768]{0:T(1024)S(1)}, s32[768]{0:T(1024)}, u32[]{:S(2)}) copy-start(s32[768]{0:T(1024)} %param.7) | copy-start | bytes 9220
  8.1 140.2 %reduce-scatter.2.cloned.1.call-start = ((), (), s32[]{:S(2)}) async-start(), calls=%async_computation.1 | async-start | bytes 3932160 | tf_op jit(solution)/shard_map/reduce_scatter | solution.py:134
  22.5 36.1 %collective-permute-start.13 = (bf16[216,2048]{1,0:T(8,128)(2,1)}, bf16[216,2048]{1,0:T(8,128)(2,1)}, u32[]{:S(2)}, u32[]{:S(2)}) collective-permute-start(bf16[216,2048]{1,0:T(8,128)(2,1)} %get-tuple-element.16), channel_id=1, source_target_pairs={{0,12},{4,0},{8,4},{12,8},{1,13},{5,1},{9,5},{13,9},{2,14},{6,2},{... | collective-permute-start | bytes 2654216 | tf_op jit(solution)/shard_map/ppermute | solution.py:129
  27.7 89.0 %collective-permute-start.8 = (bf16[216,2048]{1,0:T(8,128)(2,1)S(1)}, bf16[216,2048]{1,0:T(8,128)(2,1)}, u32[]{:S(2)}, u32[]{:S(2)}) collective-permute-start(bf16[216,2048]{1,0:T(8,128)(2,1)S(1)} %get-tuple-element.15), channel_id=1, source_target_pairs={{0,8},{4,12},{8,0},{12,4},{1,9},{5,13},{9,1},{13,5},{2,10},{6,14},... | collective-permute-start | bytes 2654216 | tf_op jit(solution)/shard_map/ppermute | solution.py:129
  27.7 91.1 %collective-permute-start.3 = (bf16[216,2048]{1,0:T(8,128)(2,1)S(1)}, bf16[216,2048]{1,0:T(8,128)(2,1)}, u32[]{:S(2)}, u32[]{:S(2)}) collective-permute-start(bf16[216,2048]{1,0:T(8,128)(2,1)S(1)} %get-tuple-element.14), channel_id=1, source_target_pairs={{0,4},{4,8},{8,12},{12,0},{1,5},{5,9},{9,13},{13,1},{2,6},{6,10},{... | collective-permute-start | bytes 2654216 | tf_op jit(solution)/shard_map/ppermute | solution.py:129
  37.1 99.7 %collective-permute-start.1 = (f32[216,64]{1,0:T(8,128)S(1)}, f32[216,64]{1,0:T(8,128)S(1)}, u32[]{:S(2)}, u32[]{:S(2)}) collective-permute-start(f32[216,64]{1,0:T(8,128)S(1)} %get-tuple-element.31), channel_id=1, source_target_pairs={{0,2},{1,3},{2,0},{3,1},{4,6},{5,7},{6,4},{7,5},{8,10},{9,11},{10,... | collective-permute-start | bytes 165896 | tf_op jit(solution)/shard_map/ppermute | solution.py:157
  38.7 101.9 %collective-permute-start.2 = (f32[216,64]{1,0:T(8,128)S(1)}, f32[216,64]{1,0:T(8,128)S(1)}, u32[]{:S(2)}, u32[]{:S(2)}) collective-permute-start(f32[216,64]{1,0:T(8,128)S(1)} %get-tuple-element.32), channel_id=1, source_target_pairs={{0,3},{1,2},{2,1},{3,0},{4,7},{5,6},{6,5},{7,4},{8,11},{9,10},{10,... | collective-permute-start | bytes 165896 | tf_op jit(solution)/shard_map/ppermute | solution.py:157
  61.2 59.5 %copy-start.2 = (bf16[8,2048,128]{2,1,0:T(8,128)(2,1)S(1)}, bf16[8,2048,128]{2,1,0:T(8,128)(2,1)}, u32[]{:S(2)}) copy-start(bf16[8,2048,128]{2,1,0:T(8,128)(2,1)} %param.10) | copy-start | bytes 12582916
  64.5 60.3 %collective-permute-start.15 = (f32[216,64]{1,0:T(8,128)S(1)}, f32[216,64]{1,0:T(8,128)S(1)}, u32[]{:S(2)}, u32[]{:S(2)}) collective-permute-start(f32[216,64]{1,0:T(8,128)S(1)} %get-tuple-element.25), channel_id=1, source_target_pairs={{0,2},{1,3},{2,0},{3,1},{4,6},{5,7},{6,4},{7,5},{8,10},{9,11},{10,... | collective-permute-start | bytes 165896 | tf_op jit(solution)/shard_map/ppermute | solution.py:157
  116.6 8.8 %collective-permute-start.16 = (f32[216,64]{1,0:T(8,128)S(1)}, f32[216,64]{1,0:T(8,128)S(1)}, u32[]{:S(2)}, u32[]{:S(2)}) collective-permute-start(f32[216,64]{1,0:T(8,128)S(1)} %get-tuple-element.26), channel_id=1, source_target_pairs={{0,3},{1,2},{2,1},{3,0},{4,7},{5,6},{6,5},{7,4},{8,11},{9,10},{10,... | collective-permute-start | bytes 165896 | tf_op jit(solution)/shard_map/ppermute | solution.py:157
  118.8 7.4 %collective-permute-start.14 = (f32[216,64]{1,0:T(8,128)S(1)}, f32[216,64]{1,0:T(8,128)S(1)}, u32[]{:S(2)}, u32[]{:S(2)}) collective-permute-start(f32[216,64]{1,0:T(8,128)S(1)} %get-tuple-element.17), channel_id=1, source_target_pairs={{0,1},{1,0},{2,3},{3,2},{4,5},{5,4},{6,7},{7,6},{8,9},{9,8},{10,11... | collective-permute-start | bytes 165896 | tf_op jit(solution)/shard_map/ppermute | solution.py:157
  124.8 6.0 %collective-permute-start.10 = (f32[216,64]{1,0:T(8,128)S(1)}, f32[216,64]{1,0:T(8,128)S(1)}, u32[]{:S(2)}, u32[]{:S(2)}) collective-permute-start(f32[216,64]{1,0:T(8,128)S(1)} %get-tuple-element.27), channel_id=1, source_target_pairs={{0,2},{1,3},{2,0},{3,1},{4,6},{5,7},{6,4},{7,5},{8,10},{9,11},{10,... | collective-permute-start | bytes 165896 | tf_op jit(solution)/shard_map/ppermute | solution.py:157
  125.4 5.8 %collective-permute-start.11 = (f32[216,64]{1,0:T(8,128)S(1)}, f32[216,64]{1,0:T(8,128)S(1)}, u32[]{:S(2)}, u32[]{:S(2)}) collective-permute-start(f32[216,64]{1,0:T(8,128)S(1)} %get-tuple-element.28), channel_id=1, source_target_pairs={{0,3},{1,2},{2,1},{3,0},{4,7},{5,6},{6,5},{7,4},{8,11},{9,10},{10,... | collective-permute-start | bytes 165896 | tf_op jit(solution)/shard_map/ppermute | solution.py:157
  126.2 6.5 %collective-permute-start.9 = (f32[216,64]{1,0:T(8,128)S(1)}, f32[216,64]{1,0:T(8,128)S(1)}, u32[]{:S(2)}, u32[]{:S(2)}) collective-permute-start(f32[216,64]{1,0:T(8,128)S(1)} %get-tuple-element.19), channel_id=1, source_target_pairs={{0,1},{1,0},{2,3},{3,2},{4,5},{5,4},{6,7},{7,6},{8,9},{9,8},{10,11... | collective-permute-start | bytes 165896 | tf_op jit(solution)/shard_map/ppermute | solution.py:157
  130.8 5.8 %collective-permute-start.5 = (f32[216,64]{1,0:T(8,128)S(1)}, f32[216,64]{1,0:T(8,128)S(1)}, u32[]{:S(2)}, u32[]{:S(2)}) collective-permute-start(f32[216,64]{1,0:T(8,128)S(1)} %get-tuple-element.29), channel_id=1, source_target_pairs={{0,2},{1,3},{2,0},{3,1},{4,6},{5,7},{6,4},{7,5},{8,10},{9,11},{10,... | collective-permute-start | bytes 165896 | tf_op jit(solution)/shard_map/ppermute | solution.py:157
  131.3 5.4 %collective-permute-start.6 = (f32[216,64]{1,0:T(8,128)S(1)}, f32[216,64]{1,0:T(8,128)S(1)}, u32[]{:S(2)}, u32[]{:S(2)}) collective-permute-start(f32[216,64]{1,0:T(8,128)S(1)} %get-tuple-element.30), channel_id=1, source_target_pairs={{0,3},{1,2},{2,1},{3,0},{4,7},{5,6},{6,5},{7,4},{8,11},{9,10},{10,... | collective-permute-start | bytes 165896 | tf_op jit(solution)/shard_map/ppermute | solution.py:157
  132.7 3.9 %collective-permute-start.4 = (f32[216,64]{1,0:T(8,128)S(1)}, f32[216,64]{1,0:T(8,128)S(1)}, u32[]{:S(2)}, u32[]{:S(2)}) collective-permute-start(f32[216,64]{1,0:T(8,128)S(1)} %get-tuple-element.21), channel_id=1, source_target_pairs={{0,1},{1,0},{2,3},{3,2},{4,5},{5,4},{6,7},{7,6},{8,9},{9,8},{10,11... | collective-permute-start | bytes 165896 | tf_op jit(solution)/shard_map/ppermute | solution.py:157
  136.6 3.9 %collective-permute-start = (f32[216,64]{1,0:T(8,128)S(1)}, f32[216,64]{1,0:T(8,128)S(1)}, u32[]{:S(2)}, u32[]{:S(2)}) collective-permute-start(f32[216,64]{1,0:T(8,128)S(1)} %get-tuple-element.23), channel_id=1, source_target_pairs={{0,1},{1,0},{2,3},{3,2},{4,5},{5,4},{6,7},{7,6},{8,9},{9,8},{10,11... | collective-permute-start | bytes 165896 | tf_op jit(solution)/shard_map/ppermute | solution.py:157
  136.6 7.9 %collective-permute-start.17 = (f32[216,64]{1,0:T(8,128)S(1)}, f32[216,64]{1,0:T(8,128)S(1)}, u32[]{:S(2)}, u32[]{:S(2)}) collective-permute-start(f32[216,64]{1,0:T(8,128)S(1)} %add_add_fusion), channel_id=1, source_target_pairs={{0,4},{4,8},{8,12},{12,0},{1,5},{5,9},{9,13},{13,1},{2,6},{6,10},{... | collective-permute-start | bytes 165896 | tf_op jit(solution)/shard_map/ppermute | solution.py:161
  136.6 11.7 %collective-permute-start.12 = (f32[216,64]{1,0:T(8,128)S(1)}, f32[216,64]{1,0:T(8,128)S(1)}, u32[]{:S(2)}, u32[]{:S(2)}) collective-permute-start(f32[216,64]{1,0:T(8,128)S(1)} %add_add_fusion.1), channel_id=1, source_target_pairs={{0,8},{4,12},{8,0},{12,4},{1,9},{5,13},{9,1},{13,5},{2,10},{6,14},... | collective-permute-start | bytes 165896 | tf_op jit(solution)/shard_map/ppermute | solution.py:161
  136.8 11.5 %collective-permute-start.7 = (f32[216,64]{1,0:T(8,128)S(1)}, f32[216,64]{1,0:T(8,128)S(1)}, u32[]{:S(2)}, u32[]{:S(2)}) collective-permute-start(f32[216,64]{1,0:T(8,128)S(1)} %add_add_fusion.2), channel_id=1, source_target_pairs={{0,12},{4,0},{8,4},{12,8},{1,13},{5,1},{9,5},{13,9},{2,14},{6,2},{... | collective-permute-start | bytes 165896 | tf_op jit(solution)/shard_map/ppermute | solution.py:161
  148.3 1.2 copy-start
  149.6 1.1 copy-start.1
Sparse Core Ops, SparseCore 0:
  9.8 37.7 all-gather.1
Sparse Core Ops, SparseCore 1:
  16.5 45.0 reduce-scatter.1

commit v2 on v0

v2 whole, which is shorter than its diff:
```python
import functools

import jax
import jax.numpy as jnp
from jax import lax
from jax.experimental import pallas as pl
from jax.experimental.pallas import tpu as pltpu
from jax.sharding import PartitionSpec as P

adapter_scale = 0.5
VMEM_BYTES = 24 * 1024 * 1024
VMEM = pl.BlockSpec(memory_space=pltpu.VMEM)
SMEM = pl.BlockSpec(memory_space=pltpu.SMEM)
PARAMS = pltpu.CompilerParams(vmem_limit_bytes=VMEM_BYTES)


def place_rows(index, start, tokens_ref, block_ref):
    local = lax.broadcasted_iota(jnp.int32, (block_ref.shape[0], index.shape[1]), 0)
    choose = (local + start == index).astype(jnp.bfloat16)
    block_ref[...] = jnp.dot(
        choose, tokens_ref[...], preferred_element_type=jnp.float32
    ).astype(jnp.bfloat16)


def route_kernel(
    homes, held, light, shift, place_ref, request_ref, entry_ref, tokens_ref, index_ref, heavy_ref, block_ref
):
    rows = tokens_ref.shape[0]
    adapters = entry_ref.shape[0]
    span = (held + 1) * light
    onehot = lax.broadcasted_iota(jnp.int32, (adapters, rows), 0) == request_ref[...]
    earlier = lax.broadcasted_iota(jnp.int32, (rows, rows), 0) < lax.broadcasted_iota(
        jnp.int32, (rows, rows), 1
    )
    before = jnp.dot(
        onehot.astype(jnp.bfloat16), earlier.astype(jnp.bfloat16), preferred_element_type=jnp.float32
    )
    position = jnp.sum(jnp.where(onehot, before, 0.0), axis=0, keepdims=True).astype(jnp.int32)
    slot = jnp.sum(jnp.where(onehot, entry_ref[...], 0), axis=0, keepdims=True)
    home = slot // held
    relative = lax.rem(home - place_ref[0] + homes, homes)
    inside = jnp.where(
        position < light, (slot - home * held) * light + position, held * light + position - light
    )
    index = relative * span + inside
    index_ref[...] = index
    heavy = jnp.max(jnp.where(position >= light, slot, 0), axis=1, keepdims=True)
    heavy_ref[...] = jnp.broadcast_to(heavy, heavy_ref.shape)
    place_rows(index, shift * span, tokens_ref, block_ref)


def pack_kernel(span, shifts, index_ref, tokens_ref, *block_refs):
    for shift, block_ref in zip(shifts, block_refs):
        place_rows(index_ref[...], shift * span, tokens_ref, block_ref)


def entry_places(held):
    return (held + 2) // 2


def shrink_kernel(held, light, rank, pieces, value_side, scalar_ref, block_ref, down_ref, *out_refs):
    groups = entry_places(held)

    def product(e):
        if e > held:
            return jnp.zeros((light, 2 * rank), jnp.float32)
        factor = down_ref[e] if e < held else down_ref[scalar_ref[1]]
        value = jnp.dot(
            block_ref[e * light : (e + 1) * light, :], factor, preferred_element_type=jnp.float32
        )
        return value if e < held else jnp.where(scalar_ref[2] == 1, value, 0.0)

    piece = scalar_ref[0]
    for g in range(groups):
        first, second = product(g), product(g + groups)
        key = jnp.concatenate([first[:, :rank], second[:, :rank]], axis=1)
        value = jnp.concatenate([first[:, rank:], second[:, rank:]], axis=1)
        for o in range(pieces):
            out_refs[o][g * light : (g + 1) * light, :] = jnp.where(
                (piece ^ o) >= value_side, value, key
            )


def split_pair(value):
    high = value.astype(jnp.bfloat16)
    low = (value - high.astype(jnp.float32)).astype(jnp.bfloat16)
    return high, low


def finish_kernel(homes, held, light, rank, shifts, place_ref, index_ref, base_ref, up_ref, *refs):
    count = len(shifts)
    shrink_refs, out_ref, high_ref, low_ref = refs[:count], refs[count], refs[count + 1], refs[count + 2]
    span = (held + 1) * light
    rows = base_ref.shape[0]
    groups = entry_places(held)
    local = []
    for n, r in enumerate(shifts):
        home = lax.rem(place_ref[0] + r, homes)
        for e in range(held + 1):
            entry = home * held + e if e < held else place_ref[1]
            g, side = e % groups, e // groups
            high, low = split_pair(
                shrink_refs[n][g * light : (g + 1) * light, side * rank : (side + 1) * rank]
            )
            factor = up_ref[entry]
            delta = jnp.dot(high, factor, preferred_element_type=jnp.float32) + jnp.dot(
                low, factor, preferred_element_type=jnp.float32
            )
            high, low = split_pair(delta)
            start = n * span + e * light
            high_ref[start : start + light, :] = high
            low_ref[start : start + light, :] = low
        local.append(lax.broadcasted_iota(jnp.int32, (rows, span), 1) + r * span == index_ref[...])
    delta = base_ref[...]
    for n in range(count):
        choose = local[n].astype(jnp.bfloat16)
        delta = delta + adapter_scale * (
            jnp.dot(choose, high_ref[n * span : (n + 1) * span, :], preferred_element_type=jnp.float32)
            + jnp.dot(choose, low_ref[n * span : (n + 1) * span, :], preferred_element_type=jnp.float32)
        )
    out_ref[...] = delta.astype(out_ref.dtype)


def finish(scalars, index, base, up, shrinks, shifts, dtype, homes, held, light):
    rows, columns = base.shape
    span = (held + 1) * light
    return pl.pallas_call(
        functools.partial(finish_kernel, homes, held, light, up.shape[1], shifts),
        out_shape=jax.ShapeDtypeStruct((rows, columns), dtype),
        in_specs=[SMEM] + [VMEM] * (3 + len(shifts)),
        out_specs=VMEM,
        scratch_shapes=[pltpu.VMEM((len(shifts) * span, columns), jnp.bfloat16)] * 2,
        compiler_params=PARAMS,
        name="finish",
    )(scalars, index, base, up, *shrinks)


def line_gather(value, axis):
    size = lax.axis_size(axis)
    found = {0: value}
    for step in (1, -1):
        moving = value
        for hop in range(1, size):
            pairs = [(i, i + step) for i in range(size) if 0 <= i + step < size and 0 <= i - step * (hop - 1) < size]
            moving = lax.ppermute(moving, axis, pairs)
            found[-step * hop] = moving
    return found


def gather_up(adapter_up, place, homes):
    teams = lax.axis_size("groups")
    held, rank, columns = adapter_up.shape
    share = rank // teams
    team = lax.axis_index("groups")
    found = line_gather(lax.dynamic_slice_in_dim(adapter_up, team * share, share, 1), "batch")
    ordered = jnp.concatenate(
        [
            functools.reduce(
                lambda kept, hop: jnp.where(place + hop == home, found[hop], kept),
                sorted(found),
                jnp.zeros_like(found[0]),
            )
            for home in range(homes)
        ],
        axis=0,
    )
    shares = [ordered] + [
        lax.ppermute(ordered, "groups", [(i, (i + s) % teams) for i in range(teams)])
        for s in range(1, teams)
    ]
    return jnp.concatenate(
        [
            functools.reduce(
                lambda kept, s: jnp.where(lax.rem(team + teams - s, teams) == part, shares[s], kept),
                range(1, teams),
                shares[0],
            )
            for part in range(teams)
        ],
        axis=1,
    )


def reduce_base(tokens, weight, piece, pieces, columns):
    rows, width = tokens.shape
    bit = 1
    blocks = weight.reshape(width, pieces // 2, 2, columns)
    own = piece & 1

    def part(side):
        chosen = lax.dynamic_index_in_dim(blocks, side, axis=2, keepdims=False)
        return jnp.dot(
            tokens, chosen.reshape(width, pieces // 2 * columns), preferred_element_type=jnp.float32
        )

    sent = part(1 - own)
    kept = part(own) + lax.ppermute(sent, "tensor", [(i, i ^ 1) for i in range(pieces)])
    while 2 * bit < pieces:
        bit *= 2
        own = (piece // bit) & 1
        view = kept.reshape(rows, -1, 2, columns)
        sent = lax.dynamic_index_in_dim(view, 1 - own, axis=2, keepdims=False).reshape(rows, -1)
        kept = lax.dynamic_index_in_dim(view, own, axis=2, keepdims=False).reshape(rows, -1)
        kept = kept + lax.ppermute(sent, "tensor", [(i, i ^ bit) for i in range(pieces)])
    return kept


def on_device(tokens, request_adapter, adapter_entry, key_value_weight, adapter_down, adapter_up):
    rows, width = tokens.shape
    adapters = adapter_entry.shape[0]
    held, rank, columns = adapter_up.shape
    value_side = key_value_weight.shape[1] // 2 // columns
    homes = lax.axis_size("batch")
    pieces = lax.axis_size("tensor")
    place = lax.axis_index("batch").astype(jnp.int32)
    piece = lax.axis_index("tensor").astype(jnp.int32)
    light = rows // adapters
    span = (held + 1) * light
    order = sorted(range(1, homes), key=lambda r: (-min(r, homes - r), r))
    block_shape = jax.ShapeDtypeStruct((span, width), jnp.bfloat16)

    index, heavy, first = pl.pallas_call(
        functools.partial(route_kernel, homes, held, light, order[0]),
        out_shape=[
            jax.ShapeDtypeStruct((1, rows), jnp.int32),
            jax.ShapeDtypeStruct((8, 128), jnp.int32),
            block_shape,
        ],
        in_specs=[SMEM, VMEM, VMEM, VMEM],
        out_specs=[VMEM] * 3,
        compiler_params=PARAMS,
        name="route",
    )(place.reshape(1), request_adapter.reshape(1, rows), adapter_entry.reshape(-1, 1), tokens)
    later = order[1:] + [0]
    rest = pl.pallas_call(
        functools.partial(pack_kernel, span, later),
        out_shape=[block_shape] * len(later),
        in_specs=[VMEM] * 2,
        out_specs=[VMEM] * len(later),
        compiler_params=PARAMS,
        name="pack",
    )(index, tokens)
    blocks = {order[0]: first, **dict(zip(later, rest))}

    arrived = {0: blocks[0]}
    for r in order:
        arrived[r] = lax.ppermute(blocks[r], "batch", [(i, (i + r) % homes) for i in range(homes)])
    up = gather_up(adapter_up, place, homes)
    held_tokens, _ = lax.optimization_barrier((tokens, rest))
    base = reduce_base(held_tokens, key_value_weight, piece, pieces, columns)

    heavy = heavy[0, 0]
    heavy_here = (heavy // held == place).astype(jnp.int32)
    scalars = jnp.stack([piece, lax.rem(heavy, held), heavy_here])
    shrinks = {}
    for r in [0] + order:
        parts = pl.pallas_call(
            functools.partial(shrink_kernel, held, light, rank, pieces, value_side),
            out_shape=[jax.ShapeDtypeStruct((entry_places(held) * light, 2 * rank), jnp.float32)] * pieces,
            in_specs=[SMEM, VMEM, VMEM],
            out_specs=[VMEM] * pieces,
            compiler_params=PARAMS,
            name="shrink",
        )(scalars, arrived[r], adapter_down)
        total = parts[0]
        for o in range(1, pieces):
            total = total + lax.ppermute(parts[o], "tensor", [(i, i ^ o) for i in range(pieces)])
        if r:
            total = lax.ppermute(total, "batch", [(i, (i - r) % homes) for i in range(homes)])
        shrinks[r] = total

    places = jnp.stack([place, heavy])
    column = index.reshape(rows, 1)
    early = [0] + order[:-1]
    running = finish(
        places, column, base, up, [shrinks[r] for r in early], early, jnp.float32, homes, held, light
    )
    return finish(
        places, column, running, up, [shrinks[order[-1]]], order[-1:], jnp.bfloat16, homes, held, light
    )


def solution(mesh):
    in_specs = (
        P(("groups", "batch"), "tensor"),
        P(("groups", "batch")),
        P(),
        P("tensor", None),
        P("batch", "tensor", None),
        P("batch", None, "tensor"),
    )
    out_specs = P(("groups", "batch"), "tensor")
    return jax.shard_map(
        on_device, mesh=mesh, in_specs=in_specs, out_specs=out_specs, check_vma=False
    )
```

time: 259 us -> 182 us (0.70)
  blocking collectives: 145 us -> 0 us
  starting transfers between devices: 4.82 us -> 40.2 us
  Pallas kernels: 0 us -> 16.8 us
  waiting for transfers between devices: 62.8 us -> 74.8 us
  local copies, waits for them, and re-layouts: 15.2 us -> 27 us
  between operations: 13.5 us -> 3.25 us
  other arithmetic: 5.45 us -> 13.1 us
  matrix products: 11.9 us -> 6.28 us
    all_to_all x1 -> x0, blocking collectives: 145 us -> none  [on_device(): lax.all_to_all(outgoing, 'batch', split_axis=0, concat_axis=0, tiled=True)]
    ppermute x0 -> x27, waiting for transfers between devices: none -> 74.8 us  [the longest x6 51.7 us: line_gather(): moving = lax.ppermute(moving, axis, pairs)]
    ppermute x0 -> x27, starting transfers between devices: none -> 40.2 us  [the longest x6 11.6 us: line_gather(): moving = lax.ppermute(moving, axis, pairs)]
    all_to_all x1 -> x0, waiting for transfers between devices: 36.1 us -> none  [on_device(): lax.all_to_all(adapter_delta, 'batch', split_axis=0, concat_axis=0, tiled...]
    psum x1 -> x0, waiting for transfers between devices: 26.7 us -> none  [on_device(): down_product = lax.psum(down_product, 'tensor')]
    unnamed x6 -> x81, local copies, waits for them, and re-layouts: 0.01 us -> 19 us
    pallas_call x0 -> x8, Pallas kernels: none -> 16.8 us  [the longest x4 8.7 us: on_device(): pl.pallas_call(functools.partial(shrink_kernel, held, light, rank, pieces...]
    scatter x1 -> x0, local copies, waits for them, and re-layouts: 11.6 us -> none  [on_device(): jnp.zeros((entry_total, feat_width), tokens.dtype).at[entry_index]]
  transfers between devices with their start and end apart: 3 -> 27, of which waited for: 2 -> 8; matrix products, arithmetic and copies ran while one was open for 5% -> 19% of each run, Pallas kernels for 0% -> 8%
where the time goes in v2:
time: 182 us; the launch traced here: 181 us
  waiting for transfers between devices  74.8 us (41%)
  starting transfers between devices  40.2 us (22%)
  local copies, waits for them, and re-layouts  27 us (15%)
  Pallas kernels  16.8 us (9%)
  other arithmetic  13.1 us (7%)
  matrix products  6.28 us (3%)
  between operations  3.25 us (2%)
    ppermute x6, waiting for transfers between devices, line_gather(): moving = lax.ppermute(moving, axis, pairs)  51.7 us
    ppermute x12, waiting for transfers between devices, on_device(): lax.ppermute(parts[o], 'tensor', [(i, i ^ o) for i in range(pieces)])  20.9 us
    unnamed x81, local copies, waits for them, and re-layouts  19 us
    ppermute x6, starting transfers between devices, line_gather(): moving = lax.ppermute(moving, axis, pairs)  11.6 us
    ppermute x3, starting transfers between devices, on_device(): lax.ppermute(total, 'batch', [(i, (i - r) % homes) for i in range(homes)])  10.5 us
    pallas_call x4, Pallas kernels, on_device(): pl.pallas_call(functools.partial(shrink_kernel, held, light, rank, pieces...  8.7 us
    ppermute x12, starting transfers between devices, on_device(): lax.ppermute(parts[o], 'tensor', [(i, i ^ o) for i in range(pieces)])  7.58 us
    ppermute x3, starting transfers between devices, on_device(): lax.ppermute(blocks[r], 'batch', [(i, (i + r) % homes) for i in range(hom...  7.47 us
  transfers between devices with their start and end apart: 27, of which 8 were waited for; matrix products, arithmetic and copies ran while one was open for 19% of the time, Pallas kernels for 8%

profile of v2, /device:TPU:0, one launch (start us, length us, event | category | flops | bytes accessed | tf_op | source)
XLA Modules:
  0.0 181.3 jit_solution(2314584071975315844)
XLA Ops:
  0.0 1.6 constant_dynamic-slice_fusion
  1.6 4.9 %collective-permute-start.5 = (bf16[8,32,256]{2,1,0:T(8,128)(2,1)}, bf16[8,32,256]{2,1,0:T(8,128)(2,1)S(1)}, u32[]{:S(2)}, u32[]{:S(2)}) collective-permute-start(bf16[8,32,256]{2,1,0:T(8,128)(2,1)} %constant_dynamic-slice_fusion), channel_id=1, source_target_pairs={{0,4},{4,8},{8,12},{1,5},{5,9},{9,13},{2,6},{6,10},{10,14},{3,7},{... | collective-permute-start | bytes 393224 | tf_op jit(solution)/shard_map/ppermute | solution.py:145
  6.5 1.3 collective-permute-start.2
  9.2 1.9 %copy-done.2 = bf16[768,2048]{1,0:T(8,128)(2,1)S(1)} copy-done((bf16[768,2048]{1,0:T(8,128)(2,1)S(1)}, bf16[768,2048]{1,0:T(8,128)(2,1)}, u32[]{:S(2)}) %copy-start.2) | copy-done | bytes 3145752
  11.1 2.0 %route.1 = (s32[1,768]{1,0:T(1,128)S(1)}, s32[8,128]{1,0:T(8,128)S(1)}, bf16[216,2048]{1,0:T(8,128)(2,1)}) custom-call(s32[1]{0:T(128)} %bitcast.place_ref, s32[1,768]{1,0:T(1,128)S(1)} %reshape.32.request_ref, s32[32,1]{1,0:T(8,128)S(1)} %copy.17.entry_ref, bf16[768,2048]{1,0:T(8,128)(2,1)S(1)} %copy-done.2), custom_call_target="tpu_custom_call" | custom-call | tf_op jit(solution)/shard_map/route/pallas_call | solution.py:222
  13.1 3.6 %collective-permute-start.12 = (bf16[216,2048]{1,0:T(8,128)(2,1)}, bf16[216,2048]{1,0:T(8,128)(2,1)}, u32[]{:S(2)}, u32[]{:S(2)}) collective-permute-start(bf16[216,2048]{1,0:T(8,128)(2,1)} %get-tuple-element.38), channel_id=1, source_target_pairs={{0,8},{4,12},{8,0},{12,4},{1,9},{5,13},{9,1},{13,5},{2,10},{6,14},... | collective-permute-start | bytes 2654216 | tf_op jit(solution)/shard_map/ppermute | solution.py:247
  16.8 2.5 %pack.1 = (bf16[216,2048]{1,0:T(8,128)(2,1)}, bf16[216,2048]{1,0:T(8,128)(2,1)}, bf16[216,2048]{1,0:T(8,128)(2,1)S(1)}) custom-call(s32[1,768]{1,0:T(1,128)S(1)} %get-tuple-element.29.index_ref, bf16[768,2048]{1,0:T(8,128)(2,1)S(1)} %copy-done.3), custom_call_target="tpu_custom_call" | custom-call | tf_op jit(solution)/shard_map/pack/pallas_call | solution.py:235
  19.3 1.0 copy-done.4
  20.3 1.6 collective-permute-start.17
  21.9 2.2 %collective-permute-start.22 = (bf16[216,2048]{1,0:T(8,128)(2,1)}, bf16[216,2048]{1,0:T(8,128)(2,1)}, u32[]{:S(2)}, u32[]{:S(2)}) collective-permute-start(bf16[216,2048]{1,0:T(8,128)(2,1)} %get-tuple-element.31), channel_id=1, source_target_pairs={{0,12},{4,0},{8,4},{12,8},{1,13},{5,1},{9,5},{13,9},{2,14},{6,2},{... | collective-permute-start | bytes 2654216 | tf_op jit(solution)/shard_map/ppermute | solution.py:247
  24.1 6.5 %copy.18 = bf16[2048,1024]{0,1:T(8,128)(2,1)} copy(bf16[2048,1024]{1,0:T(8,128)(2,1)} %param.9) | data formatting | bytes 8388608 | tf_op args[3]
  30.6 1.3 collective-permute-start.6
  31.9 1.3 collective-permute-start.3
  33.2 4.1 %constant_dynamic-slice_fusion.4 = (bf16[2048,2,1,256]{0,3,2,1:T(8,128)(2,1)}, bf16[2048,2,1,256]{0,3,2,1:T(8,128)(2,1)S(1)}) fusion(bf16[2048,2,2,256]{0,3,2,1:T(8,128)(2,1)} %bitcast.20, s32[]{:T(128)S(6)} %select_n.209, s32[]{:T(128)S(6)} %select_n.210), kind=kLoop, calls=%fused_computation.18 | loop fusion | bytes 8388616 | tf_op jit(solution)/shard_map/jit(dynamic_index_in_dim)/dynamic_slice | solution.py:191
  37.3 1.3 collective-permute-start.7
  38.6 43.4 %collective-permute-done.3 = bf16[8,32,256]{2,1,0:T(8,128)(2,1)} collective-permute-done((bf16[8,32,256]{2,1,0:T(8,128)(2,1)S(1)}, bf16[8,32,256]{2,1,0:T(8,128)(2,1)}, u32[]{:S(2)}, u32[]{:S(2)}) %collective-permute-start.3) | collective-permute-done | bytes 131104 | tf_op jit(solution)/shard_map/ppermute | solution.py:145
  82.0 1.5 collective-permute-start.4
  83.5 3.0 %fusion = f32[768,512]{0,1:T(8,128)} fusion(bf16[768,2048]{1,0:T(8,128)(2,1)S(1)} %copy-done.3, bf16[2048,512]{0,1:T(8,128)(2,1)S(1)} %bitcast.22), kind=kOutput, calls=%fused_computation.21 | convolution fusion | flops 1610612736 | bytes 6815744 | tf_op jit(solution)/shard_map/dot_general | solution.py:192
  90.0 2.2 %copy-done = bf16[8,2048,128]{2,1,0:T(8,128)(2,1)S(1)} copy-done((bf16[8,2048,128]{2,1,0:T(8,128)(2,1)S(1)}, bf16[8,2048,128]{2,1,0:T(8,128)(2,1)}, u32[]{:S(2)}) %copy-start) | copy-done | bytes 4194328
  92.2 1.2 copy-done.5
  93.3 1.4 shrink.4
  94.8 8.3 %collective-permute-done.4 = bf16[8,32,256]{2,1,0:T(8,128)(2,1)} collective-permute-done((bf16[8,32,256]{2,1,0:T(8,128)(2,1)}, bf16[8,32,256]{2,1,0:T(8,128)(2,1)}, u32[]{:S(2)}, u32[]{:S(2)}) %collective-permute-start.4) | collective-permute-done | bytes 131104 | tf_op jit(solution)/shard_map/ppermute | solution.py:145
  103.1 1.1 select_select_fusion
  104.2 1.1 select_select_fusion.1
  105.6 1.6 collective-permute-start.10
  107.3 2.7 %collective-permute-done.10 = f32[120,128]{1,0:T(8,128)S(1)} collective-permute-done((f32[120,128]{1,0:T(8,128)S(1)}, f32[120,128]{1,0:T(8,128)S(1)}, u32[]{:S(2)}, u32[]{:S(2)}) %collective-permute-start.10) | collective-permute-done | bytes 61472 | tf_op jit(solution)/shard_map/ppermute | solution.py:267
  111.7 2.6 %collective-permute-done.11 = f32[120,128]{1,0:T(8,128)S(1)} collective-permute-done((f32[120,128]{1,0:T(8,128)S(1)}, f32[120,128]{1,0:T(8,128)S(1)}, u32[]{:S(2)}, u32[]{:S(2)}) %collective-permute-start.11) | collective-permute-done | bytes 61472 | tf_op jit(solution)/shard_map/ppermute | solution.py:267
  114.3 1.6 collective-permute-start.8
  116.9 1.6 add_add_fusion.3.refs_0_
  118.4 2.2 %copy-done.1 = bf16[8,2048,128]{2,1,0:T(8,128)(2,1)S(1)} copy-done((bf16[8,2048,128]{2,1,0:T(8,128)(2,1)S(1)}, bf16[8,2048,128]{2,1,0:T(8,128)(2,1)}, u32[]{:S(2)}) %copy-start.1) | copy-done | bytes 4194328
  120.6 2.7 %shrink.5 = (f32[120,128]{1,0:T(8,128)S(1)}, f32[120,128]{1,0:T(8,128)}, f32[120,128]{1,0:T(8,128)}, f32[120,128]{1,0:T(8,128)}) custom-call(s32[3]{0:T(128)S(1)} %pad_add_fusion.1.scalar_ref, bf16[216,2048]{1,0:T(8,128)(2,1)} %collective-permute-done.12.block_ref, bf16[8,2048,128]{2,1,0:T(8,128)(2,1)S(1)} %copy-done.1), custom_call_target="tpu_custom_call" | custom-call | tf_op jit(solution)/shard_map/shrink/pallas_call | solution.py:257
  123.9 1.4 collective-permute-start.14
  125.4 2.6 %shrink.6 = (f32[120,128]{1,0:T(8,128)S(1)}, f32[120,128]{1,0:T(8,128)}, f32[120,128]{1,0:T(8,128)S(1)}, f32[120,128]{1,0:T(8,128)S(1)}) custom-call(s32[3]{0:T(128)S(1)} %pad_add_fusion.1.scalar_ref, bf16[216,2048]{1,0:T(8,128)(2,1)} %collective-permute-done.17.block_ref, bf16[8,2048,128]{2,1,0:T(8,128)(2,1)S(1)} %copy-done.1), custom_call_target="tpu_custom_call" | custom-call | tf_op jit(solution)/shard_map/shrink/pallas_call | solution.py:257
  130.4 2.0 %shrink.7 = (f32[120,128]{1,0:T(8,128)S(1)}, f32[120,128]{1,0:T(8,128)S(1)}, f32[120,128]{1,0:T(8,128)S(1)}, f32[120,128]{1,0:T(8,128)S(1)}) custom-call(s32[3]{0:T(128)S(1)} %pad_add_fusion.1.scalar_ref, bf16[216,2048]{1,0:T(8,128)(2,1)} %collective-permute-done.22.block_ref, bf16[8,2048,128]{2,1,0:T(8,128)(2,1)S(1)} %copy-done.1), custom_call_target="tpu_custom_call" | custom-call | tf_op jit(solution)/shard_map/shrink/pallas_call | solution.py:257
  132.8 2.4 %broadcast_select_fusion.1 = (bf16[32,32,256]{2,1,0:T(8,128)(2,1)}, bf16[32,32,256]{2,1,0:T(8,128)(2,1)}) fusion(bf16[32,32,256]{2,1,0:T(8,128)(2,1)} %collective-permute-done.8, pred[]{:T(512)S(6)} %eq.93, bf16[8,32,256]{2,1,0:T(8,128)(2,1)S(1)} %copy-done.29, bf16[8,32,256]{2,1,0:T(8,128)(2,1)S(1)} %copy-done.31, bf16[8,32,256]{2,1,0:T(8,128)(2,1)S(1)} %copy-done.33, ...), kind=kLoop, calls=%fused_computation.5 | loop fusion | flops 1310720 | bytes 2097154 | tf_op jit(solution)/shard_map/jit(_where)/select_n | solution.py:174
  135.2 3.2 %convolution_add_fusion = f32[768,512]{0,1:T(8,128)S(1)} fusion(f32[768,512]{0,1:T(8,128)} %collective-permute-done, bf16[768,2048]{1,0:T(8,128)(2,1)S(1)} %copy-done.3, bf16[2048,512]{0,1:T(8,128)(2,1)S(1)} %bitcast.21), kind=kOutput, calls=%fused_computation | convolution fusion | flops 1611005952 | bytes 8388608 | tf_op jit(solution)/shard_map/dot_general | solution.py:192
  138.7 1.2 copy.26
  139.9 1.4 collective-permute-start.1
  141.4 1.3 pad_maximum_fusion.up_ref
  146.5 15.4 %collective-permute-done.19 = f32[120,128]{1,0:T(8,128)S(1)} collective-permute-done((f32[120,128]{1,0:T(8,128)S(1)}, f32[120,128]{1,0:T(8,128)S(1)}, u32[]{:S(2)}, u32[]{:S(2)}) %collective-permute-start.19) | collective-permute-done | bytes 61472 | tf_op jit(solution)/shard_map/ppermute | solution.py:267
  162.0 8.4 %collective-permute-start.16 = (f32[120,128]{1,0:T(8,128)S(1)}, f32[120,128]{1,0:T(8,128)S(1)}, u32[]{:S(2)}, u32[]{:S(2)}) collective-permute-start(f32[120,128]{1,0:T(8,128)S(1)} %add_add_fusion.2), channel_id=1, source_target_pairs={{0,8},{4,12},{8,0},{12,4},{1,9},{5,13},{9,1},{13,5},{2,10},{6,14},... | collective-permute-start | bytes 184328 | tf_op jit(solution)/shard_map/ppermute | solution.py:269
  170.5 1.5 add_add_fusion.1
  171.9 1.2 collective-permute-start.21
  174.3 1.2 bitcast_add_fusion.base_ref
  175.6 1.2 collective-permute-done.21.refs_2_
  176.8 1.6 finish.2.base_ref
  178.4 1.0 collective-permute-done.26.refs_0_
  179.4 1.9 %finish.3 = bf16[768,256]{1,0:T(8,128)(2,1)} custom-call(s32[2]{0:T(128)S(1)} %pad_add_fusion.place_ref, s32[768,1]{1,0:T(8,128)S(1)} %copy.23.index_ref, f32[768,256]{1,0:T(8,128)S(1)} %finish.2.base_ref, bf16[32,64,256]{2,1,0:T(8,128)(2,1)S(1)} %pad_maximum_fusion.up_ref, f32[120,128]{1,0:T(8,128)S(1)} %collective-permute-done.26.refs_0_), custom_call_target="tpu_custom_call" | custom-call | tf_op jit(solution)/shard_map/finish/pallas_call | solution.py:127
  (118 shorter events, 13.9 us)
Async XLA Ops:
  1.6 29.0 %collective-permute-start.5 = (bf16[8,32,256]{2,1,0:T(8,128)(2,1)}, bf16[8,32,256]{2,1,0:T(8,128)(2,1)S(1)}, u32[]{:S(2)}, u32[]{:S(2)}) collective-permute-start(bf16[8,32,256]{2,1,0:T(8,128)(2,1)} %constant_dynamic-slice_fusion), channel_id=1, source_target_pairs={{0,4},{4,8},{8,12},{1,5},{5,9},{9,13},{2,6},{6,10},{10,14},{3,7},{... | collective-permute-start | bytes 393224 | tf_op jit(solution)/shard_map/ppermute | solution.py:145
  6.5 25.4 %collective-permute-start.2 = (bf16[8,32,256]{2,1,0:T(8,128)(2,1)}, bf16[8,32,256]{2,1,0:T(8,128)(2,1)S(1)}, u32[]{:S(2)}, u32[]{:S(2)}) collective-permute-start(bf16[8,32,256]{2,1,0:T(8,128)(2,1)} %constant_dynamic-slice_fusion), channel_id=1, source_target_pairs={{4,0},{8,4},{12,8},{5,1},{9,5},{13,9},{6,2},{10,6},{14,10},{7,3},{... | collective-permute-start | bytes 393224 | tf_op jit(solution)/shard_map/ppermute | solution.py:145
  11.1 5.7 %copy-start.3 = (bf16[768,2048]{1,0:T(8,128)(2,1)S(1)}, bf16[768,2048]{1,0:T(8,128)(2,1)}, u32[]{:S(2)}) copy-start(bf16[768,2048]{1,0:T(8,128)(2,1)} %tokens_ref.3) | copy-start | bytes 9437188
  13.1 105.3 %collective-permute-start.12 = (bf16[216,2048]{1,0:T(8,128)(2,1)}, bf16[216,2048]{1,0:T(8,128)(2,1)}, u32[]{:S(2)}, u32[]{:S(2)}) collective-permute-start(bf16[216,2048]{1,0:T(8,128)(2,1)} %get-tuple-element.38), channel_id=1, source_target_pairs={{0,8},{4,12},{8,0},{12,4},{1,9},{5,13},{9,1},{13,5},{2,10},{6,14},... | collective-permute-start | bytes 2654216 | tf_op jit(solution)/shard_map/ppermute | solution.py:247
  20.3 103.6 %collective-permute-start.17 = (bf16[216,2048]{1,0:T(8,128)(2,1)}, bf16[216,2048]{1,0:T(8,128)(2,1)}, u32[]{:S(2)}, u32[]{:S(2)}) collective-permute-start(bf16[216,2048]{1,0:T(8,128)(2,1)} %get-tuple-element.30), channel_id=1, source_target_pairs={{0,4},{4,8},{8,12},{12,0},{1,5},{5,9},{9,13},{13,1},{2,6},{6,10},{... | collective-permute-start | bytes 2654216 | tf_op jit(solution)/shard_map/ppermute | solution.py:247
  21.9 108.0 %collective-permute-start.22 = (bf16[216,2048]{1,0:T(8,128)(2,1)}, bf16[216,2048]{1,0:T(8,128)(2,1)}, u32[]{:S(2)}, u32[]{:S(2)}) collective-permute-start(bf16[216,2048]{1,0:T(8,128)(2,1)} %get-tuple-element.31), channel_id=1, source_target_pairs={{0,12},{4,0},{8,4},{12,8},{1,13},{5,1},{9,5},{13,9},{2,14},{6,2},{... | collective-permute-start | bytes 2654216 | tf_op jit(solution)/shard_map/ppermute | solution.py:247
  30.6 6.7 %collective-permute-start.6 = (bf16[8,32,256]{2,1,0:T(8,128)(2,1)S(1)}, bf16[8,32,256]{2,1,0:T(8,128)(2,1)}, u32[]{:S(2)}, u32[]{:S(2)}) collective-permute-start(bf16[8,32,256]{2,1,0:T(8,128)(2,1)S(1)} %collective-permute-done.5), channel_id=1, source_target_pairs={{4,8},{8,12},{5,9},{9,13},{6,10},{10,14},{7,11},{11,15},{20,24},{2... | collective-permute-start | bytes 393224 | tf_op jit(solution)/shard_map/ppermute | solution.py:145
  31.9 5.4 %copy-start.25 = (bf16[8,32,256]{2,1,0:T(8,128)(2,1)}, bf16[8,32,256]{2,1,0:T(8,128)(2,1)S(1)}, u32[]{:S(2)}) copy-start(bf16[8,32,256]{2,1,0:T(8,128)(2,1)S(1)} %collective-permute-done.2) | copy-start | bytes 393220
  31.9 50.1 %collective-permute-start.3 = (bf16[8,32,256]{2,1,0:T(8,128)(2,1)S(1)}, bf16[8,32,256]{2,1,0:T(8,128)(2,1)}, u32[]{:S(2)}, u32[]{:S(2)}) collective-permute-start(bf16[8,32,256]{2,1,0:T(8,128)(2,1)S(1)} %collective-permute-done.2), channel_id=1, source_target_pairs={{4,0},{8,4},{5,1},{9,5},{6,2},{10,6},{7,3},{11,7},{20,16},{24,20},... | collective-permute-start | bytes 393224 | tf_op jit(solution)/shard_map/ppermute | solution.py:145
  37.3 57.4 %collective-permute-start.7 = (bf16[8,32,256]{2,1,0:T(8,128)(2,1)}, bf16[8,32,256]{2,1,0:T(8,128)(2,1)}, u32[]{:S(2)}, u32[]{:S(2)}) collective-permute-start(bf16[8,32,256]{2,1,0:T(8,128)(2,1)} %collective-permute-done.6), channel_id=1, source_target_pairs={{8,12},{9,13},{10,14},{11,15},{24,28},{25,29},{26,30},{27,31}} | collective-permute-start | bytes 393224 | tf_op jit(solution)/shard_map/ppermute | solution.py:145
  82.0 21.1 %collective-permute-start.4 = (bf16[8,32,256]{2,1,0:T(8,128)(2,1)}, bf16[8,32,256]{2,1,0:T(8,128)(2,1)}, u32[]{:S(2)}, u32[]{:S(2)}) collective-permute-start(bf16[8,32,256]{2,1,0:T(8,128)(2,1)} %collective-permute-done.3), channel_id=1, source_target_pairs={{4,0},{5,1},{6,2},{7,3},{20,16},{21,17},{22,18},{23,19}} | collective-permute-start | bytes 393224 | tf_op jit(solution)/shard_map/ppermute | solution.py:145
  93.3 9.8 %copy-start.26 = (bf16[8,32,256]{2,1,0:T(8,128)(2,1)S(1)}, bf16[8,32,256]{2,1,0:T(8,128)(2,1)}, u32[]{:S(2)}) copy-start(bf16[8,32,256]{2,1,0:T(8,128)(2,1)} %copy-done.25) | copy-start | bytes 393220
  93.3 9.8 %copy-start.27 = (bf16[8,64,256]{2,1,0:T(8,128)(2,1)S(1)}, bf16[8,64,256]{2,1,0:T(8,128)(2,1)}, u32[]{:S(2)}) copy-start(bf16[8,64,256]{2,1,0:T(8,128)(2,1)} %param.11) | copy-start | bytes 786436
  94.7 12.6 %copy-start.7 = (f32[120,128]{1,0:T(8,128)}, f32[120,128]{1,0:T(8,128)S(1)}, u32[]{:S(2)}) copy-start(f32[120,128]{1,0:T(8,128)S(1)} %get-tuple-element.34) | copy-start | bytes 184324
  94.7 10.8 %collective-permute-start.9 = (f32[120,128]{1,0:T(8,128)S(1)}, f32[120,128]{1,0:T(8,128)S(1)}, u32[]{:S(2)}, u32[]{:S(2)}) collective-permute-start(f32[120,128]{1,0:T(8,128)S(1)} %get-tuple-element.35), channel_id=1, source_target_pairs={{0,1},{1,0},{2,3},{3,2},{4,5},{5,4},{6,7},{7,6},{8,9},{9,8},{10,11... | collective-permute-start | bytes 184328 | tf_op jit(solution)/shard_map/ppermute | solution.py:267
  103.1 32.1 %collective-permute-start = (f32[768,512]{0,1:T(8,128)}, f32[768,512]{0,1:T(8,128)}, u32[]{:S(2)}, u32[]{:S(2)}) collective-permute-start(f32[768,512]{0,1:T(8,128)} %fusion), channel_id=1, source_target_pairs={{0,1},{1,0},{2,3},{3,2},{4,5},{5,4},{6,7},{7,6},{8,9},{9,8},{10,11... | collective-permute-start | bytes 4718600 | tf_op jit(solution)/shard_map/ppermute | solution.py:197
  104.2 7.5 %copy-start.28 = (bf16[8,32,256]{2,1,0:T(8,128)(2,1)}, bf16[8,32,256]{2,1,0:T(8,128)(2,1)S(1)}, u32[]{:S(2)}) copy-start(bf16[8,32,256]{2,1,0:T(8,128)(2,1)S(1)} %select_select_fusion) | copy-start | bytes 393220
  105.3 9.0 %copy-start.30 = (bf16[8,32,256]{2,1,0:T(8,128)(2,1)}, bf16[8,32,256]{2,1,0:T(8,128)(2,1)S(1)}, u32[]{:S(2)}) copy-start(bf16[8,32,256]{2,1,0:T(8,128)(2,1)S(1)} %select_select_fusion.1) | copy-start | bytes 393220
  105.5 8.8 %copy-start.32 = (bf16[8,32,256]{2,1,0:T(8,128)(2,1)}, bf16[8,32,256]{2,1,0:T(8,128)(2,1)S(1)}, u32[]{:S(2)}) copy-start(bf16[8,32,256]{2,1,0:T(8,128)(2,1)S(1)} %select_select_fusion.2) | copy-start | bytes 393220
  105.6 4.5 %collective-permute-start.10 = (f32[120,128]{1,0:T(8,128)S(1)}, f32[120,128]{1,0:T(8,128)S(1)}, u32[]{:S(2)}, u32[]{:S(2)}) collective-permute-start(f32[120,128]{1,0:T(8,128)S(1)} %get-tuple-element.36), channel_id=1, source_target_pairs={{0,2},{1,3},{2,0},{3,1},{4,6},{5,7},{6,4},{7,5},{8,10},{9,11},{10,... | collective-permute-start | bytes 184328 | tf_op jit(solution)/shard_map/ppermute | solution.py:267
  107.3 7.0 %copy-start.34 = (bf16[8,32,256]{2,1,0:T(8,128)(2,1)}, bf16[8,32,256]{2,1,0:T(8,128)(2,1)S(1)}, u32[]{:S(2)}) copy-start(bf16[8,32,256]{2,1,0:T(8,128)(2,1)S(1)} %select_select_fusion.3) | copy-start | bytes 393220
  110.0 5.9 %copy-start.37 = (f32[120,128]{1,0:T(8,128)}, f32[120,128]{1,0:T(8,128)S(1)}, u32[]{:S(2)}) copy-start(f32[120,128]{1,0:T(8,128)S(1)} %collective-permute-done.10) | copy-start | bytes 184324
  110.0 4.3 %collective-permute-start.11 = (f32[120,128]{1,0:T(8,128)S(1)}, f32[120,128]{1,0:T(8,128)S(1)}, u32[]{:S(2)}, u32[]{:S(2)}) collective-permute-start(f32[120,128]{1,0:T(8,128)S(1)} %get-tuple-element.37), channel_id=1, source_target_pairs={{0,3},{1,2},{2,1},{3,0},{4,7},{5,6},{6,5},{7,4},{8,11},{9,10},{10,... | collective-permute-start | bytes 184328 | tf_op jit(solution)/shard_map/ppermute | solution.py:267
  114.3 18.1 %collective-permute-start.8 = (bf16[32,32,256]{2,1,0:T(8,128)(2,1)}, bf16[32,32,256]{2,1,0:T(8,128)(2,1)}, u32[]{:S(2)}, u32[]{:S(2)}) collective-permute-start(bf16[32,32,256]{2,1,0:T(8,128)(2,1)} %pad_maximum_fusion.1), channel_id=1, source_target_pairs={{0,16},{16,0},{1,17},{17,1},{2,18},{18,2},{3,19},{19,3},{4,20},{20... | collective-permute-start | bytes 1572872 | tf_op jit(solution)/shard_map/ppermute | solution.py:168
  123.9 18.7 %collective-permute-start.13 = (f32[120,128]{1,0:T(8,128)}, f32[120,128]{1,0:T(8,128)}, u32[]{:S(2)}, u32[]{:S(2)}) collective-permute-start(f32[120,128]{1,0:T(8,128)} %get-tuple-element.40), channel_id=1, source_target_pairs={{0,1},{1,0},{2,3},{3,2},{4,5},{5,4},{6,7},{7,6},{8,9},{9,8},{10,11... | collective-permute-start | bytes 184328 | tf_op jit(solution)/shard_map/ppermute | solution.py:267
  123.9 19.4 %collective-permute-start.14 = (f32[120,128]{1,0:T(8,128)}, f32[120,128]{1,0:T(8,128)}, u32[]{:S(2)}, u32[]{:S(2)}) collective-permute-start(f32[120,128]{1,0:T(8,128)} %get-tuple-element.41), channel_id=1, source_target_pairs={{0,2},{1,3},{2,0},{3,1},{4,6},{5,7},{6,4},{7,5},{8,10},{9,11},{10,... | collective-permute-start | bytes 184328 | tf_op jit(solution)/shard_map/ppermute | solution.py:267
  129.9 14.1 %collective-permute-start.15 = (f32[120,128]{1,0:T(8,128)}, f32[120,128]{1,0:T(8,128)}, u32[]{:S(2)}, u32[]{:S(2)}) collective-permute-start(f32[120,128]{1,0:T(8,128)} %get-tuple-element.42), channel_id=1, source_target_pairs={{0,3},{1,2},{2,1},{3,0},{4,7},{5,6},{6,5},{7,4},{8,11},{9,10},{10,... | collective-permute-start | bytes 184328 | tf_op jit(solution)/shard_map/ppermute | solution.py:267
  132.4 6.1 %copy-start.8 = (f32[120,128]{1,0:T(8,128)}, f32[120,128]{1,0:T(8,128)S(1)}, u32[]{:S(2)}) copy-start(f32[120,128]{1,0:T(8,128)S(1)} %get-tuple-element.47) | copy-start | bytes 184324
  132.4 6.1 %copy-start.14 = (f32[120,128]{1,0:T(8,128)}, f32[120,128]{1,0:T(8,128)S(1)}, u32[]{:S(2)}) copy-start(f32[120,128]{1,0:T(8,128)S(1)} %get-tuple-element.50) | copy-start | bytes 184324
  132.4 6.1 %copy-start.16 = (f32[120,128]{1,0:T(8,128)}, f32[120,128]{1,0:T(8,128)S(1)}, u32[]{:S(2)}) copy-start(f32[120,128]{1,0:T(8,128)S(1)} %get-tuple-element.49) | copy-start | bytes 184324
  132.4 6.1 %copy-start.18 = (f32[120,128]{1,0:T(8,128)}, f32[120,128]{1,0:T(8,128)S(1)}, u32[]{:S(2)}) copy-start(f32[120,128]{1,0:T(8,128)S(1)} %get-tuple-element.48) | copy-start | bytes 184324
  132.5 13.3 %collective-permute-start.18 = (f32[120,128]{1,0:T(8,128)}, f32[120,128]{1,0:T(8,128)}, u32[]{:S(2)}, u32[]{:S(2)}) collective-permute-start(f32[120,128]{1,0:T(8,128)} %get-tuple-element.44), channel_id=1, source_target_pairs={{0,1},{1,0},{2,3},{3,2},{4,5},{5,4},{6,7},{7,6},{8,9},{9,8},{10,11... | collective-permute-start | bytes 184328 | tf_op jit(solution)/shard_map/ppermute | solution.py:267
  138.6 4.7 %copy-start.21 = (f32[120,128]{1,0:T(8,128)S(1)}, f32[120,128]{1,0:T(8,128)}, u32[]{:S(2)}) copy-start(f32[120,128]{1,0:T(8,128)} %copy-done.20) | copy-start | bytes 184324
  138.6 5.3 %copy-start.19 = (f32[120,128]{1,0:T(8,128)S(1)}, f32[120,128]{1,0:T(8,128)}, u32[]{:S(2)}) copy-start(f32[120,128]{1,0:T(8,128)} %copy-done.18) | copy-start | bytes 184324
  138.7 6.2 %copy-start.13 = (f32[120,128]{1,0:T(8,128)S(1)}, f32[120,128]{1,0:T(8,128)}, u32[]{:S(2)}) copy-start(f32[120,128]{1,0:T(8,128)} %copy-done.12) | copy-start | bytes 184324
  138.7 7.1 %copy-start.17 = (f32[120,128]{1,0:T(8,128)S(1)}, f32[120,128]{1,0:T(8,128)}, u32[]{:S(2)}) copy-start(f32[120,128]{1,0:T(8,128)} %copy-done.16) | copy-start | bytes 184324
  138.7 23.2 %copy-start.15 = (f32[120,128]{1,0:T(8,128)S(1)}, f32[120,128]{1,0:T(8,128)}, u32[]{:S(2)}) copy-start(f32[120,128]{1,0:T(8,128)} %copy-done.14) | copy-start | bytes 184324
  138.7 31.8 %copy-start.11 = (f32[120,128]{1,0:T(8,128)S(1)}, f32[120,128]{1,0:T(8,128)}, u32[]{:S(2)}) copy-start(f32[120,128]{1,0:T(8,128)} %copy-done.10) | copy-start | bytes 184324
  138.7 34.4 %copy-start.9 = (f32[120,128]{1,0:T(8,128)S(1)}, f32[120,128]{1,0:T(8,128)}, u32[]{:S(2)}) copy-start(f32[120,128]{1,0:T(8,128)} %copy-done.8) | copy-start | bytes 184324
  139.9 34.4 %collective-permute-start.1 = (f32[768,256]{1,0:T(8,128)}, f32[768,256]{1,0:T(8,128)}, u32[]{:S(2)}, u32[]{:S(2)}) collective-permute-start(f32[768,256]{1,0:T(8,128)} %bitcast.9), channel_id=1, source_target_pairs={{0,2},{1,3},{2,0},{3,1},{4,6},{5,7},{6,4},{7,5},{8,10},{9,11},{10,... | collective-permute-start | bytes 2359304 | tf_op jit(solution)/shard_map/ppermute | solution.py:204
  142.7 19.2 %collective-permute-start.19 = (f32[120,128]{1,0:T(8,128)S(1)}, f32[120,128]{1,0:T(8,128)S(1)}, u32[]{:S(2)}, u32[]{:S(2)}) collective-permute-start(f32[120,128]{1,0:T(8,128)S(1)} %copy-done.23), channel_id=1, source_target_pairs={{0,2},{1,3},{2,0},{3,1},{4,6},{5,7},{6,4},{7,5},{8,10},{9,11},{10,... | collective-permute-start | bytes 184328 | tf_op jit(solution)/shard_map/ppermute | solution.py:267
  143.3 18.7 %collective-permute-start.20 = (f32[120,128]{1,0:T(8,128)S(1)}, f32[120,128]{1,0:T(8,128)S(1)}, u32[]{:S(2)}, u32[]{:S(2)}) collective-permute-start(f32[120,128]{1,0:T(8,128)S(1)} %copy-done.21), channel_id=1, source_target_pairs={{0,3},{1,2},{2,1},{3,0},{4,7},{5,6},{6,5},{7,4},{8,11},{9,10},{10,... | collective-permute-start | bytes 184328 | tf_op jit(solution)/shard_map/ppermute | solution.py:267
  144.0 27.9 %collective-permute-start.23 = (f32[120,128]{1,0:T(8,128)S(1)}, f32[120,128]{1,0:T(8,128)S(1)}, u32[]{:S(2)}, u32[]{:S(2)}) collective-permute-start(f32[120,128]{1,0:T(8,128)S(1)} %copy-done.19), channel_id=1, source_target_pairs={{0,1},{1,0},{2,3},{3,2},{4,5},{5,4},{6,7},{7,6},{8,9},{9,8},{10,11... | collective-permute-start | bytes 184328 | tf_op jit(solution)/shard_map/ppermute | solution.py:267
  145.8 27.3 %collective-permute-start.24 = (f32[120,128]{1,0:T(8,128)S(1)}, f32[120,128]{1,0:T(8,128)S(1)}, u32[]{:S(2)}, u32[]{:S(2)}) collective-permute-start(f32[120,128]{1,0:T(8,128)S(1)} %copy-done.17), channel_id=1, source_target_pairs={{0,2},{1,3},{2,0},{3,1},{4,6},{5,7},{6,4},{7,5},{8,10},{9,11},{10,... | collective-permute-start | bytes 184328 | tf_op jit(solution)/shard_map/ppermute | solution.py:267
  161.8 11.3 %collective-permute-start.25 = (f32[120,128]{1,0:T(8,128)S(1)}, f32[120,128]{1,0:T(8,128)S(1)}, u32[]{:S(2)}, u32[]{:S(2)}) collective-permute-start(f32[120,128]{1,0:T(8,128)S(1)} %copy-done.15), channel_id=1, source_target_pairs={{0,3},{1,2},{2,1},{3,0},{4,7},{5,6},{6,5},{7,4},{8,11},{9,10},{10,... | collective-permute-start | bytes 184328 | tf_op jit(solution)/shard_map/ppermute | solution.py:267
  162.0 13.6 %collective-permute-start.16 = (f32[120,128]{1,0:T(8,128)S(1)}, f32[120,128]{1,0:T(8,128)S(1)}, u32[]{:S(2)}, u32[]{:S(2)}) collective-permute-start(f32[120,128]{1,0:T(8,128)S(1)} %add_add_fusion.2), channel_id=1, source_target_pairs={{0,8},{4,12},{8,0},{12,4},{1,9},{5,13},{9,1},{13,5},{2,10},{6,14},... | collective-permute-start | bytes 184328 | tf_op jit(solution)/shard_map/ppermute | solution.py:269
  171.9 4.8 %collective-permute-start.21 = (f32[120,128]{1,0:T(8,128)}, f32[120,128]{1,0:T(8,128)S(1)}, u32[]{:S(2)}, u32[]{:S(2)}) collective-permute-start(f32[120,128]{1,0:T(8,128)} %add_add_fusion.1), channel_id=1, source_target_pairs={{0,12},{4,0},{8,4},{12,8},{1,13},{5,1},{9,5},{13,9},{2,14},{6,2},{... | collective-permute-start | bytes 184328 | tf_op jit(solution)/shard_map/ppermute | solution.py:269
  173.2 6.2 %collective-permute-start.26 = (f32[120,128]{1,0:T(8,128)S(1)}, f32[120,128]{1,0:T(8,128)S(1)}, u32[]{:S(2)}, u32[]{:S(2)}) collective-permute-start(f32[120,128]{1,0:T(8,128)S(1)} %add_add_fusion), channel_id=1, source_target_pairs={{0,4},{4,8},{8,12},{12,0},{1,5},{5,9},{9,13},{13,1},{2,6},{6,10},{... | collective-permute-start | bytes 184328 | tf_op jit(solution)/shard_map/ppermute | solution.py:269
  (18 other events, 39.1 us)

commit v3 on v2

--- a/solution.py
+++ b/solution.py
@@ -10,6 +10,7 @@
 adapter_scale = 0.5
 VMEM_BYTES = 24 * 1024 * 1024
 VMEM = pl.BlockSpec(memory_space=pltpu.VMEM)
+ANY = pl.BlockSpec(memory_space=pl.ANY)
 SMEM = pl.BlockSpec(memory_space=pltpu.SMEM)
 PARAMS = pltpu.CompilerParams(vmem_limit_bytes=VMEM_BYTES)
 
@@ -23,7 +24,7 @@
 
 
 def route_kernel(
-    homes, held, light, shift, place_ref, request_ref, entry_ref, tokens_ref, index_ref, heavy_ref, block_ref
+    homes, held, light, shift, place_ref, entry_ref, request_ref, tokens_ref, index_ref, heavy_ref, block_ref
 ):
     rows = tokens_ref.shape[0]
     adapters = entry_ref.shape[0]
@@ -36,7 +37,9 @@
         onehot.astype(jnp.bfloat16), earlier.astype(jnp.bfloat16), preferred_element_type=jnp.float32
     )
     position = jnp.sum(jnp.where(onehot, before, 0.0), axis=0, keepdims=True).astype(jnp.int32)
-    slot = jnp.sum(jnp.where(onehot, entry_ref[...], 0), axis=0, keepdims=True)
+    slot = jnp.zeros_like(position)
+    for a in range(adapters):
+        slot = jnp.where(request_ref[...] == a, entry_ref[a], slot)
     home = slot // held
     relative = lax.rem(home - place_ref[0] + homes, homes)
     inside = jnp.where(
@@ -49,7 +52,8 @@
     place_rows(index, shift * span, tokens_ref, block_ref)
 
 
-def pack_kernel(span, shifts, index_ref, tokens_ref, *block_refs):
+def pack_kernel(span, shifts, waited, index_ref, tokens_ref, *refs):
+    block_refs = refs[waited:]
     for shift, block_ref in zip(shifts, block_refs):
         place_rows(index_ref[...], shift * span, tokens_ref, block_ref)
 
@@ -58,7 +62,8 @@
     return (held + 2) // 2
 
 
-def shrink_kernel(held, light, rank, pieces, value_side, scalar_ref, block_ref, down_ref, *out_refs):
+def shrink_kernel(held, light, rank, pieces, value_side, waited, scalar_ref, block_ref, down_ref, *refs):
+    out_refs = refs[waited:]
     groups = entry_places(held)
 
     def product(e):
@@ -87,8 +92,9 @@
     return high, low
 
 
-def finish_kernel(homes, held, light, rank, shifts, place_ref, index_ref, base_ref, up_ref, *refs):
+def finish_kernel(homes, held, light, rank, shifts, waited, place_ref, index_ref, base_ref, up_ref, *refs):
     count = len(shifts)
+    refs = refs[:count] + refs[count + waited :]
     shrink_refs, out_ref, high_ref, low_ref = refs[:count], refs[count], refs[count + 1], refs[count + 2]
     span = (held + 1) * light
     rows = base_ref.shape[0]
@@ -121,38 +127,49 @@
     out_ref[...] = delta.astype(out_ref.dtype)
 
 
-def finish(scalars, index, base, up, shrinks, shifts, dtype, homes, held, light):
+def finish(scalars, index, base, up, shrinks, after, shifts, dtype, homes, held, light):
     rows, columns = base.shape
     span = (held + 1) * light
     return pl.pallas_call(
-        functools.partial(finish_kernel, homes, held, light, up.shape[1], shifts),
+        functools.partial(finish_kernel, homes, held, light, up.shape[1], shifts, len(after)),
         out_shape=jax.ShapeDtypeStruct((rows, columns), dtype),
-        in_specs=[SMEM] + [VMEM] * (3 + len(shifts)),
+        in_specs=[SMEM] + [VMEM] * (3 + len(shifts)) + [ANY] * len(after),
         out_specs=VMEM,
         scratch_shapes=[pltpu.VMEM((len(shifts) * span, columns), jnp.bfloat16)] * 2,
         compiler_params=PARAMS,
         name="finish",
-    )(scalars, index, base, up, *shrinks)
-
-
-def line_gather(value, axis):
-    size = lax.axis_size(axis)
-    found = {0: value}
-    for step in (1, -1):
-        moving = value
-        for hop in range(1, size):
-            pairs = [(i, i + step) for i in range(size) if 0 <= i + step < size and 0 <= i - step * (hop - 1) < size]
-            moving = lax.ppermute(moving, axis, pairs)
-            found[-step * hop] = moving
-    return found
-
-
-def gather_up(adapter_up, place, homes):
+    )(scalars, index, base, up, *shrinks, *after)
+
+
+def gate_kernel(value_ref, *refs):
+    pass
+
+
+def gate(value, after):
+    return pl.pallas_call(
+        gate_kernel,
+        out_shape=jax.ShapeDtypeStruct(value.shape, value.dtype),
+        in_specs=[ANY] * (1 + len(after)),
+        out_specs=ANY,
+        input_output_aliases={0: 0},
+        name="gate",
+    )(value, *after)
+
+
+def line_step(moving, hop, size):
+    return [
+        lax.ppermute(
+            value,
+            "batch",
+            [(i, i + step) for i in range(size) if 0 <= i + step < size and 0 <= i - step * (hop - 1) < size],
+        )
+        for value, step in zip(moving, (1, -1))
+    ]
+
+
+def join_up(found, place, homes):
     teams = lax.axis_size("groups")
-    held, rank, columns = adapter_up.shape
-    share = rank // teams
     team = lax.axis_index("groups")
-    found = line_gather(lax.dynamic_slice_in_dim(adapter_up, team * share, share, 1), "batch")
     ordered = jnp.concatenate(
         [
             functools.reduce(
@@ -181,28 +198,48 @@
     )
 
 
-def reduce_base(tokens, weight, piece, pieces, columns):
+def base_kernel(waited, block_ref, tokens_ref, weight_ref, *refs):
+    refs[waited][...] = jnp.dot(tokens_ref[...], weight_ref[...], preferred_element_type=jnp.float32)
+
+
+def base_part(tokens, weight, blocks, columns, after):
     rows, width = tokens.shape
+    count = blocks.shape[0]
+    return pl.pallas_call(
+        functools.partial(base_kernel, len(after)),
+        out_shape=jax.ShapeDtypeStruct((rows, count * columns), jnp.float32),
+        grid_spec=pltpu.PrefetchScalarGridSpec(
+            num_scalar_prefetch=1,
+            grid=(count,),
+            in_specs=[
+                pl.BlockSpec((rows, width), lambda j, chosen: (0, 0)),
+                pl.BlockSpec((width, columns), lambda j, chosen: (0, chosen[j])),
+            ]
+            + [ANY] * len(after),
+            out_specs=pl.BlockSpec((rows, columns), lambda j, chosen: (0, j)),
+        ),
+        compiler_params=PARAMS,
+        name="base",
+    )(blocks, tokens, weight, *after)
+
+
+def reduce_base(tokens, weight, piece, pieces, columns, after):
+    keep = [0]
+    bit = pieces // 2
+    while bit > 1:
+        keep = keep + [p + bit for p in keep]
+        bit //= 2
+    keep = jnp.array(keep, jnp.int32)
+    sent = base_part(tokens, weight, piece ^ keep ^ 1, columns, after)
+    kept = base_part(tokens, weight, piece ^ keep, columns, [sent])
     bit = 1
-    blocks = weight.reshape(width, pieces // 2, 2, columns)
-    own = piece & 1
-
-    def part(side):
-        chosen = lax.dynamic_index_in_dim(blocks, side, axis=2, keepdims=False)
-        return jnp.dot(
-            tokens, chosen.reshape(width, pieces // 2 * columns), preferred_element_type=jnp.float32
-        )
-
-    sent = part(1 - own)
-    kept = part(own) + lax.ppermute(sent, "tensor", [(i, i ^ 1) for i in range(pieces)])
-    while 2 * bit < pieces:
+    while True:
+        kept = kept + lax.ppermute(sent, "tensor", [(i, i ^ bit) for i in range(pieces)])
         bit *= 2
-        own = (piece // bit) & 1
-        view = kept.reshape(rows, -1, 2, columns)
-        sent = lax.dynamic_index_in_dim(view, 1 - own, axis=2, keepdims=False).reshape(rows, -1)
-        kept = lax.dynamic_index_in_dim(view, own, axis=2, keepdims=False).reshape(rows, -1)
-        kept = kept + lax.ppermute(sent, "tensor", [(i, i ^ bit) for i in range(pieces)])
-    return kept
+        if bit >= pieces:
+            return kept
+        half = kept.shape[1] // 2
+        kept, sent = kept[:, :half], kept[:, half:]
 
 
 def on_device(tokens, request_adapter, adapter_entry, key_value_weight, adapter_down, adapter_up):
@@ -219,6 +256,13 @@
     order = sorted(range(1, homes), key=lambda r: (-min(r, homes - r), r))
     block_shape = jax.ShapeDtypeStruct((span, width), jnp.bfloat16)
 
+    teams = lax.axis_size("groups")
+    share = rank // teams
+    own_up = lax.dynamic_slice_in_dim(adapter_up, lax.axis_index("groups") * share, share, 1)
+    found = {0: own_up}
+    moving = line_step([own_up] * 2, 1, homes)
+    found[-1], found[1] = moving
+
     index, heavy, first = pl.pallas_call(
         functools.partial(route_kernel, homes, held, light, order[0]),
         out_shape=[
@@ -226,57 +270,64 @@
             jax.ShapeDtypeStruct((8, 128), jnp.int32),
             block_shape,
         ],
-        in_specs=[SMEM, VMEM, VMEM, VMEM],
+        in_specs=[SMEM, SMEM, VMEM, VMEM],
         out_specs=[VMEM] * 3,
         compiler_params=PARAMS,
         name="route",
-    )(place.reshape(1), request_adapter.reshape(1, rows), adapter_entry.reshape(-1, 1), tokens)
+    )(place.reshape(1), adapter_entry, request_adapter.reshape(1, rows), tokens)
     later = order[1:] + [0]
     rest = pl.pallas_call(
-        functools.partial(pack_kernel, span, later),
+        functools.partial(pack_kernel, span, later, len(moving)),
         out_shape=[block_shape] * len(later),
-        in_specs=[VMEM] * 2,
+        in_specs=[VMEM] * 2 + [ANY] * len(moving),
         out_specs=[VMEM] * len(later),
         compiler_params=PARAMS,
         name="pack",
-    )(index, tokens)
+    )(index, tokens, *moving)
     blocks = {order[0]: first, **dict(zip(later, rest))}
 
     arrived = {0: blocks[0]}
     for r in order:
         arrived[r] = lax.ppermute(blocks[r], "batch", [(i, (i + r) % homes) for i in range(homes)])
-    up = gather_up(adapter_up, place, homes)
-    held_tokens, _ = lax.optimization_barrier((tokens, rest))
-    base = reduce_base(held_tokens, key_value_weight, piece, pieces, columns)
+    base = reduce_base(tokens, key_value_weight, piece, pieces, columns, [blocks[0]])
+    for hop in range(2, homes):
+        if hop > 2:
+            moving = [gate(value, [base]) for value in moving]
+        moving = line_step(moving, hop, homes)
+        found[-hop], found[hop] = moving
+    up = join_up(found, place, homes)
 
     heavy = heavy[0, 0]
     heavy_here = (heavy // held == place).astype(jnp.int32)
     scalars = jnp.stack([piece, lax.rem(heavy, held), heavy_here])
     shrinks = {}
+    after = [base]
     for r in [0] + order:
         parts = pl.pallas_call(
-            functools.partial(shrink_kernel, held, light, rank, pieces, value_side),
+            functools.partial(shrink_kernel, held, light, rank, pieces, value_side, len(after)),
             out_shape=[jax.ShapeDtypeStruct((entry_places(held) * light, 2 * rank), jnp.float32)] * pieces,
-            in_specs=[SMEM, VMEM, VMEM],
+            in_specs=[SMEM, VMEM, VMEM] + [ANY] * len(after),
             out_specs=[VMEM] * pieces,
             compiler_params=PARAMS,
             name="shrink",
-        )(scalars, arrived[r], adapter_down)
+        )(scalars, arrived[r], adapter_down, *after)
         total = parts[0]
         for o in range(1, pieces):
             total = total + lax.ppermute(parts[o], "tensor", [(i, i ^ o) for i in range(pieces)])
+        after = [total]
         if r:
-            total = lax.ppermute(total, "batch", [(i, (i - r) % homes) for i in range(homes)])
-        shrinks[r] = total
+            shrinks[r] = lax.ppermute(total, "batch", [(i, (i - r) % homes) for i in range(homes)])
+        else:
+            shrinks[r] = total
 
     places = jnp.stack([place, heavy])
     column = index.reshape(rows, 1)
     early = [0] + order[:-1]
     running = finish(
-        places, column, base, up, [shrinks[r] for r in early], early, jnp.float32, homes, held, light
+        places, column, base, up, [shrinks[r] for r in early], after, early, jnp.float32, homes, held, light
     )
     return finish(
-        places, column, running, up, [shrinks[order[-1]]], order[-1:], jnp.bfloat16, homes, held, light
+        places, column, running, up, [shrinks[order[-1]]], [], order[-1:], jnp.bfloat16, homes, held, light
     )
 
 

time: 182 us -> 140 us (0.77)
  waiting for transfers between devices: 74.8 us -> 63.8 us
  local copies, waits for them, and re-layouts: 27 us -> 16.3 us
  starting transfers between devices: 40.2 us -> 30.8 us
  other arithmetic: 13.1 us -> 4.4 us
  matrix products: 6.28 us -> 0 us
  Pallas kernels: 16.8 us -> 21.2 us
    ppermute x8 -> x7, waiting for transfers between devices: 51.7 us -> 18.1 us  [the longest x6 14.7 us: line_step(): lax.ppermute(value, 'batch', [(i, i + step) for i in range(size) if 0 <=...]
    ppermute x3, waiting for transfers between devices: 0.01 us -> 32 us  [on_device(): lax.ppermute(blocks[r], 'batch', [(i, (i + r) % homes) for i in range(hom...]
    ppermute x12, waiting for transfers between devices: 20.9 us -> 2.76 us  [on_device(): lax.ppermute(parts[o], 'tensor', [(i, i ^ o) for i in range(pieces)])]
    ppermute x1 -> x2, waiting for transfers between devices: 0.01 us -> 10.7 us  [reduce_base(): lax.ppermute(sent, 'tensor', [(i, i ^ bit) for i in range(pieces)])]
    dot_general x2 -> x0, matrix products: 6.28 us -> none  [part(): jnp.dot(tokens, chosen.reshape(width, pieces // 2 * columns), preferred_e...]
    ppermute x3, starting transfers between devices: 10.5 us -> 4.43 us  [on_device(): lax.ppermute(total, 'batch', [(i, (i - r) % homes) for i in range(homes)])]
    unnamed x81 -> x36, local copies, waits for them, and re-layouts: 19 us -> 12.9 us
    pallas_call x1 -> x5, Pallas kernels: 2.54 us -> 8.24 us  [the longest x2 5.92 us: base_part(): pl.pallas_call(functools.partial(base_kernel, len(after)), out_shape=jax....]
  transfers between devices with their start and end apart: 27 -> 27, of which waited for: 8 -> 8; matrix products, arithmetic and copies ran while one was open for 19% -> 5% of each run, Pallas kernels for 8% -> 10%
where the time goes in v3:
time: 140 us; the launch traced here: 139 us
  waiting for transfers between devices  63.8 us (46%)
  starting transfers between devices  30.8 us (22%)
  Pallas kernels  21.2 us (15%)
  local copies, waits for them, and re-layouts  16.3 us (12%)
  other arithmetic  4.4 us (3%)
  between operations  2.63 us (2%)
    ppermute x3, waiting for transfers between devices, on_device(): lax.ppermute(blocks[r], 'batch', [(i, (i + r) % homes) for i in range(hom...  32 us
    ppermute x6, waiting for transfers between devices, line_step(): lax.ppermute(value, 'batch', [(i, i + step) for i in range(size) if 0 <=...  14.7 us
    unnamed x36, local copies, waits for them, and re-layouts  12.9 us
    ppermute x2, waiting for transfers between devices, reduce_base(): lax.ppermute(sent, 'tensor', [(i, i ^ bit) for i in range(pieces)])  10.7 us
    ppermute x6, starting transfers between devices, line_step(): lax.ppermute(value, 'batch', [(i, i + step) for i in range(size) if 0 <=...  10.1 us
    ppermute x12, starting transfers between devices, on_device(): lax.ppermute(parts[o], 'tensor', [(i, i ^ o) for i in range(pieces)])  7.83 us
    pallas_call x4, Pallas kernels, on_device(): pl.pallas_call(functools.partial(shrink_kernel, held, light, rank, pieces...  6.8 us
    pallas_call x2, Pallas kernels, base_part(): pl.pallas_call(functools.partial(base_kernel, len(after)), out_shape=jax....  5.92 us
  transfers between devices with their start and end apart: 27, of which 8 were waited for; matrix products, arithmetic and copies ran while one was open for 5% of the time, Pallas kernels for 10%

profile of v3, /device:TPU:0, one launch (start us, length us, event | category | flops | bytes accessed | tf_op | source)
XLA Modules:
  0.0 139.1 jit_solution(7648569559362377303)
XLA Ops:
  0.0 0.9 constant_dynamic-slice_fusion
  0.9 4.9 %collective-permute-start = (bf16[8,32,256]{2,1,0:T(8,128)(2,1)S(1)}, bf16[8,32,256]{2,1,0:T(8,128)(2,1)S(1)}, u32[]{:S(2)}, u32[]{:S(2)}) collective-permute-start(bf16[8,32,256]{2,1,0:T(8,128)(2,1)S(1)} %constant_dynamic-slice_fusion), channel_id=1, source_target_pairs={{0,4},{4,8},{8,12},{1,5},{5,9},{9,13},{2,6},{6,10},{10,14},{3,7},{... | collective-permute-start | bytes 393224 | tf_op jit(solution)/shard_map/ppermute | solution.py:161
  5.9 1.3 collective-permute-start.1
  7.2 0.7 reshape.7.request_ref
  7.9 1.9 %copy-done.3 = bf16[768,2048]{1,0:T(8,128)(2,1)S(1)} copy-done((bf16[768,2048]{1,0:T(8,128)(2,1)S(1)}, bf16[768,2048]{1,0:T(8,128)(2,1)}, u32[]{:S(2)}) %copy-start.3) | copy-done | bytes 3145752
  9.8 0.7 copy-done.9
  10.4 2.6 %route.1 = (s32[1,768]{1,0:T(1,128)S(1)}, s32[8,128]{1,0:T(8,128)S(1)}, bf16[216,2048]{1,0:T(8,128)(2,1)}) custom-call(s32[1]{0:T(128)} %bitcast.place_ref, s32[32]{0:T(128)S(1)} %copy-done.9, s32[1,768]{1,0:T(1,128)S(1)} %reshape.7.request_ref, bf16[768,2048]{1,0:T(8,128)(2,1)S(1)} %copy-done.3), custom_call_target="tpu_custom_call" | custom-call | tf_op jit(solution)/shard_map/route/pallas_call | solution.py:266
  13.0 2.3 %pack.1 = (bf16[216,2048]{1,0:T(8,128)(2,1)S(1)}, bf16[216,2048]{1,0:T(8,128)(2,1)S(1)}, bf16[216,2048]{1,0:T(8,128)(2,1)S(1)}) custom-call(s32[1,768]{1,0:T(1,128)S(1)} %get-tuple-element.28.index_ref, bf16[768,2048]{1,0:T(8,128)(2,1)S(1)} %copy-done.4, bf16[8,32,256]{2,1,0:T(8,128)(2,1)S(1)} %collective-permute-done.refs_0_, ...), custom_call_target="tpu_custom_call" | custom-call | tf_op jit(solution)/shard_map/pack/pallas_call | solution.py:279
  15.4 0.9 copy-done.10
  16.3 2.2 %copy-done.7 = bf16[2048,1024]{1,0:T(8,128)(2,1)S(1)} copy-done((bf16[2048,1024]{1,0:T(8,128)(2,1)S(1)}, bf16[2048,1024]{1,0:T(8,128)(2,1)}, u32[]{:S(2)}) %copy-start.7) | copy-done | bytes 4194328
  18.5 3.0 %base.2.refs_0_ = f32[768,512]{1,0:T(8,128)S(1)} custom-call(s32[2]{0:T(128)S(1)} %broadcast_xor_fusion.block_ref, bf16[768,2048]{1,0:T(8,128)(2,1)S(1)} %copy-done.4, bf16[2048,1024]{1,0:T(8,128)(2,1)S(1)} %copy-done.7, bf16[216,2048]{1,0:T(8,128)(2,1)S(1)} %get-tuple-element.29.refs_0_.block_ref), custom_call_target="tpu_custom_call" | custom-call | tf_op jit(solution)/shard_map/base/pallas_call | solution.py:208
  21.5 3.0 %base.3 = f32[768,512]{1,0:T(8,128)S(1)} custom-call(s32[2]{0:T(128)S(1)} %multiply_xor_fusion.block_ref, bf16[768,2048]{1,0:T(8,128)(2,1)S(1)} %copy-done.4, bf16[2048,1024]{1,0:T(8,128)(2,1)S(1)} %copy-done.8, f32[768,512]{1,0:T(8,128)S(1)} %base.2.refs_0_), custom_call_target="tpu_custom_call" | custom-call | tf_op jit(solution)/shard_map/base/pallas_call | solution.py:208
  25.3 1.1 slice.13
  26.3 1.5 %collective-permute-start.3 = (f32[768,256]{1,0:T(8,128)}, f32[768,256]{1,0:T(8,128)}, u32[]{:S(2)}, u32[]{:S(2)}) collective-permute-start(f32[768,256]{1,0:T(8,128)} %slice.13), channel_id=1, source_target_pairs={{0,2},{1,3},{2,0},{3,1},{4,6},{5,7},{6,4},{7,5},{8,10},{9,11},{10,... | collective-permute-start | bytes 2359304 | tf_op jit(solution)/shard_map/ppermute | solution.py:237
  27.8 3.7 %collective-permute-start.12 = (bf16[216,2048]{1,0:T(8,128)(2,1)}, bf16[216,2048]{1,0:T(8,128)(2,1)}, u32[]{:S(2)}, u32[]{:S(2)}) collective-permute-start(bf16[216,2048]{1,0:T(8,128)(2,1)} %get-tuple-element.34), channel_id=1, source_target_pairs={{0,8},{4,12},{8,0},{12,4},{1,9},{5,13},{9,1},{13,5},{2,10},{6,14},... | collective-permute-start | bytes 2654216 | tf_op jit(solution)/shard_map/ppermute | solution.py:291
  34.3 1.6 %collective-permute-start.17 = (bf16[216,2048]{1,0:T(8,128)(2,1)}, bf16[216,2048]{1,0:T(8,128)(2,1)S(1)}, u32[]{:S(2)}, u32[]{:S(2)}) collective-permute-start(bf16[216,2048]{1,0:T(8,128)(2,1)} %copy-done.10), channel_id=1, source_target_pairs={{0,4},{4,8},{8,12},{12,0},{1,5},{5,9},{9,13},{13,1},{2,6},{6,10},{... | collective-permute-start | bytes 2654216 | tf_op jit(solution)/shard_map/ppermute | solution.py:291
  36.0 10.3 %collective-permute-done.3 = f32[768,256]{1,0:T(8,128)} collective-permute-done((f32[768,256]{1,0:T(8,128)}, f32[768,256]{1,0:T(8,128)}, u32[]{:S(2)}, u32[]{:S(2)}) %collective-permute-start.3) | collective-permute-done | bytes 786464 | tf_op jit(solution)/shard_map/ppermute | solution.py:237
  46.2 1.5 %slice_add_fusion.refs_0_.base_ref = f32[768,256]{1,0:T(8,128)S(1)} fusion(f32[768,256]{1,0:T(8,128)} %collective-permute-done.3, f32[768,512]{1,0:T(8,128)} %copy-done.11), kind=kLoop, calls=%fused_computation.1 | loop fusion | flops 196608 | bytes 2359296 | tf_op jit(solution)/shard_map/add | solution.py:237
  47.7 2.2 %copy-done = bf16[8,2048,128]{2,1,0:T(8,128)(2,1)S(1)} copy-done((bf16[8,2048,128]{2,1,0:T(8,128)(2,1)S(1)}, bf16[8,2048,128]{2,1,0:T(8,128)(2,1)}, u32[]{:S(2)}) %copy-start) | copy-done | bytes 4194328
  49.9 1.4 shrink.4
  51.3 1.6 %collective-permute-start.10 = (f32[120,128]{1,0:T(8,128)S(1)}, f32[120,128]{1,0:T(8,128)S(1)}, u32[]{:S(2)}, u32[]{:S(2)}) collective-permute-start(f32[120,128]{1,0:T(8,128)S(1)} %get-tuple-element.32), channel_id=1, source_target_pairs={{0,2},{1,3},{2,0},{3,1},{4,6},{5,7},{6,4},{7,5},{8,10},{9,11},{10,... | collective-permute-start | bytes 184328 | tf_op jit(solution)/shard_map/ppermute | solution.py:316
  52.9 0.6 collective-permute-start.9
  53.5 2.1 %collective-permute-done.10 = f32[120,128]{1,0:T(8,128)S(1)} collective-permute-done((f32[120,128]{1,0:T(8,128)S(1)}, f32[120,128]{1,0:T(8,128)S(1)}, u32[]{:S(2)}, u32[]{:S(2)}) %collective-permute-start.10) | collective-permute-done | bytes 61472 | tf_op jit(solution)/shard_map/ppermute | solution.py:316
  55.6 0.7 collective-permute-start.6
  56.3 0.7 collective-permute-done.11
  56.9 1.3 collective-permute-start.4
  58.2 32.0 %collective-permute-done.12.block_ref = bf16[216,2048]{1,0:T(8,128)(2,1)} collective-permute-done((bf16[216,2048]{1,0:T(8,128)(2,1)}, bf16[216,2048]{1,0:T(8,128)(2,1)}, u32[]{:S(2)}, u32[]{:S(2)}) %collective-permute-start.12) | collective-permute-done | bytes 884768 | tf_op jit(solution)/shard_map/ppermute | solution.py:291
  90.2 2.7 %shrink.5 = (f32[120,128]{1,0:T(8,128)S(1)}, f32[120,128]{1,0:T(8,128)}, f32[120,128]{1,0:T(8,128)}, f32[120,128]{1,0:T(8,128)S(1)}) custom-call(s32[3]{0:T(128)S(1)} %pad_add_fusion.1.scalar_ref, bf16[216,2048]{1,0:T(8,128)(2,1)} %collective-permute-done.12.block_ref, bf16[8,2048,128]{2,1,0:T(8,128)(2,1)S(1)} %copy-done.1, f32[120,128]{1,0:T(8,128)S(1)} %add_add_fusion.3.refs_0_), custom_call_target="tpu_custom_call" | custom-call | tf_op jit(solution)/shard_map/shrink/pallas_call | solution.py:306
  93.4 1.3 collective-permute-start.15
  95.0 0.7 copy.13.value_ref
  95.6 0.7 copy-done.14
  96.3 1.6 %copy.12.value_ref = bf16[8,32,256]{2,1,0:T(8,128)(2,1)} copy(bf16[8,32,256]{2,1,0:T(8,128)(2,1)} %copy-done.14) | data formatting | bytes 262144
  97.8 0.7 collective-permute-start.7
  98.5 1.3 collective-permute-start.5
  99.8 0.9 add_add_fusion.2.refs_0_
  100.8 2.2 %copy-done.2 = bf16[8,2048,128]{2,1,0:T(8,128)(2,1)S(1)} copy-done((bf16[8,2048,128]{2,1,0:T(8,128)(2,1)S(1)}, bf16[8,2048,128]{2,1,0:T(8,128)(2,1)}, u32[]{:S(2)}) %copy-start.2) | copy-done | bytes 4194328
  103.0 1.4 shrink.6
  105.2 1.0 collective-permute-start.20
  106.2 14.7 %collective-permute-done.5 = bf16[8,32,256]{2,1,0:T(8,128)(2,1)S(1)} collective-permute-done((bf16[8,32,256]{2,1,0:T(8,128)(2,1)}, bf16[8,32,256]{2,1,0:T(8,128)(2,1)S(1)}, u32[]{:S(2)}, u32[]{:S(2)}) %collective-permute-start.5) | collective-permute-done | bytes 131104 | tf_op jit(solution)/shard_map/ppermute | solution.py:161
  121.7 1.6 %collective-permute-start.8 = (bf16[32,32,256]{2,1,0:T(8,128)(2,1)S(1)}, bf16[32,32,256]{2,1,0:T(8,128)(2,1)S(1)}, u32[]{:S(2)}, u32[]{:S(2)}) collective-permute-start(bf16[32,32,256]{2,1,0:T(8,128)(2,1)S(1)} %pad_maximum_fusion.1), channel_id=1, source_target_pairs={{0,16},{16,0},{1,17},{17,1},{2,18},{18,2},{3,19},{19,3},{4,20},{20... | collective-permute-start | bytes 1572872 | tf_op jit(solution)/shard_map/ppermute | solution.py:185
  123.3 1.4 shrink.7
  125.3 1.3 collective-permute-start.25
  126.6 0.6 pad_add_fusion.place_ref
  127.2 2.0 %collective-permute-start.16 = (f32[120,128]{1,0:T(8,128)S(1)}, f32[120,128]{1,0:T(8,128)S(1)}, u32[]{:S(2)}, u32[]{:S(2)}) collective-permute-start(f32[120,128]{1,0:T(8,128)S(1)} %add_add_fusion.2.refs_0_), channel_id=1, source_target_pairs={{0,8},{4,12},{8,0},{12,4},{1,9},{5,13},{9,1},{13,5},{2,10},{6,14},... | collective-permute-start | bytes 184328 | tf_op jit(solution)/shard_map/ppermute | solution.py:319
  129.2 1.9 %collective-permute-start.21 = (f32[120,128]{1,0:T(8,128)S(1)}, f32[120,128]{1,0:T(8,128)S(1)}, u32[]{:S(2)}, u32[]{:S(2)}) collective-permute-start(f32[120,128]{1,0:T(8,128)S(1)} %add_add_fusion.1.refs_0_), channel_id=1, source_target_pairs={{0,12},{4,0},{8,4},{12,8},{1,13},{5,1},{9,5},{13,9},{2,14},{6,2},{... | collective-permute-start | bytes 184328 | tf_op jit(solution)/shard_map/ppermute | solution.py:319
  131.7 3.3 %collective-permute-done.8 = bf16[32,32,256]{2,1,0:T(8,128)(2,1)S(1)} collective-permute-done((bf16[32,32,256]{2,1,0:T(8,128)(2,1)S(1)}, bf16[32,32,256]{2,1,0:T(8,128)(2,1)S(1)}, u32[]{:S(2)}, u32[]{:S(2)}) %collective-permute-start.8) | collective-permute-done | bytes 524320 | tf_op jit(solution)/shard_map/ppermute | solution.py:185
  135.2 1.6 %finish.2.base_ref = f32[768,256]{1,0:T(8,128)S(1)} custom-call(s32[2]{0:T(128)S(1)} %pad_add_fusion.place_ref, s32[768,1]{1,0:T(8,128)S(1)} %copy.11.index_ref, f32[768,256]{1,0:T(8,128)S(1)} %copy-done.6, bf16[32,64,256]{2,1,0:T(8,128)(2,1)S(1)} %pad_maximum_fusion.up_ref, f32[120,128]{1,0:T(8,128)S(1)} %add_add_fusion.3.refs_0_, ...), custom_call_target="tpu_custom_call" | custom-call | tf_op jit(solution)/shard_map/finish/pallas_call | solution.py:133
  137.2 1.9 %finish.3 = bf16[768,256]{1,0:T(8,128)(2,1)} custom-call(s32[2]{0:T(128)S(1)} %pad_add_fusion.place_ref, s32[768,1]{1,0:T(8,128)S(1)} %copy.11.index_ref, f32[768,256]{1,0:T(8,128)S(1)} %finish.2.base_ref, bf16[32,64,256]{2,1,0:T(8,128)(2,1)S(1)} %pad_maximum_fusion.up_ref, f32[120,128]{1,0:T(8,128)S(1)} %collective-permute-done.26.refs_0_), custom_call_target="tpu_custom_call" | custom-call | tf_op jit(solution)/shard_map/finish/pallas_call | solution.py:133
  (76 shorter events, 5.5 us)
Async XLA Ops:
  0.9 12.1 %collective-permute-start = (bf16[8,32,256]{2,1,0:T(8,128)(2,1)S(1)}, bf16[8,32,256]{2,1,0:T(8,128)(2,1)S(1)}, u32[]{:S(2)}, u32[]{:S(2)}) collective-permute-start(bf16[8,32,256]{2,1,0:T(8,128)(2,1)S(1)} %constant_dynamic-slice_fusion), channel_id=1, source_target_pairs={{0,4},{4,8},{8,12},{1,5},{5,9},{9,13},{2,6},{6,10},{10,14},{3,7},{... | collective-permute-start | bytes 393224 | tf_op jit(solution)/shard_map/ppermute | solution.py:161
  5.9 7.2 %collective-permute-start.1 = (bf16[8,32,256]{2,1,0:T(8,128)(2,1)S(1)}, bf16[8,32,256]{2,1,0:T(8,128)(2,1)S(1)}, u32[]{:S(2)}, u32[]{:S(2)}) collective-permute-start(bf16[8,32,256]{2,1,0:T(8,128)(2,1)S(1)} %constant_dynamic-slice_fusion), channel_id=1, source_target_pairs={{4,0},{8,4},{12,8},{5,1},{9,5},{13,9},{6,2},{10,6},{14,10},{7,3},{... | collective-permute-start | bytes 393224 | tf_op jit(solution)/shard_map/ppermute | solution.py:161
  7.9 1.9 %copy-start.3 = (bf16[768,2048]{1,0:T(8,128)(2,1)S(1)}, bf16[768,2048]{1,0:T(8,128)(2,1)}, u32[]{:S(2)}) copy-start(bf16[768,2048]{1,0:T(8,128)(2,1)} %tokens_ref.7) | copy-start | bytes 9437188
  9.7 0.7 copy-start.9
  10.4 2.6 %copy-start.4 = (bf16[768,2048]{1,0:T(8,128)(2,1)S(1)}, bf16[768,2048]{1,0:T(8,128)(2,1)}, u32[]{:S(2)}) copy-start(bf16[768,2048]{1,0:T(8,128)(2,1)} %tokens_ref.7) | copy-start | bytes 9437188
  15.4 0.9 copy-start.10
  16.3 2.2 %copy-start.7 = (bf16[2048,1024]{1,0:T(8,128)(2,1)S(1)}, bf16[2048,1024]{1,0:T(8,128)(2,1)}, u32[]{:S(2)}) copy-start(bf16[2048,1024]{1,0:T(8,128)(2,1)} %weight_ref.3) | copy-start | bytes 12582916
  18.5 3.1 %copy-start.8 = (bf16[2048,1024]{1,0:T(8,128)(2,1)S(1)}, bf16[2048,1024]{1,0:T(8,128)(2,1)}, u32[]{:S(2)}) copy-start(bf16[2048,1024]{1,0:T(8,128)(2,1)} %weight_ref.3) | copy-start | bytes 12582916
  21.4 3.5 %collective-permute-start.2 = (f32[768,512]{1,0:T(8,128)S(1)}, f32[768,512]{1,0:T(8,128)S(1)}, u32[]{:S(2)}, u32[]{:S(2)}) collective-permute-start(f32[768,512]{1,0:T(8,128)S(1)} %base.2.refs_0_), channel_id=1, source_target_pairs={{0,1},{1,0},{2,3},{3,2},{4,5},{5,4},{6,7},{7,6},{8,9},{9,8},{10,11... | collective-permute-start | bytes 4718600 | tf_op jit(solution)/shard_map/ppermute | solution.py:237
  25.3 6.7 %copy-start.11 = (f32[768,512]{1,0:T(8,128)}, f32[768,512]{1,0:T(8,128)S(1)}, u32[]{:S(2)}) copy-start(f32[768,512]{1,0:T(8,128)S(1)} %add.88) | copy-start | bytes 4718596
  26.3 19.9 %collective-permute-start.3 = (f32[768,256]{1,0:T(8,128)}, f32[768,256]{1,0:T(8,128)}, u32[]{:S(2)}, u32[]{:S(2)}) collective-permute-start(f32[768,256]{1,0:T(8,128)} %slice.13), channel_id=1, source_target_pairs={{0,2},{1,3},{2,0},{3,1},{4,6},{5,7},{6,4},{7,5},{8,10},{9,11},{10,... | collective-permute-start | bytes 2359304 | tf_op jit(solution)/shard_map/ppermute | solution.py:237
  27.8 62.4 %collective-permute-start.12 = (bf16[216,2048]{1,0:T(8,128)(2,1)}, bf16[216,2048]{1,0:T(8,128)(2,1)}, u32[]{:S(2)}, u32[]{:S(2)}) collective-permute-start(bf16[216,2048]{1,0:T(8,128)(2,1)} %get-tuple-element.34), channel_id=1, source_target_pairs={{0,8},{4,12},{8,0},{12,4},{1,9},{5,13},{9,1},{13,5},{2,10},{6,14},... | collective-permute-start | bytes 2654216 | tf_op jit(solution)/shard_map/ppermute | solution.py:291
  34.3 66.5 %collective-permute-start.17 = (bf16[216,2048]{1,0:T(8,128)(2,1)}, bf16[216,2048]{1,0:T(8,128)(2,1)S(1)}, u32[]{:S(2)}, u32[]{:S(2)}) collective-permute-start(bf16[216,2048]{1,0:T(8,128)(2,1)} %copy-done.10), channel_id=1, source_target_pairs={{0,4},{4,8},{8,12},{12,0},{1,5},{5,9},{9,13},{13,1},{2,6},{6,10},{... | collective-permute-start | bytes 2654216 | tf_op jit(solution)/shard_map/ppermute | solution.py:291
  47.7 2.2 %copy-start = (bf16[8,2048,128]{2,1,0:T(8,128)(2,1)S(1)}, bf16[8,2048,128]{2,1,0:T(8,128)(2,1)}, u32[]{:S(2)}) copy-start(bf16[8,2048,128]{2,1,0:T(8,128)(2,1)} %down_ref.7) | copy-start | bytes 12582916
  49.9 1.4 %copy-start.5 = (f32[768,256]{1,0:T(8,128)}, f32[768,256]{1,0:T(8,128)S(1)}, u32[]{:S(2)}) copy-start(f32[768,256]{1,0:T(8,128)S(1)} %slice_add_fusion.refs_0_.base_ref) | copy-start | bytes 2359300
  49.9 40.3 %copy-start.1 = (bf16[8,2048,128]{2,1,0:T(8,128)(2,1)S(1)}, bf16[8,2048,128]{2,1,0:T(8,128)(2,1)}, u32[]{:S(2)}) copy-start(bf16[8,2048,128]{2,1,0:T(8,128)(2,1)} %down_ref.7) | copy-start | bytes 12582916
  51.3 4.3 %collective-permute-start.10 = (f32[120,128]{1,0:T(8,128)S(1)}, f32[120,128]{1,0:T(8,128)S(1)}, u32[]{:S(2)}, u32[]{:S(2)}) collective-permute-start(f32[120,128]{1,0:T(8,128)S(1)} %get-tuple-element.32), channel_id=1, source_target_pairs={{0,2},{1,3},{2,0},{3,1},{4,6},{5,7},{6,4},{7,5},{8,10},{9,11},{10,... | collective-permute-start | bytes 184328 | tf_op jit(solution)/shard_map/ppermute | solution.py:316
  52.9 4.0 %collective-permute-start.11 = (f32[120,128]{1,0:T(8,128)S(1)}, f32[120,128]{1,0:T(8,128)S(1)}, u32[]{:S(2)}, u32[]{:S(2)}) collective-permute-start(f32[120,128]{1,0:T(8,128)S(1)} %get-tuple-element.33), channel_id=1, source_target_pairs={{0,3},{1,2},{2,1},{3,0},{4,7},{5,6},{6,5},{7,4},{8,11},{9,10},{10,... | collective-permute-start | bytes 184328 | tf_op jit(solution)/shard_map/ppermute | solution.py:316
  52.9 5.3 %collective-permute-start.9 = (f32[120,128]{1,0:T(8,128)S(1)}, f32[120,128]{1,0:T(8,128)S(1)}, u32[]{:S(2)}, u32[]{:S(2)}) collective-permute-start(f32[120,128]{1,0:T(8,128)S(1)} %get-tuple-element.31), channel_id=1, source_target_pairs={{0,1},{1,0},{2,3},{3,2},{4,5},{5,4},{6,7},{7,6},{8,9},{9,8},{10,11... | collective-permute-start | bytes 184328 | tf_op jit(solution)/shard_map/ppermute | solution.py:316
  55.6 37.9 %collective-permute-start.6 = (bf16[8,32,256]{2,1,0:T(8,128)(2,1)S(1)}, bf16[8,32,256]{2,1,0:T(8,128)(2,1)S(1)}, u32[]{:S(2)}, u32[]{:S(2)}) collective-permute-start(bf16[8,32,256]{2,1,0:T(8,128)(2,1)S(1)} %collective-permute-done.refs_0_), channel_id=1, source_target_pairs={{4,8},{8,12},{5,9},{9,13},{6,10},{10,14},{7,11},{11,15},{20,24},{2... | collective-permute-start | bytes 393224 | tf_op jit(solution)/shard_map/ppermute | solution.py:161
  56.9 38.7 %collective-permute-start.4 = (bf16[8,32,256]{2,1,0:T(8,128)(2,1)S(1)}, bf16[8,32,256]{2,1,0:T(8,128)(2,1)S(1)}, u32[]{:S(2)}, u32[]{:S(2)}) collective-permute-start(bf16[8,32,256]{2,1,0:T(8,128)(2,1)S(1)} %collective-permute-done.1.refs_1_), channel_id=1, source_target_pairs={{4,0},{8,4},{5,1},{9,5},{6,2},{10,6},{7,3},{11,7},{20,16},{24,20},... | collective-permute-start | bytes 393224 | tf_op jit(solution)/shard_map/ppermute | solution.py:161
  92.9 5.0 %collective-permute-start.13 = (f32[120,128]{1,0:T(8,128)}, f32[120,128]{1,0:T(8,128)}, u32[]{:S(2)}, u32[]{:S(2)}) collective-permute-start(f32[120,128]{1,0:T(8,128)} %get-tuple-element.36), channel_id=1, source_target_pairs={{0,1},{1,0},{2,3},{3,2},{4,5},{5,4},{6,7},{7,6},{8,9},{9,8},{10,11... | collective-permute-start | bytes 184328 | tf_op jit(solution)/shard_map/ppermute | solution.py:316
  92.9 5.6 %collective-permute-start.14 = (f32[120,128]{1,0:T(8,128)}, f32[120,128]{1,0:T(8,128)}, u32[]{:S(2)}, u32[]{:S(2)}) collective-permute-start(f32[120,128]{1,0:T(8,128)} %get-tuple-element.37), channel_id=1, source_target_pairs={{0,2},{1,3},{2,0},{3,1},{4,6},{5,7},{6,4},{7,5},{8,10},{9,11},{10,... | collective-permute-start | bytes 184328 | tf_op jit(solution)/shard_map/ppermute | solution.py:316
  93.4 2.2 %copy-start.12 = (bf16[8,32,256]{2,1,0:T(8,128)(2,1)}, bf16[8,32,256]{2,1,0:T(8,128)(2,1)S(1)}, u32[]{:S(2)}) copy-start(bf16[8,32,256]{2,1,0:T(8,128)(2,1)S(1)} %collective-permute-done.6) | copy-start | bytes 393220
  93.4 6.4 %collective-permute-start.15 = (f32[120,128]{1,0:T(8,128)S(1)}, f32[120,128]{1,0:T(8,128)}, u32[]{:S(2)}, u32[]{:S(2)}) collective-permute-start(f32[120,128]{1,0:T(8,128)S(1)} %get-tuple-element.38), channel_id=1, source_target_pairs={{0,3},{1,2},{2,1},{3,0},{4,7},{5,6},{6,5},{7,4},{8,11},{9,10},{10,... | collective-permute-start | bytes 184328 | tf_op jit(solution)/shard_map/ppermute | solution.py:316
  95.6 0.7 copy-start.14
  96.3 27.0 %collective-permute-start.22 = (bf16[216,2048]{1,0:T(8,128)(2,1)S(1)}, bf16[216,2048]{1,0:T(8,128)(2,1)S(1)}, u32[]{:S(2)}, u32[]{:S(2)}) collective-permute-start(bf16[216,2048]{1,0:T(8,128)(2,1)S(1)} %get-tuple-element.44), channel_id=1, source_target_pairs={{0,12},{4,0},{8,4},{12,8},{1,13},{5,1},{9,5},{13,9},{2,14},{6,2},{... | collective-permute-start | bytes 2654216 | tf_op jit(solution)/shard_map/ppermute | solution.py:291
  97.8 7.3 %collective-permute-start.7 = (bf16[8,32,256]{2,1,0:T(8,128)(2,1)}, bf16[8,32,256]{2,1,0:T(8,128)(2,1)S(1)}, u32[]{:S(2)}, u32[]{:S(2)}) collective-permute-start(bf16[8,32,256]{2,1,0:T(8,128)(2,1)} %gate.3), channel_id=1, source_target_pairs={{8,12},{9,13},{10,14},{11,15},{24,28},{25,29},{26,30},{27,31}} | collective-permute-start | bytes 393224 | tf_op jit(solution)/shard_map/ppermute | solution.py:161
  98.5 22.4 %collective-permute-start.5 = (bf16[8,32,256]{2,1,0:T(8,128)(2,1)}, bf16[8,32,256]{2,1,0:T(8,128)(2,1)S(1)}, u32[]{:S(2)}, u32[]{:S(2)}) collective-permute-start(bf16[8,32,256]{2,1,0:T(8,128)(2,1)} %gate.2), channel_id=1, source_target_pairs={{4,0},{5,1},{6,2},{7,3},{20,16},{21,17},{22,18},{23,19}} | collective-permute-start | bytes 393224 | tf_op jit(solution)/shard_map/ppermute | solution.py:161
  100.8 2.2 %copy-start.2 = (bf16[8,2048,128]{2,1,0:T(8,128)(2,1)S(1)}, bf16[8,2048,128]{2,1,0:T(8,128)(2,1)}, u32[]{:S(2)}) copy-start(bf16[8,2048,128]{2,1,0:T(8,128)(2,1)} %down_ref.7) | copy-start | bytes 12582916
  102.9 18.0 %copy-start.13 = (bf16[8,32,256]{2,1,0:T(8,128)(2,1)S(1)}, bf16[8,32,256]{2,1,0:T(8,128)(2,1)}, u32[]{:S(2)}) copy-start(bf16[8,32,256]{2,1,0:T(8,128)(2,1)} %copy-done.12) | copy-start | bytes 393220
  102.9 18.0 %copy-start.15 = (bf16[8,32,256]{2,1,0:T(8,128)(2,1)S(1)}, bf16[8,32,256]{2,1,0:T(8,128)(2,1)}, u32[]{:S(2)}) copy-start(bf16[8,32,256]{2,1,0:T(8,128)(2,1)} %copy-done.14) | copy-start | bytes 393220
  102.9 18.0 %copy-start.16 = (bf16[8,64,256]{2,1,0:T(8,128)(2,1)S(1)}, bf16[8,64,256]{2,1,0:T(8,128)(2,1)}, u32[]{:S(2)}) copy-start(bf16[8,64,256]{2,1,0:T(8,128)(2,1)} %param.12) | copy-start | bytes 786436
  104.3 18.9 %collective-permute-start.18 = (f32[120,128]{1,0:T(8,128)S(1)}, f32[120,128]{1,0:T(8,128)S(1)}, u32[]{:S(2)}, u32[]{:S(2)}) collective-permute-start(f32[120,128]{1,0:T(8,128)S(1)} %get-tuple-element.41), channel_id=1, source_target_pairs={{0,1},{1,0},{2,3},{3,2},{4,5},{5,4},{6,7},{7,6},{8,9},{9,8},{10,11... | collective-permute-start | bytes 184328 | tf_op jit(solution)/shard_map/ppermute | solution.py:316
  104.6 18.6 %collective-permute-start.19 = (f32[120,128]{1,0:T(8,128)S(1)}, f32[120,128]{1,0:T(8,128)S(1)}, u32[]{:S(2)}, u32[]{:S(2)}) collective-permute-start(f32[120,128]{1,0:T(8,128)S(1)} %get-tuple-element.42), channel_id=1, source_target_pairs={{0,2},{1,3},{2,0},{3,1},{4,6},{5,7},{6,4},{7,5},{8,10},{9,11},{10,... | collective-permute-start | bytes 184328 | tf_op jit(solution)/shard_map/ppermute | solution.py:316
  105.2 18.1 %collective-permute-start.20 = (f32[120,128]{1,0:T(8,128)S(1)}, f32[120,128]{1,0:T(8,128)S(1)}, u32[]{:S(2)}, u32[]{:S(2)}) collective-permute-start(f32[120,128]{1,0:T(8,128)S(1)} %get-tuple-element.43), channel_id=1, source_target_pairs={{0,3},{1,2},{2,1},{3,0},{4,7},{5,6},{6,5},{7,4},{8,11},{9,10},{10,... | collective-permute-start | bytes 184328 | tf_op jit(solution)/shard_map/ppermute | solution.py:316
  121.7 13.4 %collective-permute-start.8 = (bf16[32,32,256]{2,1,0:T(8,128)(2,1)S(1)}, bf16[32,32,256]{2,1,0:T(8,128)(2,1)S(1)}, u32[]{:S(2)}, u32[]{:S(2)}) collective-permute-start(bf16[32,32,256]{2,1,0:T(8,128)(2,1)S(1)} %pad_maximum_fusion.1), channel_id=1, source_target_pairs={{0,16},{16,0},{1,17},{17,1},{2,18},{18,2},{3,19},{19,3},{4,20},{20... | collective-permute-start | bytes 1572872 | tf_op jit(solution)/shard_map/ppermute | solution.py:185
  124.7 4.5 %collective-permute-start.23 = (f32[120,128]{1,0:T(8,128)S(1)}, f32[120,128]{1,0:T(8,128)S(1)}, u32[]{:S(2)}, u32[]{:S(2)}) collective-permute-start(f32[120,128]{1,0:T(8,128)S(1)} %get-tuple-element.46), channel_id=1, source_target_pairs={{0,1},{1,0},{2,3},{3,2},{4,5},{5,4},{6,7},{7,6},{8,9},{9,8},{10,11... | collective-permute-start | bytes 184328 | tf_op jit(solution)/shard_map/ppermute | solution.py:316
  124.7 6.4 %collective-permute-start.24 = (f32[120,128]{1,0:T(8,128)S(1)}, f32[120,128]{1,0:T(8,128)S(1)}, u32[]{:S(2)}, u32[]{:S(2)}) collective-permute-start(f32[120,128]{1,0:T(8,128)S(1)} %get-tuple-element.47), channel_id=1, source_target_pairs={{0,2},{1,3},{2,0},{3,1},{4,6},{5,7},{6,4},{7,5},{8,10},{9,11},{10,... | collective-permute-start | bytes 184328 | tf_op jit(solution)/shard_map/ppermute | solution.py:316
  125.3 5.8 %collective-permute-start.25 = (f32[120,128]{1,0:T(8,128)S(1)}, f32[120,128]{1,0:T(8,128)S(1)}, u32[]{:S(2)}, u32[]{:S(2)}) collective-permute-start(f32[120,128]{1,0:T(8,128)S(1)} %get-tuple-element.48), channel_id=1, source_target_pairs={{0,3},{1,2},{2,1},{3,0},{4,7},{5,6},{6,5},{7,4},{8,11},{9,10},{10,... | collective-permute-start | bytes 184328 | tf_op jit(solution)/shard_map/ppermute | solution.py:316
  127.2 8.0 %collective-permute-start.16 = (f32[120,128]{1,0:T(8,128)S(1)}, f32[120,128]{1,0:T(8,128)S(1)}, u32[]{:S(2)}, u32[]{:S(2)}) collective-permute-start(f32[120,128]{1,0:T(8,128)S(1)} %add_add_fusion.2.refs_0_), channel_id=1, source_target_pairs={{0,8},{4,12},{8,0},{12,4},{1,9},{5,13},{9,1},{13,5},{2,10},{6,14},... | collective-permute-start | bytes 184328 | tf_op jit(solution)/shard_map/ppermute | solution.py:319
  129.2 6.0 %collective-permute-start.21 = (f32[120,128]{1,0:T(8,128)S(1)}, f32[120,128]{1,0:T(8,128)S(1)}, u32[]{:S(2)}, u32[]{:S(2)}) collective-permute-start(f32[120,128]{1,0:T(8,128)S(1)} %add_add_fusion.1.refs_0_), channel_id=1, source_target_pairs={{0,12},{4,0},{8,4},{12,8},{1,13},{5,1},{9,5},{13,9},{2,14},{6,2},{... | collective-permute-start | bytes 184328 | tf_op jit(solution)/shard_map/ppermute | solution.py:319
  131.1 4.1 %copy-start.6 = (f32[768,256]{1,0:T(8,128)S(1)}, f32[768,256]{1,0:T(8,128)}, u32[]{:S(2)}) copy-start(f32[768,256]{1,0:T(8,128)} %copy-done.5) | copy-start | bytes 2359300
  131.1 6.1 %collective-permute-start.26 = (f32[120,128]{1,0:T(8,128)S(1)}, f32[120,128]{1,0:T(8,128)S(1)}, u32[]{:S(2)}, u32[]{:S(2)}) collective-permute-start(f32[120,128]{1,0:T(8,128)S(1)} %add_add_fusion.refs_3_), channel_id=1, source_target_pairs={{0,4},{4,8},{8,12},{12,0},{1,5},{5,9},{9,13},{13,1},{2,6},{6,10},{... | collective-permute-start | bytes 184328 | tf_op jit(solution)/shard_map/ppermute | solution.py:319

commit v4 on v3

v4 whole, which is shorter than its diff:
```python
import functools

import jax
import jax.numpy as jnp
from jax import lax
from jax.experimental import pallas as pl
from jax.experimental.pallas import tpu as pltpu
from jax.sharding import PartitionSpec as P

adapter_scale = 0.5
VMEM_BYTES = 24 * 1024 * 1024
VMEM = pl.BlockSpec(memory_space=pltpu.VMEM)
ANY = pl.BlockSpec(memory_space=pl.ANY)
SMEM = pl.BlockSpec(memory_space=pltpu.SMEM)
COST = pl.CostEstimate(flops=1, bytes_accessed=1, transcendentals=0)
PARAMS = pltpu.CompilerParams(vmem_limit_bytes=VMEM_BYTES)


def place_rows(index, start, tokens_ref, block_ref):
    local = lax.broadcasted_iota(jnp.int32, (block_ref.shape[0], index.shape[1]), 0)
    choose = (local + start == index).astype(jnp.bfloat16)
    block_ref[...] = jnp.dot(
        choose, tokens_ref[...], preferred_element_type=jnp.float32
    ).astype(jnp.bfloat16)


def route_kernel(
    homes, held, light, shift, place_ref, entry_hbm, request_hbm, tokens_hbm,
    index_ref, heavy_ref, block_ref, entry_ref, request_ref, tokens_ref, sems,
):
    loads = [
        pltpu.make_async_copy(source, target, sems.at[n])
        for n, (source, target) in enumerate(
            [(request_hbm, request_ref), (entry_hbm, entry_ref), (tokens_hbm, tokens_ref)]
        )
    ]
    for load in loads:
        load.start()
    rows = tokens_ref.shape[0]
    adapters = entry_ref.shape[0]
    span = (held + 1) * light
    earlier = (
        lax.broadcasted_iota(jnp.int32, (rows, rows), 0) < lax.broadcasted_iota(jnp.int32, (rows, rows), 1)
    ).astype(jnp.bfloat16)
    loads[0].wait()
    request = request_ref[...].reshape(1, rows)
    onehot = lax.broadcasted_iota(jnp.int32, (adapters, rows), 0) == request
    before = jnp.dot(onehot.astype(jnp.bfloat16), earlier, preferred_element_type=jnp.float32)
    position = jnp.sum(jnp.where(onehot, before, 0.0), axis=0, keepdims=True).astype(jnp.int32)
    loads[1].wait()
    slot = jnp.zeros_like(position)
    for a in range(adapters):
        slot = jnp.where(request == a, entry_ref[a], slot)
    home = slot // held
    relative = lax.rem(home - place_ref[0] + homes, homes)
    inside = jnp.where(
        position < light, (slot - home * held) * light + position, held * light + position - light
    )
    index = relative * span + inside
    index_ref[...] = index
    heavy = jnp.max(jnp.where(position >= light, slot, 0), axis=1, keepdims=True)
    heavy_ref[...] = jnp.broadcast_to(heavy, heavy_ref.shape)
    loads[2].wait()
    place_rows(index, shift * span, tokens_ref, block_ref)


def pack_kernel(span, shifts, index_ref, tokens_ref, mark_ref, *block_refs):
    mark_ref[...] = jnp.zeros_like(mark_ref)
    for shift, block_ref in zip(shifts, block_refs):
        place_rows(index_ref[...], shift * span, tokens_ref, block_ref)


def entry_places(held):
    return (held + 2) // 2


def shrink_kernel(held, light, rank, value_side, waited, passed, scalar_ref, block_ref, down_ref, *refs):
    passed_refs, out_ref, left_refs = refs[waited : waited + passed], refs[waited + passed], refs[waited + passed + 1 :]
    groups = entry_places(held)

    def product(e):
        if e > held:
            return jnp.zeros((light, 2 * rank), jnp.float32)
        factor = down_ref[e] if e < held else down_ref[scalar_ref[1]]
        value = jnp.dot(
            block_ref[e * light : (e + 1) * light, :], factor, preferred_element_type=jnp.float32
        )
        return value if e < held else jnp.where(scalar_ref[2] == 1, value, 0.0)

    on_value_side = scalar_ref[0] >= value_side
    for g in range(groups):
        first, second = product(g), product(g + groups)
        key = jnp.concatenate([first[:, :rank], second[:, :rank]], axis=1)
        value = jnp.concatenate([first[:, rank:], second[:, rank:]], axis=1)
        out_ref[g * light : (g + 1) * light, :] = jnp.where(on_value_side, value, key)
        out_ref[(groups + g) * light : (groups + g + 1) * light, :] = jnp.where(on_value_side, key, value)
    for source, target in zip(passed_refs, left_refs):
        target[...] = source[...]


def split_pair(value):
    high = value.astype(jnp.bfloat16)
    low = (value - high.astype(jnp.float32)).astype(jnp.bfloat16)
    return high, low


def finish_kernel(homes, held, light, rank, shifts, waited, place_ref, index_ref, base_ref, up_ref, *refs):
    count = len(shifts)
    refs = refs[:count] + refs[count + waited :]
    shrink_refs, out_ref, high_ref, low_ref = refs[:count], refs[count], refs[count + 1], refs[count + 2]
    span = (held + 1) * light
    rows = base_ref.shape[0]
    groups = entry_places(held)
    local = []
    for n, r in enumerate(shifts):
        home = lax.rem(place_ref[0] + r, homes)
        for e in range(held + 1):
            entry = home * held + e if e < held else place_ref[1]
            g, side = e % groups, e // groups
            high, low = split_pair(
                shrink_refs[n][g * light : (g + 1) * light, side * rank : (side + 1) * rank]
            )
            factor = up_ref[entry]
            delta = jnp.dot(high, factor, preferred_element_type=jnp.float32) + jnp.dot(
                low, factor, preferred_element_type=jnp.float32
            )
            high, low = split_pair(delta)
            start = n * span + e * light
            high_ref[start : start + light, :] = high
            low_ref[start : start + light, :] = low
        local.append(lax.broadcasted_iota(jnp.int32, (rows, span), 1) + r * span == index_ref[...])
    delta = base_ref[...]
    for n in range(count):
        choose = local[n].astype(jnp.bfloat16)
        delta = delta + adapter_scale * (
            jnp.dot(choose, high_ref[n * span : (n + 1) * span, :], preferred_element_type=jnp.float32)
            + jnp.dot(choose, low_ref[n * span : (n + 1) * span, :], preferred_element_type=jnp.float32)
        )
    out_ref[...] = delta.astype(out_ref.dtype)


def finish(scalars, index, base, up, shrinks, after, shifts, dtype, homes, held, light):
    rows, columns = base.shape
    span = (held + 1) * light
    return pl.pallas_call(
        functools.partial(finish_kernel, homes, held, light, up.shape[1], shifts, len(after)),
        out_shape=jax.ShapeDtypeStruct((rows, columns), dtype),
        in_specs=[SMEM] + [VMEM] * (3 + len(shifts)) + [ANY] * len(after),
        out_specs=VMEM,
        scratch_shapes=[pltpu.VMEM((len(shifts) * span, columns), jnp.bfloat16)] * 2,
        compiler_params=PARAMS,
        cost_estimate=COST,
        name="finish",
    )(scalars, index, base, up, *shrinks, *after)


def join_kernel(first_ref, second_ref, after_ref, out_ref):
    count = first_ref.shape[0]
    out_ref[:count] = first_ref[...]
    out_ref[count:] = second_ref[...]


def join(first, second, after):
    return pl.pallas_call(
        join_kernel,
        out_shape=jax.ShapeDtypeStruct((2 * first.shape[0], *first.shape[1:]), first.dtype),
        in_specs=[VMEM, VMEM, ANY],
        out_specs=VMEM,
        compiler_params=PARAMS,
        cost_estimate=COST,
        name="join",
    )(first, second, after)


def line_gather(value, place, homes, after):
    if homes == 4:
        beside = lax.ppermute(value, "batch", [(0, 1), (1, 0), (2, 3), (3, 2)])
        across = lax.ppermute(join(value, beside, after), "batch", [(1, 2), (2, 1)])
        beyond = lax.ppermute(across, "batch", [(1, 0), (2, 3)])
        far = jnp.where((place == 1) | (place == 2), across, beyond)
        near, next_to = far[: value.shape[0]], far[value.shape[0] :]
        even = place % 2 == 0
        low, high = jnp.where(even, value, beside), jnp.where(even, beside, value)
        left = place < 2
        return jnp.concatenate(
            [
                jnp.where(left, low, next_to),
                jnp.where(left, high, near),
                jnp.where(left, near, low),
                jnp.where(left, next_to, high),
            ],
            axis=0,
        )
    bit = 1
    while bit < homes:
        other = lax.ppermute(value, "batch", [(i, i ^ bit) for i in range(homes)])
        first = (place // bit) % 2 == 0
        value = jnp.concatenate([jnp.where(first, value, other), jnp.where(first, other, value)], axis=0)
        bit *= 2
    return value


def gather_up(adapter_up, place, homes, after):
    teams = lax.axis_size("groups")
    team = lax.axis_index("groups")
    share = adapter_up.shape[1] // teams
    ordered = line_gather(lax.dynamic_slice_in_dim(adapter_up, team * share, share, 1), place, homes, after)
    shares = [ordered] + [
        lax.ppermute(ordered, "groups", [(i, (i + s) % teams) for i in range(teams)])
        for s in range(1, teams)
    ]
    return jnp.concatenate(
        [
            functools.reduce(
                lambda kept, s: jnp.where(lax.rem(team + teams - s, teams) == part, shares[s], kept),
                range(1, teams),
                shares[0],
            )
            for part in range(teams)
        ],
        axis=1,
    )


def base_kernel(waited, block_ref, tokens_ref, weight_ref, *refs):
    refs[waited][...] = jnp.dot(tokens_ref[...], weight_ref[...], preferred_element_type=jnp.float32)


def base_part(tokens, weight, blocks, columns, slab, slabs, after):
    rows, width = tokens.shape[0] // slabs, tokens.shape[1]
    count = blocks.shape[0]
    return pl.pallas_call(
        functools.partial(base_kernel, len(after)),
        out_shape=jax.ShapeDtypeStruct((rows, count * columns), jnp.float32),
        grid_spec=pltpu.PrefetchScalarGridSpec(
            num_scalar_prefetch=1,
            grid=(count,),
            in_specs=[
                pl.BlockSpec((rows, width), lambda j, chosen: (slab, 0)),
                pl.BlockSpec((width, columns), lambda j, chosen: (0, chosen[j])),
            ]
            + [ANY] * len(after),
            out_specs=pl.BlockSpec((rows, columns), lambda j, chosen: (0, j)),
        ),
        compiler_params=PARAMS,
        cost_estimate=COST,
        name="base",
    )(blocks, tokens, weight, *after)


def reduce_base(tokens, weight, piece, pieces, columns, slab, slabs, after):
    keep = [0]
    bit = pieces // 2
    while bit > 1:
        keep = keep + [p + bit for p in keep]
        bit //= 2
    keep = jnp.array(keep, jnp.int32)
    sent = base_part(tokens, weight, piece ^ keep ^ 1, columns, slab, slabs, after)
    kept = base_part(tokens, weight, piece ^ keep, columns, slab, slabs, [sent])
    bit = 1
    while True:
        kept = kept + lax.ppermute(sent, "tensor", [(i, i ^ bit) for i in range(pieces)])
        bit *= 2
        if bit >= pieces:
            return kept
        half = kept.shape[1] // 2
        kept, sent = kept[:, :half], kept[:, half:]


def on_device(tokens, request_adapter, adapter_entry, key_value_weight, adapter_down, adapter_up):
    rows, width = tokens.shape
    adapters = adapter_entry.shape[0]
    held, rank, columns = adapter_up.shape
    value_side = key_value_weight.shape[1] // 2 // columns
    homes = lax.axis_size("batch")
    pieces = lax.axis_size("tensor")
    place = lax.axis_index("batch").astype(jnp.int32)
    piece = lax.axis_index("tensor").astype(jnp.int32)
    light = rows // adapters
    span = (held + 1) * light
    order = sorted(range(1, homes), key=lambda r: (-min(r, homes - r), r))
    block_shape = jax.ShapeDtypeStruct((span, width), jnp.bfloat16)

    index, heavy, first = pl.pallas_call(
        functools.partial(route_kernel, homes, held, light, order[0]),
        out_shape=[
            jax.ShapeDtypeStruct((1, rows), jnp.int32),
            jax.ShapeDtypeStruct((8, 128), jnp.int32),
            block_shape,
        ],
        in_specs=[SMEM, ANY, ANY, ANY],
        out_specs=[VMEM] * 3,
        scratch_shapes=[
            pltpu.SMEM(adapter_entry.shape, jnp.int32),
            pltpu.VMEM((rows,), jnp.int32),
            pltpu.VMEM(tokens.shape, jnp.bfloat16),
            pltpu.SemaphoreType.DMA((3,)),
        ],
        compiler_params=PARAMS,
        cost_estimate=COST,
        name="route",
    )(place.reshape(1), adapter_entry, request_adapter, tokens)
    up = gather_up(adapter_up, place, homes, index)

    def pack(shifts):
        return pl.pallas_call(
            functools.partial(pack_kernel, span, shifts),
            out_shape=[jax.ShapeDtypeStruct((8, 128), jnp.int32)] + [block_shape] * len(shifts),
            in_specs=[VMEM] * 2,
            out_specs=[VMEM] * (1 + len(shifts)),
            compiler_params=PARAMS,
            cost_estimate=COST,
            name="pack",
        )(index, tokens)

    def send(block, r):
        return lax.ppermute(block, "batch", [(i, (i + r) % homes) for i in range(homes)])

    arrived = {order[0]: send(first, order[0])}
    later = order[1:] + [0]
    packed, *blocks = pack(later)
    for r, block in zip(later, blocks):
        arrived[r] = send(block, r) if r else block

    heavy = heavy[0, 0]
    heavy_here = (heavy // held == place).astype(jnp.int32)
    scalars = jnp.stack([piece, lax.rem(heavy, held), heavy_here])
    height = entry_places(held) * light

    def shrink(block, after, passed):
        return pl.pallas_call(
            functools.partial(shrink_kernel, held, light, rank, value_side, len(after), len(passed)),
            out_shape=[jax.ShapeDtypeStruct((2 * height, 2 * rank), jnp.float32)]
            + [jax.ShapeDtypeStruct(p.shape, p.dtype) for p in passed],
            in_specs=[SMEM, VMEM, VMEM] + [ANY] * len(after) + [VMEM] * len(passed),
            out_specs=[VMEM] * (1 + len(passed)),
            compiler_params=PARAMS,
            cost_estimate=COST,
            name="shrink",
        )(scalars, block, adapter_down, *after, *passed)

    def combine(value):
        bit = 1
        while bit < pieces // 2:
            value = value + lax.ppermute(value, "tensor", [(i, i ^ bit) for i in range(pieces)])
            bit *= 2
        total = value[:height] + lax.ppermute(value[height:], "tensor", [(i, i ^ bit) for i in range(pieces)])
        return total

    early = order[:-1] + [0]
    totals = []
    after = [packed]
    for r in early:
        (value,) = shrink(arrived[r], after, [])
        totals.append(combine(value))
    slabs = 2
    base = jnp.concatenate(
        [
            reduce_base(tokens, key_value_weight, piece, pieces, columns, slab, slabs, [packed])
            for slab in range(slabs)
        ],
        axis=0,
    )
    value, *totals = shrink(arrived[order[-1]], [], totals)
    last = combine(value)

    def give_back(total, r):
        return lax.ppermute(total, "batch", [(i, (i - r) % homes) for i in range(homes)]) if r else total

    shrinks = [give_back(total, r) for total, r in zip(totals, early)]
    places = jnp.stack([place, heavy])
    column = index.reshape(rows, 1)
    running = finish(places, column, base, up, shrinks, [last], early, jnp.float32, homes, held, light)
    shrinks = [give_back(last, order[-1])]
    return finish(places, column, running, up, shrinks, [], order[-1:], jnp.bfloat16, homes, held, light)


def solution(mesh):
    in_specs = (
        P(("groups", "batch"), "tensor"),
        P(("groups", "batch")),
        P(),
        P("tensor", None),
        P("batch", "tensor", None),
        P("batch", None, "tensor"),
    )
    out_specs = P(("groups", "batch"), "tensor")
    return jax.shard_map(
        on_device, mesh=mesh, in_specs=in_specs, out_specs=out_specs, check_vma=False
    )
```

time: 140 us -> 143 us (1.021)
  Pallas kernels: 21.2 us -> 25 us
  waiting for transfers between devices: 63.8 us -> 66.2 us
  local copies, waits for them, and re-layouts: 16.3 us -> 14.3 us
  starting transfers between devices: 30.8 us -> 29.2 us
    ppermute x25 -> x18, waiting for transfers between devices: 53.1 us -> 66.2 us  [the longest x1 42.4 us: line_gather(): beyond = lax.ppermute(across, 'batch', [(1, 0), (2, 3)])]
    ppermute x2 -> x4, waiting for transfers between devices: 10.7 us -> 0.01 us  [reduce_base(): lax.ppermute(sent, 'tensor', [(i, i ^ bit) for i in range(pieces)])]
    pallas_call x2 -> x4, Pallas kernels: 5.92 us -> 8.95 us  [base_part(): pl.pallas_call(functools.partial(base_kernel, len(after)), out_shape=jax....]
    ppermute x25 -> x18, starting transfers between devices: 29.3 us -> 26.5 us  [the longest x3 12.4 us: send(): lax.ppermute(block, 'batch', [(i, (i + r) % homes) for i in range(homes)])]
    pallas_call x7 -> x6, Pallas kernels: 9.13 us -> 10 us  [the longest x4 6.98 us: shrink(): pl.pallas_call(functools.partial(shrink_kernel, held, light, rank, value_...]
    unnamed x36 -> x32, local copies, waits for them, and re-layouts: 12.9 us -> 12.6 us
  transfers between devices with their start and end apart: 27 -> 22, of which waited for: 8 -> 6; matrix products, arithmetic and copies ran while one was open for 5% -> 4% of each run, Pallas kernels for 10% -> 16%
where the time goes in v4:
time: 143 us
  waiting for transfers between devices  66.2 us (46%)
  starting transfers between devices  29.2 us (20%)
  Pallas kernels  25 us (17%)
  local copies, waits for them, and re-layouts  14.3 us (10%)
  other arithmetic  4.81 us (3%)
  between operations  2.94 us (2%)
    ppermute x1, waiting for transfers between devices, line_gather(): beyond = lax.ppermute(across, 'batch', [(1, 0), (2, 3)])  42.4 us
    ppermute x4, waiting for transfers between devices, combine(): lax.ppermute(value[height:], 'tensor', [(i, i ^ bit) for i in range(piece...  19.7 us
    unnamed x32, local copies, waits for them, and re-layouts  12.6 us
    ppermute x3, starting transfers between devices, send(): lax.ppermute(block, 'batch', [(i, (i + r) % homes) for i in range(homes)])  12.4 us
    pallas_call x4, Pallas kernels, base_part(): pl.pallas_call(functools.partial(base_kernel, len(after)), out_shape=jax....  8.95 us
    pallas_call x4, Pallas kernels, shrink(): pl.pallas_call(functools.partial(shrink_kernel, held, light, rank, value_...  6.98 us
    ppermute x4, starting transfers between devices, combine(): lax.ppermute(value[height:], 'tensor', [(i, i ^ bit) for i in range(piece...  5.13 us
    pallas_call x2, Pallas kernels, finish(): pl.pallas_call(functools.partial(finish_kernel, homes, held, light, up.sh...  3.52 us
  transfers between devices with their start and end apart: 22, of which 6 were waited for; matrix products, arithmetic and copies ran while one was open for 4% of the time, Pallas kernels for 16%

profile of v4, /device:TPU:0, one launch (start us, length us, event | category | flops | bytes accessed | tf_op | source)
XLA Modules:
  0.0 142.5 jit_solution(15077758653507708059)
XLA Ops:
  0.0 0.9 constant_dynamic-slice_fusion.first_ref
  0.9 3.1 %collective-permute-start.4 = (bf16[8,32,256]{2,1,0:T(8,128)(2,1)S(1)}, bf16[8,32,256]{2,1,0:T(8,128)(2,1)S(1)}, u32[]{:S(2)}, u32[]{:S(2)}) collective-permute-start(bf16[8,32,256]{2,1,0:T(8,128)(2,1)S(1)} %constant_dynamic-slice_fusion.first_ref), channel_id=1, source_target_pairs={{0,4},{4,0},{8,12},{12,8},{1,5},{5,1},{9,13},{13,9},{2,6},{6,2},{1... | collective-permute-start | bytes 393224 | tf_op jit(solution)/shard_map/ppermute | solution.py:177
  4.0 1.9 %copy-done = bf16[768,2048]{1,0:T(8,128)(2,1)S(1)} copy-done((bf16[768,2048]{1,0:T(8,128)(2,1)S(1)}, bf16[768,2048]{1,0:T(8,128)(2,1)}, u32[]{:S(2)}) %copy-start) | copy-done | bytes 3145752
  5.9 0.7 copy-done.13
  6.6 0.7 copy-done.14
  7.2 2.6 %route.1 = (s32[1,768]{1,0:T(1,128)S(1)}, s32[8,128]{1,0:T(8,128)S(1)}, bf16[216,2048]{1,0:T(8,128)(2,1)}) custom-call(s32[1]{0:T(128)} %bitcast.place_ref, s32[32]{0:T(128)S(1)} %copy-done.14, s32[768]{0:T(1024)S(1)} %copy-done.13, bf16[768,2048]{1,0:T(8,128)(2,1)S(1)} %copy-done), custom_call_target="tpu_custom_call" | custom-call | flops 1 | bytes 1 | tf_op jit(solution)/shard_map/route/pallas_call | solution.py:284
  9.8 0.7 join.1
  10.5 1.4 collective-permute-start.5
  11.9 2.3 %pack.1 = (s32[8,128]{1,0:T(8,128)S(1)}, bf16[216,2048]{1,0:T(8,128)(2,1)}, bf16[216,2048]{1,0:T(8,128)(2,1)S(1)}, bf16[216,2048]{1,0:T(8,128)(2,1)S(1)}) custom-call(s32[1,768]{1,0:T(1,128)S(1)} %get-tuple-element.17.index_ref.after_ref, bf16[768,2048]{1,0:T(8,128)(2,1)S(1)} %copy-done.1), custom_call_target="tpu_custom_call" | custom-call | flops 1 | bytes 1 | tf_op jit(solution)/shard_map/pack/pallas_call | solution.py:306
  14.3 0.9 copy-done.11
  15.2 0.9 copy-done.15
  16.1 3.7 %collective-permute-start.12 = (bf16[216,2048]{1,0:T(8,128)(2,1)}, bf16[216,2048]{1,0:T(8,128)(2,1)}, u32[]{:S(2)}, u32[]{:S(2)}) collective-permute-start(bf16[216,2048]{1,0:T(8,128)(2,1)} %get-tuple-element.21), channel_id=1, source_target_pairs={{0,4},{4,8},{8,12},{12,0},{1,5},{5,9},{9,13},{13,1},{2,6},{6,10},{... | collective-permute-start | bytes 2654216 | tf_op jit(solution)/shard_map/ppermute | solution.py:317
  19.8 0.5 slice.45
  22.9 2.2 %copy-done.2 = bf16[8,2048,128]{2,1,0:T(8,128)(2,1)S(1)} copy-done((bf16[8,2048,128]{2,1,0:T(8,128)(2,1)S(1)}, bf16[8,2048,128]{2,1,0:T(8,128)(2,1)}, u32[]{:S(2)}) %copy-start.2) | copy-done | bytes 4194328
  25.1 1.2 copy-done.12
  26.3 1.4 shrink.6
  27.7 1.3 collective-permute-start.6
  29.0 2.8 %base.4.refs_0_ = f32[384,512]{1,0:T(8,128)} custom-call(s32[2]{0:T(128)S(1)} %broadcast_xor_fusion.block_ref, bf16[768,2048]{1,0:T(8,128)(2,1)S(1)} %copy-done.1, bf16[2048,1024]{1,0:T(8,128)(2,1)S(1)} %copy-done.5, s32[8,128]{1,0:T(8,128)S(1)} %get-tuple-element.18.refs_0_), custom_call_target="tpu_custom_call" | custom-call | flops 1 | bytes 1 | tf_op jit(solution)/shard_map/base/pallas_call | solution.py:232
  31.8 0.5 collective-permute-start
  32.3 2.1 %base.6.refs_0_ = f32[384,512]{1,0:T(8,128)S(1)} custom-call(s32[2]{0:T(128)S(1)} %broadcast_xor_fusion.block_ref, bf16[768,2048]{1,0:T(8,128)(2,1)S(1)} %copy-done.1, bf16[2048,1024]{1,0:T(8,128)(2,1)S(1)} %copy-done.5, s32[8,128]{1,0:T(8,128)S(1)} %get-tuple-element.18.refs_0_), custom_call_target="tpu_custom_call" | custom-call | flops 1 | bytes 1 | tf_op jit(solution)/shard_map/base/pallas_call | solution.py:232
  34.4 2.1 %base.5 = f32[384,512]{1,0:T(8,128)S(1)} custom-call(s32[2]{0:T(128)S(1)} %multiply_xor_fusion.block_ref, bf16[768,2048]{1,0:T(8,128)(2,1)S(1)} %copy-done.1, bf16[2048,1024]{1,0:T(8,128)(2,1)S(1)} %copy-done.5, f32[384,512]{1,0:T(8,128)} %base.4.refs_0_), custom_call_target="tpu_custom_call" | custom-call | flops 1 | bytes 1 | tf_op jit(solution)/shard_map/base/pallas_call | solution.py:232
  36.5 0.9 copy-done.8
  37.4 2.1 %base.7 = f32[384,512]{1,0:T(8,128)S(1)} custom-call(s32[2]{0:T(128)S(1)} %multiply_xor_fusion.block_ref, bf16[768,2048]{1,0:T(8,128)(2,1)S(1)} %copy-done.1, bf16[2048,1024]{1,0:T(8,128)(2,1)S(1)} %copy-done.5, f32[384,512]{1,0:T(8,128)S(1)} %base.6.refs_0_), custom_call_target="tpu_custom_call" | custom-call | flops 1 | bytes 1 | tf_op jit(solution)/shard_map/base/pallas_call | solution.py:232
  39.5 0.9 copy-done.6
  40.5 0.7 pad_add_fusion.place_ref
  41.3 42.4 %collective-permute-done.6 = bf16[16,32,256]{2,1,0:T(8,128)(2,1)} collective-permute-done((bf16[16,32,256]{2,1,0:T(8,128)(2,1)}, bf16[16,32,256]{2,1,0:T(8,128)(2,1)}, u32[]{:S(2)}, u32[]{:S(2)}) %collective-permute-start.6) | collective-permute-done | bytes 262176 | tf_op jit(solution)/shard_map/ppermute | solution.py:179
  83.8 8.7 %collective-permute-start.8 = (bf16[216,2048]{1,0:T(8,128)(2,1)}, bf16[216,2048]{1,0:T(8,128)(2,1)S(1)}, u32[]{:S(2)}, u32[]{:S(2)}) collective-permute-start(bf16[216,2048]{1,0:T(8,128)(2,1)} %copy-done.15), channel_id=1, source_target_pairs={{0,12},{4,0},{8,4},{12,8},{1,13},{5,1},{9,5},{13,9},{2,14},{6,2},{... | collective-permute-start | bytes 2654216 | tf_op jit(solution)/shard_map/ppermute | solution.py:317
  92.5 1.0 broadcast_select_fusion.2
  93.4 1.0 broadcast_select_fusion.8
  94.5 1.6 %collective-permute-start.16 = (f32[120,128]{1,0:T(8,128)S(1)}, f32[120,128]{1,0:T(8,128)S(1)}, u32[]{:S(2)}, u32[]{:S(2)}) collective-permute-start(f32[120,128]{1,0:T(8,128)S(1)} %slice.71), channel_id=1, source_target_pairs={{0,2},{1,3},{2,0},{3,1},{4,6},{5,7},{6,4},{7,5},{8,10},{9,11},{10,... | collective-permute-start | bytes 184328 | tf_op jit(solution)/shard_map/ppermute | solution.py:347
  96.1 2.2 %copy-done.3 = bf16[8,2048,128]{2,1,0:T(8,128)(2,1)S(1)} copy-done((bf16[8,2048,128]{2,1,0:T(8,128)(2,1)S(1)}, bf16[8,2048,128]{2,1,0:T(8,128)(2,1)}, u32[]{:S(2)}) %copy-start.3) | copy-done | bytes 4194328
  98.2 2.2 %shrink.5 = f32[240,128]{1,0:T(8,128)S(1)} custom-call(s32[3]{0:T(128)S(1)} %pad_add_fusion.1.scalar_ref, bf16[216,2048]{1,0:T(8,128)(2,1)} %collective-permute-done.12.block_ref, bf16[8,2048,128]{2,1,0:T(8,128)(2,1)S(1)} %copy-done.3, s32[8,128]{1,0:T(8,128)S(1)} %get-tuple-element.18.refs_0_), custom_call_target="tpu_custom_call" | custom-call | flops 1 | bytes 1 | tf_op jit(solution)/shard_map/shrink/pallas_call | solution.py:331
  100.7 2.1 %shrink.4 = f32[240,128]{1,0:T(8,128)S(1)} custom-call(s32[3]{0:T(128)S(1)} %pad_add_fusion.1.scalar_ref, bf16[216,2048]{1,0:T(8,128)(2,1)} %collective-permute-done.9.block_ref, bf16[8,2048,128]{2,1,0:T(8,128)(2,1)S(1)} %copy-done.4, s32[8,128]{1,0:T(8,128)S(1)} %get-tuple-element.18.refs_0_), custom_call_target="tpu_custom_call" | custom-call | flops 1 | bytes 1 | tf_op jit(solution)/shard_map/shrink/pallas_call | solution.py:331
  102.8 1.6 %collective-permute-start.7 = (bf16[32,32,256]{2,1,0:T(8,128)(2,1)S(1)}, bf16[32,32,256]{2,1,0:T(8,128)(2,1)S(1)}, u32[]{:S(2)}, u32[]{:S(2)}) collective-permute-start(bf16[32,32,256]{2,1,0:T(8,128)(2,1)S(1)} %pad_maximum_fusion.2), channel_id=1, source_target_pairs={{0,16},{16,0},{1,17},{17,1},{2,18},{18,2},{3,19},{19,3},{4,20},{20... | collective-permute-start | bytes 1572872 | tf_op jit(solution)/shard_map/ppermute | solution.py:209
  104.6 0.5 collective-permute-start.14
  105.2 1.3 add.49
  106.5 1.6 %collective-permute-start.1 = (f32[384,256]{1,0:T(8,128)S(1)}, f32[384,256]{1,0:T(8,128)S(1)}, u32[]{:S(2)}, u32[]{:S(2)}) collective-permute-start(f32[384,256]{1,0:T(8,128)S(1)} %slice.61), channel_id=1, source_target_pairs={{0,2},{1,3},{2,0},{3,1},{4,6},{5,7},{6,4},{7,5},{8,10},{9,11},{10,... | collective-permute-start | bytes 1179656 | tf_op jit(solution)/shard_map/ppermute | solution.py:262
  108.2 0.6 collective-permute-start.3
  109.0 1.5 %collective-permute-start.11 = (f32[120,128]{1,0:T(8,128)S(1)}, f32[120,128]{1,0:T(8,128)S(1)}, u32[]{:S(2)}, u32[]{:S(2)}) collective-permute-start(f32[120,128]{1,0:T(8,128)S(1)} %slice.67), channel_id=1, source_target_pairs={{0,2},{1,3},{2,0},{3,1},{4,6},{5,7},{6,4},{7,5},{8,10},{9,11},{10,... | collective-permute-start | bytes 184328 | tf_op jit(solution)/shard_map/ppermute | solution.py:347
  110.4 17.0 %collective-permute-done.11 = f32[120,128]{1,0:T(8,128)S(1)} collective-permute-done((f32[120,128]{1,0:T(8,128)S(1)}, f32[120,128]{1,0:T(8,128)S(1)}, u32[]{:S(2)}, u32[]{:S(2)}) %collective-permute-start.11) | collective-permute-done | bytes 61472 | tf_op jit(solution)/shard_map/ppermute | solution.py:347
  127.5 1.4 shrink.7
  129.3 0.9 collective-permute-done.19
  130.2 1.6 %collective-permute-start.20 = (f32[120,128]{1,0:T(8,128)S(1)}, f32[120,128]{1,0:T(8,128)S(1)}, u32[]{:S(2)}, u32[]{:S(2)}) collective-permute-start(f32[120,128]{1,0:T(8,128)S(1)} %slice.73), channel_id=1, source_target_pairs={{0,2},{1,3},{2,0},{3,1},{4,6},{5,7},{6,4},{7,5},{8,10},{9,11},{10,... | collective-permute-start | bytes 184328 | tf_op jit(solution)/shard_map/ppermute | solution.py:347
  131.9 2.6 %collective-permute-done.20 = f32[120,128]{1,0:T(8,128)S(1)} collective-permute-done((f32[120,128]{1,0:T(8,128)S(1)}, f32[120,128]{1,0:T(8,128)S(1)}, u32[]{:S(2)}, u32[]{:S(2)}) %collective-permute-start.20) | collective-permute-done | bytes 61472 | tf_op jit(solution)/shard_map/ppermute | solution.py:347
  134.5 1.2 collective-permute-start.21
  135.8 1.6 %finish.2.base_ref = f32[768,256]{1,0:T(8,128)S(1)} custom-call(s32[2]{0:T(128)S(1)} %pad_add_fusion.place_ref, s32[768,1]{1,0:T(8,128)S(1)} %copy.10.index_ref, f32[768,256]{1,0:T(8,128)S(1)} %pad_maximum_fusion.1.base_ref, bf16[32,64,256]{2,1,0:T(8,128)(2,1)S(1)} %pad_maximum_fusion.up_ref, f32[120,128]{1,0:T(8,128)S(1)} %collective-permute-done.17.refs_0_, ...), custom_call_target="tpu_custom_call" | custom-call | flops 1 | bytes 1 | tf_op jit(solution)/shard_map/finish/pallas_call | solution.py:145
  137.5 3.1 %collective-permute-done.21.refs_0_ = f32[120,128]{1,0:T(8,128)S(1)} collective-permute-done((f32[120,128]{1,0:T(8,128)S(1)}, f32[120,128]{1,0:T(8,128)S(1)}, u32[]{:S(2)}, u32[]{:S(2)}) %collective-permute-start.21) | collective-permute-done | bytes 61472 | tf_op jit(solution)/shard_map/ppermute | solution.py:368
  140.6 1.9 %finish.3 = bf16[768,256]{1,0:T(8,128)(2,1)} custom-call(s32[2]{0:T(128)S(1)} %pad_add_fusion.place_ref, s32[768,1]{1,0:T(8,128)S(1)} %copy.10.index_ref, f32[768,256]{1,0:T(8,128)S(1)} %finish.2.base_ref, bf16[32,64,256]{2,1,0:T(8,128)(2,1)S(1)} %pad_maximum_fusion.up_ref, f32[120,128]{1,0:T(8,128)S(1)} %collective-permute-done.21.refs_0_), custom_call_target="tpu_custom_call" | custom-call | flops 1 | bytes 1 | tf_op jit(solution)/shard_map/finish/pallas_call | solution.py:145
  (72 shorter events, 1.8 us)
Async XLA Ops:
  0.9 8.9 %collective-permute-start.4 = (bf16[8,32,256]{2,1,0:T(8,128)(2,1)S(1)}, bf16[8,32,256]{2,1,0:T(8,128)(2,1)S(1)}, u32[]{:S(2)}, u32[]{:S(2)}) collective-permute-start(bf16[8,32,256]{2,1,0:T(8,128)(2,1)S(1)} %constant_dynamic-slice_fusion.first_ref), channel_id=1, source_target_pairs={{0,4},{4,0},{8,12},{12,8},{1,5},{5,1},{9,13},{13,9},{2,6},{6,2},{1... | collective-permute-start | bytes 393224 | tf_op jit(solution)/shard_map/ppermute | solution.py:177
  4.0 1.9 %copy-start = (bf16[768,2048]{1,0:T(8,128)(2,1)S(1)}, bf16[768,2048]{1,0:T(8,128)(2,1)}, u32[]{:S(2)}) copy-start(bf16[768,2048]{1,0:T(8,128)(2,1)} %tokens_ref.9) | copy-start | bytes 9437188
  5.9 0.7 copy-start.13
  6.6 0.7 copy-start.14
  7.2 4.7 %copy-start.1 = (bf16[768,2048]{1,0:T(8,128)(2,1)S(1)}, bf16[768,2048]{1,0:T(8,128)(2,1)}, u32[]{:S(2)}) copy-start(bf16[768,2048]{1,0:T(8,128)(2,1)} %tokens_ref.9) | copy-start | bytes 9437188
  10.5 17.2 %collective-permute-start.5 = (bf16[16,32,256]{2,1,0:T(8,128)(2,1)}, bf16[16,32,256]{2,1,0:T(8,128)(2,1)}, u32[]{:S(2)}, u32[]{:S(2)}) collective-permute-start(bf16[16,32,256]{2,1,0:T(8,128)(2,1)} %join.1), channel_id=1, source_target_pairs={{4,8},{8,4},{5,9},{9,5},{6,10},{10,6},{7,11},{11,7},{20,24},{24,20... | collective-permute-start | bytes 786440 | tf_op jit(solution)/shard_map/ppermute | solution.py:178
  14.3 0.9 copy-start.11
  15.2 0.9 copy-start.15
  16.1 78.3 %collective-permute-start.12 = (bf16[216,2048]{1,0:T(8,128)(2,1)}, bf16[216,2048]{1,0:T(8,128)(2,1)}, u32[]{:S(2)}, u32[]{:S(2)}) collective-permute-start(bf16[216,2048]{1,0:T(8,128)(2,1)} %get-tuple-element.21), channel_id=1, source_target_pairs={{0,4},{4,8},{8,12},{12,0},{1,5},{5,9},{9,13},{13,1},{2,6},{6,10},{... | collective-permute-start | bytes 2654216 | tf_op jit(solution)/shard_map/ppermute | solution.py:317
  19.8 80.6 %collective-permute-start.9 = (bf16[216,2048]{1,0:T(8,128)(2,1)}, bf16[216,2048]{1,0:T(8,128)(2,1)}, u32[]{:S(2)}, u32[]{:S(2)}) collective-permute-start(bf16[216,2048]{1,0:T(8,128)(2,1)} %get-tuple-element.20), channel_id=1, source_target_pairs={{0,8},{4,12},{8,0},{12,4},{1,9},{5,13},{9,1},{13,5},{2,10},{6,14},... | collective-permute-start | bytes 2654216 | tf_op jit(solution)/shard_map/ppermute | solution.py:317
  22.9 2.2 %copy-start.2 = (bf16[8,2048,128]{2,1,0:T(8,128)(2,1)S(1)}, bf16[8,2048,128]{2,1,0:T(8,128)(2,1)}, u32[]{:S(2)}) copy-start(bf16[8,2048,128]{2,1,0:T(8,128)(2,1)} %down_ref.7) | copy-start | bytes 12582916
  25.1 1.2 copy-start.12
  26.3 2.7 %copy-start.5 = (bf16[2048,1024]{1,0:T(8,128)(2,1)S(1)}, bf16[2048,1024]{1,0:T(8,128)(2,1)}, u32[]{:S(2)}) copy-start(bf16[2048,1024]{1,0:T(8,128)(2,1)} %weight_ref.7) | copy-start | bytes 12582916
  27.7 13.6 %collective-permute-start.15 = (f32[240,128]{1,0:T(8,128)S(1)}, f32[240,128]{1,0:T(8,128)S(1)}, u32[]{:S(2)}, u32[]{:S(2)}) collective-permute-start(f32[240,128]{1,0:T(8,128)S(1)} %shrink.6), channel_id=1, source_target_pairs={{0,1},{1,0},{2,3},{3,2},{4,5},{5,4},{6,7},{7,6},{8,9},{9,8},{10,11... | collective-permute-start | bytes 368648 | tf_op jit(solution)/shard_map/ppermute | solution.py:345
  27.7 56.0 %collective-permute-start.6 = (bf16[16,32,256]{2,1,0:T(8,128)(2,1)}, bf16[16,32,256]{2,1,0:T(8,128)(2,1)}, u32[]{:S(2)}, u32[]{:S(2)}) collective-permute-start(bf16[16,32,256]{2,1,0:T(8,128)(2,1)} %collective-permute-done.5), channel_id=1, source_target_pairs={{4,0},{8,12},{5,1},{9,13},{6,2},{10,14},{7,3},{11,15},{20,16},{24,... | collective-permute-start | bytes 786440 | tf_op jit(solution)/shard_map/ppermute | solution.py:179
  31.8 72.8 %collective-permute-start = (f32[384,512]{1,0:T(8,128)}, f32[384,512]{1,0:T(8,128)}, u32[]{:S(2)}, u32[]{:S(2)}) collective-permute-start(f32[384,512]{1,0:T(8,128)} %base.4.refs_0_), channel_id=1, source_target_pairs={{0,1},{1,0},{2,3},{3,2},{4,5},{5,4},{6,7},{7,6},{8,9},{9,8},{10,11... | collective-permute-start | bytes 2359304 | tf_op jit(solution)/shard_map/ppermute | solution.py:262
  34.4 2.1 %copy-start.10 = (f32[384,512]{1,0:T(8,128)}, f32[384,512]{1,0:T(8,128)S(1)}, u32[]{:S(2)}) copy-start(f32[384,512]{1,0:T(8,128)S(1)} %base.6.refs_0_) | copy-start | bytes 2359300
  36.4 0.9 copy-start.8
  39.5 0.9 copy-start.6
  41.2 65.2 %collective-permute-start.2 = (f32[384,512]{1,0:T(8,128)}, f32[384,512]{1,0:T(8,128)S(1)}, u32[]{:S(2)}, u32[]{:S(2)}) collective-permute-start(f32[384,512]{1,0:T(8,128)} %copy-done.10), channel_id=1, source_target_pairs={{0,1},{1,0},{2,3},{3,2},{4,5},{5,4},{6,7},{7,6},{8,9},{9,8},{10,11... | collective-permute-start | bytes 2359304 | tf_op jit(solution)/shard_map/ppermute | solution.py:262
  83.8 43.7 %collective-permute-start.8 = (bf16[216,2048]{1,0:T(8,128)(2,1)}, bf16[216,2048]{1,0:T(8,128)(2,1)S(1)}, u32[]{:S(2)}, u32[]{:S(2)}) collective-permute-start(bf16[216,2048]{1,0:T(8,128)(2,1)} %copy-done.15), channel_id=1, source_target_pairs={{0,12},{4,0},{8,4},{12,8},{1,13},{5,1},{9,5},{13,9},{2,14},{6,2},{... | collective-permute-start | bytes 2654216 | tf_op jit(solution)/shard_map/ppermute | solution.py:317
  94.5 9.9 %collective-permute-start.16 = (f32[120,128]{1,0:T(8,128)S(1)}, f32[120,128]{1,0:T(8,128)S(1)}, u32[]{:S(2)}, u32[]{:S(2)}) collective-permute-start(f32[120,128]{1,0:T(8,128)S(1)} %slice.71), channel_id=1, source_target_pairs={{0,2},{1,3},{2,0},{3,1},{4,6},{5,7},{6,4},{7,5},{8,10},{9,11},{10,... | collective-permute-start | bytes 184328 | tf_op jit(solution)/shard_map/ppermute | solution.py:347
  96.1 2.2 %copy-start.3 = (bf16[8,2048,128]{2,1,0:T(8,128)(2,1)S(1)}, bf16[8,2048,128]{2,1,0:T(8,128)(2,1)}, u32[]{:S(2)}) copy-start(bf16[8,2048,128]{2,1,0:T(8,128)(2,1)} %down_ref.7) | copy-start | bytes 12582916
  98.2 2.5 %copy-start.4 = (bf16[8,2048,128]{2,1,0:T(8,128)(2,1)S(1)}, bf16[8,2048,128]{2,1,0:T(8,128)(2,1)}, u32[]{:S(2)}) copy-start(bf16[8,2048,128]{2,1,0:T(8,128)(2,1)} %down_ref.7) | copy-start | bytes 12582916
  100.4 2.4 %collective-permute-start.13 = (f32[240,128]{1,0:T(8,128)S(1)}, f32[240,128]{1,0:T(8,128)S(1)}, u32[]{:S(2)}, u32[]{:S(2)}) collective-permute-start(f32[240,128]{1,0:T(8,128)S(1)} %shrink.5), channel_id=1, source_target_pairs={{0,1},{1,0},{2,3},{3,2},{4,5},{5,4},{6,7},{7,6},{8,9},{9,8},{10,11... | collective-permute-start | bytes 368648 | tf_op jit(solution)/shard_map/ppermute | solution.py:345
  100.7 4.4 %copy-start.9 = (f32[384,512]{1,0:T(8,128)S(1)}, f32[384,512]{1,0:T(8,128)}, u32[]{:S(2)}) copy-start(f32[384,512]{1,0:T(8,128)} %copy-done.8) | copy-start | bytes 2359300
  102.8 5.3 %copy-start.7 = (f32[384,512]{1,0:T(8,128)S(1)}, f32[384,512]{1,0:T(8,128)}, u32[]{:S(2)}) copy-start(f32[384,512]{1,0:T(8,128)} %copy-done.6) | copy-start | bytes 2359300
  102.8 26.2 %collective-permute-start.7 = (bf16[32,32,256]{2,1,0:T(8,128)(2,1)S(1)}, bf16[32,32,256]{2,1,0:T(8,128)(2,1)S(1)}, u32[]{:S(2)}, u32[]{:S(2)}) collective-permute-start(bf16[32,32,256]{2,1,0:T(8,128)(2,1)S(1)} %pad_maximum_fusion.2), channel_id=1, source_target_pairs={{0,16},{16,0},{1,17},{17,1},{2,18},{18,2},{3,19},{19,3},{4,20},{20... | collective-permute-start | bytes 1572872 | tf_op jit(solution)/shard_map/ppermute | solution.py:209
  104.4 3.8 %collective-permute-start.10 = (f32[240,128]{1,0:T(8,128)S(1)}, f32[240,128]{1,0:T(8,128)S(1)}, u32[]{:S(2)}, u32[]{:S(2)}) collective-permute-start(f32[240,128]{1,0:T(8,128)S(1)} %shrink.4), channel_id=1, source_target_pairs={{0,1},{1,0},{2,3},{3,2},{4,5},{5,4},{6,7},{7,6},{8,9},{9,8},{10,11... | collective-permute-start | bytes 368648 | tf_op jit(solution)/shard_map/ppermute | solution.py:345
  104.6 4.4 %collective-permute-start.14 = (f32[120,128]{1,0:T(8,128)S(1)}, f32[120,128]{1,0:T(8,128)S(1)}, u32[]{:S(2)}, u32[]{:S(2)}) collective-permute-start(f32[120,128]{1,0:T(8,128)S(1)} %slice.69), channel_id=1, source_target_pairs={{0,2},{1,3},{2,0},{3,1},{4,6},{5,7},{6,4},{7,5},{8,10},{9,11},{10,... | collective-permute-start | bytes 184328 | tf_op jit(solution)/shard_map/ppermute | solution.py:347
  106.5 22.8 %collective-permute-start.1 = (f32[384,256]{1,0:T(8,128)S(1)}, f32[384,256]{1,0:T(8,128)S(1)}, u32[]{:S(2)}, u32[]{:S(2)}) collective-permute-start(f32[384,256]{1,0:T(8,128)S(1)} %slice.61), channel_id=1, source_target_pairs={{0,2},{1,3},{2,0},{3,1},{4,6},{5,7},{6,4},{7,5},{8,10},{9,11},{10,... | collective-permute-start | bytes 1179656 | tf_op jit(solution)/shard_map/ppermute | solution.py:262
  108.2 23.6 %collective-permute-start.3 = (f32[384,256]{1,0:T(8,128)S(1)}, f32[384,256]{1,0:T(8,128)S(1)}, u32[]{:S(2)}, u32[]{:S(2)}) collective-permute-start(f32[384,256]{1,0:T(8,128)S(1)} %slice.63), channel_id=1, source_target_pairs={{0,2},{1,3},{2,0},{3,1},{4,6},{5,7},{6,4},{7,5},{8,10},{9,11},{10,... | collective-permute-start | bytes 1179656 | tf_op jit(solution)/shard_map/ppermute | solution.py:262
  109.0 18.5 %collective-permute-start.11 = (f32[120,128]{1,0:T(8,128)S(1)}, f32[120,128]{1,0:T(8,128)S(1)}, u32[]{:S(2)}, u32[]{:S(2)}) collective-permute-start(f32[120,128]{1,0:T(8,128)S(1)} %slice.67), channel_id=1, source_target_pairs={{0,2},{1,3},{2,0},{3,1},{4,6},{5,7},{6,4},{7,5},{8,10},{9,11},{10,... | collective-permute-start | bytes 184328 | tf_op jit(solution)/shard_map/ppermute | solution.py:347
  128.9 1.3 collective-permute-start.19
  128.9 6.9 %collective-permute-start.17 = (f32[120,128]{1,0:T(8,128)S(1)}, f32[120,128]{1,0:T(8,128)S(1)}, u32[]{:S(2)}, u32[]{:S(2)}) collective-permute-start(f32[120,128]{1,0:T(8,128)S(1)} %get-tuple-element.23), channel_id=1, source_target_pairs={{0,8},{4,12},{8,0},{12,4},{1,9},{5,13},{9,1},{13,5},{2,10},{6,14},... | collective-permute-start | bytes 184328 | tf_op jit(solution)/shard_map/ppermute | solution.py:368
  129.0 6.9 %collective-permute-start.18 = (f32[120,128]{1,0:T(8,128)S(1)}, f32[120,128]{1,0:T(8,128)S(1)}, u32[]{:S(2)}, u32[]{:S(2)}) collective-permute-start(f32[120,128]{1,0:T(8,128)S(1)} %get-tuple-element.24), channel_id=1, source_target_pairs={{0,12},{4,0},{8,4},{12,8},{1,13},{5,1},{9,5},{13,9},{2,14},{6,2},{... | collective-permute-start | bytes 184328 | tf_op jit(solution)/shard_map/ppermute | solution.py:368
  130.2 4.3 %collective-permute-start.20 = (f32[120,128]{1,0:T(8,128)S(1)}, f32[120,128]{1,0:T(8,128)S(1)}, u32[]{:S(2)}, u32[]{:S(2)}) collective-permute-start(f32[120,128]{1,0:T(8,128)S(1)} %slice.73), channel_id=1, source_target_pairs={{0,2},{1,3},{2,0},{3,1},{4,6},{5,7},{6,4},{7,5},{8,10},{9,11},{10,... | collective-permute-start | bytes 184328 | tf_op jit(solution)/shard_map/ppermute | solution.py:347
  134.5 6.1 %collective-permute-start.21 = (f32[120,128]{1,0:T(8,128)S(1)}, f32[120,128]{1,0:T(8,128)S(1)}, u32[]{:S(2)}, u32[]{:S(2)}) collective-permute-start(f32[120,128]{1,0:T(8,128)S(1)} %slice_add_fusion.2.refs_3_), channel_id=1, source_target_pairs={{0,4},{4,8},{8,12},{12,0},{1,5},{5,9},{9,13},{13,1},{2,6},{6,10},{... | collective-permute-start | bytes 184328 | tf_op jit(solution)/shard_map/ppermute | solution.py:368

commit v5 on v4

--- a/solution.py
+++ b/solution.py
@@ -9,8 +9,10 @@
 
 adapter_scale = 0.5
 VMEM_BYTES = 24 * 1024 * 1024
+WIDE = pltpu.CompilerParams(vmem_limit_bytes=60 * 1024 * 1024)
 VMEM = pl.BlockSpec(memory_space=pltpu.VMEM)
 ANY = pl.BlockSpec(memory_space=pl.ANY)
+HBM = pl.BlockSpec(memory_space=pltpu.HBM)
 SMEM = pl.BlockSpec(memory_space=pltpu.SMEM)
 COST = pl.CostEstimate(flops=1, bytes_accessed=1, transcendentals=0)
 PARAMS = pltpu.CompilerParams(vmem_limit_bytes=VMEM_BYTES)
@@ -64,10 +66,17 @@
     place_rows(index, shift * span, tokens_ref, block_ref)
 
 
-def pack_kernel(span, shifts, index_ref, tokens_ref, mark_ref, *block_refs):
+def pack_kernel(span, shifts, index_ref, tokens_ref, mark_ref, *refs):
+    count = len(shifts)
+    block_refs, buffer, sems = refs[:count], refs[count], refs[count + 1]
     mark_ref[...] = jnp.zeros_like(mark_ref)
-    for shift, block_ref in zip(shifts, block_refs):
-        place_rows(index_ref[...], shift * span, tokens_ref, block_ref)
+    stores = []
+    for n, shift in enumerate(shifts):
+        place_rows(index_ref[...], shift * span, tokens_ref, buffer.at[n])
+        stores.append(pltpu.make_async_copy(buffer.at[n], block_refs[n], sems.at[n]))
+        stores[-1].start()
+    for store in stores:
+        store.wait()
 
 
 def entry_places(held):
@@ -113,9 +122,8 @@
     groups = entry_places(held)
     local = []
     for n, r in enumerate(shifts):
-        home = lax.rem(place_ref[0] + r, homes)
         for e in range(held + 1):
-            entry = home * held + e if e < held else place_ref[1]
+            entry = r * held + e if e < held else place_ref[0]
             g, side = e % groups, e // groups
             high, low = split_pair(
                 shrink_refs[n][g * light : (g + 1) * light, side * rank : (side + 1) * rank]
@@ -154,57 +162,15 @@
     )(scalars, index, base, up, *shrinks, *after)
 
 
-def join_kernel(first_ref, second_ref, after_ref, out_ref):
-    count = first_ref.shape[0]
-    out_ref[:count] = first_ref[...]
-    out_ref[count:] = second_ref[...]
-
-
-def join(first, second, after):
-    return pl.pallas_call(
-        join_kernel,
-        out_shape=jax.ShapeDtypeStruct((2 * first.shape[0], *first.shape[1:]), first.dtype),
-        in_specs=[VMEM, VMEM, ANY],
-        out_specs=VMEM,
-        compiler_params=PARAMS,
-        cost_estimate=COST,
-        name="join",
-    )(first, second, after)
-
-
-def line_gather(value, place, homes, after):
-    if homes == 4:
-        beside = lax.ppermute(value, "batch", [(0, 1), (1, 0), (2, 3), (3, 2)])
-        across = lax.ppermute(join(value, beside, after), "batch", [(1, 2), (2, 1)])
-        beyond = lax.ppermute(across, "batch", [(1, 0), (2, 3)])
-        far = jnp.where((place == 1) | (place == 2), across, beyond)
-        near, next_to = far[: value.shape[0]], far[value.shape[0] :]
-        even = place % 2 == 0
-        low, high = jnp.where(even, value, beside), jnp.where(even, beside, value)
-        left = place < 2
-        return jnp.concatenate(
-            [
-                jnp.where(left, low, next_to),
-                jnp.where(left, high, near),
-                jnp.where(left, near, low),
-                jnp.where(left, next_to, high),
-            ],
-            axis=0,
-        )
-    bit = 1
-    while bit < homes:
-        other = lax.ppermute(value, "batch", [(i, i ^ bit) for i in range(homes)])
-        first = (place // bit) % 2 == 0
-        value = jnp.concatenate([jnp.where(first, value, other), jnp.where(first, other, value)], axis=0)
-        bit *= 2
-    return value
-
-
-def gather_up(adapter_up, place, homes, after):
+def gather_up(adapter_up, homes):
     teams = lax.axis_size("groups")
     team = lax.axis_index("groups")
     share = adapter_up.shape[1] // teams
-    ordered = line_gather(lax.dynamic_slice_in_dim(adapter_up, team * share, share, 1), place, homes, after)
+    own = lax.dynamic_slice_in_dim(adapter_up, team * share, share, 1)
+    found = [
+        lax.ppermute(own, "batch", [(i, (i - r) % homes) for i in range(homes)]) for r in range(1, homes)
+    ]
+    ordered = jnp.concatenate([own] + found, axis=0)
     shares = [ordered] + [
         lax.ppermute(ordered, "groups", [(i, (i + s) % teams) for i in range(teams)])
         for s in range(1, teams)
@@ -219,7 +185,7 @@
             for part in range(teams)
         ],
         axis=1,
-    )
+    ), found
 
 
 def base_kernel(waited, block_ref, tokens_ref, weight_ref, *refs):
@@ -281,6 +247,7 @@
     order = sorted(range(1, homes), key=lambda r: (-min(r, homes - r), r))
     block_shape = jax.ShapeDtypeStruct((span, width), jnp.bfloat16)
 
+    up, found = gather_up(adapter_up, homes)
     index, heavy, first = pl.pallas_call(
         functools.partial(route_kernel, homes, held, light, order[0]),
         out_shape=[
@@ -288,7 +255,7 @@
             jax.ShapeDtypeStruct((8, 128), jnp.int32),
             block_shape,
         ],
-        in_specs=[SMEM, ANY, ANY, ANY],
+        in_specs=[SMEM, HBM, HBM, HBM],
         out_specs=[VMEM] * 3,
         scratch_shapes=[
             pltpu.SMEM(adapter_entry.shape, jnp.int32),
@@ -296,19 +263,21 @@
             pltpu.VMEM(tokens.shape, jnp.bfloat16),
             pltpu.SemaphoreType.DMA((3,)),
         ],
-        compiler_params=PARAMS,
+        compiler_params=WIDE,
         cost_estimate=COST,
         name="route",
     )(place.reshape(1), adapter_entry, request_adapter, tokens)
-    up = gather_up(adapter_up, place, homes, index)
-
     def pack(shifts):
         return pl.pallas_call(
             functools.partial(pack_kernel, span, shifts),
             out_shape=[jax.ShapeDtypeStruct((8, 128), jnp.int32)] + [block_shape] * len(shifts),
             in_specs=[VMEM] * 2,
-            out_specs=[VMEM] * (1 + len(shifts)),
-            compiler_params=PARAMS,
+            out_specs=[VMEM] + [HBM] * len(shifts),
+            scratch_shapes=[
+                pltpu.VMEM((len(shifts), span, width), jnp.bfloat16),
+                pltpu.SemaphoreType.DMA((len(shifts),)),
+            ],
+            compiler_params=WIDE,
             cost_estimate=COST,
             name="pack",
         )(index, tokens)
@@ -368,7 +337,7 @@
         return lax.ppermute(total, "batch", [(i, (i - r) % homes) for i in range(homes)]) if r else total
 
     shrinks = [give_back(total, r) for total, r in zip(totals, early)]
-    places = jnp.stack([place, heavy])
+    places = lax.rem(heavy - place * held + adapters, adapters).reshape(1)
     column = index.reshape(rows, 1)
     running = finish(places, column, base, up, shrinks, [last], early, jnp.float32, homes, held, light)
     shrinks = [give_back(last, order[-1])]

time: 143 us -> 143 us (level)
  the two profiles are of different devices: /device:TPU:0 before, /device:TPU:4 now
where the time goes in v5:
time: 143 us; the launch traced here: 142 us
  waiting for transfers between devices  59.8 us (42%)
  starting transfers between devices  35.7 us (25%)
  Pallas kernels  27.9 us (20%)
  local copies, waits for them, and re-layouts  9.9 us (7%)
  other arithmetic  5.85 us (4%)
  between operations  3.26 us (2%)
    ppermute x3, waiting for transfers between devices, gather_up(): lax.ppermute(own, 'batch', [(i, (i - r) % homes) for i in range(homes)])  36.1 us
    ppermute x4, waiting for transfers between devices, combine(): lax.ppermute(value[height:], 'tensor', [(i, i ^ bit) for i in range(piece...  19.4 us
    ppermute x3, starting transfers between devices, give_back(): lax.ppermute(total, 'batch', [(i, (i - r) % homes) for i in range(homes)])  19 us
    pallas_call x4, Pallas kernels, base_part(): pl.pallas_call(functools.partial(base_kernel, len(after)), out_shape=jax....  8.98 us
    unnamed x26, local copies, waits for them, and re-layouts  8.43 us
    pallas_call x4, Pallas kernels, shrink(): pl.pallas_call(functools.partial(shrink_kernel, held, light, rank, value_...  6.95 us
    pallas_call x1, Pallas kernels, pack(): pl.pallas_call(functools.partial(pack_kernel, span, shifts), out_shape=[j...  5.74 us
    ppermute x3, starting transfers between devices, gather_up(): lax.ppermute(own, 'batch', [(i, (i - r) % homes) for i in range(homes)])  4.67 us
  transfers between devices with their start and end apart: 22, of which 5 were waited for; matrix products, arithmetic and copies ran while one was open for 5% of the time, Pallas kernels for 12%

profile of v5, /device:TPU:4, one launch (start us, length us, event | category | flops | bytes accessed | tf_op | source)
XLA Modules:
  0.0 142.5 jit_solution(14776314963985020368)
XLA Ops:
  0.0 3.8 %route.1 = (s32[1,768]{1,0:T(1,128)}, s32[8,128]{1,0:T(8,128)}, bf16[216,2048]{1,0:T(8,128)(2,1)}) custom-call(s32[1]{0:T(128)} %bitcast.place_ref, s32[32]{0:T(128)} %entry_hbm.1, s32[768]{0:T(1024)} %request_hbm.1, bf16[768,2048]{1,0:T(8,128)(2,1)} %tokens_ref.9), custom_call_target="tpu_custom_call" | custom-call | flops 1 | bytes 1 | tf_op jit(solution)/shard_map/route/pallas_call | solution.py:251
  3.8 5.7 %pack.1 = (s32[8,128]{1,0:T(8,128)}, bf16[216,2048]{1,0:T(8,128)(2,1)}, bf16[216,2048]{1,0:T(8,128)(2,1)}, bf16[216,2048]{1,0:T(8,128)(2,1)}) custom-call(s32[1,768]{1,0:T(1,128)} %get-tuple-element.17.index_ref, bf16[768,2048]{1,0:T(8,128)(2,1)} %tokens_ref.9), custom_call_target="tpu_custom_call" | custom-call | flops 1 | bytes 1 | tf_op jit(solution)/shard_map/pack/pallas_call | solution.py:271
  9.5 1.6 %collective-permute-start.12 = (bf16[216,2048]{1,0:T(8,128)(2,1)}, bf16[216,2048]{1,0:T(8,128)(2,1)}, u32[]{:S(2)}, u32[]{:S(2)}) collective-permute-start(bf16[216,2048]{1,0:T(8,128)(2,1)} %get-tuple-element.21), channel_id=1, source_target_pairs={{0,4},{4,8},{8,12},{12,0},{1,5},{5,9},{9,13},{13,1},{2,6},{6,10},{... | collective-permute-start | bytes 2654216 | tf_op jit(solution)/shard_map/ppermute | solution.py:286
  11.2 2.3 %collective-permute-start.4 = (bf16[8,32,256]{2,1,0:T(8,128)(2,1)S(1)}, bf16[8,32,256]{2,1,0:T(8,128)(2,1)S(1)}, u32[]{:S(2)}, u32[]{:S(2)}) collective-permute-start(bf16[8,32,256]{2,1,0:T(8,128)(2,1)S(1)} %constant_dynamic-slice_fusion), channel_id=1, source_target_pairs={{0,12},{4,0},{8,4},{12,8},{1,13},{5,1},{9,5},{13,9},{2,14},{6,2},{... | collective-permute-start | bytes 393224 | tf_op jit(solution)/shard_map/ppermute | solution.py:171
  13.5 0.8 collective-permute-start.5
  14.3 1.6 %collective-permute-start.6 = (bf16[8,32,256]{2,1,0:T(8,128)(2,1)S(1)}, bf16[8,32,256]{2,1,0:T(8,128)(2,1)S(1)}, u32[]{:S(2)}, u32[]{:S(2)}) collective-permute-start(bf16[8,32,256]{2,1,0:T(8,128)(2,1)S(1)} %constant_dynamic-slice_fusion), channel_id=1, source_target_pairs={{0,4},{4,8},{8,12},{12,0},{1,5},{5,9},{9,13},{13,1},{2,6},{6,10},{... | collective-permute-start | bytes 393224 | tf_op jit(solution)/shard_map/ppermute | solution.py:171
  15.9 1.2 slice.39
  19.4 2.2 %copy-done.2 = bf16[8,2048,128]{2,1,0:T(8,128)(2,1)S(1)} copy-done((bf16[8,2048,128]{2,1,0:T(8,128)(2,1)S(1)}, bf16[8,2048,128]{2,1,0:T(8,128)(2,1)}, u32[]{:S(2)}) %copy-start.2) | copy-done | bytes 4194328
  21.6 1.2 copy-done.7
  22.8 0.7 copy-done.8
  23.5 1.4 shrink.6
  24.9 10.3 %collective-permute-done.4 = bf16[8,32,256]{2,1,0:T(8,128)(2,1)S(1)} collective-permute-done((bf16[8,32,256]{2,1,0:T(8,128)(2,1)S(1)}, bf16[8,32,256]{2,1,0:T(8,128)(2,1)S(1)}, u32[]{:S(2)}, u32[]{:S(2)}) %collective-permute-start.4) | collective-permute-done | bytes 131104 | tf_op jit(solution)/shard_map/ppermute | solution.py:171
  35.2 2.4 %collective-permute-start.9 = (bf16[216,2048]{1,0:T(8,128)(2,1)}, bf16[216,2048]{1,0:T(8,128)(2,1)}, u32[]{:S(2)}, u32[]{:S(2)}) collective-permute-start(bf16[216,2048]{1,0:T(8,128)(2,1)} %get-tuple-element.20), channel_id=1, source_target_pairs={{0,8},{4,12},{8,0},{12,4},{1,9},{5,13},{9,1},{13,5},{2,10},{6,14},... | collective-permute-start | bytes 2654216 | tf_op jit(solution)/shard_map/ppermute | solution.py:286
  37.5 25.8 %collective-permute-done.5 = bf16[8,32,256]{2,1,0:T(8,128)(2,1)S(1)} collective-permute-done((bf16[8,32,256]{2,1,0:T(8,128)(2,1)S(1)}, bf16[8,32,256]{2,1,0:T(8,128)(2,1)S(1)}, u32[]{:S(2)}, u32[]{:S(2)}) %collective-permute-start.5) | collective-permute-done | bytes 131104 | tf_op jit(solution)/shard_map/ppermute | solution.py:171
  63.4 0.8 pad_maximum_fusion.2
  64.2 0.5 collective-permute-start.7
  64.8 1.6 %collective-permute-start.16 = (f32[120,128]{1,0:T(8,128)S(1)}, f32[120,128]{1,0:T(8,128)S(1)}, u32[]{:S(2)}, u32[]{:S(2)}) collective-permute-start(f32[120,128]{1,0:T(8,128)S(1)} %slice.61), channel_id=1, source_target_pairs={{0,2},{1,3},{2,0},{3,1},{4,6},{5,7},{6,4},{7,5},{8,10},{9,11},{10,... | collective-permute-start | bytes 184328 | tf_op jit(solution)/shard_map/ppermute | solution.py:316
  66.3 2.2 %copy-done.5 = bf16[2048,1024]{1,0:T(8,128)(2,1)S(1)} copy-done((bf16[2048,1024]{1,0:T(8,128)(2,1)S(1)}, bf16[2048,1024]{1,0:T(8,128)(2,1)}, u32[]{:S(2)}) %copy-start.5) | copy-done | bytes 4194328
  68.5 2.8 %base.4.refs_0_ = f32[384,512]{1,0:T(8,128)} custom-call(s32[2]{0:T(128)S(1)} %broadcast_xor_fusion.block_ref, bf16[768,2048]{1,0:T(8,128)(2,1)S(1)} %copy-done.1, bf16[2048,1024]{1,0:T(8,128)(2,1)S(1)} %copy-done.5, s32[8,128]{1,0:T(8,128)S(1)} %copy-done.8), custom_call_target="tpu_custom_call" | custom-call | flops 1 | bytes 1 | tf_op jit(solution)/shard_map/base/pallas_call | solution.py:198
  71.3 2.1 %base.6.refs_0_ = f32[384,512]{1,0:T(8,128)S(1)} custom-call(s32[2]{0:T(128)S(1)} %broadcast_xor_fusion.block_ref, bf16[768,2048]{1,0:T(8,128)(2,1)S(1)} %copy-done.1, bf16[2048,1024]{1,0:T(8,128)(2,1)S(1)} %copy-done.5, s32[8,128]{1,0:T(8,128)S(1)} %copy-done.8), custom_call_target="tpu_custom_call" | custom-call | flops 1 | bytes 1 | tf_op jit(solution)/shard_map/base/pallas_call | solution.py:198
  73.4 0.6 collective-permute-start.2
  74.0 2.1 %base.5 = f32[384,512]{1,0:T(8,128)S(1)} custom-call(s32[2]{0:T(128)S(1)} %multiply_xor_fusion.block_ref, bf16[768,2048]{1,0:T(8,128)(2,1)S(1)} %copy-done.1, bf16[2048,1024]{1,0:T(8,128)(2,1)S(1)} %copy-done.6, f32[384,512]{1,0:T(8,128)} %base.4.refs_0_), custom_call_target="tpu_custom_call" | custom-call | flops 1 | bytes 1 | tf_op jit(solution)/shard_map/base/pallas_call | solution.py:198
  76.1 2.1 %base.7 = f32[384,512]{1,0:T(8,128)S(1)} custom-call(s32[2]{0:T(128)S(1)} %multiply_xor_fusion.block_ref, bf16[768,2048]{1,0:T(8,128)(2,1)S(1)} %copy-done.1, bf16[2048,1024]{1,0:T(8,128)(2,1)S(1)} %copy-done.6, f32[384,512]{1,0:T(8,128)S(1)} %base.6.refs_0_), custom_call_target="tpu_custom_call" | custom-call | flops 1 | bytes 1 | tf_op jit(solution)/shard_map/base/pallas_call | solution.py:198
  78.7 0.2 copy.10.index_ref
  79.0 0.9 slice_add_fusion.3.refs_2_
  79.9 2.2 %copy-done.3 = bf16[8,2048,128]{2,1,0:T(8,128)(2,1)S(1)} copy-done((bf16[8,2048,128]{2,1,0:T(8,128)(2,1)S(1)}, bf16[8,2048,128]{2,1,0:T(8,128)(2,1)}, u32[]{:S(2)}) %copy-start.3) | copy-done | bytes 4194328
  82.1 2.2 %shrink.5 = f32[240,128]{1,0:T(8,128)S(1)} custom-call(s32[3]{0:T(128)S(1)} %pad_add_fusion.scalar_ref, bf16[216,2048]{1,0:T(8,128)(2,1)} %collective-permute-done.12.block_ref, bf16[8,2048,128]{2,1,0:T(8,128)(2,1)S(1)} %copy-done.3, s32[8,128]{1,0:T(8,128)S(1)} %copy-done.9), custom_call_target="tpu_custom_call" | custom-call | flops 1 | bytes 1 | tf_op jit(solution)/shard_map/shrink/pallas_call | solution.py:300
  84.3 0.1 collective-permute-start.13
  84.4 1.1 broadcast_select_fusion.1
  85.5 2.0 %shrink.4 = f32[240,128]{1,0:T(8,128)S(1)} custom-call(s32[3]{0:T(128)S(1)} %pad_add_fusion.scalar_ref, bf16[216,2048]{1,0:T(8,128)(2,1)} %collective-permute-done.9.block_ref, bf16[8,2048,128]{2,1,0:T(8,128)(2,1)S(1)} %copy-done.4, s32[8,128]{1,0:T(8,128)S(1)} %copy-done.9), custom_call_target="tpu_custom_call" | custom-call | flops 1 | bytes 1 | tf_op jit(solution)/shard_map/shrink/pallas_call | solution.py:300
  87.5 0.5 collective-permute-start.10
  88.1 0.6 collective-permute-start.14
  88.8 1.3 add.49
  90.1 1.5 %collective-permute-start.1 = (f32[384,256]{1,0:T(8,128)S(1)}, f32[384,256]{1,0:T(8,128)S(1)}, u32[]{:S(2)}, u32[]{:S(2)}) collective-permute-start(f32[384,256]{1,0:T(8,128)S(1)} %slice.53), channel_id=1, source_target_pairs={{0,2},{1,3},{2,0},{3,1},{4,6},{5,7},{6,4},{7,5},{8,10},{9,11},{10,... | collective-permute-start | bytes 1179656 | tf_op jit(solution)/shard_map/ppermute | solution.py:228
  91.6 1.3 add.51
  93.0 0.6 collective-permute-start.3
  93.6 1.5 %collective-permute-start.11 = (f32[120,128]{1,0:T(8,128)S(1)}, f32[120,128]{1,0:T(8,128)S(1)}, u32[]{:S(2)}, u32[]{:S(2)}) collective-permute-start(f32[120,128]{1,0:T(8,128)S(1)} %slice.57), channel_id=1, source_target_pairs={{0,2},{1,3},{2,0},{3,1},{4,6},{5,7},{6,4},{7,5},{8,10},{9,11},{10,... | collective-permute-start | bytes 184328 | tf_op jit(solution)/shard_map/ppermute | solution.py:316
  95.2 15.5 %collective-permute-done.11 = f32[120,128]{1,0:T(8,128)S(1)} collective-permute-done((f32[120,128]{1,0:T(8,128)S(1)}, f32[120,128]{1,0:T(8,128)S(1)}, u32[]{:S(2)}, u32[]{:S(2)}) %collective-permute-start.11) | collective-permute-done | bytes 61472 | tf_op jit(solution)/shard_map/ppermute | solution.py:316
  110.7 1.4 shrink.7
  112.1 1.8 %collective-permute-start.17 = (f32[120,128]{1,0:T(8,128)S(1)}, f32[120,128]{1,0:T(8,128)S(1)}, u32[]{:S(2)}, u32[]{:S(2)}) collective-permute-start(f32[120,128]{1,0:T(8,128)S(1)} %get-tuple-element.23), channel_id=1, source_target_pairs={{0,8},{4,12},{8,0},{12,4},{1,9},{5,13},{9,1},{13,5},{2,10},{6,14},... | collective-permute-start | bytes 184328 | tf_op jit(solution)/shard_map/ppermute | solution.py:337
  114.0 16.6 %collective-permute-start.18 = (f32[120,128]{1,0:T(8,128)S(1)}, f32[120,128]{1,0:T(8,128)S(1)}, u32[]{:S(2)}, u32[]{:S(2)}) collective-permute-start(f32[120,128]{1,0:T(8,128)S(1)} %get-tuple-element.24), channel_id=1, source_target_pairs={{0,12},{4,0},{8,4},{12,8},{1,13},{5,1},{9,5},{13,9},{2,14},{6,2},{... | collective-permute-start | bytes 184328 | tf_op jit(solution)/shard_map/ppermute | solution.py:337
  130.7 0.4 collective-permute-start.20
  131.1 0.1 slice_add_fusion
  131.2 3.8 %collective-permute-done.20 = f32[120,128]{1,0:T(8,128)S(1)} collective-permute-done((f32[120,128]{1,0:T(8,128)S(1)}, f32[120,128]{1,0:T(8,128)S(1)}, u32[]{:S(2)}, u32[]{:S(2)}) %collective-permute-start.20) | collective-permute-done | bytes 61472 | tf_op jit(solution)/shard_map/ppermute | solution.py:316
  135.0 0.5 collective-permute-start.21
  135.6 1.1 finish.2.base_ref
  136.8 4.3 %collective-permute-done.21.refs_0_ = f32[120,128]{1,0:T(8,128)S(1)} collective-permute-done((f32[120,128]{1,0:T(8,128)S(1)}, f32[120,128]{1,0:T(8,128)S(1)}, u32[]{:S(2)}, u32[]{:S(2)}) %collective-permute-start.21) | collective-permute-done | bytes 61472 | tf_op jit(solution)/shard_map/ppermute | solution.py:337
  141.1 1.4 finish.3
  (62 shorter events, 0.6 us)
Async XLA Ops:
  0.0 11.2 %copy-start = (bf16[8,64,256]{2,1,0:T(8,128)(2,1)S(1)}, bf16[8,64,256]{2,1,0:T(8,128)(2,1)}, u32[]{:S(2)}) copy-start(bf16[8,64,256]{2,1,0:T(8,128)(2,1)} %param.13) | copy-start | bytes 786436
  9.5 69.4 %collective-permute-start.12 = (bf16[216,2048]{1,0:T(8,128)(2,1)}, bf16[216,2048]{1,0:T(8,128)(2,1)}, u32[]{:S(2)}, u32[]{:S(2)}) collective-permute-start(bf16[216,2048]{1,0:T(8,128)(2,1)} %get-tuple-element.21), channel_id=1, source_target_pairs={{0,4},{4,8},{8,12},{12,0},{1,5},{5,9},{9,13},{13,1},{2,6},{6,10},{... | collective-permute-start | bytes 2654216 | tf_op jit(solution)/shard_map/ppermute | solution.py:286
  11.2 24.0 %collective-permute-start.4 = (bf16[8,32,256]{2,1,0:T(8,128)(2,1)S(1)}, bf16[8,32,256]{2,1,0:T(8,128)(2,1)S(1)}, u32[]{:S(2)}, u32[]{:S(2)}) collective-permute-start(bf16[8,32,256]{2,1,0:T(8,128)(2,1)S(1)} %constant_dynamic-slice_fusion), channel_id=1, source_target_pairs={{0,12},{4,0},{8,4},{12,8},{1,13},{5,1},{9,5},{13,9},{2,14},{6,2},{... | collective-permute-start | bytes 393224 | tf_op jit(solution)/shard_map/ppermute | solution.py:171
  13.5 49.9 %collective-permute-start.5 = (bf16[8,32,256]{2,1,0:T(8,128)(2,1)S(1)}, bf16[8,32,256]{2,1,0:T(8,128)(2,1)S(1)}, u32[]{:S(2)}, u32[]{:S(2)}) collective-permute-start(bf16[8,32,256]{2,1,0:T(8,128)(2,1)S(1)} %constant_dynamic-slice_fusion), channel_id=1, source_target_pairs={{0,8},{4,12},{8,0},{12,4},{1,9},{5,13},{9,1},{13,5},{2,10},{6,14},... | collective-permute-start | bytes 393224 | tf_op jit(solution)/shard_map/ppermute | solution.py:171
  14.3 49.1 %collective-permute-start.6 = (bf16[8,32,256]{2,1,0:T(8,128)(2,1)S(1)}, bf16[8,32,256]{2,1,0:T(8,128)(2,1)S(1)}, u32[]{:S(2)}, u32[]{:S(2)}) collective-permute-start(bf16[8,32,256]{2,1,0:T(8,128)(2,1)S(1)} %constant_dynamic-slice_fusion), channel_id=1, source_target_pairs={{0,4},{4,8},{8,12},{12,0},{1,5},{5,9},{9,13},{13,1},{2,6},{6,10},{... | collective-permute-start | bytes 393224 | tf_op jit(solution)/shard_map/ppermute | solution.py:171
  19.4 2.2 %copy-start.2 = (bf16[8,2048,128]{2,1,0:T(8,128)(2,1)S(1)}, bf16[8,2048,128]{2,1,0:T(8,128)(2,1)}, u32[]{:S(2)}) copy-start(bf16[8,2048,128]{2,1,0:T(8,128)(2,1)} %down_ref.7) | copy-start | bytes 12582916
  21.6 1.2 copy-start.7
  22.8 0.7 copy-start.8
  23.5 42.9 %copy-start.1 = (bf16[768,2048]{1,0:T(8,128)(2,1)S(1)}, bf16[768,2048]{1,0:T(8,128)(2,1)}, u32[]{:S(2)}) copy-start(bf16[768,2048]{1,0:T(8,128)(2,1)} %tokens_ref.9) | copy-start | bytes 9437188
  24.8 39.9 %collective-permute-start.15 = (f32[240,128]{1,0:T(8,128)S(1)}, f32[240,128]{1,0:T(8,128)S(1)}, u32[]{:S(2)}, u32[]{:S(2)}) collective-permute-start(f32[240,128]{1,0:T(8,128)S(1)} %shrink.6), channel_id=1, source_target_pairs={{0,1},{1,0},{2,3},{3,2},{4,5},{5,4},{6,7},{7,6},{8,9},{9,8},{10,11... | collective-permute-start | bytes 368648 | tf_op jit(solution)/shard_map/ppermute | solution.py:314
  35.2 50.3 %collective-permute-start.9 = (bf16[216,2048]{1,0:T(8,128)(2,1)}, bf16[216,2048]{1,0:T(8,128)(2,1)}, u32[]{:S(2)}, u32[]{:S(2)}) collective-permute-start(bf16[216,2048]{1,0:T(8,128)(2,1)} %get-tuple-element.20), channel_id=1, source_target_pairs={{0,8},{4,12},{8,0},{12,4},{1,9},{5,13},{9,1},{13,5},{2,10},{6,14},... | collective-permute-start | bytes 2654216 | tf_op jit(solution)/shard_map/ppermute | solution.py:286
  64.2 20.1 %collective-permute-start.7 = (bf16[32,32,256]{2,1,0:T(8,128)(2,1)}, bf16[32,32,256]{2,1,0:T(8,128)(2,1)}, u32[]{:S(2)}, u32[]{:S(2)}) collective-permute-start(bf16[32,32,256]{2,1,0:T(8,128)(2,1)} %pad_maximum_fusion.2), channel_id=1, source_target_pairs={{0,16},{16,0},{1,17},{17,1},{2,18},{18,2},{3,19},{19,3},{4,20},{20... | collective-permute-start | bytes 1572872 | tf_op jit(solution)/shard_map/ppermute | solution.py:175
  64.7 1.6 %copy-start.10 = (f32[240,128]{1,0:T(8,128)}, f32[240,128]{1,0:T(8,128)S(1)}, u32[]{:S(2)}) copy-start(f32[240,128]{1,0:T(8,128)S(1)} %add.58) | copy-start | bytes 368644
  64.8 8.6 %collective-permute-start.16 = (f32[120,128]{1,0:T(8,128)S(1)}, f32[120,128]{1,0:T(8,128)S(1)}, u32[]{:S(2)}, u32[]{:S(2)}) collective-permute-start(f32[120,128]{1,0:T(8,128)S(1)} %slice.61), channel_id=1, source_target_pairs={{0,2},{1,3},{2,0},{3,1},{4,6},{5,7},{6,4},{7,5},{8,10},{9,11},{10,... | collective-permute-start | bytes 184328 | tf_op jit(solution)/shard_map/ppermute | solution.py:316
  66.3 2.2 %copy-start.5 = (bf16[2048,1024]{1,0:T(8,128)(2,1)S(1)}, bf16[2048,1024]{1,0:T(8,128)(2,1)}, u32[]{:S(2)}) copy-start(bf16[2048,1024]{1,0:T(8,128)(2,1)} %weight_ref.7) | copy-start | bytes 12582916
  71.3 2.7 %copy-start.6 = (bf16[2048,1024]{1,0:T(8,128)(2,1)S(1)}, bf16[2048,1024]{1,0:T(8,128)(2,1)}, u32[]{:S(2)}) copy-start(bf16[2048,1024]{1,0:T(8,128)(2,1)} %weight_ref.7) | copy-start | bytes 12582916
  71.3 17.5 %collective-permute-start = (f32[384,512]{1,0:T(8,128)}, f32[384,512]{1,0:T(8,128)}, u32[]{:S(2)}, u32[]{:S(2)}) collective-permute-start(f32[384,512]{1,0:T(8,128)} %base.4.refs_0_), channel_id=1, source_target_pairs={{0,1},{1,0},{2,3},{3,2},{4,5},{5,4},{6,7},{7,6},{8,9},{9,8},{10,11... | collective-permute-start | bytes 2359304 | tf_op jit(solution)/shard_map/ppermute | solution.py:228
  73.4 2.6 %copy-start.11 = (f32[120,128]{1,0:T(8,128)}, f32[120,128]{1,0:T(8,128)S(1)}, u32[]{:S(2)}) copy-start(f32[120,128]{1,0:T(8,128)S(1)} %collective-permute-done.16) | copy-start | bytes 184324
  73.4 18.2 %collective-permute-start.2 = (f32[384,512]{1,0:T(8,128)S(1)}, f32[384,512]{1,0:T(8,128)}, u32[]{:S(2)}, u32[]{:S(2)}) collective-permute-start(f32[384,512]{1,0:T(8,128)S(1)} %base.6.refs_0_), channel_id=1, source_target_pairs={{0,1},{1,0},{2,3},{3,2},{4,5},{5,4},{6,7},{7,6},{8,9},{9,8},{10,11... | collective-permute-start | bytes 2359304 | tf_op jit(solution)/shard_map/ppermute | solution.py:228
  76.1 2.7 %copy-start.12 = (s32[1,768]{1,0:T(1,128)S(1)}, s32[1,768]{1,0:T(1,128)}, u32[]{:S(2)}) copy-start(s32[1,768]{1,0:T(1,128)} %get-tuple-element.17.index_ref) | copy-start | bytes 9220
  76.1 3.8 %copy-start.9 = (s32[8,128]{1,0:T(8,128)S(1)}, s32[8,128]{1,0:T(8,128)}, u32[]{:S(2)}) copy-start(s32[8,128]{1,0:T(8,128)} %get-tuple-element.18.refs_0_) | copy-start | bytes 12292
  78.9 31.8 %collective-permute-start.8 = (bf16[216,2048]{1,0:T(8,128)(2,1)}, bf16[216,2048]{1,0:T(8,128)(2,1)S(1)}, u32[]{:S(2)}, u32[]{:S(2)}) collective-permute-start(bf16[216,2048]{1,0:T(8,128)(2,1)} %get-tuple-element.19), channel_id=1, source_target_pairs={{0,12},{4,0},{8,4},{12,8},{1,13},{5,1},{9,5},{13,9},{2,14},{6,2},{... | collective-permute-start | bytes 2654216 | tf_op jit(solution)/shard_map/ppermute | solution.py:286
  79.9 2.2 %copy-start.3 = (bf16[8,2048,128]{2,1,0:T(8,128)(2,1)S(1)}, bf16[8,2048,128]{2,1,0:T(8,128)(2,1)}, u32[]{:S(2)}) copy-start(bf16[8,2048,128]{2,1,0:T(8,128)(2,1)} %down_ref.7) | copy-start | bytes 12582916
  82.1 3.4 %copy-start.4 = (bf16[8,2048,128]{2,1,0:T(8,128)(2,1)S(1)}, bf16[8,2048,128]{2,1,0:T(8,128)(2,1)}, u32[]{:S(2)}) copy-start(bf16[8,2048,128]{2,1,0:T(8,128)(2,1)} %down_ref.7) | copy-start | bytes 12582916
  84.3 3.8 %collective-permute-start.13 = (f32[240,128]{1,0:T(8,128)S(1)}, f32[240,128]{1,0:T(8,128)S(1)}, u32[]{:S(2)}, u32[]{:S(2)}) collective-permute-start(f32[240,128]{1,0:T(8,128)S(1)} %shrink.5), channel_id=1, source_target_pairs={{0,1},{1,0},{2,3},{3,2},{4,5},{5,4},{6,7},{7,6},{8,9},{9,8},{10,11... | collective-permute-start | bytes 368648 | tf_op jit(solution)/shard_map/ppermute | solution.py:314
  87.5 6.0 %collective-permute-start.10 = (f32[240,128]{1,0:T(8,128)S(1)}, f32[240,128]{1,0:T(8,128)S(1)}, u32[]{:S(2)}, u32[]{:S(2)}) collective-permute-start(f32[240,128]{1,0:T(8,128)S(1)} %shrink.4), channel_id=1, source_target_pairs={{0,1},{1,0},{2,3},{3,2},{4,5},{5,4},{6,7},{7,6},{8,9},{9,8},{10,11... | collective-permute-start | bytes 368648 | tf_op jit(solution)/shard_map/ppermute | solution.py:314
  88.1 7.1 %collective-permute-start.14 = (f32[120,128]{1,0:T(8,128)S(1)}, f32[120,128]{1,0:T(8,128)S(1)}, u32[]{:S(2)}, u32[]{:S(2)}) collective-permute-start(f32[120,128]{1,0:T(8,128)S(1)} %slice.59), channel_id=1, source_target_pairs={{0,2},{1,3},{2,0},{3,1},{4,6},{5,7},{6,4},{7,5},{8,10},{9,11},{10,... | collective-permute-start | bytes 184328 | tf_op jit(solution)/shard_map/ppermute | solution.py:316
  90.1 40.5 %collective-permute-start.1 = (f32[384,256]{1,0:T(8,128)S(1)}, f32[384,256]{1,0:T(8,128)S(1)}, u32[]{:S(2)}, u32[]{:S(2)}) collective-permute-start(f32[384,256]{1,0:T(8,128)S(1)} %slice.53), channel_id=1, source_target_pairs={{0,2},{1,3},{2,0},{3,1},{4,6},{5,7},{6,4},{7,5},{8,10},{9,11},{10,... | collective-permute-start | bytes 1179656 | tf_op jit(solution)/shard_map/ppermute | solution.py:228
  93.0 38.1 %collective-permute-start.3 = (f32[384,256]{1,0:T(8,128)S(1)}, f32[384,256]{1,0:T(8,128)S(1)}, u32[]{:S(2)}, u32[]{:S(2)}) collective-permute-start(f32[384,256]{1,0:T(8,128)S(1)} %slice.55), channel_id=1, source_target_pairs={{0,2},{1,3},{2,0},{3,1},{4,6},{5,7},{6,4},{7,5},{8,10},{9,11},{10,... | collective-permute-start | bytes 1179656 | tf_op jit(solution)/shard_map/ppermute | solution.py:228
  93.6 17.1 %collective-permute-start.11 = (f32[120,128]{1,0:T(8,128)S(1)}, f32[120,128]{1,0:T(8,128)S(1)}, u32[]{:S(2)}, u32[]{:S(2)}) collective-permute-start(f32[120,128]{1,0:T(8,128)S(1)} %slice.57), channel_id=1, source_target_pairs={{0,2},{1,3},{2,0},{3,1},{4,6},{5,7},{6,4},{7,5},{8,10},{9,11},{10,... | collective-permute-start | bytes 184328 | tf_op jit(solution)/shard_map/ppermute | solution.py:316
  112.1 18.6 %collective-permute-start.19 = (f32[240,128]{1,0:T(8,128)S(1)}, f32[240,128]{1,0:T(8,128)S(1)}, u32[]{:S(2)}, u32[]{:S(2)}) collective-permute-start(f32[240,128]{1,0:T(8,128)S(1)} %get-tuple-element.26), channel_id=1, source_target_pairs={{0,1},{1,0},{2,3},{3,2},{4,5},{5,4},{6,7},{7,6},{8,9},{9,8},{10,11... | collective-permute-start | bytes 368648 | tf_op jit(solution)/shard_map/ppermute | solution.py:314
  112.1 23.5 %collective-permute-start.17 = (f32[120,128]{1,0:T(8,128)S(1)}, f32[120,128]{1,0:T(8,128)S(1)}, u32[]{:S(2)}, u32[]{:S(2)}) collective-permute-start(f32[120,128]{1,0:T(8,128)S(1)} %get-tuple-element.23), channel_id=1, source_target_pairs={{0,8},{4,12},{8,0},{12,4},{1,9},{5,13},{9,1},{13,5},{2,10},{6,14},... | collective-permute-start | bytes 184328 | tf_op jit(solution)/shard_map/ppermute | solution.py:337
  114.0 21.7 %collective-permute-start.18 = (f32[120,128]{1,0:T(8,128)S(1)}, f32[120,128]{1,0:T(8,128)S(1)}, u32[]{:S(2)}, u32[]{:S(2)}) collective-permute-start(f32[120,128]{1,0:T(8,128)S(1)} %get-tuple-element.24), channel_id=1, source_target_pairs={{0,12},{4,0},{8,4},{12,8},{1,13},{5,1},{9,5},{13,9},{2,14},{6,2},{... | collective-permute-start | bytes 184328 | tf_op jit(solution)/shard_map/ppermute | solution.py:337
  130.7 4.3 %collective-permute-start.20 = (f32[120,128]{1,0:T(8,128)S(1)}, f32[120,128]{1,0:T(8,128)S(1)}, u32[]{:S(2)}, u32[]{:S(2)}) collective-permute-start(f32[120,128]{1,0:T(8,128)S(1)} %slice.63), channel_id=1, source_target_pairs={{0,2},{1,3},{2,0},{3,1},{4,6},{5,7},{6,4},{7,5},{8,10},{9,11},{10,... | collective-permute-start | bytes 184328 | tf_op jit(solution)/shard_map/ppermute | solution.py:316
  135.0 6.1 %collective-permute-start.21 = (f32[120,128]{1,0:T(8,128)S(1)}, f32[120,128]{1,0:T(8,128)S(1)}, u32[]{:S(2)}, u32[]{:S(2)}) collective-permute-start(f32[120,128]{1,0:T(8,128)S(1)} %slice_add_fusion.2.refs_3_), channel_id=1, source_target_pairs={{0,4},{4,8},{8,12},{12,0},{1,5},{5,9},{9,13},{13,1},{2,6},{6,10},{... | collective-permute-start | bytes 184328 | tf_op jit(solution)/shard_map/ppermute | solution.py:337

commit v6 on v5

--- a/solution.py
+++ b/solution.py
@@ -27,18 +27,17 @@
 
 
 def route_kernel(
-    homes, held, light, shift, place_ref, entry_hbm, request_hbm, tokens_hbm,
-    index_ref, heavy_ref, block_ref, entry_ref, request_ref, tokens_ref, sems,
+    homes, held, light, place_ref, entry_hbm, request_hbm, index_ref, heavy_ref, entry_ref, request_ref, sems
 ):
     loads = [
         pltpu.make_async_copy(source, target, sems.at[n])
         for n, (source, target) in enumerate(
-            [(request_hbm, request_ref), (entry_hbm, entry_ref), (tokens_hbm, tokens_ref)]
+            [(request_hbm, request_ref), (entry_hbm, entry_ref)]
         )
     ]
     for load in loads:
         load.start()
-    rows = tokens_ref.shape[0]
+    rows = request_ref.shape[0]
     adapters = entry_ref.shape[0]
     span = (held + 1) * light
     earlier = (
@@ -62,8 +61,6 @@
     index_ref[...] = index
     heavy = jnp.max(jnp.where(position >= light, slot, 0), axis=1, keepdims=True)
     heavy_ref[...] = jnp.broadcast_to(heavy, heavy_ref.shape)
-    loads[2].wait()
-    place_rows(index, shift * span, tokens_ref, block_ref)
 
 
 def pack_kernel(span, shifts, index_ref, tokens_ref, mark_ref, *refs):
@@ -162,6 +159,23 @@
     )(scalars, index, base, up, *shrinks, *after)
 
 
+def gate_kernel(*refs):
+    pass
+
+
+def gate(blocks, after):
+    return pl.pallas_call(
+        gate_kernel,
+        out_shape=[jax.ShapeDtypeStruct(b.shape, b.dtype) for b in blocks],
+        in_specs=[HBM] * len(blocks) + [ANY] * len(after),
+        out_specs=[HBM] * len(blocks),
+        input_output_aliases={n: n for n in range(len(blocks))},
+        compiler_params=WIDE,
+        cost_estimate=COST,
+        name="gate",
+    )(*blocks, *after)
+
+
 def gather_up(adapter_up, homes):
     teams = lax.axis_size("groups")
     team = lax.axis_index("groups")
@@ -248,25 +262,23 @@
     block_shape = jax.ShapeDtypeStruct((span, width), jnp.bfloat16)
 
     up, found = gather_up(adapter_up, homes)
-    index, heavy, first = pl.pallas_call(
-        functools.partial(route_kernel, homes, held, light, order[0]),
+    index, heavy = pl.pallas_call(
+        functools.partial(route_kernel, homes, held, light),
         out_shape=[
             jax.ShapeDtypeStruct((1, rows), jnp.int32),
             jax.ShapeDtypeStruct((8, 128), jnp.int32),
-            block_shape,
         ],
-        in_specs=[SMEM, HBM, HBM, HBM],
-        out_specs=[VMEM] * 3,
+        in_specs=[SMEM, HBM, HBM],
+        out_specs=[VMEM] * 2,
         scratch_shapes=[
             pltpu.SMEM(adapter_entry.shape, jnp.int32),
             pltpu.VMEM((rows,), jnp.int32),
-            pltpu.VMEM(tokens.shape, jnp.bfloat16),
-            pltpu.SemaphoreType.DMA((3,)),
+            pltpu.SemaphoreType.DMA((2,)),
         ],
         compiler_params=WIDE,
         cost_estimate=COST,
         name="route",
-    )(place.reshape(1), adapter_entry, request_adapter, tokens)
+    )(place.reshape(1), adapter_entry, request_adapter)
     def pack(shifts):
         return pl.pallas_call(
             functools.partial(pack_kernel, span, shifts),
@@ -285,11 +297,10 @@
     def send(block, r):
         return lax.ppermute(block, "batch", [(i, (i + r) % homes) for i in range(homes)])
 
-    arrived = {order[0]: send(first, order[0])}
-    later = order[1:] + [0]
-    packed, *blocks = pack(later)
-    for r, block in zip(later, blocks):
-        arrived[r] = send(block, r) if r else block
+    packed, own_block, *blocks = pack([0] + order)
+    arrived = {0: own_block}
+    for r, block in zip(order, gate(blocks, found)):
+        arrived[r] = send(block, r)
 
     heavy = heavy[0, 0]
     heavy_here = (heavy // held == place).astype(jnp.int32)

time: 143 us -> 137 us (0.958)
  the two profiles are of different devices: /device:TPU:4 before, /device:TPU:0 now
where the time goes in v6:
time: 137 us
  waiting for transfers between devices  48.8 us (36%)
  starting transfers between devices  41.8 us (31%)
  Pallas kernels  26.6 us (19%)
  local copies, waits for them, and re-layouts  10.4 us (8%)
  other arithmetic  5.88 us (4%)
  between operations  3.15 us (2%)
    ppermute x3, waiting for transfers between devices, send(): lax.ppermute(block, 'batch', [(i, (i + r) % homes) for i in range(homes)])  24.5 us
    ppermute x3, starting transfers between devices, give_back(): lax.ppermute(total, 'batch', [(i, (i - r) % homes) for i in range(homes)])  21.3 us
    ppermute x4, waiting for transfers between devices, combine(): lax.ppermute(value[height:], 'tensor', [(i, i ^ bit) for i in range(piece...  16.9 us
    pallas_call x4, Pallas kernels, base_part(): pl.pallas_call(functools.partial(base_kernel, len(after)), out_shape=jax....  9.01 us
    unnamed x38, local copies, waits for them, and re-layouts  8.93 us
    pallas_call x4, Pallas kernels, shrink(): pl.pallas_call(functools.partial(shrink_kernel, held, light, rank, value_...  6.95 us
    pallas_call x1, Pallas kernels, pack(): pl.pallas_call(functools.partial(pack_kernel, span, shifts), out_shape=[j...  6.45 us
    ppermute x3, starting transfers between devices, gather_up(): lax.ppermute(own, 'batch', [(i, (i - r) % homes) for i in range(homes)])  6.11 us
  transfers between devices with their start and end apart: 22, of which 6 were waited for; matrix products, arithmetic and copies ran while one was open for 5% of the time, Pallas kernels for 18%

profile of v6, /device:TPU:0, one launch (start us, length us, event | category | flops | bytes accessed | tf_op | source)
XLA Modules:
  0.0 136.6 jit_solution(14060632416175986221)
XLA Ops:
  0.0 0.9 copy-done
  1.0 5.1 %collective-permute-start.4 = (bf16[8,32,256]{2,1,0:T(8,128)(2,1)S(1)}, bf16[8,32,256]{2,1,0:T(8,128)(2,1)S(1)}, u32[]{:S(2)}, u32[]{:S(2)}) collective-permute-start(bf16[8,32,256]{2,1,0:T(8,128)(2,1)S(1)} %constant_dynamic-slice_fusion), channel_id=1, source_target_pairs={{0,12},{4,0},{8,4},{12,8},{1,13},{5,1},{9,5},{13,9},{2,14},{6,2},{... | collective-permute-start | bytes 393224 | tf_op jit(solution)/shard_map/ppermute | solution.py:185
  6.1 1.0 collective-permute-start.6
  7.1 1.7 %route.1 = (s32[1,768]{1,0:T(1,128)}, s32[8,128]{1,0:T(8,128)}) custom-call(s32[1]{0:T(128)} %bitcast.place_ref, s32[32]{0:T(128)} %entry_hbm.1, s32[768]{0:T(1024)} %request_hbm.1), custom_call_target="tpu_custom_call" | custom-call | flops 1 | bytes 1 | tf_op jit(solution)/shard_map/route/pallas_call | solution.py:265
  8.8 6.5 %pack.1 = (s32[8,128]{1,0:T(8,128)}, bf16[216,2048]{1,0:T(8,128)(2,1)}, bf16[216,2048]{1,0:T(8,128)(2,1)}, bf16[216,2048]{1,0:T(8,128)(2,1)}, bf16[216,2048]{1,0:T(8,128)(2,1)}) custom-call(s32[1,768]{1,0:T(1,128)} %get-tuple-element.20.index_ref, bf16[768,2048]{1,0:T(8,128)(2,1)} %tokens_ref.9), custom_call_target="tpu_custom_call" | custom-call | flops 1 | bytes 1 | tf_op jit(solution)/shard_map/pack/pallas_call | solution.py:283
  15.3 2.0 %collective-permute-done.5.refs_4_ = bf16[8,32,256]{2,1,0:T(8,128)(2,1)S(1)} collective-permute-done((bf16[8,32,256]{2,1,0:T(8,128)(2,1)S(1)}, bf16[8,32,256]{2,1,0:T(8,128)(2,1)S(1)}, u32[]{:S(2)}, u32[]{:S(2)}) %collective-permute-start.5) | collective-permute-done | bytes 131104 | tf_op jit(solution)/shard_map/ppermute | solution.py:185
  17.3 0.6 copy-done.12
  18.0 0.7 collective-permute-start.12
  18.6 1.2 slice.39
  22.1 2.2 %copy-done.2 = bf16[8,2048,128]{2,1,0:T(8,128)(2,1)S(1)} copy-done((bf16[8,2048,128]{2,1,0:T(8,128)(2,1)S(1)}, bf16[8,2048,128]{2,1,0:T(8,128)(2,1)}, u32[]{:S(2)}) %copy-start.2) | copy-done | bytes 4194328
  24.3 0.7 copy-done.8
  25.0 1.4 %shrink.6 = f32[240,128]{1,0:T(8,128)S(1)} custom-call(s32[3]{0:T(128)S(1)} %pad_add_fusion.scalar_ref, bf16[216,2048]{1,0:T(8,128)(2,1)S(1)} %copy-done.7, bf16[8,2048,128]{2,1,0:T(8,128)(2,1)S(1)} %copy-done.2, s32[8,128]{1,0:T(8,128)S(1)} %copy-done.8), custom_call_target="tpu_custom_call" | custom-call | flops 1 | bytes 1 | tf_op jit(solution)/shard_map/shrink/pallas_call | solution.py:311
  26.4 2.0 %collective-permute-start.9 = (bf16[216,2048]{1,0:T(8,128)(2,1)}, bf16[216,2048]{1,0:T(8,128)(2,1)}, u32[]{:S(2)}, u32[]{:S(2)}) collective-permute-start(bf16[216,2048]{1,0:T(8,128)(2,1)} %get-tuple-element.26), channel_id=1, source_target_pairs={{0,8},{4,12},{8,0},{12,4},{1,9},{5,13},{9,1},{13,5},{2,10},{6,14},... | collective-permute-start | bytes 2654216 | tf_op jit(solution)/shard_map/ppermute | solution.py:298
  28.4 0.9 pad_maximum_fusion.2
  29.3 1.5 %collective-permute-start.7 = (bf16[32,32,256]{2,1,0:T(8,128)(2,1)}, bf16[32,32,256]{2,1,0:T(8,128)(2,1)}, u32[]{:S(2)}, u32[]{:S(2)}) collective-permute-start(bf16[32,32,256]{2,1,0:T(8,128)(2,1)} %pad_maximum_fusion.2), channel_id=1, source_target_pairs={{0,16},{16,0},{1,17},{17,1},{2,18},{18,2},{3,19},{19,3},{4,20},{20... | collective-permute-start | bytes 1572872 | tf_op jit(solution)/shard_map/ppermute | solution.py:189
  30.8 1.6 %collective-permute-start.16 = (f32[120,128]{1,0:T(8,128)S(1)}, f32[120,128]{1,0:T(8,128)S(1)}, u32[]{:S(2)}, u32[]{:S(2)}) collective-permute-start(f32[120,128]{1,0:T(8,128)S(1)} %slice.61), channel_id=1, source_target_pairs={{0,2},{1,3},{2,0},{3,1},{4,6},{5,7},{6,4},{7,5},{8,10},{9,11},{10,... | collective-permute-start | bytes 184328 | tf_op jit(solution)/shard_map/ppermute | solution.py:327
  32.4 2.2 %copy-done.5 = bf16[2048,1024]{1,0:T(8,128)(2,1)S(1)} copy-done((bf16[2048,1024]{1,0:T(8,128)(2,1)S(1)}, bf16[2048,1024]{1,0:T(8,128)(2,1)}, u32[]{:S(2)}) %copy-start.5) | copy-done | bytes 4194328
  34.6 2.8 %base.4.refs_0_ = f32[384,512]{1,0:T(8,128)} custom-call(s32[2]{0:T(128)S(1)} %broadcast_xor_fusion.block_ref, bf16[768,2048]{1,0:T(8,128)(2,1)S(1)} %copy-done.1, bf16[2048,1024]{1,0:T(8,128)(2,1)S(1)} %copy-done.5, s32[8,128]{1,0:T(8,128)S(1)} %copy-done.8), custom_call_target="tpu_custom_call" | custom-call | flops 1 | bytes 1 | tf_op jit(solution)/shard_map/base/pallas_call | solution.py:212
  37.4 2.1 %base.6.refs_0_ = f32[384,512]{1,0:T(8,128)S(1)} custom-call(s32[2]{0:T(128)S(1)} %broadcast_xor_fusion.block_ref, bf16[768,2048]{1,0:T(8,128)(2,1)S(1)} %copy-done.1, bf16[2048,1024]{1,0:T(8,128)(2,1)S(1)} %copy-done.5, s32[8,128]{1,0:T(8,128)S(1)} %copy-done.8), custom_call_target="tpu_custom_call" | custom-call | flops 1 | bytes 1 | tf_op jit(solution)/shard_map/base/pallas_call | solution.py:212
  39.5 0.6 collective-permute-start.2
  40.1 2.1 %base.5 = f32[384,512]{1,0:T(8,128)S(1)} custom-call(s32[2]{0:T(128)S(1)} %multiply_xor_fusion.block_ref, bf16[768,2048]{1,0:T(8,128)(2,1)S(1)} %copy-done.1, bf16[2048,1024]{1,0:T(8,128)(2,1)S(1)} %copy-done.6, f32[384,512]{1,0:T(8,128)} %base.4.refs_0_), custom_call_target="tpu_custom_call" | custom-call | flops 1 | bytes 1 | tf_op jit(solution)/shard_map/base/pallas_call | solution.py:212
  42.2 2.1 %base.7 = f32[384,512]{1,0:T(8,128)S(1)} custom-call(s32[2]{0:T(128)S(1)} %multiply_xor_fusion.block_ref, bf16[768,2048]{1,0:T(8,128)(2,1)S(1)} %copy-done.1, bf16[2048,1024]{1,0:T(8,128)(2,1)S(1)} %copy-done.6, f32[384,512]{1,0:T(8,128)S(1)} %base.6.refs_0_), custom_call_target="tpu_custom_call" | custom-call | flops 1 | bytes 1 | tf_op jit(solution)/shard_map/base/pallas_call | solution.py:212
  44.8 0.2 copy.13.index_ref
  45.0 3.0 %collective-permute-start.8 = (bf16[216,2048]{1,0:T(8,128)(2,1)}, bf16[216,2048]{1,0:T(8,128)(2,1)S(1)}, u32[]{:S(2)}, u32[]{:S(2)}) collective-permute-start(bf16[216,2048]{1,0:T(8,128)(2,1)} %get-tuple-element.25), channel_id=1, source_target_pairs={{0,12},{4,0},{8,4},{12,8},{1,13},{5,1},{9,5},{13,9},{2,14},{6,2},{... | collective-permute-start | bytes 2654216 | tf_op jit(solution)/shard_map/ppermute | solution.py:298
  48.0 0.9 slice_add_fusion.3.refs_2_
  48.9 2.2 %copy-done.3 = bf16[8,2048,128]{2,1,0:T(8,128)(2,1)S(1)} copy-done((bf16[8,2048,128]{2,1,0:T(8,128)(2,1)S(1)}, bf16[8,2048,128]{2,1,0:T(8,128)(2,1)}, u32[]{:S(2)}) %copy-start.3) | copy-done | bytes 4194328
  51.1 2.2 %shrink.5 = f32[240,128]{1,0:T(8,128)S(1)} custom-call(s32[3]{0:T(128)S(1)} %pad_add_fusion.scalar_ref, bf16[216,2048]{1,0:T(8,128)(2,1)} %collective-permute-done.12.block_ref, bf16[8,2048,128]{2,1,0:T(8,128)(2,1)S(1)} %copy-done.3, s32[8,128]{1,0:T(8,128)S(1)} %copy-done.9), custom_call_target="tpu_custom_call" | custom-call | flops 1 | bytes 1 | tf_op jit(solution)/shard_map/shrink/pallas_call | solution.py:311
  53.3 1.1 broadcast_select_fusion.1
  54.5 24.5 %collective-permute-done.9.block_ref = bf16[216,2048]{1,0:T(8,128)(2,1)} collective-permute-done((bf16[216,2048]{1,0:T(8,128)(2,1)}, bf16[216,2048]{1,0:T(8,128)(2,1)}, u32[]{:S(2)}, u32[]{:S(2)}) %collective-permute-start.9) | collective-permute-done | bytes 884768 | tf_op jit(solution)/shard_map/ppermute | solution.py:298
  79.0 2.0 %shrink.4 = f32[240,128]{1,0:T(8,128)S(1)} custom-call(s32[3]{0:T(128)S(1)} %pad_add_fusion.scalar_ref, bf16[216,2048]{1,0:T(8,128)(2,1)} %collective-permute-done.9.block_ref, bf16[8,2048,128]{2,1,0:T(8,128)(2,1)S(1)} %copy-done.4, s32[8,128]{1,0:T(8,128)S(1)} %copy-done.9), custom_call_target="tpu_custom_call" | custom-call | flops 1 | bytes 1 | tf_op jit(solution)/shard_map/shrink/pallas_call | solution.py:311
  81.1 1.6 %collective-permute-start.14 = (f32[120,128]{1,0:T(8,128)S(1)}, f32[120,128]{1,0:T(8,128)S(1)}, u32[]{:S(2)}, u32[]{:S(2)}) collective-permute-start(f32[120,128]{1,0:T(8,128)S(1)} %slice.59), channel_id=1, source_target_pairs={{0,2},{1,3},{2,0},{3,1},{4,6},{5,7},{6,4},{7,5},{8,10},{9,11},{10,... | collective-permute-start | bytes 184328 | tf_op jit(solution)/shard_map/ppermute | solution.py:327
  82.7 1.3 add.49
  84.0 0.6 collective-permute-start.1
  84.6 1.3 add.51
  85.9 1.6 %collective-permute-start.3 = (f32[384,256]{1,0:T(8,128)S(1)}, f32[384,256]{1,0:T(8,128)S(1)}, u32[]{:S(2)}, u32[]{:S(2)}) collective-permute-start(f32[384,256]{1,0:T(8,128)S(1)} %slice.55), channel_id=1, source_target_pairs={{0,2},{1,3},{2,0},{3,1},{4,6},{5,7},{6,4},{7,5},{8,10},{9,11},{10,... | collective-permute-start | bytes 1179656 | tf_op jit(solution)/shard_map/ppermute | solution.py:242
  87.5 0.6 collective-permute-start.11
  88.1 16.9 %collective-permute-done.11 = f32[120,128]{1,0:T(8,128)S(1)} collective-permute-done((f32[120,128]{1,0:T(8,128)S(1)}, f32[120,128]{1,0:T(8,128)S(1)}, u32[]{:S(2)}, u32[]{:S(2)}) %collective-permute-start.11) | collective-permute-done | bytes 61472 | tf_op jit(solution)/shard_map/ppermute | solution.py:327
  105.1 1.4 %shrink.7 = (f32[240,128]{1,0:T(8,128)S(1)}, f32[120,128]{1,0:T(8,128)S(1)}, f32[120,128]{1,0:T(8,128)S(1)}, f32[120,128]{1,0:T(8,128)S(1)}) custom-call(s32[3]{0:T(128)S(1)} %pad_add_fusion.scalar_ref, bf16[216,2048]{1,0:T(8,128)(2,1)S(1)} %collective-permute-done.8.block_ref, bf16[8,2048,128]{2,1,0:T(8,128)(2,1)S(1)} %copy-done.4, ...), custom_call_target="tpu_custom_call" | custom-call | flops 1 | bytes 1 | tf_op jit(solution)/shard_map/shrink/pallas_call | solution.py:311
  106.6 1.2 collective-permute-done.19
  107.9 0.6 collective-permute-start.20
  108.5 0.1 slice_add_fusion
  108.5 9.0 %collective-permute-start.17 = (f32[120,128]{1,0:T(8,128)S(1)}, f32[120,128]{1,0:T(8,128)S(1)}, u32[]{:S(2)}, u32[]{:S(2)}) collective-permute-start(f32[120,128]{1,0:T(8,128)S(1)} %get-tuple-element.29), channel_id=1, source_target_pairs={{0,8},{4,12},{8,0},{12,4},{1,9},{5,13},{9,1},{13,5},{2,10},{6,14},... | collective-permute-start | bytes 184328 | tf_op jit(solution)/shard_map/ppermute | solution.py:348
  117.5 11.6 %collective-permute-start.18 = (f32[120,128]{1,0:T(8,128)S(1)}, f32[120,128]{1,0:T(8,128)S(1)}, u32[]{:S(2)}, u32[]{:S(2)}) collective-permute-start(f32[120,128]{1,0:T(8,128)S(1)} %get-tuple-element.30), channel_id=1, source_target_pairs={{0,12},{4,0},{8,4},{12,8},{1,13},{5,1},{9,5},{13,9},{2,14},{6,2},{... | collective-permute-start | bytes 184328 | tf_op jit(solution)/shard_map/ppermute | solution.py:348
  129.2 0.7 collective-permute-start.21
  129.9 1.9 %collective-permute-done.18.refs_1_ = f32[120,128]{1,0:T(8,128)S(1)} collective-permute-done((f32[120,128]{1,0:T(8,128)S(1)}, f32[120,128]{1,0:T(8,128)S(1)}, u32[]{:S(2)}, u32[]{:S(2)}) %collective-permute-start.18) | collective-permute-done | bytes 61472 | tf_op jit(solution)/shard_map/ppermute | solution.py:348
  131.9 1.1 finish.2.base_ref
  133.0 2.3 %collective-permute-done.21.refs_0_ = f32[120,128]{1,0:T(8,128)S(1)} collective-permute-done((f32[120,128]{1,0:T(8,128)S(1)}, f32[120,128]{1,0:T(8,128)S(1)}, u32[]{:S(2)}, u32[]{:S(2)}) %collective-permute-start.21) | collective-permute-done | bytes 61472 | tf_op jit(solution)/shard_map/ppermute | solution.py:348
  135.3 1.4 finish.3
  (75 shorter events, 0.8 us)
Async XLA Ops:
  0.0 1.0 copy-start
  1.0 14.3 %collective-permute-start.4 = (bf16[8,32,256]{2,1,0:T(8,128)(2,1)S(1)}, bf16[8,32,256]{2,1,0:T(8,128)(2,1)S(1)}, u32[]{:S(2)}, u32[]{:S(2)}) collective-permute-start(bf16[8,32,256]{2,1,0:T(8,128)(2,1)S(1)} %constant_dynamic-slice_fusion), channel_id=1, source_target_pairs={{0,12},{4,0},{8,4},{12,8},{1,13},{5,1},{9,5},{13,9},{2,14},{6,2},{... | collective-permute-start | bytes 393224 | tf_op jit(solution)/shard_map/ppermute | solution.py:185
  6.1 11.2 %collective-permute-start.5 = (bf16[8,32,256]{2,1,0:T(8,128)(2,1)S(1)}, bf16[8,32,256]{2,1,0:T(8,128)(2,1)S(1)}, u32[]{:S(2)}, u32[]{:S(2)}) collective-permute-start(bf16[8,32,256]{2,1,0:T(8,128)(2,1)S(1)} %constant_dynamic-slice_fusion), channel_id=1, source_target_pairs={{0,8},{4,12},{8,0},{12,4},{1,9},{5,13},{9,1},{13,5},{2,10},{6,14},... | collective-permute-start | bytes 393224 | tf_op jit(solution)/shard_map/ppermute | solution.py:185
  6.1 11.2 %collective-permute-start.6 = (bf16[8,32,256]{2,1,0:T(8,128)(2,1)S(1)}, bf16[8,32,256]{2,1,0:T(8,128)(2,1)S(1)}, u32[]{:S(2)}, u32[]{:S(2)}) collective-permute-start(bf16[8,32,256]{2,1,0:T(8,128)(2,1)S(1)} %constant_dynamic-slice_fusion), channel_id=1, source_target_pairs={{0,4},{4,8},{8,12},{12,0},{1,5},{5,9},{9,13},{13,1},{2,6},{6,10},{... | collective-permute-start | bytes 393224 | tf_op jit(solution)/shard_map/ppermute | solution.py:185
  15.3 6.8 %copy-start.7 = (bf16[216,2048]{1,0:T(8,128)(2,1)S(1)}, bf16[216,2048]{1,0:T(8,128)(2,1)}, u32[]{:S(2)}) copy-start(bf16[216,2048]{1,0:T(8,128)(2,1)} %get-tuple-element.28.block_ref) | copy-start | bytes 2654212
  15.3 2.0 %copy-start.10 = (bf16[8,32,256]{2,1,0:T(8,128)(2,1)}, bf16[8,32,256]{2,1,0:T(8,128)(2,1)S(1)}, u32[]{:S(2)}) copy-start(bf16[8,32,256]{2,1,0:T(8,128)(2,1)S(1)} %collective-permute-done.4.refs_3_) | copy-start | bytes 393220
  17.3 0.7 copy-start.12
  17.3 0.7 copy-start.14
  18.0 27.0 %collective-permute-start.12 = (bf16[216,2048]{1,0:T(8,128)(2,1)}, bf16[216,2048]{1,0:T(8,128)(2,1)}, u32[]{:S(2)}, u32[]{:S(2)}) collective-permute-start(bf16[216,2048]{1,0:T(8,128)(2,1)} %get-tuple-element.27), channel_id=1, source_target_pairs={{0,4},{4,8},{8,12},{12,0},{1,5},{5,9},{9,13},{13,1},{2,6},{6,10},{... | collective-permute-start | bytes 2654216 | tf_op jit(solution)/shard_map/ppermute | solution.py:298
  22.1 2.2 %copy-start.2 = (bf16[8,2048,128]{2,1,0:T(8,128)(2,1)S(1)}, bf16[8,2048,128]{2,1,0:T(8,128)(2,1)}, u32[]{:S(2)}) copy-start(bf16[8,2048,128]{2,1,0:T(8,128)(2,1)} %down_ref.7) | copy-start | bytes 12582916
  24.3 0.7 copy-start.8
  25.0 3.4 %copy-start.11 = (bf16[8,32,256]{2,1,0:T(8,128)(2,1)S(1)}, bf16[8,32,256]{2,1,0:T(8,128)(2,1)}, u32[]{:S(2)}) copy-start(bf16[8,32,256]{2,1,0:T(8,128)(2,1)} %copy-done.10) | copy-start | bytes 393220
  25.0 3.4 %copy-start.13 = (bf16[8,32,256]{2,1,0:T(8,128)(2,1)S(1)}, bf16[8,32,256]{2,1,0:T(8,128)(2,1)}, u32[]{:S(2)}) copy-start(bf16[8,32,256]{2,1,0:T(8,128)(2,1)} %copy-done.12) | copy-start | bytes 393220
  25.0 3.4 %copy-start.15 = (bf16[8,32,256]{2,1,0:T(8,128)(2,1)S(1)}, bf16[8,32,256]{2,1,0:T(8,128)(2,1)}, u32[]{:S(2)}) copy-start(bf16[8,32,256]{2,1,0:T(8,128)(2,1)} %copy-done.14) | copy-start | bytes 393220
  25.0 7.4 %copy-start.1 = (bf16[768,2048]{1,0:T(8,128)(2,1)S(1)}, bf16[768,2048]{1,0:T(8,128)(2,1)}, u32[]{:S(2)}) copy-start(bf16[768,2048]{1,0:T(8,128)(2,1)} %tokens_ref.9) | copy-start | bytes 9437188
  26.4 4.4 %collective-permute-start.15 = (f32[240,128]{1,0:T(8,128)S(1)}, f32[240,128]{1,0:T(8,128)S(1)}, u32[]{:S(2)}, u32[]{:S(2)}) collective-permute-start(f32[240,128]{1,0:T(8,128)S(1)} %shrink.6), channel_id=1, source_target_pairs={{0,1},{1,0},{2,3},{3,2},{4,5},{5,4},{6,7},{7,6},{8,9},{9,8},{10,11... | collective-permute-start | bytes 368648 | tf_op jit(solution)/shard_map/ppermute | solution.py:325
  26.4 52.6 %collective-permute-start.9 = (bf16[216,2048]{1,0:T(8,128)(2,1)}, bf16[216,2048]{1,0:T(8,128)(2,1)}, u32[]{:S(2)}, u32[]{:S(2)}) collective-permute-start(bf16[216,2048]{1,0:T(8,128)(2,1)} %get-tuple-element.26), channel_id=1, source_target_pairs={{0,8},{4,12},{8,0},{12,4},{1,9},{5,13},{9,1},{13,5},{2,10},{6,14},... | collective-permute-start | bytes 2654216 | tf_op jit(solution)/shard_map/ppermute | solution.py:298
  29.3 24.0 %collective-permute-start.7 = (bf16[32,32,256]{2,1,0:T(8,128)(2,1)}, bf16[32,32,256]{2,1,0:T(8,128)(2,1)}, u32[]{:S(2)}, u32[]{:S(2)}) collective-permute-start(bf16[32,32,256]{2,1,0:T(8,128)(2,1)} %pad_maximum_fusion.2), channel_id=1, source_target_pairs={{0,16},{16,0},{1,17},{17,1},{2,18},{18,2},{3,19},{19,3},{4,20},{20... | collective-permute-start | bytes 1572872 | tf_op jit(solution)/shard_map/ppermute | solution.py:189
  30.8 6.6 %copy-start.16 = (f32[240,128]{1,0:T(8,128)}, f32[240,128]{1,0:T(8,128)S(1)}, u32[]{:S(2)}) copy-start(f32[240,128]{1,0:T(8,128)S(1)} %add.58) | copy-start | bytes 368644
  30.8 8.7 %collective-permute-start.16 = (f32[120,128]{1,0:T(8,128)S(1)}, f32[120,128]{1,0:T(8,128)S(1)}, u32[]{:S(2)}, u32[]{:S(2)}) collective-permute-start(f32[120,128]{1,0:T(8,128)S(1)} %slice.61), channel_id=1, source_target_pairs={{0,2},{1,3},{2,0},{3,1},{4,6},{5,7},{6,4},{7,5},{8,10},{9,11},{10,... | collective-permute-start | bytes 184328 | tf_op jit(solution)/shard_map/ppermute | solution.py:327
  32.4 2.2 %copy-start.5 = (bf16[2048,1024]{1,0:T(8,128)(2,1)S(1)}, bf16[2048,1024]{1,0:T(8,128)(2,1)}, u32[]{:S(2)}) copy-start(bf16[2048,1024]{1,0:T(8,128)(2,1)} %weight_ref.7) | copy-start | bytes 12582916
  37.4 2.7 %copy-start.6 = (bf16[2048,1024]{1,0:T(8,128)(2,1)S(1)}, bf16[2048,1024]{1,0:T(8,128)(2,1)}, u32[]{:S(2)}) copy-start(bf16[2048,1024]{1,0:T(8,128)(2,1)} %weight_ref.7) | copy-start | bytes 12582916
  37.4 45.3 %collective-permute-start = (f32[384,512]{1,0:T(8,128)}, f32[384,512]{1,0:T(8,128)}, u32[]{:S(2)}, u32[]{:S(2)}) collective-permute-start(f32[384,512]{1,0:T(8,128)} %base.4.refs_0_), channel_id=1, source_target_pairs={{0,1},{1,0},{2,3},{3,2},{4,5},{5,4},{6,7},{7,6},{8,9},{9,8},{10,11... | collective-permute-start | bytes 2359304 | tf_op jit(solution)/shard_map/ppermute | solution.py:242
  39.5 2.6 %copy-start.17 = (f32[120,128]{1,0:T(8,128)}, f32[120,128]{1,0:T(8,128)S(1)}, u32[]{:S(2)}) copy-start(f32[120,128]{1,0:T(8,128)S(1)} %collective-permute-done.16) | copy-start | bytes 184324
  39.5 45.1 %collective-permute-start.2 = (f32[384,512]{1,0:T(8,128)S(1)}, f32[384,512]{1,0:T(8,128)}, u32[]{:S(2)}, u32[]{:S(2)}) collective-permute-start(f32[384,512]{1,0:T(8,128)S(1)} %base.6.refs_0_), channel_id=1, source_target_pairs={{0,1},{1,0},{2,3},{3,2},{4,5},{5,4},{6,7},{7,6},{8,9},{9,8},{10,11... | collective-permute-start | bytes 2359304 | tf_op jit(solution)/shard_map/ppermute | solution.py:242
  42.2 2.7 %copy-start.18 = (s32[1,768]{1,0:T(1,128)S(1)}, s32[1,768]{1,0:T(1,128)}, u32[]{:S(2)}) copy-start(s32[1,768]{1,0:T(1,128)} %get-tuple-element.20.index_ref) | copy-start | bytes 9220
  42.2 6.7 %copy-start.9 = (s32[8,128]{1,0:T(8,128)S(1)}, s32[8,128]{1,0:T(8,128)}, u32[]{:S(2)}) copy-start(s32[8,128]{1,0:T(8,128)} %get-tuple-element.21.refs_0_) | copy-start | bytes 12292
  45.0 60.1 %collective-permute-start.8 = (bf16[216,2048]{1,0:T(8,128)(2,1)}, bf16[216,2048]{1,0:T(8,128)(2,1)S(1)}, u32[]{:S(2)}, u32[]{:S(2)}) collective-permute-start(bf16[216,2048]{1,0:T(8,128)(2,1)} %get-tuple-element.25), channel_id=1, source_target_pairs={{0,12},{4,0},{8,4},{12,8},{1,13},{5,1},{9,5},{13,9},{2,14},{6,2},{... | collective-permute-start | bytes 2654216 | tf_op jit(solution)/shard_map/ppermute | solution.py:298
  48.9 2.2 %copy-start.3 = (bf16[8,2048,128]{2,1,0:T(8,128)(2,1)S(1)}, bf16[8,2048,128]{2,1,0:T(8,128)(2,1)}, u32[]{:S(2)}) copy-start(bf16[8,2048,128]{2,1,0:T(8,128)(2,1)} %down_ref.7) | copy-start | bytes 12582916
  51.1 27.9 %copy-start.4 = (bf16[8,2048,128]{2,1,0:T(8,128)(2,1)S(1)}, bf16[8,2048,128]{2,1,0:T(8,128)(2,1)}, u32[]{:S(2)}) copy-start(bf16[8,2048,128]{2,1,0:T(8,128)(2,1)} %down_ref.7) | copy-start | bytes 12582916
  53.2 27.8 %collective-permute-start.13 = (f32[240,128]{1,0:T(8,128)S(1)}, f32[240,128]{1,0:T(8,128)S(1)}, u32[]{:S(2)}, u32[]{:S(2)}) collective-permute-start(f32[240,128]{1,0:T(8,128)S(1)} %shrink.5), channel_id=1, source_target_pairs={{0,1},{1,0},{2,3},{3,2},{4,5},{5,4},{6,7},{7,6},{8,9},{9,8},{10,11... | collective-permute-start | bytes 368648 | tf_op jit(solution)/shard_map/ppermute | solution.py:325
  81.0 6.5 %collective-permute-start.10 = (f32[240,128]{1,0:T(8,128)S(1)}, f32[240,128]{1,0:T(8,128)S(1)}, u32[]{:S(2)}, u32[]{:S(2)}) collective-permute-start(f32[240,128]{1,0:T(8,128)S(1)} %shrink.4), channel_id=1, source_target_pairs={{0,1},{1,0},{2,3},{3,2},{4,5},{5,4},{6,7},{7,6},{8,9},{9,8},{10,11... | collective-permute-start | bytes 368648 | tf_op jit(solution)/shard_map/ppermute | solution.py:325
  81.1 7.1 %collective-permute-start.14 = (f32[120,128]{1,0:T(8,128)S(1)}, f32[120,128]{1,0:T(8,128)S(1)}, u32[]{:S(2)}, u32[]{:S(2)}) collective-permute-start(f32[120,128]{1,0:T(8,128)S(1)} %slice.59), channel_id=1, source_target_pairs={{0,2},{1,3},{2,0},{3,1},{4,6},{5,7},{6,4},{7,5},{8,10},{9,11},{10,... | collective-permute-start | bytes 184328 | tf_op jit(solution)/shard_map/ppermute | solution.py:327
  84.0 22.5 %collective-permute-start.1 = (f32[384,256]{1,0:T(8,128)S(1)}, f32[384,256]{1,0:T(8,128)S(1)}, u32[]{:S(2)}, u32[]{:S(2)}) collective-permute-start(f32[384,256]{1,0:T(8,128)S(1)} %slice.53), channel_id=1, source_target_pairs={{0,2},{1,3},{2,0},{3,1},{4,6},{5,7},{6,4},{7,5},{8,10},{9,11},{10,... | collective-permute-start | bytes 1179656 | tf_op jit(solution)/shard_map/ppermute | solution.py:242
  85.9 22.5 %collective-permute-start.3 = (f32[384,256]{1,0:T(8,128)S(1)}, f32[384,256]{1,0:T(8,128)S(1)}, u32[]{:S(2)}, u32[]{:S(2)}) collective-permute-start(f32[384,256]{1,0:T(8,128)S(1)} %slice.55), channel_id=1, source_target_pairs={{0,2},{1,3},{2,0},{3,1},{4,6},{5,7},{6,4},{7,5},{8,10},{9,11},{10,... | collective-permute-start | bytes 1179656 | tf_op jit(solution)/shard_map/ppermute | solution.py:242
  87.5 17.5 %collective-permute-start.11 = (f32[120,128]{1,0:T(8,128)S(1)}, f32[120,128]{1,0:T(8,128)S(1)}, u32[]{:S(2)}, u32[]{:S(2)}) collective-permute-start(f32[120,128]{1,0:T(8,128)S(1)} %slice.57), channel_id=1, source_target_pairs={{0,2},{1,3},{2,0},{3,1},{4,6},{5,7},{6,4},{7,5},{8,10},{9,11},{10,... | collective-permute-start | bytes 184328 | tf_op jit(solution)/shard_map/ppermute | solution.py:327
  106.5 1.3 collective-permute-start.19
  107.9 21.3 %collective-permute-start.20 = (f32[120,128]{1,0:T(8,128)S(1)}, f32[120,128]{1,0:T(8,128)S(1)}, u32[]{:S(2)}, u32[]{:S(2)}) collective-permute-start(f32[120,128]{1,0:T(8,128)S(1)} %slice.63), channel_id=1, source_target_pairs={{0,2},{1,3},{2,0},{3,1},{4,6},{5,7},{6,4},{7,5},{8,10},{9,11},{10,... | collective-permute-start | bytes 184328 | tf_op jit(solution)/shard_map/ppermute | solution.py:327
  108.5 21.4 %collective-permute-start.17 = (f32[120,128]{1,0:T(8,128)S(1)}, f32[120,128]{1,0:T(8,128)S(1)}, u32[]{:S(2)}, u32[]{:S(2)}) collective-permute-start(f32[120,128]{1,0:T(8,128)S(1)} %get-tuple-element.29), channel_id=1, source_target_pairs={{0,8},{4,12},{8,0},{12,4},{1,9},{5,13},{9,1},{13,5},{2,10},{6,14},... | collective-permute-start | bytes 184328 | tf_op jit(solution)/shard_map/ppermute | solution.py:348
  117.5 14.3 %collective-permute-start.18 = (f32[120,128]{1,0:T(8,128)S(1)}, f32[120,128]{1,0:T(8,128)S(1)}, u32[]{:S(2)}, u32[]{:S(2)}) collective-permute-start(f32[120,128]{1,0:T(8,128)S(1)} %get-tuple-element.30), channel_id=1, source_target_pairs={{0,12},{4,0},{8,4},{12,8},{1,13},{5,1},{9,5},{13,9},{2,14},{6,2},{... | collective-permute-start | bytes 184328 | tf_op jit(solution)/shard_map/ppermute | solution.py:348
  129.2 6.1 %collective-permute-start.21 = (f32[120,128]{1,0:T(8,128)S(1)}, f32[120,128]{1,0:T(8,128)S(1)}, u32[]{:S(2)}, u32[]{:S(2)}) collective-permute-start(f32[120,128]{1,0:T(8,128)S(1)} %slice_add_fusion.2.refs_3_), channel_id=1, source_target_pairs={{0,4},{4,8},{8,12},{12,0},{1,5},{5,9},{9,13},{13,1},{2,6},{6,10},{... | collective-permute-start | bytes 184328 | tf_op jit(solution)/shard_map/ppermute | solution.py:348

commit v7 on v6

--- a/solution.py
+++ b/solution.py
@@ -159,17 +159,18 @@
     )(scalars, index, base, up, *shrinks, *after)
 
 
-def gate_kernel(*refs):
-    pass
+def gate_kernel(waiting, *refs):
+    refs[waiting][...] = jnp.zeros_like(refs[waiting])
 
 
 def gate(blocks, after):
     return pl.pallas_call(
-        gate_kernel,
-        out_shape=[jax.ShapeDtypeStruct(b.shape, b.dtype) for b in blocks],
+        functools.partial(gate_kernel, len(blocks) + len(after)),
+        out_shape=[jax.ShapeDtypeStruct((8, 128), jnp.int32)]
+        + [jax.ShapeDtypeStruct(b.shape, b.dtype) for b in blocks],
         in_specs=[HBM] * len(blocks) + [ANY] * len(after),
-        out_specs=[HBM] * len(blocks),
-        input_output_aliases={n: n for n in range(len(blocks))},
+        out_specs=[VMEM] + [HBM] * len(blocks),
+        input_output_aliases={n: n + 1 for n in range(len(blocks))},
         compiler_params=WIDE,
         cost_estimate=COST,
         name="gate",
@@ -299,7 +300,8 @@
 
     packed, own_block, *blocks = pack([0] + order)
     arrived = {0: own_block}
-    for r, block in zip(order, gate(blocks, found)):
+    mark, *blocks = gate(blocks, found)
+    for r, block in zip(order, blocks):
         arrived[r] = send(block, r)
 
     heavy = heavy[0, 0]
@@ -327,20 +329,20 @@
         total = value[:height] + lax.ppermute(value[height:], "tensor", [(i, i ^ bit) for i in range(pieces)])
         return total
 
-    early = order[:-1] + [0]
-    totals = []
-    after = [packed]
-    for r in early:
-        (value,) = shrink(arrived[r], after, [])
-        totals.append(combine(value))
     slabs = 2
     base = jnp.concatenate(
         [
-            reduce_base(tokens, key_value_weight, piece, pieces, columns, slab, slabs, [packed])
+            reduce_base(tokens, key_value_weight, piece, pieces, columns, slab, slabs, [mark])
             for slab in range(slabs)
         ],
         axis=0,
     )
+    early = order[:-1] + [0]
+    totals = []
+    done = [base[:8], base[-8:]]
+    for r in early:
+        (value,) = shrink(arrived[r], done if r == order[0] else [packed], [])
+        totals.append(combine(value))
     value, *totals = shrink(arrived[order[-1]], [], totals)
     last = combine(value)
 

time: 137 us -> 129 us (0.942)
  starting transfers between devices: 41.8 us -> 26.7 us
  local copies, waits for them, and re-layouts: 10.4 us -> 14.8 us
    ppermute x3, starting transfers between devices: 21.3 us -> 5.8 us  [give_back(): lax.ppermute(total, 'batch', [(i, (i - r) % homes) for i in range(homes)])]
    ppermute x4, waiting for transfers between devices: 16.9 us -> 2.72 us  [combine(): lax.ppermute(value[height:], 'tensor', [(i, i ^ bit) for i in range(piece...]
    ppermute x3, waiting for transfers between devices: 24.5 us -> 37.8 us  [send(): lax.ppermute(block, 'batch', [(i, (i + r) % homes) for i in range(homes)])]
    unnamed x38 -> x34, local copies, waits for them, and re-layouts: 8.93 us -> 11.1 us
    slice x2, local copies, waits for them, and re-layouts: 0.05 us -> 1.58 us  [reduce_base(): kept, sent = (kept[:, :half], kept[:, half:])]
  transfers between devices with their start and end apart: 22 -> 22, of which waited for: 6 -> 10; matrix products, arithmetic and copies ran while one was open for 5% -> 8% of each run, Pallas kernels for 18% -> 18%
where the time goes in v7:
time: 129 us; the launch traced here: 128 us
  waiting for transfers between devices  48.4 us (38%)
  Pallas kernels  27.2 us (21%)
  starting transfers between devices  26.7 us (21%)
  local copies, waits for them, and re-layouts  14.8 us (11%)
  other arithmetic  7 us (5%)
  between operations  3.82 us (3%)
    ppermute x3, waiting for transfers between devices, send(): lax.ppermute(block, 'batch', [(i, (i + r) % homes) for i in range(homes)])  37.8 us
    unnamed x34, local copies, waits for them, and re-layouts  11.1 us
    pallas_call x4, Pallas kernels, base_part(): pl.pallas_call(functools.partial(base_kernel, len(after)), out_shape=jax....  8.96 us
    pallas_call x4, Pallas kernels, shrink(): pl.pallas_call(functools.partial(shrink_kernel, held, light, rank, value_...  6.94 us
    pallas_call x1, Pallas kernels, pack(): pl.pallas_call(functools.partial(pack_kernel, span, shifts), out_shape=[j...  6.48 us
    ppermute x3, starting transfers between devices, gather_up(): lax.ppermute(own, 'batch', [(i, (i - r) % homes) for i in range(homes)])  6.06 us
    ppermute x3, starting transfers between devices, give_back(): lax.ppermute(total, 'batch', [(i, (i - r) % homes) for i in range(homes)])  5.8 us
    ppermute x3, starting transfers between devices, send(): lax.ppermute(block, 'batch', [(i, (i + r) % homes) for i in range(homes)])  5.59 us
  transfers between devices with their start and end apart: 22, of which 10 were waited for; matrix products, arithmetic and copies ran while one was open for 8% of the time, Pallas kernels for 18%

profile of v7, /device:TPU:0, one launch (start us, length us, event | category | flops | bytes accessed | tf_op | source)
XLA Modules:
  0.0 127.9 jit_solution(16056442898301433117)
XLA Ops:
  0.0 0.9 copy-done
  1.6 5.0 %collective-permute-start = (bf16[8,32,256]{2,1,0:T(8,128)(2,1)}, bf16[8,32,256]{2,1,0:T(8,128)(2,1)S(1)}, u32[]{:S(2)}, u32[]{:S(2)}) collective-permute-start(bf16[8,32,256]{2,1,0:T(8,128)(2,1)} %constant_dynamic-slice_fusion), channel_id=1, source_target_pairs={{0,12},{4,0},{8,4},{12,8},{1,13},{5,1},{9,5},{13,9},{2,14},{6,2},{... | collective-permute-start | bytes 393224 | tf_op jit(solution)/shard_map/ppermute | solution.py:186
  6.7 1.0 collective-permute-start.2
  7.7 1.7 %route.1 = (s32[1,768]{1,0:T(1,128)}, s32[8,128]{1,0:T(8,128)}) custom-call(s32[1]{0:T(128)} %bitcast.place_ref, s32[32]{0:T(128)} %entry_hbm.1, s32[768]{0:T(1024)} %request_hbm.1), custom_call_target="tpu_custom_call" | custom-call | flops 1 | bytes 1 | tf_op jit(solution)/shard_map/route/pallas_call | solution.py:266
  9.4 6.5 %pack.1 = (s32[8,128]{1,0:T(8,128)}, bf16[216,2048]{1,0:T(8,128)(2,1)}, bf16[216,2048]{1,0:T(8,128)(2,1)}, bf16[216,2048]{1,0:T(8,128)(2,1)}, bf16[216,2048]{1,0:T(8,128)(2,1)}) custom-call(s32[1,768]{1,0:T(1,128)} %get-tuple-element.21.index_ref, bf16[768,2048]{1,0:T(8,128)(2,1)} %tokens_ref.9), custom_call_target="tpu_custom_call" | custom-call | flops 1 | bytes 1 | tf_op jit(solution)/shard_map/pack/pallas_call | solution.py:284
  15.9 2.2 %collective-permute-done.1.refs_4_ = bf16[8,32,256]{2,1,0:T(8,128)(2,1)} collective-permute-done((bf16[8,32,256]{2,1,0:T(8,128)(2,1)}, bf16[8,32,256]{2,1,0:T(8,128)(2,1)}, u32[]{:S(2)}, u32[]{:S(2)}) %collective-permute-start.1) | collective-permute-done | bytes 131104 | tf_op jit(solution)/shard_map/ppermute | solution.py:186
  18.8 2.2 %copy-done.5 = bf16[2048,1024]{1,0:T(8,128)(2,1)S(1)} copy-done((bf16[2048,1024]{1,0:T(8,128)(2,1)S(1)}, bf16[2048,1024]{1,0:T(8,128)(2,1)}, u32[]{:S(2)}) %copy-start.5) | copy-done | bytes 4194328
  21.7 2.1 %base.4.refs_0_ = f32[384,512]{1,0:T(8,128)S(1)} custom-call(s32[2]{0:T(128)S(1)} %broadcast_xor_fusion.block_ref, bf16[768,2048]{1,0:T(8,128)(2,1)S(1)} %copy-done.1, bf16[2048,1024]{1,0:T(8,128)(2,1)S(1)} %copy-done.5, s32[8,128]{1,0:T(8,128)S(1)} %copy-done.10), custom_call_target="tpu_custom_call" | custom-call | flops 1 | bytes 1 | tf_op jit(solution)/shard_map/base/pallas_call | solution.py:213
  23.8 0.9 collective-permute-start.12
  24.7 2.8 %base.6.refs_0_ = f32[384,512]{1,0:T(8,128)} custom-call(s32[2]{0:T(128)S(1)} %broadcast_xor_fusion.block_ref, bf16[768,2048]{1,0:T(8,128)(2,1)S(1)} %copy-done.1, bf16[2048,1024]{1,0:T(8,128)(2,1)S(1)} %copy-done.5, s32[8,128]{1,0:T(8,128)S(1)} %copy-done.10), custom_call_target="tpu_custom_call" | custom-call | flops 1 | bytes 1 | tf_op jit(solution)/shard_map/base/pallas_call | solution.py:213
  27.7 2.1 %base.5 = f32[384,512]{1,0:T(8,128)S(1)} custom-call(s32[2]{0:T(128)S(1)} %multiply_xor_fusion.block_ref, bf16[768,2048]{1,0:T(8,128)(2,1)S(1)} %copy-done.1, bf16[2048,1024]{1,0:T(8,128)(2,1)S(1)} %copy-done.6, f32[384,512]{1,0:T(8,128)S(1)} %base.4.refs_0_), custom_call_target="tpu_custom_call" | custom-call | flops 1 | bytes 1 | tf_op jit(solution)/shard_map/base/pallas_call | solution.py:213
  30.0 0.9 copy-done.11
  30.9 0.8 slice.61
  31.7 1.5 %collective-permute-start.4 = (f32[384,256]{1,0:T(8,128)}, f32[384,256]{1,0:T(8,128)}, u32[]{:S(2)}, u32[]{:S(2)}) collective-permute-start(f32[384,256]{1,0:T(8,128)} %slice.61), channel_id=1, source_target_pairs={{0,2},{1,3},{2,0},{3,1},{4,6},{5,7},{6,4},{7,5},{8,10},{9,11},{10,... | collective-permute-start | bytes 1179656 | tf_op jit(solution)/shard_map/ppermute | solution.py:243
  33.1 2.0 %collective-permute-start.9 = (bf16[216,2048]{1,0:T(8,128)(2,1)}, bf16[216,2048]{1,0:T(8,128)(2,1)}, u32[]{:S(2)}, u32[]{:S(2)}) collective-permute-start(bf16[216,2048]{1,0:T(8,128)(2,1)} %get-tuple-element.27), channel_id=1, source_target_pairs={{0,8},{4,12},{8,0},{12,4},{1,9},{5,13},{9,1},{13,5},{2,10},{6,14},... | collective-permute-start | bytes 2654216 | tf_op jit(solution)/shard_map/ppermute | solution.py:299
  35.2 1.3 slice.45
  39.3 2.2 %copy-done.2 = bf16[8,2048,128]{2,1,0:T(8,128)(2,1)S(1)} copy-done((bf16[8,2048,128]{2,1,0:T(8,128)(2,1)S(1)}, bf16[8,2048,128]{2,1,0:T(8,128)(2,1)}, u32[]{:S(2)}) %copy-start.2) | copy-done | bytes 4194328
  41.5 1.2 copy-done.8
  42.7 1.4 %shrink.6 = f32[240,128]{1,0:T(8,128)S(1)} custom-call(s32[3]{0:T(128)S(1)} %pad_add_fusion.scalar_ref, bf16[216,2048]{1,0:T(8,128)(2,1)S(1)} %copy-done.8, bf16[8,2048,128]{2,1,0:T(8,128)(2,1)S(1)} %copy-done.2, s32[8,128]{1,0:T(8,128)S(1)} %copy-done.9), custom_call_target="tpu_custom_call" | custom-call | flops 1 | bytes 1 | tf_op jit(solution)/shard_map/shrink/pallas_call | solution.py:313
  44.1 0.8 copy-done.7
  44.8 2.1 %base.7 = f32[384,512]{1,0:T(8,128)S(1)} custom-call(s32[2]{0:T(128)S(1)} %multiply_xor_fusion.block_ref, bf16[768,2048]{1,0:T(8,128)(2,1)S(1)} %copy-done.1, bf16[2048,1024]{1,0:T(8,128)(2,1)S(1)} %copy-done.7, f32[384,512]{1,0:T(8,128)} %base.6.refs_0_), custom_call_target="tpu_custom_call" | custom-call | flops 1 | bytes 1 | tf_op jit(solution)/shard_map/base/pallas_call | solution.py:213
  46.9 1.3 add.52
  48.2 0.8 slice.63
  50.4 0.9 add.58
  51.4 1.6 %collective-permute-start.16 = (f32[120,128]{1,0:T(8,128)S(1)}, f32[120,128]{1,0:T(8,128)S(1)}, u32[]{:S(2)}, u32[]{:S(2)}) collective-permute-start(f32[120,128]{1,0:T(8,128)S(1)} %slice.71), channel_id=1, source_target_pairs={{0,2},{1,3},{2,0},{3,1},{4,6},{5,7},{6,4},{7,5},{8,10},{9,11},{10,... | collective-permute-start | bytes 184328 | tf_op jit(solution)/shard_map/ppermute | solution.py:329
  52.9 2.2 %copy-done.3 = bf16[8,2048,128]{2,1,0:T(8,128)(2,1)S(1)} copy-done((bf16[8,2048,128]{2,1,0:T(8,128)(2,1)S(1)}, bf16[8,2048,128]{2,1,0:T(8,128)(2,1)}, u32[]{:S(2)}) %copy-start.3) | copy-done | bytes 4194328
  55.1 2.2 %shrink.5 = f32[240,128]{1,0:T(8,128)S(1)} custom-call(s32[3]{0:T(128)S(1)} %pad_add_fusion.scalar_ref, bf16[216,2048]{1,0:T(8,128)(2,1)} %collective-permute-done.12.block_ref, bf16[8,2048,128]{2,1,0:T(8,128)(2,1)S(1)} %copy-done.3, s32[8,128]{1,0:T(8,128)S(1)} %copy-done.9), custom_call_target="tpu_custom_call" | custom-call | flops 1 | bytes 1 | tf_op jit(solution)/shard_map/shrink/pallas_call | solution.py:313
  57.3 1.1 pad_maximum_fusion.2
  58.6 2.6 %collective-permute-start.8 = (bf16[216,2048]{1,0:T(8,128)(2,1)S(1)}, bf16[216,2048]{1,0:T(8,128)(2,1)S(1)}, u32[]{:S(2)}, u32[]{:S(2)}) collective-permute-start(bf16[216,2048]{1,0:T(8,128)(2,1)S(1)} %copy-done.15), channel_id=1, source_target_pairs={{0,12},{4,0},{8,4},{12,8},{1,13},{5,1},{9,5},{13,9},{2,14},{6,2},{... | collective-permute-start | bytes 2654216 | tf_op jit(solution)/shard_map/ppermute | solution.py:299
  61.3 1.6 %collective-permute-start.7 = (bf16[32,32,256]{2,1,0:T(8,128)(2,1)S(1)}, bf16[32,32,256]{2,1,0:T(8,128)(2,1)S(1)}, u32[]{:S(2)}, u32[]{:S(2)}) collective-permute-start(bf16[32,32,256]{2,1,0:T(8,128)(2,1)S(1)} %pad_maximum_fusion.2), channel_id=1, source_target_pairs={{0,16},{16,0},{1,17},{17,1},{2,18},{18,2},{3,19},{19,3},{4,20},{20... | collective-permute-start | bytes 1572872 | tf_op jit(solution)/shard_map/ppermute | solution.py:190
  62.9 1.1 slice_add_fusion.1
  64.6 1.1 slice_add_fusion
  65.7 20.2 %collective-permute-done.9.block_ref = bf16[216,2048]{1,0:T(8,128)(2,1)} collective-permute-done((bf16[216,2048]{1,0:T(8,128)(2,1)}, bf16[216,2048]{1,0:T(8,128)(2,1)}, u32[]{:S(2)}, u32[]{:S(2)}) %collective-permute-start.9) | collective-permute-done | bytes 884768 | tf_op jit(solution)/shard_map/ppermute | solution.py:299
  85.9 2.0 %shrink.4 = f32[240,128]{1,0:T(8,128)S(1)} custom-call(s32[3]{0:T(128)S(1)} %pad_add_fusion.scalar_ref, bf16[216,2048]{1,0:T(8,128)(2,1)} %collective-permute-done.9.block_ref, bf16[8,2048,128]{2,1,0:T(8,128)(2,1)S(1)} %copy-done.4, f32[8,256]{1,0:T(8,128)S(1)} %slice.64.refs_0_, f32[8,256]{1,0:T(8,128)S(1)} %slice.65.refs_1_), custom_call_target="tpu_custom_call" | custom-call | flops 1 | bytes 1 | tf_op jit(solution)/shard_map/shrink/pallas_call | solution.py:313
  88.0 1.3 %collective-permute-done.10 = f32[240,128]{1,0:T(8,128)S(1)} collective-permute-done((f32[240,128]{1,0:T(8,128)S(1)}, f32[240,128]{1,0:T(8,128)S(1)}, u32[]{:S(2)}, u32[]{:S(2)}) %collective-permute-start.10) | collective-permute-done | bytes 122912 | tf_op jit(solution)/shard_map/ppermute | solution.py:327
  89.3 1.6 %collective-permute-start.11 = (f32[120,128]{1,0:T(8,128)S(1)}, f32[120,128]{1,0:T(8,128)S(1)}, u32[]{:S(2)}, u32[]{:S(2)}) collective-permute-start(f32[120,128]{1,0:T(8,128)S(1)} %slice.67), channel_id=1, source_target_pairs={{0,2},{1,3},{2,0},{3,1},{4,6},{5,7},{6,4},{7,5},{8,10},{9,11},{10,... | collective-permute-start | bytes 184328 | tf_op jit(solution)/shard_map/ppermute | solution.py:329
  90.9 2.7 %collective-permute-done.11 = f32[120,128]{1,0:T(8,128)S(1)} collective-permute-done((f32[120,128]{1,0:T(8,128)S(1)}, f32[120,128]{1,0:T(8,128)S(1)}, u32[]{:S(2)}, u32[]{:S(2)}) %collective-permute-start.11) | collective-permute-done | bytes 61472 | tf_op jit(solution)/shard_map/ppermute | solution.py:329
  93.6 17.5 %collective-permute-done.8.block_ref = bf16[216,2048]{1,0:T(8,128)(2,1)S(1)} collective-permute-done((bf16[216,2048]{1,0:T(8,128)(2,1)S(1)}, bf16[216,2048]{1,0:T(8,128)(2,1)S(1)}, u32[]{:S(2)}, u32[]{:S(2)}) %collective-permute-start.8) | collective-permute-done | bytes 884768 | tf_op jit(solution)/shard_map/ppermute | solution.py:299
  111.1 1.4 %shrink.7 = (f32[240,128]{1,0:T(8,128)S(1)}, f32[120,128]{1,0:T(8,128)S(1)}, f32[120,128]{1,0:T(8,128)S(1)}, f32[120,128]{1,0:T(8,128)S(1)}) custom-call(s32[3]{0:T(128)S(1)} %pad_add_fusion.scalar_ref, bf16[216,2048]{1,0:T(8,128)(2,1)S(1)} %collective-permute-done.8.block_ref, bf16[8,2048,128]{2,1,0:T(8,128)(2,1)S(1)} %copy-done.4, ...), custom_call_target="tpu_custom_call" | custom-call | flops 1 | bytes 1 | tf_op jit(solution)/shard_map/shrink/pallas_call | solution.py:313
  112.5 1.1 broadcast_select_fusion.1
  113.9 1.6 %collective-permute-start.20 = (f32[120,128]{1,0:T(8,128)S(1)}, f32[120,128]{1,0:T(8,128)S(1)}, u32[]{:S(2)}, u32[]{:S(2)}) collective-permute-start(f32[120,128]{1,0:T(8,128)S(1)} %slice.73), channel_id=1, source_target_pairs={{0,2},{1,3},{2,0},{3,1},{4,6},{5,7},{6,4},{7,5},{8,10},{9,11},{10,... | collective-permute-start | bytes 184328 | tf_op jit(solution)/shard_map/ppermute | solution.py:329
  115.5 3.7 %collective-permute-start.17 = (f32[120,128]{1,0:T(8,128)S(1)}, f32[120,128]{1,0:T(8,128)S(1)}, u32[]{:S(2)}, u32[]{:S(2)}) collective-permute-start(f32[120,128]{1,0:T(8,128)S(1)} %get-tuple-element.31), channel_id=1, source_target_pairs={{0,8},{4,12},{8,0},{12,4},{1,9},{5,13},{9,1},{13,5},{2,10},{6,14},... | collective-permute-start | bytes 184328 | tf_op jit(solution)/shard_map/ppermute | solution.py:350
  119.3 1.2 collective-permute-start.18
  120.5 0.9 collective-permute-start.21
  121.4 1.8 %collective-permute-done.17.refs_0_ = f32[120,128]{1,0:T(8,128)S(1)} collective-permute-done((f32[120,128]{1,0:T(8,128)S(1)}, f32[120,128]{1,0:T(8,128)S(1)}, u32[]{:S(2)}, u32[]{:S(2)}) %collective-permute-start.17) | collective-permute-done | bytes 61472 | tf_op jit(solution)/shard_map/ppermute | solution.py:350
  123.5 1.1 finish.2.base_ref
  124.7 1.9 %collective-permute-done.21.refs_0_ = f32[120,128]{1,0:T(8,128)S(1)} collective-permute-done((f32[120,128]{1,0:T(8,128)S(1)}, f32[120,128]{1,0:T(8,128)S(1)}, u32[]{:S(2)}, u32[]{:S(2)}) %collective-permute-start.21) | collective-permute-done | bytes 61472 | tf_op jit(solution)/shard_map/ppermute | solution.py:350
  126.5 1.4 %finish.3 = bf16[768,256]{1,0:T(8,128)(2,1)} custom-call(s32[1]{0:T(128)} %bitcast.2.place_ref, s32[768,1]{1,0:T(8,128)S(1)} %copy.13.index_ref, f32[768,256]{1,0:T(8,128)S(1)} %finish.2.base_ref, bf16[32,64,256]{2,1,0:T(8,128)(2,1)S(1)} %pad_maximum_fusion.up_ref, f32[120,128]{1,0:T(8,128)S(1)} %collective-permute-done.21.refs_0_), custom_call_target="tpu_custom_call" | custom-call | flops 1 | bytes 1 | tf_op jit(solution)/shard_map/finish/pallas_call | solution.py:150
  (73 shorter events, 4.9 us)
Async XLA Ops:
  0.0 1.0 copy-start
  1.6 17.2 %copy-start.1 = (bf16[768,2048]{1,0:T(8,128)(2,1)S(1)}, bf16[768,2048]{1,0:T(8,128)(2,1)}, u32[]{:S(2)}) copy-start(bf16[768,2048]{1,0:T(8,128)(2,1)} %tokens_ref.9) | copy-start | bytes 9437188
  1.6 14.3 %collective-permute-start = (bf16[8,32,256]{2,1,0:T(8,128)(2,1)}, bf16[8,32,256]{2,1,0:T(8,128)(2,1)S(1)}, u32[]{:S(2)}, u32[]{:S(2)}) collective-permute-start(bf16[8,32,256]{2,1,0:T(8,128)(2,1)} %constant_dynamic-slice_fusion), channel_id=1, source_target_pairs={{0,12},{4,0},{8,4},{12,8},{1,13},{5,1},{9,5},{13,9},{2,14},{6,2},{... | collective-permute-start | bytes 393224 | tf_op jit(solution)/shard_map/ppermute | solution.py:186
  6.7 11.5 %collective-permute-start.1 = (bf16[8,32,256]{2,1,0:T(8,128)(2,1)}, bf16[8,32,256]{2,1,0:T(8,128)(2,1)}, u32[]{:S(2)}, u32[]{:S(2)}) collective-permute-start(bf16[8,32,256]{2,1,0:T(8,128)(2,1)} %constant_dynamic-slice_fusion), channel_id=1, source_target_pairs={{0,8},{4,12},{8,0},{12,4},{1,9},{5,13},{9,1},{13,5},{2,10},{6,14},... | collective-permute-start | bytes 393224 | tf_op jit(solution)/shard_map/ppermute | solution.py:186
  6.7 11.5 %collective-permute-start.2 = (bf16[8,32,256]{2,1,0:T(8,128)(2,1)}, bf16[8,32,256]{2,1,0:T(8,128)(2,1)}, u32[]{:S(2)}, u32[]{:S(2)}) collective-permute-start(bf16[8,32,256]{2,1,0:T(8,128)(2,1)} %constant_dynamic-slice_fusion), channel_id=1, source_target_pairs={{0,4},{4,8},{8,12},{12,0},{1,5},{5,9},{9,13},{13,1},{2,6},{6,10},{... | collective-permute-start | bytes 393224 | tf_op jit(solution)/shard_map/ppermute | solution.py:186
  15.9 2.3 %copy-start.13 = (bf16[8,32,256]{2,1,0:T(8,128)(2,1)}, bf16[8,32,256]{2,1,0:T(8,128)(2,1)S(1)}, u32[]{:S(2)}) copy-start(bf16[8,32,256]{2,1,0:T(8,128)(2,1)S(1)} %collective-permute-done.refs_3_) | copy-start | bytes 393220
  18.8 2.2 %copy-start.5 = (bf16[2048,1024]{1,0:T(8,128)(2,1)S(1)}, bf16[2048,1024]{1,0:T(8,128)(2,1)}, u32[]{:S(2)}) copy-start(bf16[2048,1024]{1,0:T(8,128)(2,1)} %weight_ref.7) | copy-start | bytes 12582916
  21.0 0.7 copy-start.10
  23.7 6.1 %collective-permute-start.3 = (f32[384,512]{1,0:T(8,128)S(1)}, f32[384,512]{1,0:T(8,128)S(1)}, u32[]{:S(2)}, u32[]{:S(2)}) collective-permute-start(f32[384,512]{1,0:T(8,128)S(1)} %base.4.refs_0_), channel_id=1, source_target_pairs={{0,1},{1,0},{2,3},{3,2},{4,5},{5,4},{6,7},{7,6},{8,9},{9,8},{10,11... | collective-permute-start | bytes 2359304 | tf_op jit(solution)/shard_map/ppermute | solution.py:243
  23.8 3.9 %copy-start.6 = (bf16[2048,1024]{1,0:T(8,128)(2,1)S(1)}, bf16[2048,1024]{1,0:T(8,128)(2,1)}, u32[]{:S(2)}) copy-start(bf16[2048,1024]{1,0:T(8,128)(2,1)} %weight_ref.7) | copy-start | bytes 12582916
  23.8 29.1 %collective-permute-start.12 = (bf16[216,2048]{1,0:T(8,128)(2,1)}, bf16[216,2048]{1,0:T(8,128)(2,1)}, u32[]{:S(2)}, u32[]{:S(2)}) collective-permute-start(bf16[216,2048]{1,0:T(8,128)(2,1)} %get-tuple-element.28), channel_id=1, source_target_pairs={{0,4},{4,8},{8,12},{12,0},{1,5},{5,9},{9,13},{13,1},{2,6},{6,10},{... | collective-permute-start | bytes 2654216 | tf_op jit(solution)/shard_map/ppermute | solution.py:299
  27.5 19.4 %collective-permute-start.5 = (f32[384,512]{1,0:T(8,128)}, f32[384,512]{1,0:T(8,128)}, u32[]{:S(2)}, u32[]{:S(2)}) collective-permute-start(f32[384,512]{1,0:T(8,128)} %base.6.refs_0_), channel_id=1, source_target_pairs={{0,1},{1,0},{2,3},{3,2},{4,5},{5,4},{6,7},{7,6},{8,9},{9,8},{10,11... | collective-permute-start | bytes 2359304 | tf_op jit(solution)/shard_map/ppermute | solution.py:243
  29.8 9.5 %copy-start.9 = (s32[8,128]{1,0:T(8,128)S(1)}, s32[8,128]{1,0:T(8,128)}, u32[]{:S(2)}) copy-start(s32[8,128]{1,0:T(8,128)} %get-tuple-element.29.refs_0_) | copy-start | bytes 12292
  30.0 0.9 copy-start.11
  31.7 29.7 %collective-permute-start.4 = (f32[384,256]{1,0:T(8,128)}, f32[384,256]{1,0:T(8,128)}, u32[]{:S(2)}, u32[]{:S(2)}) collective-permute-start(f32[384,256]{1,0:T(8,128)} %slice.61), channel_id=1, source_target_pairs={{0,2},{1,3},{2,0},{3,1},{4,6},{5,7},{6,4},{7,5},{8,10},{9,11},{10,... | collective-permute-start | bytes 1179656 | tf_op jit(solution)/shard_map/ppermute | solution.py:243
  33.1 52.8 %collective-permute-start.9 = (bf16[216,2048]{1,0:T(8,128)(2,1)}, bf16[216,2048]{1,0:T(8,128)(2,1)}, u32[]{:S(2)}, u32[]{:S(2)}) collective-permute-start(bf16[216,2048]{1,0:T(8,128)(2,1)} %get-tuple-element.27), channel_id=1, source_target_pairs={{0,8},{4,12},{8,0},{12,4},{1,9},{5,13},{9,1},{13,5},{2,10},{6,14},... | collective-permute-start | bytes 2654216 | tf_op jit(solution)/shard_map/ppermute | solution.py:299
  39.3 2.2 %copy-start.2 = (bf16[8,2048,128]{2,1,0:T(8,128)(2,1)S(1)}, bf16[8,2048,128]{2,1,0:T(8,128)(2,1)}, u32[]{:S(2)}) copy-start(bf16[8,2048,128]{2,1,0:T(8,128)(2,1)} %down_ref.7) | copy-start | bytes 12582916
  41.5 1.2 copy-start.8
  42.7 2.2 %copy-start.7 = (bf16[2048,1024]{1,0:T(8,128)(2,1)S(1)}, bf16[2048,1024]{1,0:T(8,128)(2,1)}, u32[]{:S(2)}) copy-start(bf16[2048,1024]{1,0:T(8,128)(2,1)} %weight_ref.7) | copy-start | bytes 12582916
  44.0 6.4 %collective-permute-start.15 = (f32[240,128]{1,0:T(8,128)S(1)}, f32[240,128]{1,0:T(8,128)}, u32[]{:S(2)}, u32[]{:S(2)}) collective-permute-start(f32[240,128]{1,0:T(8,128)S(1)} %shrink.6), channel_id=1, source_target_pairs={{0,1},{1,0},{2,3},{3,2},{4,5},{5,4},{6,7},{7,6},{8,9},{9,8},{10,11... | collective-permute-start | bytes 368648 | tf_op jit(solution)/shard_map/ppermute | solution.py:327
  46.9 3.3 %copy-start.16 = (s32[1,768]{1,0:T(1,128)S(1)}, s32[1,768]{1,0:T(1,128)}, u32[]{:S(2)}) copy-start(s32[1,768]{1,0:T(1,128)} %get-tuple-element.21.index_ref) | copy-start | bytes 9220
  49.0 8.3 %copy-start.14 = (bf16[8,32,256]{2,1,0:T(8,128)(2,1)S(1)}, bf16[8,32,256]{2,1,0:T(8,128)(2,1)}, u32[]{:S(2)}) copy-start(bf16[8,32,256]{2,1,0:T(8,128)(2,1)} %copy-done.13) | copy-start | bytes 393220
  49.0 15.0 %collective-permute-start.6 = (f32[384,256]{1,0:T(8,128)}, f32[384,256]{1,0:T(8,128)}, u32[]{:S(2)}, u32[]{:S(2)}) collective-permute-start(f32[384,256]{1,0:T(8,128)} %slice.63), channel_id=1, source_target_pairs={{0,2},{1,3},{2,0},{3,1},{4,6},{5,7},{6,4},{7,5},{8,10},{9,11},{10,... | collective-permute-start | bytes 1179656 | tf_op jit(solution)/shard_map/ppermute | solution.py:243
  51.4 36.6 %collective-permute-start.16 = (f32[120,128]{1,0:T(8,128)S(1)}, f32[120,128]{1,0:T(8,128)S(1)}, u32[]{:S(2)}, u32[]{:S(2)}) collective-permute-start(f32[120,128]{1,0:T(8,128)S(1)} %slice.71), channel_id=1, source_target_pairs={{0,2},{1,3},{2,0},{3,1},{4,6},{5,7},{6,4},{7,5},{8,10},{9,11},{10,... | collective-permute-start | bytes 184328 | tf_op jit(solution)/shard_map/ppermute | solution.py:329
  52.9 2.2 %copy-start.3 = (bf16[8,2048,128]{2,1,0:T(8,128)(2,1)S(1)}, bf16[8,2048,128]{2,1,0:T(8,128)(2,1)}, u32[]{:S(2)}) copy-start(bf16[8,2048,128]{2,1,0:T(8,128)(2,1)} %down_ref.7) | copy-start | bytes 12582916
  55.1 3.5 %copy-start.15 = (bf16[216,2048]{1,0:T(8,128)(2,1)S(1)}, bf16[216,2048]{1,0:T(8,128)(2,1)}, u32[]{:S(2)}) copy-start(bf16[216,2048]{1,0:T(8,128)(2,1)} %get-tuple-element.26) | copy-start | bytes 2654212
  55.1 7.8 %copy-start.12 = (f32[384,512]{1,0:T(8,128)S(1)}, f32[384,512]{1,0:T(8,128)}, u32[]{:S(2)}) copy-start(f32[384,512]{1,0:T(8,128)} %copy-done.11) | copy-start | bytes 2359300
  55.1 30.8 %copy-start.4 = (bf16[8,2048,128]{2,1,0:T(8,128)(2,1)S(1)}, bf16[8,2048,128]{2,1,0:T(8,128)(2,1)}, u32[]{:S(2)}) copy-start(bf16[8,2048,128]{2,1,0:T(8,128)(2,1)} %down_ref.7) | copy-start | bytes 12582916
  57.3 1.4 %collective-permute-start.13 = (f32[240,128]{1,0:T(8,128)S(1)}, f32[240,128]{1,0:T(8,128)S(1)}, u32[]{:S(2)}, u32[]{:S(2)}) collective-permute-start(f32[240,128]{1,0:T(8,128)S(1)} %shrink.5), channel_id=1, source_target_pairs={{0,1},{1,0},{2,3},{3,2},{4,5},{5,4},{6,7},{7,6},{8,9},{9,8},{10,11... | collective-permute-start | bytes 368648 | tf_op jit(solution)/shard_map/ppermute | solution.py:327
  58.6 52.5 %collective-permute-start.8 = (bf16[216,2048]{1,0:T(8,128)(2,1)S(1)}, bf16[216,2048]{1,0:T(8,128)(2,1)S(1)}, u32[]{:S(2)}, u32[]{:S(2)}) collective-permute-start(bf16[216,2048]{1,0:T(8,128)(2,1)S(1)} %copy-done.15), channel_id=1, source_target_pairs={{0,12},{4,0},{8,4},{12,8},{1,13},{5,1},{9,5},{13,9},{2,14},{6,2},{... | collective-permute-start | bytes 2654216 | tf_op jit(solution)/shard_map/ppermute | solution.py:299
  61.3 51.2 %collective-permute-start.7 = (bf16[32,32,256]{2,1,0:T(8,128)(2,1)S(1)}, bf16[32,32,256]{2,1,0:T(8,128)(2,1)S(1)}, u32[]{:S(2)}, u32[]{:S(2)}) collective-permute-start(bf16[32,32,256]{2,1,0:T(8,128)(2,1)S(1)} %pad_maximum_fusion.2), channel_id=1, source_target_pairs={{0,16},{16,0},{1,17},{17,1},{2,18},{18,2},{3,19},{19,3},{4,20},{20... | collective-permute-start | bytes 1572872 | tf_op jit(solution)/shard_map/ppermute | solution.py:190
  64.0 26.9 %collective-permute-start.14 = (f32[120,128]{1,0:T(8,128)S(1)}, f32[120,128]{1,0:T(8,128)S(1)}, u32[]{:S(2)}, u32[]{:S(2)}) collective-permute-start(f32[120,128]{1,0:T(8,128)S(1)} %slice.69), channel_id=1, source_target_pairs={{0,2},{1,3},{2,0},{3,1},{4,6},{5,7},{6,4},{7,5},{8,10},{9,11},{10,... | collective-permute-start | bytes 184328 | tf_op jit(solution)/shard_map/ppermute | solution.py:329
  87.9 1.4 %collective-permute-start.10 = (f32[240,128]{1,0:T(8,128)S(1)}, f32[240,128]{1,0:T(8,128)S(1)}, u32[]{:S(2)}, u32[]{:S(2)}) collective-permute-start(f32[240,128]{1,0:T(8,128)S(1)} %shrink.4), channel_id=1, source_target_pairs={{0,1},{1,0},{2,3},{3,2},{4,5},{5,4},{6,7},{7,6},{8,9},{9,8},{10,11... | collective-permute-start | bytes 368648 | tf_op jit(solution)/shard_map/ppermute | solution.py:327
  89.3 4.3 %collective-permute-start.11 = (f32[120,128]{1,0:T(8,128)S(1)}, f32[120,128]{1,0:T(8,128)S(1)}, u32[]{:S(2)}, u32[]{:S(2)}) collective-permute-start(f32[120,128]{1,0:T(8,128)S(1)} %slice.67), channel_id=1, source_target_pairs={{0,2},{1,3},{2,0},{3,1},{4,6},{5,7},{6,4},{7,5},{8,10},{9,11},{10,... | collective-permute-start | bytes 184328 | tf_op jit(solution)/shard_map/ppermute | solution.py:329
  112.5 1.3 %collective-permute-start.19 = (f32[240,128]{1,0:T(8,128)S(1)}, f32[240,128]{1,0:T(8,128)S(1)}, u32[]{:S(2)}, u32[]{:S(2)}) collective-permute-start(f32[240,128]{1,0:T(8,128)S(1)} %get-tuple-element.34), channel_id=1, source_target_pairs={{0,1},{1,0},{2,3},{3,2},{4,5},{5,4},{6,7},{7,6},{8,9},{9,8},{10,11... | collective-permute-start | bytes 368648 | tf_op jit(solution)/shard_map/ppermute | solution.py:327
  113.9 6.6 %collective-permute-start.20 = (f32[120,128]{1,0:T(8,128)S(1)}, f32[120,128]{1,0:T(8,128)S(1)}, u32[]{:S(2)}, u32[]{:S(2)}) collective-permute-start(f32[120,128]{1,0:T(8,128)S(1)} %slice.73), channel_id=1, source_target_pairs={{0,2},{1,3},{2,0},{3,1},{4,6},{5,7},{6,4},{7,5},{8,10},{9,11},{10,... | collective-permute-start | bytes 184328 | tf_op jit(solution)/shard_map/ppermute | solution.py:329
  115.5 7.6 %collective-permute-start.17 = (f32[120,128]{1,0:T(8,128)S(1)}, f32[120,128]{1,0:T(8,128)S(1)}, u32[]{:S(2)}, u32[]{:S(2)}) collective-permute-start(f32[120,128]{1,0:T(8,128)S(1)} %get-tuple-element.31), channel_id=1, source_target_pairs={{0,8},{4,12},{8,0},{12,4},{1,9},{5,13},{9,1},{13,5},{2,10},{6,14},... | collective-permute-start | bytes 184328 | tf_op jit(solution)/shard_map/ppermute | solution.py:350
  119.3 4.3 %collective-permute-start.18 = (f32[120,128]{1,0:T(8,128)S(1)}, f32[120,128]{1,0:T(8,128)S(1)}, u32[]{:S(2)}, u32[]{:S(2)}) collective-permute-start(f32[120,128]{1,0:T(8,128)S(1)} %get-tuple-element.32), channel_id=1, source_target_pairs={{0,12},{4,0},{8,4},{12,8},{1,13},{5,1},{9,5},{13,9},{2,14},{6,2},{... | collective-permute-start | bytes 184328 | tf_op jit(solution)/shard_map/ppermute | solution.py:350
  120.5 6.1 %collective-permute-start.21 = (f32[120,128]{1,0:T(8,128)S(1)}, f32[120,128]{1,0:T(8,128)S(1)}, u32[]{:S(2)}, u32[]{:S(2)}) collective-permute-start(f32[120,128]{1,0:T(8,128)S(1)} %slice_add_fusion.2.refs_3_), channel_id=1, source_target_pairs={{0,4},{4,8},{8,12},{12,0},{1,5},{5,9},{9,13},{13,1},{2,6},{6,10},{... | collective-permute-start | bytes 184328 | tf_op jit(solution)/shard_map/ppermute | solution.py:350

commit v8 on v7

--- a/solution.py
+++ b/solution.py
@@ -80,16 +80,19 @@
     return (held + 2) // 2
 
 
-def shrink_kernel(held, light, rank, value_side, waited, passed, scalar_ref, block_ref, down_ref, *refs):
-    passed_refs, out_ref, left_refs = refs[waited : waited + passed], refs[waited + passed], refs[waited + passed + 1 :]
+def shrink_kernel(held, light, rank, value_side, count, waited, passed, scalar_ref, *refs):
+    block_refs, down_ref, refs = refs[:count], refs[count], refs[count + 1 + waited :]
+    passed_refs, out_ref, left_refs = refs[:passed], refs[passed], refs[passed + 1 :]
     groups = entry_places(held)
+    height = groups * light
 
     def product(e):
         if e > held:
-            return jnp.zeros((light, 2 * rank), jnp.float32)
+            return jnp.zeros((count * light, 2 * rank), jnp.float32)
         factor = down_ref[e] if e < held else down_ref[scalar_ref[1]]
+        rows = [block_ref[e * light : (e + 1) * light, :] for block_ref in block_refs]
         value = jnp.dot(
-            block_ref[e * light : (e + 1) * light, :], factor, preferred_element_type=jnp.float32
+            jnp.concatenate(rows, axis=0) if count > 1 else rows[0], factor, preferred_element_type=jnp.float32
         )
         return value if e < held else jnp.where(scalar_ref[2] == 1, value, 0.0)
 
@@ -98,8 +101,11 @@
         first, second = product(g), product(g + groups)
         key = jnp.concatenate([first[:, :rank], second[:, :rank]], axis=1)
         value = jnp.concatenate([first[:, rank:], second[:, rank:]], axis=1)
-        out_ref[g * light : (g + 1) * light, :] = jnp.where(on_value_side, value, key)
-        out_ref[(groups + g) * light : (groups + g + 1) * light, :] = jnp.where(on_value_side, key, value)
+        mine, other = jnp.where(on_value_side, value, key), jnp.where(on_value_side, key, value)
+        for n in range(count):
+            here, start = slice(n * light, (n + 1) * light), n * height + g * light
+            out_ref[start : start + light, :] = mine[here]
+            out_ref[count * height + start : count * height + start + light, :] = other[here]
     for source, target in zip(passed_refs, left_refs):
         target[...] = source[...]
 
@@ -223,7 +229,7 @@
             + [ANY] * len(after),
             out_specs=pl.BlockSpec((rows, columns), lambda j, chosen: (0, j)),
         ),
-        compiler_params=PARAMS,
+        compiler_params=WIDE,
         cost_estimate=COST,
         name="base",
     )(blocks, tokens, weight, *after)
@@ -309,25 +315,26 @@
     scalars = jnp.stack([piece, lax.rem(heavy, held), heavy_here])
     height = entry_places(held) * light
 
-    def shrink(block, after, passed):
+    def shrink(blocks, after, passed):
         return pl.pallas_call(
-            functools.partial(shrink_kernel, held, light, rank, value_side, len(after), len(passed)),
-            out_shape=[jax.ShapeDtypeStruct((2 * height, 2 * rank), jnp.float32)]
+            functools.partial(
+                shrink_kernel, held, light, rank, value_side, len(blocks), len(after), len(passed)
+            ),
+            out_shape=[jax.ShapeDtypeStruct((2 * len(blocks) * height, 2 * rank), jnp.float32)]
             + [jax.ShapeDtypeStruct(p.shape, p.dtype) for p in passed],
-            in_specs=[SMEM, VMEM, VMEM] + [ANY] * len(after) + [VMEM] * len(passed),
+            in_specs=[SMEM] + [VMEM] * (len(blocks) + 1) + [ANY] * len(after) + [VMEM] * len(passed),
             out_specs=[VMEM] * (1 + len(passed)),
             compiler_params=PARAMS,
             cost_estimate=COST,
             name="shrink",
-        )(scalars, block, adapter_down, *after, *passed)
+        )(scalars, *blocks, adapter_down, *after, *passed)
 
     def combine(value):
-        bit = 1
+        bit, half = 1, value.shape[0] // 2
         while bit < pieces // 2:
             value = value + lax.ppermute(value, "tensor", [(i, i ^ bit) for i in range(pieces)])
             bit *= 2
-        total = value[:height] + lax.ppermute(value[height:], "tensor", [(i, i ^ bit) for i in range(pieces)])
-        return total
+        return value[:half] + lax.ppermute(value[half:], "tensor", [(i, i ^ bit) for i in range(pieces)])
 
     slabs = 2
     base = jnp.concatenate(
@@ -337,13 +344,13 @@
         ],
         axis=0,
     )
-    early = order[:-1] + [0]
+    late = order[-2:]
+    early = order[:-2] + [0]
     totals = []
-    done = [base[:8], base[-8:]]
     for r in early:
-        (value,) = shrink(arrived[r], done if r == order[0] else [packed], [])
+        (value,) = shrink([arrived[r]], [packed], [])
         totals.append(combine(value))
-    value, *totals = shrink(arrived[order[-1]], [], totals)
+    value, *totals = shrink([arrived[r] for r in late], [base[:8], base[-8:]], totals)
     last = combine(value)
 
     def give_back(total, r):
@@ -353,8 +360,8 @@
     places = lax.rem(heavy - place * held + adapters, adapters).reshape(1)
     column = index.reshape(rows, 1)
     running = finish(places, column, base, up, shrinks, [last], early, jnp.float32, homes, held, light)
-    shrinks = [give_back(last, order[-1])]
-    return finish(places, column, running, up, shrinks, [], order[-1:], jnp.bfloat16, homes, held, light)
+    shrinks = [give_back(last[n * height : (n + 1) * height], r) for n, r in enumerate(late)]
+    return finish(places, column, running, up, shrinks, [], late, jnp.bfloat16, homes, held, light)
 
 
 def solution(mesh):

time: 129 us -> 134 us (1.039)
  waiting for transfers between devices: 48.4 us -> 64.7 us
  local copies, waits for them, and re-layouts: 14.8 us -> 7.53 us
  starting transfers between devices: 26.7 us -> 19.9 us
  Pallas kernels: 27.2 us -> 33.4 us
  other arithmetic: 7 us -> 5.05 us
    ppermute x4, waiting for transfers between devices: 0.01 us -> 9.11 us  [reduce_base(): lax.ppermute(sent, 'tensor', [(i, i ^ bit) for i in range(pieces)])]
    pallas_call x4, Pallas kernels: 8.96 us -> 17.8 us  [base_part(): pl.pallas_call(functools.partial(base_kernel, len(after)), out_shape=jax....]
    ppermute x4 -> x3, waiting for transfers between devices: 2.72 us -> 11.5 us  [combine(): lax.ppermute(value[half:], 'tensor', [(i, i ^ bit) for i in range(pieces)])]
    unnamed x34 -> x38, local copies, waits for them, and re-layouts: 11.1 us -> 6.09 us
    ppermute x3, starting transfers between devices: 5.8 us -> 2.15 us  [give_back(): lax.ppermute(total, 'batch', [(i, (i - r) % homes) for i in range(homes)])]
    ppermute x3, starting transfers between devices: 5.59 us -> 2.64 us  [send(): lax.ppermute(block, 'batch', [(i, (i + r) % homes) for i in range(homes)])]
    pallas_call x4 -> x3, Pallas kernels: 6.94 us -> 4.23 us  [shrink(): pl.pallas_call(functools.partial(shrink_kernel, held, light, rank, value_...]
    ppermute x4 -> x3, starting transfers between devices: 5.26 us -> 3.72 us  [combine(): lax.ppermute(value[half:], 'tensor', [(i, i ^ bit) for i in range(pieces)])]
  transfers between devices with their start and end apart: 22 -> 20, of which waited for: 10 -> 8; matrix products, arithmetic and copies ran while one was open for 8% -> 5% of each run, Pallas kernels for 18% -> 23%
where the time goes in v8:
time: 134 us
  waiting for transfers between devices  64.7 us (48%)
  Pallas kernels  33.4 us (25%)
  starting transfers between devices  19.9 us (15%)
  local copies, waits for them, and re-layouts  7.53 us (6%)
  other arithmetic  5.05 us (4%)
  between operations  3.21 us (2%)
    ppermute x3, waiting for transfers between devices, send(): lax.ppermute(block, 'batch', [(i, (i + r) % homes) for i in range(homes)])  37.3 us
    pallas_call x4, Pallas kernels, base_part(): pl.pallas_call(functools.partial(base_kernel, len(after)), out_shape=jax....  17.8 us
    ppermute x3, waiting for transfers between devices, combine(): lax.ppermute(value[half:], 'tensor', [(i, i ^ bit) for i in range(pieces)])  11.5 us
    ppermute x4, waiting for transfers between devices, reduce_base(): lax.ppermute(sent, 'tensor', [(i, i ^ bit) for i in range(pieces)])  9.11 us
    pallas_call x1, Pallas kernels, pack(): pl.pallas_call(functools.partial(pack_kernel, span, shifts), out_shape=[j...  6.48 us
    ppermute x3, starting transfers between devices, gather_up(): lax.ppermute(own, 'batch', [(i, (i - r) % homes) for i in range(homes)])  6.11 us
    unnamed x38, local copies, waits for them, and re-layouts  6.09 us
    pallas_call x3, Pallas kernels, shrink(): pl.pallas_call(functools.partial(shrink_kernel, held, light, rank, value_...  4.23 us
  transfers between devices with their start and end apart: 20, of which 8 were waited for; matrix products, arithmetic and copies ran while one was open for 5% of the time, Pallas kernels for 23%

profile of v8, /device:TPU:0, one launch (start us, length us, event | category | flops | bytes accessed | tf_op | source)
XLA Modules:
  0.0 133.8 jit_solution(13684845250904301849)
XLA Ops:
  0.0 0.9 copy-done
  1.0 5.1 %collective-permute-start = (bf16[8,32,256]{2,1,0:T(8,128)(2,1)S(1)}, bf16[8,32,256]{2,1,0:T(8,128)(2,1)S(1)}, u32[]{:S(2)}, u32[]{:S(2)}) collective-permute-start(bf16[8,32,256]{2,1,0:T(8,128)(2,1)S(1)} %constant_dynamic-slice_fusion), channel_id=1, source_target_pairs={{0,12},{4,0},{8,4},{12,8},{1,13},{5,1},{9,5},{13,9},{2,14},{6,2},{... | collective-permute-start | bytes 393224 | tf_op jit(solution)/shard_map/ppermute | solution.py:192
  6.1 1.0 collective-permute-start.2
  7.1 1.7 %route.1 = (s32[1,768]{1,0:T(1,128)}, s32[8,128]{1,0:T(8,128)}) custom-call(s32[1]{0:T(128)} %bitcast.place_ref, s32[32]{0:T(128)} %entry_hbm.1, s32[768]{0:T(1024)} %request_hbm.1), custom_call_target="tpu_custom_call" | custom-call | flops 1 | bytes 1 | tf_op jit(solution)/shard_map/route/pallas_call | solution.py:272
  8.8 6.5 %pack.1 = (s32[8,128]{1,0:T(8,128)}, bf16[216,2048]{1,0:T(8,128)(2,1)}, bf16[216,2048]{1,0:T(8,128)(2,1)}, bf16[216,2048]{1,0:T(8,128)(2,1)}, bf16[216,2048]{1,0:T(8,128)(2,1)}) custom-call(s32[1,768]{1,0:T(1,128)} %get-tuple-element.20.index_ref, bf16[768,2048]{1,0:T(8,128)(2,1)} %tokens_ref.9), custom_call_target="tpu_custom_call" | custom-call | flops 1 | bytes 1 | tf_op jit(solution)/shard_map/pack/pallas_call | solution.py:290
  15.3 1.9 %collective-permute-done.1.refs_4_ = bf16[8,32,256]{2,1,0:T(8,128)(2,1)S(1)} collective-permute-done((bf16[8,32,256]{2,1,0:T(8,128)(2,1)S(1)}, bf16[8,32,256]{2,1,0:T(8,128)(2,1)S(1)}, u32[]{:S(2)}, u32[]{:S(2)}) %collective-permute-start.1) | collective-permute-done | bytes 131104 | tf_op jit(solution)/shard_map/ppermute | solution.py:192
  17.3 0.6 copy-done.10
  18.0 0.6 gate.1
  18.6 2.6 %collective-permute-start.10 = (bf16[216,2048]{1,0:T(8,128)(2,1)}, bf16[216,2048]{1,0:T(8,128)(2,1)S(1)}, u32[]{:S(2)}, u32[]{:S(2)}) collective-permute-start(bf16[216,2048]{1,0:T(8,128)(2,1)} %get-tuple-element.27), channel_id=1, source_target_pairs={{0,8},{4,12},{8,0},{12,4},{1,9},{5,13},{9,1},{13,5},{2,10},{6,14},... | collective-permute-start | bytes 2654216 | tf_op jit(solution)/shard_map/ppermute | solution.py:305
  21.2 0.5 broadcast_xor_fusion.block_ref
  21.7 4.4 %base.4.refs_0_ = f32[384,512]{1,0:T(8,128)} custom-call(s32[2]{0:T(128)} %broadcast_xor_fusion.block_ref, bf16[768,2048]{1,0:T(8,128)(2,1)} %tokens_ref.9, bf16[2048,1024]{1,0:T(8,128)(2,1)} %weight_ref.7, s32[8,128]{1,0:T(8,128)} %get-tuple-element.24.refs_0_), custom_call_target="tpu_custom_call" | custom-call | flops 1 | bytes 1 | tf_op jit(solution)/shard_map/base/pallas_call | solution.py:219
  26.1 4.5 %base.6.refs_0_ = f32[384,512]{1,0:T(8,128)} custom-call(s32[2]{0:T(128)} %broadcast_xor_fusion.block_ref, bf16[768,2048]{1,0:T(8,128)(2,1)} %tokens_ref.9, bf16[2048,1024]{1,0:T(8,128)(2,1)} %weight_ref.7, s32[8,128]{1,0:T(8,128)} %get-tuple-element.24.refs_0_), custom_call_target="tpu_custom_call" | custom-call | flops 1 | bytes 1 | tf_op jit(solution)/shard_map/base/pallas_call | solution.py:219
  30.6 0.4 collective-permute-start.5
  31.0 1.2 slice.45
  34.4 0.1 pad_add_fusion.scalar_ref
  34.5 2.2 %copy-done.1 = bf16[8,2048,128]{2,1,0:T(8,128)(2,1)S(1)} copy-done((bf16[8,2048,128]{2,1,0:T(8,128)(2,1)S(1)}, bf16[8,2048,128]{2,1,0:T(8,128)(2,1)}, u32[]{:S(2)}) %copy-start.1) | copy-done | bytes 4194328
  36.6 1.4 %shrink.4 = f32[240,128]{1,0:T(8,128)S(1)} custom-call(s32[3]{0:T(128)S(1)} %pad_add_fusion.scalar_ref, bf16[216,2048]{1,0:T(8,128)(2,1)S(1)} %copy-done.4, bf16[8,2048,128]{2,1,0:T(8,128)(2,1)S(1)} %copy-done.1, s32[8,128]{1,0:T(8,128)S(1)} %copy-done.5), custom_call_target="tpu_custom_call" | custom-call | flops 1 | bytes 1 | tf_op jit(solution)/shard_map/shrink/pallas_call | solution.py:319
  38.1 0.2 collective-permute-start.13
  38.8 0.2 copy.13.index_ref
  39.0 0.5 multiply_xor_fusion.block_ref
  39.6 1.6 %collective-permute-start.14 = (f32[120,128]{1,0:T(8,128)S(1)}, f32[120,128]{1,0:T(8,128)S(1)}, u32[]{:S(2)}, u32[]{:S(2)}) collective-permute-start(f32[120,128]{1,0:T(8,128)S(1)} %slice.69), channel_id=1, source_target_pairs={{0,2},{1,3},{2,0},{3,1},{4,6},{5,7},{6,4},{7,5},{8,10},{9,11},{10,... | collective-permute-start | bytes 184328 | tf_op jit(solution)/shard_map/ppermute | solution.py:337
  41.2 37.3 %collective-permute-done.10.refs_0_ = bf16[216,2048]{1,0:T(8,128)(2,1)S(1)} collective-permute-done((bf16[216,2048]{1,0:T(8,128)(2,1)}, bf16[216,2048]{1,0:T(8,128)(2,1)S(1)}, u32[]{:S(2)}, u32[]{:S(2)}) %collective-permute-start.10) | collective-permute-done | bytes 884768 | tf_op jit(solution)/shard_map/ppermute | solution.py:305
  78.5 2.2 %copy-done.2 = bf16[8,2048,128]{2,1,0:T(8,128)(2,1)S(1)} copy-done((bf16[8,2048,128]{2,1,0:T(8,128)(2,1)S(1)}, bf16[8,2048,128]{2,1,0:T(8,128)(2,1)}, u32[]{:S(2)}) %copy-start.2) | copy-done | bytes 4194328
  80.7 1.4 %shrink.3 = f32[240,128]{1,0:T(8,128)S(1)} custom-call(s32[3]{0:T(128)S(1)} %pad_add_fusion.scalar_ref, bf16[216,2048]{1,0:T(8,128)(2,1)S(1)} %collective-permute-done.10.refs_0_, bf16[8,2048,128]{2,1,0:T(8,128)(2,1)S(1)} %copy-done.2, s32[8,128]{1,0:T(8,128)S(1)} %copy-done.5), custom_call_target="tpu_custom_call" | custom-call | flops 1 | bytes 1 | tf_op jit(solution)/shard_map/shrink/pallas_call | solution.py:319
  82.1 0.8 pad_maximum_fusion.2
  83.0 4.4 %base.5 = f32[384,512]{1,0:T(8,128)} custom-call(s32[2]{0:T(128)} %multiply_xor_fusion.block_ref, bf16[768,2048]{1,0:T(8,128)(2,1)} %tokens_ref.9, bf16[2048,1024]{1,0:T(8,128)(2,1)} %weight_ref.7, f32[384,512]{1,0:T(8,128)} %base.4.refs_0_), custom_call_target="tpu_custom_call" | custom-call | flops 1 | bytes 1 | tf_op jit(solution)/shard_map/base/pallas_call | solution.py:219
  87.4 4.5 %base.7 = f32[384,512]{1,0:T(8,128)} custom-call(s32[2]{0:T(128)} %multiply_xor_fusion.block_ref, bf16[768,2048]{1,0:T(8,128)(2,1)} %tokens_ref.9, bf16[2048,1024]{1,0:T(8,128)(2,1)} %weight_ref.7, f32[384,512]{1,0:T(8,128)} %base.6.refs_0_), custom_call_target="tpu_custom_call" | custom-call | flops 1 | bytes 1 | tf_op jit(solution)/shard_map/base/pallas_call | solution.py:219
  92.0 1.4 %add.44 = f32[384,512]{1,0:T(8,128)S(1)} add(f32[384,512]{1,0:T(8,128)S(1)} %copy-done.7, f32[384,512]{1,0:T(8,128)} %collective-permute-done.3) | non-fusion elementwise | flops 196608 | bytes 2359296 | tf_op jit(solution)/shard_map/add | solution.py:249
  93.4 1.6 %collective-permute-start.4 = (f32[384,256]{1,0:T(8,128)S(1)}, f32[384,256]{1,0:T(8,128)S(1)}, u32[]{:S(2)}, u32[]{:S(2)}) collective-permute-start(f32[384,256]{1,0:T(8,128)S(1)} %slice.61), channel_id=1, source_target_pairs={{0,2},{1,3},{2,0},{3,1},{4,6},{5,7},{6,4},{7,5},{8,10},{9,11},{10,... | collective-permute-start | bytes 1179656 | tf_op jit(solution)/shard_map/ppermute | solution.py:249
  95.0 0.6 collective-permute-start.12
  95.6 1.6 %collective-permute-start.7 = (bf16[32,32,256]{2,1,0:T(8,128)(2,1)S(1)}, bf16[32,32,256]{2,1,0:T(8,128)(2,1)S(1)}, u32[]{:S(2)}, u32[]{:S(2)}) collective-permute-start(bf16[32,32,256]{2,1,0:T(8,128)(2,1)S(1)} %copy-done.17), channel_id=1, source_target_pairs={{0,16},{16,0},{1,17},{17,1},{2,18},{18,2},{3,19},{19,3},{4,20},{20... | collective-permute-start | bytes 1572872 | tf_op jit(solution)/shard_map/ppermute | solution.py:196
  97.2 1.3 add.46
  98.5 7.7 %collective-permute-done.12 = f32[120,128]{1,0:T(8,128)S(1)} collective-permute-done((f32[120,128]{1,0:T(8,128)S(1)}, f32[120,128]{1,0:T(8,128)S(1)}, u32[]{:S(2)}, u32[]{:S(2)}) %collective-permute-start.12) | collective-permute-done | bytes 61472 | tf_op jit(solution)/shard_map/ppermute | solution.py:337
  106.2 1.5 %collective-permute-start.6 = (f32[384,256]{1,0:T(8,128)S(1)}, f32[384,256]{1,0:T(8,128)S(1)}, u32[]{:S(2)}, u32[]{:S(2)}) collective-permute-start(f32[384,256]{1,0:T(8,128)S(1)} %slice.63), channel_id=1, source_target_pairs={{0,2},{1,3},{2,0},{3,1},{4,6},{5,7},{6,4},{7,5},{8,10},{9,11},{10,... | collective-permute-start | bytes 1179656 | tf_op jit(solution)/shard_map/ppermute | solution.py:249
  107.8 9.1 %collective-permute-done.6 = f32[384,256]{1,0:T(8,128)S(1)} collective-permute-done((f32[384,256]{1,0:T(8,128)S(1)}, f32[384,256]{1,0:T(8,128)S(1)}, u32[]{:S(2)}, u32[]{:S(2)}) %collective-permute-start.6) | collective-permute-done | bytes 393248 | tf_op jit(solution)/shard_map/ppermute | solution.py:249
  117.1 1.5 %shrink.5 = (f32[480,128]{1,0:T(8,128)S(1)}, f32[120,128]{1,0:T(8,128)S(1)}, f32[120,128]{1,0:T(8,128)S(1)}) custom-call(s32[3]{0:T(128)S(1)} %pad_add_fusion.scalar_ref, bf16[216,2048]{1,0:T(8,128)(2,1)S(1)} %collective-permute-done.8.refs_0_, bf16[216,2048]{1,0:T(8,128)(2,1)S(1)} %collective-permute-done.9.refs_1_, bf16[8,2048,128]{2,1,0:T(8,128)(2,1)S(1)} %copy-done.3, ...), custom_call_target="tpu_custom_call" | custom-call | flops 1 | bytes 1 | tf_op jit(solution)/shard_map/shrink/pallas_call | solution.py:319
  118.7 0.1 broadcast_select_fusion.1
  118.8 1.4 %collective-permute-done.16 = f32[480,128]{1,0:T(8,128)S(1)} collective-permute-done((f32[480,128]{1,0:T(8,128)S(1)}, f32[480,128]{1,0:T(8,128)S(1)}, u32[]{:S(2)}, u32[]{:S(2)}) %collective-permute-start.16) | collective-permute-done | bytes 245792 | tf_op jit(solution)/shard_map/ppermute | solution.py:335
  120.2 1.6 %collective-permute-start.17 = (f32[240,128]{1,0:T(8,128)S(1)}, f32[240,128]{1,0:T(8,128)S(1)}, u32[]{:S(2)}, u32[]{:S(2)}) collective-permute-start(f32[240,128]{1,0:T(8,128)S(1)} %slice.71), channel_id=1, source_target_pairs={{0,2},{1,3},{2,0},{3,1},{4,6},{5,7},{6,4},{7,5},{8,10},{9,11},{10,... | collective-permute-start | bytes 368648 | tf_op jit(solution)/shard_map/ppermute | solution.py:337
  121.7 0.1 pad_maximum_fusion.up_ref
  121.8 0.1 collective-permute-start.15
  121.9 3.7 %collective-permute-done.17 = f32[240,128]{1,0:T(8,128)S(1)} collective-permute-done((f32[240,128]{1,0:T(8,128)S(1)}, f32[240,128]{1,0:T(8,128)S(1)}, u32[]{:S(2)}, u32[]{:S(2)}) %collective-permute-start.17) | collective-permute-done | bytes 122912 | tf_op jit(solution)/shard_map/ppermute | solution.py:337
  125.6 0.5 collective-permute-start.18
  126.1 1.6 %collective-permute-start.19 = (f32[120,128]{1,0:T(8,128)S(1)}, f32[120,128]{1,0:T(8,128)S(1)}, u32[]{:S(2)}, u32[]{:S(2)}) collective-permute-start(f32[120,128]{1,0:T(8,128)S(1)} %get-tuple-element.35), channel_id=1, source_target_pairs={{0,4},{4,8},{8,12},{12,0},{1,5},{5,9},{9,13},{13,1},{2,6},{6,10},{... | collective-permute-start | bytes 184328 | tf_op jit(solution)/shard_map/ppermute | solution.py:357
  127.8 0.9 finish.2.base_ref
  128.7 1.9 %collective-permute-done.18.refs_0_ = f32[120,128]{1,0:T(8,128)S(1)} collective-permute-done((f32[120,128]{1,0:T(8,128)S(1)}, f32[120,128]{1,0:T(8,128)S(1)}, u32[]{:S(2)}, u32[]{:S(2)}) %collective-permute-start.18) | collective-permute-done | bytes 61472 | tf_op jit(solution)/shard_map/ppermute | solution.py:357
  130.6 1.6 %collective-permute-done.19.refs_1_ = f32[120,128]{1,0:T(8,128)S(1)} collective-permute-done((f32[120,128]{1,0:T(8,128)S(1)}, f32[120,128]{1,0:T(8,128)S(1)}, u32[]{:S(2)}, u32[]{:S(2)}) %collective-permute-start.19) | collective-permute-done | bytes 61472 | tf_op jit(solution)/shard_map/ppermute | solution.py:357
  132.1 1.6 %finish.3 = bf16[768,256]{1,0:T(8,128)(2,1)} custom-call(s32[1]{0:T(128)} %bitcast.2.place_ref, s32[768,1]{1,0:T(8,128)S(1)} %copy.13.index_ref, f32[768,256]{1,0:T(8,128)S(1)} %finish.2.base_ref, bf16[32,64,256]{2,1,0:T(8,128)(2,1)S(1)} %pad_maximum_fusion.up_ref, f32[120,128]{1,0:T(8,128)S(1)} %collective-permute-done.18.refs_0_, ...), custom_call_target="tpu_custom_call" | custom-call | flops 1 | bytes 1 | tf_op jit(solution)/shard_map/finish/pallas_call | solution.py:156
  (70 shorter events, 0.7 us)
Async XLA Ops:
  0.0 1.0 copy-start
  1.0 81.1 %copy-start.15 = (bf16[8,32,256]{2,1,0:T(8,128)(2,1)}, bf16[8,32,256]{2,1,0:T(8,128)(2,1)S(1)}, u32[]{:S(2)}) copy-start(bf16[8,32,256]{2,1,0:T(8,128)(2,1)S(1)} %constant_dynamic-slice_fusion) | copy-start | bytes 393220
  1.0 14.3 %collective-permute-start = (bf16[8,32,256]{2,1,0:T(8,128)(2,1)S(1)}, bf16[8,32,256]{2,1,0:T(8,128)(2,1)S(1)}, u32[]{:S(2)}, u32[]{:S(2)}) collective-permute-start(bf16[8,32,256]{2,1,0:T(8,128)(2,1)S(1)} %constant_dynamic-slice_fusion), channel_id=1, source_target_pairs={{0,12},{4,0},{8,4},{12,8},{1,13},{5,1},{9,5},{13,9},{2,14},{6,2},{... | collective-permute-start | bytes 393224 | tf_op jit(solution)/shard_map/ppermute | solution.py:192
  6.1 11.2 %collective-permute-start.1 = (bf16[8,32,256]{2,1,0:T(8,128)(2,1)S(1)}, bf16[8,32,256]{2,1,0:T(8,128)(2,1)S(1)}, u32[]{:S(2)}, u32[]{:S(2)}) collective-permute-start(bf16[8,32,256]{2,1,0:T(8,128)(2,1)S(1)} %constant_dynamic-slice_fusion), channel_id=1, source_target_pairs={{0,8},{4,12},{8,0},{12,4},{1,9},{5,13},{9,1},{13,5},{2,10},{6,14},... | collective-permute-start | bytes 393224 | tf_op jit(solution)/shard_map/ppermute | solution.py:192
  6.1 11.2 %collective-permute-start.2 = (bf16[8,32,256]{2,1,0:T(8,128)(2,1)S(1)}, bf16[8,32,256]{2,1,0:T(8,128)(2,1)S(1)}, u32[]{:S(2)}, u32[]{:S(2)}) collective-permute-start(bf16[8,32,256]{2,1,0:T(8,128)(2,1)S(1)} %constant_dynamic-slice_fusion), channel_id=1, source_target_pairs={{0,4},{4,8},{8,12},{12,0},{1,5},{5,9},{9,13},{13,1},{2,6},{6,10},{... | collective-permute-start | bytes 393224 | tf_op jit(solution)/shard_map/ppermute | solution.py:192
  15.3 2.0 %copy-start.8 = (bf16[8,32,256]{2,1,0:T(8,128)(2,1)}, bf16[8,32,256]{2,1,0:T(8,128)(2,1)S(1)}, u32[]{:S(2)}) copy-start(bf16[8,32,256]{2,1,0:T(8,128)(2,1)S(1)} %collective-permute-done.refs_3_) | copy-start | bytes 393220
  17.3 0.7 copy-start.10
  17.3 0.7 copy-start.12
  18.6 59.9 %collective-permute-start.10 = (bf16[216,2048]{1,0:T(8,128)(2,1)}, bf16[216,2048]{1,0:T(8,128)(2,1)S(1)}, u32[]{:S(2)}, u32[]{:S(2)}) collective-permute-start(bf16[216,2048]{1,0:T(8,128)(2,1)} %get-tuple-element.27), channel_id=1, source_target_pairs={{0,8},{4,12},{8,0},{12,4},{1,9},{5,13},{9,1},{13,5},{2,10},{6,14},... | collective-permute-start | bytes 2654216 | tf_op jit(solution)/shard_map/ppermute | solution.py:305
  26.1 8.4 %copy-start.4 = (bf16[216,2048]{1,0:T(8,128)(2,1)S(1)}, bf16[216,2048]{1,0:T(8,128)(2,1)}, u32[]{:S(2)}) copy-start(bf16[216,2048]{1,0:T(8,128)(2,1)} %get-tuple-element.29.refs_0_) | copy-start | bytes 2654212
  26.1 8.4 %copy-start.5 = (s32[8,128]{1,0:T(8,128)S(1)}, s32[8,128]{1,0:T(8,128)}, u32[]{:S(2)}) copy-start(s32[8,128]{1,0:T(8,128)} %get-tuple-element.28.refs_2_) | copy-start | bytes 12292
  26.1 65.8 %collective-permute-start.3 = (f32[384,512]{1,0:T(8,128)}, f32[384,512]{1,0:T(8,128)}, u32[]{:S(2)}, u32[]{:S(2)}) collective-permute-start(f32[384,512]{1,0:T(8,128)} %base.4.refs_0_), channel_id=1, source_target_pairs={{0,1},{1,0},{2,3},{3,2},{4,5},{5,4},{6,7},{7,6},{8,9},{9,8},{10,11... | collective-permute-start | bytes 2359304 | tf_op jit(solution)/shard_map/ppermute | solution.py:249
  30.6 8.2 %copy-start.18 = (s32[1,768]{1,0:T(1,128)S(1)}, s32[1,768]{1,0:T(1,128)}, u32[]{:S(2)}) copy-start(s32[1,768]{1,0:T(1,128)} %get-tuple-element.20.index_ref) | copy-start | bytes 9220
  30.6 65.0 %collective-permute-start.5 = (f32[384,512]{1,0:T(8,128)}, f32[384,512]{1,0:T(8,128)}, u32[]{:S(2)}, u32[]{:S(2)}) collective-permute-start(f32[384,512]{1,0:T(8,128)} %base.6.refs_0_), channel_id=1, source_target_pairs={{0,1},{1,0},{2,3},{3,2},{4,5},{5,4},{6,7},{7,6},{8,9},{9,8},{10,11... | collective-permute-start | bytes 2359304 | tf_op jit(solution)/shard_map/ppermute | solution.py:249
  34.5 2.2 %copy-start.1 = (bf16[8,2048,128]{2,1,0:T(8,128)(2,1)S(1)}, bf16[8,2048,128]{2,1,0:T(8,128)(2,1)}, u32[]{:S(2)}) copy-start(bf16[8,2048,128]{2,1,0:T(8,128)(2,1)} %refs_2_.1) | copy-start | bytes 12582916
  38.0 44.1 %copy-start.9 = (bf16[8,32,256]{2,1,0:T(8,128)(2,1)S(1)}, bf16[8,32,256]{2,1,0:T(8,128)(2,1)}, u32[]{:S(2)}) copy-start(bf16[8,32,256]{2,1,0:T(8,128)(2,1)} %copy-done.8) | copy-start | bytes 393220
  38.0 44.1 %copy-start.11 = (bf16[8,32,256]{2,1,0:T(8,128)(2,1)S(1)}, bf16[8,32,256]{2,1,0:T(8,128)(2,1)}, u32[]{:S(2)}) copy-start(bf16[8,32,256]{2,1,0:T(8,128)(2,1)} %copy-done.10) | copy-start | bytes 393220
  38.0 44.1 %copy-start.13 = (bf16[8,32,256]{2,1,0:T(8,128)(2,1)S(1)}, bf16[8,32,256]{2,1,0:T(8,128)(2,1)}, u32[]{:S(2)}) copy-start(bf16[8,32,256]{2,1,0:T(8,128)(2,1)} %copy-done.12) | copy-start | bytes 393220
  38.1 1.5 %collective-permute-start.13 = (f32[240,128]{1,0:T(8,128)S(1)}, f32[240,128]{1,0:T(8,128)S(1)}, u32[]{:S(2)}, u32[]{:S(2)}) collective-permute-start(f32[240,128]{1,0:T(8,128)S(1)} %shrink.4), channel_id=1, source_target_pairs={{0,1},{1,0},{2,3},{3,2},{4,5},{5,4},{6,7},{7,6},{8,9},{9,8},{10,11... | collective-permute-start | bytes 368648 | tf_op jit(solution)/shard_map/ppermute | solution.py:335
  39.6 55.4 %collective-permute-start.14 = (f32[120,128]{1,0:T(8,128)S(1)}, f32[120,128]{1,0:T(8,128)S(1)}, u32[]{:S(2)}, u32[]{:S(2)}) collective-permute-start(f32[120,128]{1,0:T(8,128)S(1)} %slice.69), channel_id=1, source_target_pairs={{0,2},{1,3},{2,0},{3,1},{4,6},{5,7},{6,4},{7,5},{8,10},{9,11},{10,... | collective-permute-start | bytes 184328 | tf_op jit(solution)/shard_map/ppermute | solution.py:337
  41.2 75.9 %collective-permute-start.8 = (bf16[216,2048]{1,0:T(8,128)(2,1)}, bf16[216,2048]{1,0:T(8,128)(2,1)S(1)}, u32[]{:S(2)}, u32[]{:S(2)}) collective-permute-start(bf16[216,2048]{1,0:T(8,128)(2,1)} %get-tuple-element.25), channel_id=1, source_target_pairs={{0,4},{4,8},{8,12},{12,0},{1,5},{5,9},{9,13},{13,1},{2,6},{6,10},{... | collective-permute-start | bytes 2654216 | tf_op jit(solution)/shard_map/ppermute | solution.py:305
  78.5 2.2 %copy-start.2 = (bf16[8,2048,128]{2,1,0:T(8,128)(2,1)S(1)}, bf16[8,2048,128]{2,1,0:T(8,128)(2,1)}, u32[]{:S(2)}) copy-start(bf16[8,2048,128]{2,1,0:T(8,128)(2,1)} %refs_2_.1) | copy-start | bytes 12582916
  82.1 11.3 %collective-permute-start.11 = (f32[240,128]{1,0:T(8,128)S(1)}, f32[240,128]{1,0:T(8,128)S(1)}, u32[]{:S(2)}, u32[]{:S(2)}) collective-permute-start(f32[240,128]{1,0:T(8,128)S(1)} %shrink.3), channel_id=1, source_target_pairs={{0,1},{1,0},{2,3},{3,2},{4,5},{5,4},{6,7},{7,6},{8,9},{9,8},{10,11... | collective-permute-start | bytes 368648 | tf_op jit(solution)/shard_map/ppermute | solution.py:335
  87.4 4.6 %copy-start.7 = (f32[384,512]{1,0:T(8,128)S(1)}, f32[384,512]{1,0:T(8,128)}, u32[]{:S(2)}) copy-start(f32[384,512]{1,0:T(8,128)} %base.5) | copy-start | bytes 2359300
  91.9 3.7 %copy-start.17 = (bf16[32,32,256]{2,1,0:T(8,128)(2,1)S(1)}, bf16[32,32,256]{2,1,0:T(8,128)(2,1)}, u32[]{:S(2)}) copy-start(bf16[32,32,256]{2,1,0:T(8,128)(2,1)} %pad_maximum_fusion.2) | copy-start | bytes 1572868
  91.9 5.3 %copy-start.6 = (f32[384,512]{1,0:T(8,128)S(1)}, f32[384,512]{1,0:T(8,128)}, u32[]{:S(2)}) copy-start(f32[384,512]{1,0:T(8,128)} %base.7) | copy-start | bytes 2359300
  91.9 25.2 %collective-permute-start.9 = (bf16[216,2048]{1,0:T(8,128)(2,1)}, bf16[216,2048]{1,0:T(8,128)(2,1)S(1)}, u32[]{:S(2)}, u32[]{:S(2)}) collective-permute-start(bf16[216,2048]{1,0:T(8,128)(2,1)} %get-tuple-element.26), channel_id=1, source_target_pairs={{0,12},{4,0},{8,4},{12,8},{1,13},{5,1},{9,5},{13,9},{2,14},{6,2},{... | collective-permute-start | bytes 2654216 | tf_op jit(solution)/shard_map/ppermute | solution.py:305
  93.4 23.7 %copy-start.3 = (bf16[8,2048,128]{2,1,0:T(8,128)(2,1)S(1)}, bf16[8,2048,128]{2,1,0:T(8,128)(2,1)}, u32[]{:S(2)}) copy-start(bf16[8,2048,128]{2,1,0:T(8,128)(2,1)} %refs_2_.1) | copy-start | bytes 12582916
  93.4 14.4 %collective-permute-start.4 = (f32[384,256]{1,0:T(8,128)S(1)}, f32[384,256]{1,0:T(8,128)S(1)}, u32[]{:S(2)}, u32[]{:S(2)}) collective-permute-start(f32[384,256]{1,0:T(8,128)S(1)} %slice.61), channel_id=1, source_target_pairs={{0,2},{1,3},{2,0},{3,1},{4,6},{5,7},{6,4},{7,5},{8,10},{9,11},{10,... | collective-permute-start | bytes 1179656 | tf_op jit(solution)/shard_map/ppermute | solution.py:249
  95.0 11.3 %collective-permute-start.12 = (f32[120,128]{1,0:T(8,128)S(1)}, f32[120,128]{1,0:T(8,128)S(1)}, u32[]{:S(2)}, u32[]{:S(2)}) collective-permute-start(f32[120,128]{1,0:T(8,128)S(1)} %slice.67), channel_id=1, source_target_pairs={{0,2},{1,3},{2,0},{3,1},{4,6},{5,7},{6,4},{7,5},{8,10},{9,11},{10,... | collective-permute-start | bytes 184328 | tf_op jit(solution)/shard_map/ppermute | solution.py:337
  95.6 23.0 %collective-permute-start.7 = (bf16[32,32,256]{2,1,0:T(8,128)(2,1)S(1)}, bf16[32,32,256]{2,1,0:T(8,128)(2,1)S(1)}, u32[]{:S(2)}, u32[]{:S(2)}) collective-permute-start(bf16[32,32,256]{2,1,0:T(8,128)(2,1)S(1)} %copy-done.17), channel_id=1, source_target_pairs={{0,16},{16,0},{1,17},{17,1},{2,18},{18,2},{3,19},{19,3},{4,20},{20... | collective-permute-start | bytes 1572872 | tf_op jit(solution)/shard_map/ppermute | solution.py:196
  106.2 10.7 %collective-permute-start.6 = (f32[384,256]{1,0:T(8,128)S(1)}, f32[384,256]{1,0:T(8,128)S(1)}, u32[]{:S(2)}, u32[]{:S(2)}) collective-permute-start(f32[384,256]{1,0:T(8,128)S(1)} %slice.63), channel_id=1, source_target_pairs={{0,2},{1,3},{2,0},{3,1},{4,6},{5,7},{6,4},{7,5},{8,10},{9,11},{10,... | collective-permute-start | bytes 1179656 | tf_op jit(solution)/shard_map/ppermute | solution.py:249
  117.0 1.6 %copy-start.14 = (bf16[8,32,256]{2,1,0:T(8,128)(2,1)S(1)}, bf16[8,32,256]{2,1,0:T(8,128)(2,1)}, u32[]{:S(2)}) copy-start(bf16[8,32,256]{2,1,0:T(8,128)(2,1)} %copy-done.12) | copy-start | bytes 393220
  117.0 1.6 %copy-start.16 = (bf16[8,32,256]{2,1,0:T(8,128)(2,1)S(1)}, bf16[8,32,256]{2,1,0:T(8,128)(2,1)}, u32[]{:S(2)}) copy-start(bf16[8,32,256]{2,1,0:T(8,128)(2,1)} %copy-done.15) | copy-start | bytes 393220
  118.6 1.6 %collective-permute-start.16 = (f32[480,128]{1,0:T(8,128)S(1)}, f32[480,128]{1,0:T(8,128)S(1)}, u32[]{:S(2)}, u32[]{:S(2)}) collective-permute-start(f32[480,128]{1,0:T(8,128)S(1)} %get-tuple-element.32), channel_id=1, source_target_pairs={{0,1},{1,0},{2,3},{3,2},{4,5},{5,4},{6,7},{7,6},{8,9},{9,8},{10,11... | collective-permute-start | bytes 737288 | tf_op jit(solution)/shard_map/ppermute | solution.py:335
  120.2 5.4 %collective-permute-start.17 = (f32[240,128]{1,0:T(8,128)S(1)}, f32[240,128]{1,0:T(8,128)S(1)}, u32[]{:S(2)}, u32[]{:S(2)}) collective-permute-start(f32[240,128]{1,0:T(8,128)S(1)} %slice.71), channel_id=1, source_target_pairs={{0,2},{1,3},{2,0},{3,1},{4,6},{5,7},{6,4},{7,5},{8,10},{9,11},{10,... | collective-permute-start | bytes 368648 | tf_op jit(solution)/shard_map/ppermute | solution.py:337
  121.8 6.0 %collective-permute-start.15 = (f32[120,128]{1,0:T(8,128)S(1)}, f32[120,128]{1,0:T(8,128)S(1)}, u32[]{:S(2)}, u32[]{:S(2)}) collective-permute-start(f32[120,128]{1,0:T(8,128)S(1)} %get-tuple-element.30), channel_id=1, source_target_pairs={{0,8},{4,12},{8,0},{12,4},{1,9},{5,13},{9,1},{13,5},{2,10},{6,14},... | collective-permute-start | bytes 184328 | tf_op jit(solution)/shard_map/ppermute | solution.py:357
  125.6 4.9 %collective-permute-start.18 = (f32[120,128]{1,0:T(8,128)S(1)}, f32[120,128]{1,0:T(8,128)S(1)}, u32[]{:S(2)}, u32[]{:S(2)}) collective-permute-start(f32[120,128]{1,0:T(8,128)S(1)} %get-tuple-element.36), channel_id=1, source_target_pairs={{0,12},{4,0},{8,4},{12,8},{1,13},{5,1},{9,5},{13,9},{2,14},{6,2},{... | collective-permute-start | bytes 184328 | tf_op jit(solution)/shard_map/ppermute | solution.py:357
  126.1 6.0 %collective-permute-start.19 = (f32[120,128]{1,0:T(8,128)S(1)}, f32[120,128]{1,0:T(8,128)S(1)}, u32[]{:S(2)}, u32[]{:S(2)}) collective-permute-start(f32[120,128]{1,0:T(8,128)S(1)} %get-tuple-element.35), channel_id=1, source_target_pairs={{0,4},{4,8},{8,12},{12,0},{1,5},{5,9},{9,13},{13,1},{2,6},{6,10},{... | collective-permute-start | bytes 184328 | tf_op jit(solution)/shard_map/ppermute | solution.py:357

commit v9 on v8

--- a/solution.py
+++ b/solution.py
@@ -229,7 +229,7 @@
             + [ANY] * len(after),
             out_specs=pl.BlockSpec((rows, columns), lambda j, chosen: (0, j)),
         ),
-        compiler_params=WIDE,
+        compiler_params=PARAMS,
         cost_estimate=COST,
         name="base",
     )(blocks, tokens, weight, *after)
@@ -244,12 +244,13 @@
     keep = jnp.array(keep, jnp.int32)
     sent = base_part(tokens, weight, piece ^ keep ^ 1, columns, slab, slabs, after)
     kept = base_part(tokens, weight, piece ^ keep, columns, slab, slabs, [sent])
-    bit = 1
+    bit, first = 1, None
     while True:
         kept = kept + lax.ppermute(sent, "tensor", [(i, i ^ bit) for i in range(pieces)])
+        first = kept[:8] if first is None else first
         bit *= 2
         if bit >= pieces:
-            return kept
+            return kept, first
         half = kept.shape[1] // 2
         kept, sent = kept[:, :half], kept[:, half:]
 
@@ -337,18 +338,17 @@
         return value[:half] + lax.ppermute(value[half:], "tensor", [(i, i ^ bit) for i in range(pieces)])
 
     slabs = 2
-    base = jnp.concatenate(
-        [
-            reduce_base(tokens, key_value_weight, piece, pieces, columns, slab, slabs, [mark])
-            for slab in range(slabs)
-        ],
-        axis=0,
-    )
+    slab_sums = [
+        reduce_base(tokens, key_value_weight, piece, pieces, columns, slab, slabs, [mark])
+        for slab in range(slabs)
+    ]
+    base = jnp.concatenate([total for total, _ in slab_sums], axis=0)
+    begun = [first for _, first in slab_sums]
     late = order[-2:]
     early = order[:-2] + [0]
     totals = []
     for r in early:
-        (value,) = shrink([arrived[r]], [packed], [])
+        (value,) = shrink([arrived[r]], begun if r else [packed], [])
         totals.append(combine(value))
     value, *totals = shrink([arrived[r] for r in late], [base[:8], base[-8:]], totals)
     last = combine(value)

time: 134 us -> 124 us (0.925)
  waiting for transfers between devices: 64.7 us -> 51.2 us
  Pallas kernels: 33.4 us -> 25.9 us
  local copies, waits for them, and re-layouts: 7.53 us -> 12.4 us
  starting transfers between devices: 19.9 us -> 23.7 us
    ppermute x3, waiting for transfers between devices: 37.3 us -> 22.6 us  [send(): lax.ppermute(block, 'batch', [(i, (i + r) % homes) for i in range(homes)])]
    pallas_call x4, Pallas kernels: 17.8 us -> 9.77 us  [base_part(): pl.pallas_call(functools.partial(base_kernel, len(after)), out_shape=jax....]
    ppermute x3, starting transfers between devices: 2.64 us -> 6.48 us  [send(): lax.ppermute(block, 'batch', [(i, (i + r) % homes) for i in range(homes)])]
    unnamed x38 -> x30, local copies, waits for them, and re-layouts: 6.09 us -> 9.4 us
    ppermute x3, waiting for transfers between devices: 11.5 us -> 14.1 us  [combine(): lax.ppermute(value[half:], 'tensor', [(i, i ^ bit) for i in range(pieces)])]
  transfers between devices with their start and end apart: 20 -> 20, of which waited for: 8 -> 8; matrix products, arithmetic and copies ran while one was open for 5% -> 7% of each run, Pallas kernels for 23% -> 19%
where the time goes in v9:
time: 124 us; the launch traced here: 123 us
  waiting for transfers between devices  51.2 us (41%)
  Pallas kernels  25.9 us (21%)
  starting transfers between devices  23.7 us (19%)
  local copies, waits for them, and re-layouts  12.4 us (10%)
  other arithmetic  6.14 us (5%)
  between operations  3.91 us (3%)
    ppermute x3, waiting for transfers between devices, send(): lax.ppermute(block, 'batch', [(i, (i + r) % homes) for i in range(homes)])  22.6 us
    ppermute x3, waiting for transfers between devices, combine(): lax.ppermute(value[half:], 'tensor', [(i, i ^ bit) for i in range(pieces)])  14.1 us
    pallas_call x4, Pallas kernels, base_part(): pl.pallas_call(functools.partial(base_kernel, len(after)), out_shape=jax....  9.77 us
    unnamed x30, local copies, waits for them, and re-layouts  9.4 us
    ppermute x4, waiting for transfers between devices, reduce_base(): lax.ppermute(sent, 'tensor', [(i, i ^ bit) for i in range(pieces)])  8.8 us
    ppermute x3, starting transfers between devices, send(): lax.ppermute(block, 'batch', [(i, (i + r) % homes) for i in range(homes)])  6.48 us
    pallas_call x1, Pallas kernels, pack(): pl.pallas_call(functools.partial(pack_kernel, span, shifts), out_shape=[j...  6.46 us
    ppermute x3, starting transfers between devices, gather_up(): lax.ppermute(own, 'batch', [(i, (i - r) % homes) for i in range(homes)])  6.06 us
  transfers between devices with their start and end apart: 20, of which 8 were waited for; matrix products, arithmetic and copies ran while one was open for 7% of the time, Pallas kernels for 19%

profile of v9, /device:TPU:0, one launch (start us, length us, event | category | flops | bytes accessed | tf_op | source)
XLA Modules:
  0.0 123.2 jit_solution(1604058974985618134)
XLA Ops:
  0.0 0.9 copy-done
  1.0 0.7 constant_dynamic-slice_fusion
  1.6 5.0 %collective-permute-start = (bf16[8,32,256]{2,1,0:T(8,128)(2,1)}, bf16[8,32,256]{2,1,0:T(8,128)(2,1)S(1)}, u32[]{:S(2)}, u32[]{:S(2)}) collective-permute-start(bf16[8,32,256]{2,1,0:T(8,128)(2,1)} %constant_dynamic-slice_fusion), channel_id=1, source_target_pairs={{0,12},{4,0},{8,4},{12,8},{1,13},{5,1},{9,5},{13,9},{2,14},{6,2},{... | collective-permute-start | bytes 393224 | tf_op jit(solution)/shard_map/ppermute | solution.py:192
  6.7 1.0 collective-permute-start.2
  7.7 1.7 %route.1 = (s32[1,768]{1,0:T(1,128)}, s32[8,128]{1,0:T(8,128)}) custom-call(s32[1]{0:T(128)} %bitcast.place_ref, s32[32]{0:T(128)} %entry_hbm.1, s32[768]{0:T(1024)} %request_hbm.1), custom_call_target="tpu_custom_call" | custom-call | flops 1 | bytes 1 | tf_op jit(solution)/shard_map/route/pallas_call | solution.py:273
  9.4 6.5 %pack.1 = (s32[8,128]{1,0:T(8,128)}, bf16[216,2048]{1,0:T(8,128)(2,1)}, bf16[216,2048]{1,0:T(8,128)(2,1)}, bf16[216,2048]{1,0:T(8,128)(2,1)}, bf16[216,2048]{1,0:T(8,128)(2,1)}) custom-call(s32[1,768]{1,0:T(1,128)} %get-tuple-element.20.index_ref, bf16[768,2048]{1,0:T(8,128)(2,1)} %tokens_ref.9), custom_call_target="tpu_custom_call" | custom-call | flops 1 | bytes 1 | tf_op jit(solution)/shard_map/pack/pallas_call | solution.py:291
  15.9 2.3 %collective-permute-done.1.refs_4_ = bf16[8,32,256]{2,1,0:T(8,128)(2,1)} collective-permute-done((bf16[8,32,256]{2,1,0:T(8,128)(2,1)}, bf16[8,32,256]{2,1,0:T(8,128)(2,1)}, u32[]{:S(2)}, u32[]{:S(2)}) %collective-permute-start.1) | collective-permute-done | bytes 131104 | tf_op jit(solution)/shard_map/ppermute | solution.py:192
  18.2 0.6 gate.1
  18.8 2.6 %collective-permute-start.10 = (bf16[216,2048]{1,0:T(8,128)(2,1)}, bf16[216,2048]{1,0:T(8,128)(2,1)}, u32[]{:S(2)}, u32[]{:S(2)}) collective-permute-start(bf16[216,2048]{1,0:T(8,128)(2,1)} %get-tuple-element.27), channel_id=1, source_target_pairs={{0,8},{4,12},{8,0},{12,4},{1,9},{5,13},{9,1},{13,5},{2,10},{6,14},... | collective-permute-start | bytes 2654216 | tf_op jit(solution)/shard_map/ppermute | solution.py:306
  21.4 2.2 %copy-done.2 = bf16[2048,1024]{1,0:T(8,128)(2,1)S(1)} copy-done((bf16[2048,1024]{1,0:T(8,128)(2,1)S(1)}, bf16[2048,1024]{1,0:T(8,128)(2,1)}, u32[]{:S(2)}) %copy-start.2) | copy-done | bytes 4194328
  23.6 0.7 copy-done.8
  24.3 2.8 %base.4.refs_0_ = f32[384,512]{1,0:T(8,128)} custom-call(s32[2]{0:T(128)S(1)} %broadcast_xor_fusion.block_ref, bf16[768,2048]{1,0:T(8,128)(2,1)S(1)} %copy-done.1, bf16[2048,1024]{1,0:T(8,128)(2,1)S(1)} %copy-done.2, s32[8,128]{1,0:T(8,128)S(1)} %copy-done.8), custom_call_target="tpu_custom_call" | custom-call | flops 1 | bytes 1 | tf_op jit(solution)/shard_map/base/pallas_call | solution.py:219
  27.1 2.8 %base.6.refs_0_ = f32[384,512]{1,0:T(8,128)} custom-call(s32[2]{0:T(128)S(1)} %broadcast_xor_fusion.block_ref, bf16[768,2048]{1,0:T(8,128)(2,1)S(1)} %copy-done.1, bf16[2048,1024]{1,0:T(8,128)(2,1)S(1)} %copy-done.2, s32[8,128]{1,0:T(8,128)S(1)} %copy-done.8), custom_call_target="tpu_custom_call" | custom-call | flops 1 | bytes 1 | tf_op jit(solution)/shard_map/base/pallas_call | solution.py:219
  30.0 0.5 collective-permute-start.5
  30.5 1.3 %slice.51 = s32[1,1]{1,0:T(1,128)} slice(s32[8,128]{1,0:T(8,128)} %get-tuple-element.19), slice={[0:1], [0:1]} | slice | bytes 8 | tf_op jit(solution)/shard_map/slice | solution.py:314
  34.6 0.1 pad_add_fusion.scalar_ref
  34.6 2.2 %copy-done.4 = bf16[8,2048,128]{2,1,0:T(8,128)(2,1)S(1)} copy-done((bf16[8,2048,128]{2,1,0:T(8,128)(2,1)S(1)}, bf16[8,2048,128]{2,1,0:T(8,128)(2,1)}, u32[]{:S(2)}) %copy-start.4) | copy-done | bytes 4194328
  36.8 1.2 copy-done.7
  38.0 1.4 %shrink.4 = f32[240,128]{1,0:T(8,128)S(1)} custom-call(s32[3]{0:T(128)S(1)} %pad_add_fusion.scalar_ref, bf16[216,2048]{1,0:T(8,128)(2,1)S(1)} %copy-done.7, bf16[8,2048,128]{2,1,0:T(8,128)(2,1)S(1)} %copy-done.4, s32[8,128]{1,0:T(8,128)S(1)} %copy-done.9), custom_call_target="tpu_custom_call" | custom-call | flops 1 | bytes 1 | tf_op jit(solution)/shard_map/shrink/pallas_call | solution.py:320
  40.1 0.9 copy.13.index_ref
  41.1 0.9 add.50
  42.0 1.6 %collective-permute-start.14 = (f32[120,128]{1,0:T(8,128)S(1)}, f32[120,128]{1,0:T(8,128)S(1)}, u32[]{:S(2)}, u32[]{:S(2)}) collective-permute-start(f32[120,128]{1,0:T(8,128)S(1)} %slice.79), channel_id=1, source_target_pairs={{0,2},{1,3},{2,0},{3,1},{4,6},{5,7},{6,4},{7,5},{8,10},{9,11},{10,... | collective-permute-start | bytes 184328 | tf_op jit(solution)/shard_map/ppermute | solution.py:338
  43.6 2.2 %copy-done.3 = bf16[2048,1024]{1,0:T(8,128)(2,1)S(1)} copy-done((bf16[2048,1024]{1,0:T(8,128)(2,1)S(1)}, bf16[2048,1024]{1,0:T(8,128)(2,1)}, u32[]{:S(2)}) %copy-start.3) | copy-done | bytes 4194328
  45.7 2.1 %base.5 = f32[384,512]{1,0:T(8,128)S(1)} custom-call(s32[2]{0:T(128)S(1)} %multiply_xor_fusion.block_ref, bf16[768,2048]{1,0:T(8,128)(2,1)S(1)} %copy-done.1, bf16[2048,1024]{1,0:T(8,128)(2,1)S(1)} %copy-done.3, f32[384,512]{1,0:T(8,128)} %base.4.refs_0_), custom_call_target="tpu_custom_call" | custom-call | flops 1 | bytes 1 | tf_op jit(solution)/shard_map/base/pallas_call | solution.py:219
  47.8 2.1 %base.7 = f32[384,512]{1,0:T(8,128)S(1)} custom-call(s32[2]{0:T(128)S(1)} %multiply_xor_fusion.block_ref, bf16[768,2048]{1,0:T(8,128)(2,1)S(1)} %copy-done.1, bf16[2048,1024]{1,0:T(8,128)(2,1)S(1)} %copy-done.3, f32[384,512]{1,0:T(8,128)} %base.6.refs_0_), custom_call_target="tpu_custom_call" | custom-call | flops 1 | bytes 1 | tf_op jit(solution)/shard_map/base/pallas_call | solution.py:219
  50.0 3.8 %collective-permute-start.9 = (bf16[216,2048]{1,0:T(8,128)(2,1)S(1)}, bf16[216,2048]{1,0:T(8,128)(2,1)S(1)}, u32[]{:S(2)}, u32[]{:S(2)}) collective-permute-start(bf16[216,2048]{1,0:T(8,128)(2,1)S(1)} %copy-done.13), channel_id=1, source_target_pairs={{0,12},{4,0},{8,4},{12,8},{1,13},{5,1},{9,5},{13,9},{2,14},{6,2},{... | collective-permute-start | bytes 2654216 | tf_op jit(solution)/shard_map/ppermute | solution.py:306
  53.8 1.3 %add.44 = f32[384,512]{1,0:T(8,128)S(1)} add(f32[384,512]{1,0:T(8,128)S(1)} %base.5, f32[384,512]{1,0:T(8,128)} %collective-permute-done.3) | non-fusion elementwise | flops 196608 | bytes 2359296 | tf_op jit(solution)/shard_map/add | solution.py:249
  55.1 1.3 %add.46 = f32[384,512]{1,0:T(8,128)S(1)} add(f32[384,512]{1,0:T(8,128)S(1)} %base.7, f32[384,512]{1,0:T(8,128)} %collective-permute-done.5) | non-fusion elementwise | flops 196608 | bytes 2359296 | tf_op jit(solution)/shard_map/add | solution.py:249
  56.4 22.6 %collective-permute-done.10.refs_0_ = bf16[216,2048]{1,0:T(8,128)(2,1)} collective-permute-done((bf16[216,2048]{1,0:T(8,128)(2,1)}, bf16[216,2048]{1,0:T(8,128)(2,1)}, u32[]{:S(2)}, u32[]{:S(2)}) %collective-permute-start.10) | collective-permute-done | bytes 884768 | tf_op jit(solution)/shard_map/ppermute | solution.py:306
  79.0 2.0 %shrink.3 = f32[240,128]{1,0:T(8,128)S(1)} custom-call(s32[3]{0:T(128)S(1)} %pad_add_fusion.scalar_ref, bf16[216,2048]{1,0:T(8,128)(2,1)} %collective-permute-done.10.refs_0_, bf16[8,2048,128]{2,1,0:T(8,128)(2,1)S(1)} %copy-done.5, f32[8,512]{1,0:T(8,128)S(1)} %slice.74.refs_2_, f32[8,512]{1,0:T(8,128)S(1)} %slice.75.refs_3_), custom_call_target="tpu_custom_call" | custom-call | flops 1 | bytes 1 | tf_op jit(solution)/shard_map/shrink/pallas_call | solution.py:320
  81.1 1.1 pad_maximum_fusion.2
  82.2 1.6 %collective-permute-start.7 = (bf16[32,32,256]{2,1,0:T(8,128)(2,1)S(1)}, bf16[32,32,256]{2,1,0:T(8,128)(2,1)S(1)}, u32[]{:S(2)}, u32[]{:S(2)}) collective-permute-start(bf16[32,32,256]{2,1,0:T(8,128)(2,1)S(1)} %pad_maximum_fusion.2), channel_id=1, source_target_pairs={{0,16},{16,0},{1,17},{17,1},{2,18},{18,2},{3,19},{19,3},{4,20},{20... | collective-permute-start | bytes 1572872 | tf_op jit(solution)/shard_map/ppermute | solution.py:196
  83.8 1.6 %collective-permute-start.4 = (f32[384,256]{1,0:T(8,128)S(1)}, f32[384,256]{1,0:T(8,128)S(1)}, u32[]{:S(2)}, u32[]{:S(2)}) collective-permute-start(f32[384,256]{1,0:T(8,128)S(1)} %slice.69), channel_id=1, source_target_pairs={{0,2},{1,3},{2,0},{3,1},{4,6},{5,7},{6,4},{7,5},{8,10},{9,11},{10,... | collective-permute-start | bytes 1179656 | tf_op jit(solution)/shard_map/ppermute | solution.py:249
  85.4 0.6 collective-permute-start.12
  86.0 10.4 %collective-permute-done.12 = f32[120,128]{1,0:T(8,128)S(1)} collective-permute-done((f32[120,128]{1,0:T(8,128)S(1)}, f32[120,128]{1,0:T(8,128)S(1)}, u32[]{:S(2)}, u32[]{:S(2)}) %collective-permute-start.12) | collective-permute-done | bytes 61472 | tf_op jit(solution)/shard_map/ppermute | solution.py:338
  96.4 1.5 %collective-permute-start.6 = (f32[384,256]{1,0:T(8,128)S(1)}, f32[384,256]{1,0:T(8,128)S(1)}, u32[]{:S(2)}, u32[]{:S(2)}) collective-permute-start(f32[384,256]{1,0:T(8,128)S(1)} %slice.71), channel_id=1, source_target_pairs={{0,2},{1,3},{2,0},{3,1},{4,6},{5,7},{6,4},{7,5},{8,10},{9,11},{10,... | collective-permute-start | bytes 1179656 | tf_op jit(solution)/shard_map/ppermute | solution.py:249
  98.0 8.8 %collective-permute-done.6 = f32[384,256]{1,0:T(8,128)S(1)} collective-permute-done((f32[384,256]{1,0:T(8,128)S(1)}, f32[384,256]{1,0:T(8,128)S(1)}, u32[]{:S(2)}, u32[]{:S(2)}) %collective-permute-start.6) | collective-permute-done | bytes 393248 | tf_op jit(solution)/shard_map/ppermute | solution.py:249
  106.9 1.4 %shrink.5 = (f32[480,128]{1,0:T(8,128)S(1)}, f32[120,128]{1,0:T(8,128)S(1)}, f32[120,128]{1,0:T(8,128)S(1)}) custom-call(s32[3]{0:T(128)S(1)} %pad_add_fusion.scalar_ref, bf16[216,2048]{1,0:T(8,128)(2,1)S(1)} %collective-permute-done.8.refs_0_, bf16[216,2048]{1,0:T(8,128)(2,1)S(1)} %collective-permute-done.9.refs_1_, bf16[8,2048,128]{2,1,0:T(8,128)(2,1)S(1)} %copy-done.5, ...), custom_call_target="tpu_custom_call" | custom-call | flops 1 | bytes 1 | tf_op jit(solution)/shard_map/shrink/pallas_call | solution.py:320
  108.4 1.1 broadcast_select_fusion.1
  109.6 0.3 collective-permute-done.16
  110.0 1.6 %collective-permute-start.17 = (f32[240,128]{1,0:T(8,128)S(1)}, f32[240,128]{1,0:T(8,128)S(1)}, u32[]{:S(2)}, u32[]{:S(2)}) collective-permute-start(f32[240,128]{1,0:T(8,128)S(1)} %slice.81), channel_id=1, source_target_pairs={{0,2},{1,3},{2,0},{3,1},{4,6},{5,7},{6,4},{7,5},{8,10},{9,11},{10,... | collective-permute-start | bytes 368648 | tf_op jit(solution)/shard_map/ppermute | solution.py:338
  111.5 0.1 pad_maximum_fusion.up_ref
  111.7 3.7 %collective-permute-done.17 = f32[240,128]{1,0:T(8,128)S(1)} collective-permute-done((f32[240,128]{1,0:T(8,128)S(1)}, f32[240,128]{1,0:T(8,128)S(1)}, u32[]{:S(2)}, u32[]{:S(2)}) %collective-permute-start.17) | collective-permute-done | bytes 122912 | tf_op jit(solution)/shard_map/ppermute | solution.py:338
  115.5 2.0 %collective-permute-start.19 = (f32[120,128]{1,0:T(8,128)S(1)}, f32[120,128]{1,0:T(8,128)S(1)}, u32[]{:S(2)}, u32[]{:S(2)}) collective-permute-start(f32[120,128]{1,0:T(8,128)S(1)} %get-tuple-element.35), channel_id=1, source_target_pairs={{0,4},{4,8},{8,12},{12,0},{1,5},{5,9},{9,13},{13,1},{2,6},{6,10},{... | collective-permute-start | bytes 184328 | tf_op jit(solution)/shard_map/ppermute | solution.py:357
  117.6 0.9 finish.2.base_ref
  118.5 1.9 %collective-permute-done.18.refs_0_ = f32[120,128]{1,0:T(8,128)S(1)} collective-permute-done((f32[120,128]{1,0:T(8,128)S(1)}, f32[120,128]{1,0:T(8,128)S(1)}, u32[]{:S(2)}, u32[]{:S(2)}) %collective-permute-start.18) | collective-permute-done | bytes 61472 | tf_op jit(solution)/shard_map/ppermute | solution.py:357
  120.4 1.2 collective-permute-done.19.refs_1_
  121.6 1.6 %finish.3 = bf16[768,256]{1,0:T(8,128)(2,1)} custom-call(s32[1]{0:T(128)} %bitcast.2.place_ref, s32[768,1]{1,0:T(8,128)S(1)} %copy-done.6, f32[768,256]{1,0:T(8,128)S(1)} %finish.2.base_ref, bf16[32,64,256]{2,1,0:T(8,128)(2,1)S(1)} %pad_maximum_fusion.up_ref, f32[120,128]{1,0:T(8,128)S(1)} %collective-permute-done.18.refs_0_, ...), custom_call_target="tpu_custom_call" | custom-call | flops 1 | bytes 1 | tf_op jit(solution)/shard_map/finish/pallas_call | solution.py:156
  (64 shorter events, 0.8 us)
Async XLA Ops:
  0.0 1.0 copy-start
  1.6 19.8 %copy-start.1 = (bf16[768,2048]{1,0:T(8,128)(2,1)S(1)}, bf16[768,2048]{1,0:T(8,128)(2,1)}, u32[]{:S(2)}) copy-start(bf16[768,2048]{1,0:T(8,128)(2,1)} %tokens_ref.9) | copy-start | bytes 9437188
  1.6 14.3 %collective-permute-start = (bf16[8,32,256]{2,1,0:T(8,128)(2,1)}, bf16[8,32,256]{2,1,0:T(8,128)(2,1)S(1)}, u32[]{:S(2)}, u32[]{:S(2)}) collective-permute-start(bf16[8,32,256]{2,1,0:T(8,128)(2,1)} %constant_dynamic-slice_fusion), channel_id=1, source_target_pairs={{0,12},{4,0},{8,4},{12,8},{1,13},{5,1},{9,5},{13,9},{2,14},{6,2},{... | collective-permute-start | bytes 393224 | tf_op jit(solution)/shard_map/ppermute | solution.py:192
  6.7 11.5 %collective-permute-start.1 = (bf16[8,32,256]{2,1,0:T(8,128)(2,1)}, bf16[8,32,256]{2,1,0:T(8,128)(2,1)}, u32[]{:S(2)}, u32[]{:S(2)}) collective-permute-start(bf16[8,32,256]{2,1,0:T(8,128)(2,1)} %constant_dynamic-slice_fusion), channel_id=1, source_target_pairs={{0,8},{4,12},{8,0},{12,4},{1,9},{5,13},{9,1},{13,5},{2,10},{6,14},... | collective-permute-start | bytes 393224 | tf_op jit(solution)/shard_map/ppermute | solution.py:192
  6.7 11.5 %collective-permute-start.2 = (bf16[8,32,256]{2,1,0:T(8,128)(2,1)}, bf16[8,32,256]{2,1,0:T(8,128)(2,1)}, u32[]{:S(2)}, u32[]{:S(2)}) collective-permute-start(bf16[8,32,256]{2,1,0:T(8,128)(2,1)} %constant_dynamic-slice_fusion), channel_id=1, source_target_pairs={{0,4},{4,8},{8,12},{12,0},{1,5},{5,9},{9,13},{13,1},{2,6},{6,10},{... | collective-permute-start | bytes 393224 | tf_op jit(solution)/shard_map/ppermute | solution.py:192
  15.9 2.3 %copy-start.10 = (bf16[8,32,256]{2,1,0:T(8,128)(2,1)}, bf16[8,32,256]{2,1,0:T(8,128)(2,1)S(1)}, u32[]{:S(2)}) copy-start(bf16[8,32,256]{2,1,0:T(8,128)(2,1)S(1)} %collective-permute-done.refs_3_) | copy-start | bytes 393220
  18.8 60.2 %collective-permute-start.10 = (bf16[216,2048]{1,0:T(8,128)(2,1)}, bf16[216,2048]{1,0:T(8,128)(2,1)}, u32[]{:S(2)}, u32[]{:S(2)}) collective-permute-start(bf16[216,2048]{1,0:T(8,128)(2,1)} %get-tuple-element.27), channel_id=1, source_target_pairs={{0,8},{4,12},{8,0},{12,4},{1,9},{5,13},{9,1},{13,5},{2,10},{6,14},... | collective-permute-start | bytes 2654216 | tf_op jit(solution)/shard_map/ppermute | solution.py:306
  21.4 2.2 %copy-start.2 = (bf16[2048,1024]{1,0:T(8,128)(2,1)S(1)}, bf16[2048,1024]{1,0:T(8,128)(2,1)}, u32[]{:S(2)}) copy-start(bf16[2048,1024]{1,0:T(8,128)(2,1)} %weight_ref.7) | copy-start | bytes 12582916
  23.6 0.7 copy-start.8
  27.1 7.5 %copy-start.9 = (s32[8,128]{1,0:T(8,128)S(1)}, s32[8,128]{1,0:T(8,128)}, u32[]{:S(2)}) copy-start(s32[8,128]{1,0:T(8,128)} %get-tuple-element.29.refs_2_) | copy-start | bytes 12292
  27.1 22.8 %collective-permute-start.3 = (f32[384,512]{1,0:T(8,128)}, f32[384,512]{1,0:T(8,128)}, u32[]{:S(2)}, u32[]{:S(2)}) collective-permute-start(f32[384,512]{1,0:T(8,128)} %base.4.refs_0_), channel_id=1, source_target_pairs={{0,1},{1,0},{2,3},{3,2},{4,5},{5,4},{6,7},{7,6},{8,9},{9,8},{10,11... | collective-permute-start | bytes 2359304 | tf_op jit(solution)/shard_map/ppermute | solution.py:249
  30.0 10.1 %copy-start.14 = (s32[1,768]{1,0:T(1,128)S(1)}, s32[1,768]{1,0:T(1,128)}, u32[]{:S(2)}) copy-start(s32[1,768]{1,0:T(1,128)} %get-tuple-element.20.index_ref) | copy-start | bytes 9220
  30.0 25.1 %collective-permute-start.5 = (f32[384,512]{1,0:T(8,128)}, f32[384,512]{1,0:T(8,128)}, u32[]{:S(2)}, u32[]{:S(2)}) collective-permute-start(f32[384,512]{1,0:T(8,128)} %base.6.refs_0_), channel_id=1, source_target_pairs={{0,1},{1,0},{2,3},{3,2},{4,5},{5,4},{6,7},{7,6},{8,9},{9,8},{10,11... | collective-permute-start | bytes 2359304 | tf_op jit(solution)/shard_map/ppermute | solution.py:249
  34.6 2.2 %copy-start.4 = (bf16[8,2048,128]{2,1,0:T(8,128)(2,1)S(1)}, bf16[8,2048,128]{2,1,0:T(8,128)(2,1)}, u32[]{:S(2)}) copy-start(bf16[8,2048,128]{2,1,0:T(8,128)(2,1)} %refs_2_.1) | copy-start | bytes 12582916
  36.8 1.2 copy-start.7
  39.4 1.7 %collective-permute-start.13 = (f32[240,128]{1,0:T(8,128)S(1)}, f32[240,128]{1,0:T(8,128)}, u32[]{:S(2)}, u32[]{:S(2)}) collective-permute-start(f32[240,128]{1,0:T(8,128)S(1)} %shrink.4), channel_id=1, source_target_pairs={{0,1},{1,0},{2,3},{3,2},{4,5},{5,4},{6,7},{7,6},{8,9},{9,8},{10,11... | collective-permute-start | bytes 368648 | tf_op jit(solution)/shard_map/ppermute | solution.py:336
  42.0 43.4 %collective-permute-start.14 = (f32[120,128]{1,0:T(8,128)S(1)}, f32[120,128]{1,0:T(8,128)S(1)}, u32[]{:S(2)}, u32[]{:S(2)}) collective-permute-start(f32[120,128]{1,0:T(8,128)S(1)} %slice.79), channel_id=1, source_target_pairs={{0,2},{1,3},{2,0},{3,1},{4,6},{5,7},{6,4},{7,5},{8,10},{9,11},{10,... | collective-permute-start | bytes 184328 | tf_op jit(solution)/shard_map/ppermute | solution.py:338
  43.6 2.2 %copy-start.3 = (bf16[2048,1024]{1,0:T(8,128)(2,1)S(1)}, bf16[2048,1024]{1,0:T(8,128)(2,1)}, u32[]{:S(2)}) copy-start(bf16[2048,1024]{1,0:T(8,128)(2,1)} %weight_ref.7) | copy-start | bytes 12582916
  47.8 2.1 %copy-start.12 = (bf16[216,2048]{1,0:T(8,128)(2,1)S(1)}, bf16[216,2048]{1,0:T(8,128)(2,1)}, u32[]{:S(2)}) copy-start(bf16[216,2048]{1,0:T(8,128)(2,1)} %get-tuple-element.25) | copy-start | bytes 2654212
  47.8 2.2 %copy-start.13 = (bf16[216,2048]{1,0:T(8,128)(2,1)S(1)}, bf16[216,2048]{1,0:T(8,128)(2,1)}, u32[]{:S(2)}) copy-start(bf16[216,2048]{1,0:T(8,128)(2,1)} %get-tuple-element.26) | copy-start | bytes 2654212
  49.9 29.1 %copy-start.5 = (bf16[8,2048,128]{2,1,0:T(8,128)(2,1)S(1)}, bf16[8,2048,128]{2,1,0:T(8,128)(2,1)}, u32[]{:S(2)}) copy-start(bf16[8,2048,128]{2,1,0:T(8,128)(2,1)} %refs_2_.1) | copy-start | bytes 12582916
  49.9 57.0 %collective-permute-start.8 = (bf16[216,2048]{1,0:T(8,128)(2,1)S(1)}, bf16[216,2048]{1,0:T(8,128)(2,1)S(1)}, u32[]{:S(2)}, u32[]{:S(2)}) collective-permute-start(bf16[216,2048]{1,0:T(8,128)(2,1)S(1)} %copy-done.12), channel_id=1, source_target_pairs={{0,4},{4,8},{8,12},{12,0},{1,5},{5,9},{9,13},{13,1},{2,6},{6,10},{... | collective-permute-start | bytes 2654216 | tf_op jit(solution)/shard_map/ppermute | solution.py:306
  50.0 56.9 %collective-permute-start.9 = (bf16[216,2048]{1,0:T(8,128)(2,1)S(1)}, bf16[216,2048]{1,0:T(8,128)(2,1)S(1)}, u32[]{:S(2)}, u32[]{:S(2)}) collective-permute-start(bf16[216,2048]{1,0:T(8,128)(2,1)S(1)} %copy-done.13), channel_id=1, source_target_pairs={{0,12},{4,0},{8,4},{12,8},{1,13},{5,1},{9,5},{13,9},{2,14},{6,2},{... | collective-permute-start | bytes 2654216 | tf_op jit(solution)/shard_map/ppermute | solution.py:306
  56.4 24.7 %copy-start.11 = (bf16[8,32,256]{2,1,0:T(8,128)(2,1)S(1)}, bf16[8,32,256]{2,1,0:T(8,128)(2,1)}, u32[]{:S(2)}) copy-start(bf16[8,32,256]{2,1,0:T(8,128)(2,1)} %copy-done.10) | copy-start | bytes 393220
  81.0 2.8 %collective-permute-start.11 = (f32[240,128]{1,0:T(8,128)S(1)}, f32[240,128]{1,0:T(8,128)S(1)}, u32[]{:S(2)}, u32[]{:S(2)}) collective-permute-start(f32[240,128]{1,0:T(8,128)S(1)} %shrink.3), channel_id=1, source_target_pairs={{0,1},{1,0},{2,3},{3,2},{4,5},{5,4},{6,7},{7,6},{8,9},{9,8},{10,11... | collective-permute-start | bytes 368648 | tf_op jit(solution)/shard_map/ppermute | solution.py:336
  82.2 26.3 %collective-permute-start.7 = (bf16[32,32,256]{2,1,0:T(8,128)(2,1)S(1)}, bf16[32,32,256]{2,1,0:T(8,128)(2,1)S(1)}, u32[]{:S(2)}, u32[]{:S(2)}) collective-permute-start(bf16[32,32,256]{2,1,0:T(8,128)(2,1)S(1)} %pad_maximum_fusion.2), channel_id=1, source_target_pairs={{0,16},{16,0},{1,17},{17,1},{2,18},{18,2},{3,19},{19,3},{4,20},{20... | collective-permute-start | bytes 1572872 | tf_op jit(solution)/shard_map/ppermute | solution.py:196
  83.8 14.1 %collective-permute-start.4 = (f32[384,256]{1,0:T(8,128)S(1)}, f32[384,256]{1,0:T(8,128)S(1)}, u32[]{:S(2)}, u32[]{:S(2)}) collective-permute-start(f32[384,256]{1,0:T(8,128)S(1)} %slice.69), channel_id=1, source_target_pairs={{0,2},{1,3},{2,0},{3,1},{4,6},{5,7},{6,4},{7,5},{8,10},{9,11},{10,... | collective-permute-start | bytes 1179656 | tf_op jit(solution)/shard_map/ppermute | solution.py:249
  85.4 11.0 %collective-permute-start.12 = (f32[120,128]{1,0:T(8,128)S(1)}, f32[120,128]{1,0:T(8,128)S(1)}, u32[]{:S(2)}, u32[]{:S(2)}) collective-permute-start(f32[120,128]{1,0:T(8,128)S(1)} %slice.77), channel_id=1, source_target_pairs={{0,2},{1,3},{2,0},{3,1},{4,6},{5,7},{6,4},{7,5},{8,10},{9,11},{10,... | collective-permute-start | bytes 184328 | tf_op jit(solution)/shard_map/ppermute | solution.py:338
  96.4 10.4 %collective-permute-start.6 = (f32[384,256]{1,0:T(8,128)S(1)}, f32[384,256]{1,0:T(8,128)S(1)}, u32[]{:S(2)}, u32[]{:S(2)}) collective-permute-start(f32[384,256]{1,0:T(8,128)S(1)} %slice.71), channel_id=1, source_target_pairs={{0,2},{1,3},{2,0},{3,1},{4,6},{5,7},{6,4},{7,5},{8,10},{9,11},{10,... | collective-permute-start | bytes 1179656 | tf_op jit(solution)/shard_map/ppermute | solution.py:249
  108.3 1.6 %collective-permute-start.16 = (f32[480,128]{1,0:T(8,128)S(1)}, f32[480,128]{1,0:T(8,128)S(1)}, u32[]{:S(2)}, u32[]{:S(2)}) collective-permute-start(f32[480,128]{1,0:T(8,128)S(1)} %get-tuple-element.32), channel_id=1, source_target_pairs={{0,1},{1,0},{2,3},{3,2},{4,5},{5,4},{6,7},{7,6},{8,9},{9,8},{10,11... | collective-permute-start | bytes 737288 | tf_op jit(solution)/shard_map/ppermute | solution.py:336
  109.6 8.0 %copy-start.6 = (s32[768,1]{1,0:T(8,128)S(1)}, s32[768,1]{1,0:T(8,128)}, u32[]{:S(2)}) copy-start(s32[768,1]{1,0:T(8,128)} %copy.13.index_ref) | copy-start | bytes 9220
  110.0 5.5 %collective-permute-start.17 = (f32[240,128]{1,0:T(8,128)S(1)}, f32[240,128]{1,0:T(8,128)S(1)}, u32[]{:S(2)}, u32[]{:S(2)}) collective-permute-start(f32[240,128]{1,0:T(8,128)S(1)} %slice.81), channel_id=1, source_target_pairs={{0,2},{1,3},{2,0},{3,1},{4,6},{5,7},{6,4},{7,5},{8,10},{9,11},{10,... | collective-permute-start | bytes 368648 | tf_op jit(solution)/shard_map/ppermute | solution.py:338
  111.6 6.0 %collective-permute-start.15 = (f32[120,128]{1,0:T(8,128)S(1)}, f32[120,128]{1,0:T(8,128)S(1)}, u32[]{:S(2)}, u32[]{:S(2)}) collective-permute-start(f32[120,128]{1,0:T(8,128)S(1)} %get-tuple-element.30), channel_id=1, source_target_pairs={{0,8},{4,12},{8,0},{12,4},{1,9},{5,13},{9,1},{13,5},{2,10},{6,14},... | collective-permute-start | bytes 184328 | tf_op jit(solution)/shard_map/ppermute | solution.py:357
  115.5 4.9 %collective-permute-start.18 = (f32[120,128]{1,0:T(8,128)S(1)}, f32[120,128]{1,0:T(8,128)S(1)}, u32[]{:S(2)}, u32[]{:S(2)}) collective-permute-start(f32[120,128]{1,0:T(8,128)S(1)} %get-tuple-element.36), channel_id=1, source_target_pairs={{0,12},{4,0},{8,4},{12,8},{1,13},{5,1},{9,5},{13,9},{2,14},{6,2},{... | collective-permute-start | bytes 184328 | tf_op jit(solution)/shard_map/ppermute | solution.py:357
  115.5 6.1 %collective-permute-start.19 = (f32[120,128]{1,0:T(8,128)S(1)}, f32[120,128]{1,0:T(8,128)S(1)}, u32[]{:S(2)}, u32[]{:S(2)}) collective-permute-start(f32[120,128]{1,0:T(8,128)S(1)} %get-tuple-element.35), channel_id=1, source_target_pairs={{0,4},{4,8},{8,12},{12,0},{1,5},{5,9},{9,13},{13,1},{2,6},{6,10},{... | collective-permute-start | bytes 184328 | tf_op jit(solution)/shard_map/ppermute | solution.py:357

commit v10 on v9

--- a/solution.py
+++ b/solution.py
@@ -213,7 +213,7 @@
     refs[waited][...] = jnp.dot(tokens_ref[...], weight_ref[...], preferred_element_type=jnp.float32)
 
 
-def base_part(tokens, weight, blocks, columns, slab, slabs, after):
+def base_part(tokens, weight, blocks, columns, slab, slabs, after, params=PARAMS):
     rows, width = tokens.shape[0] // slabs, tokens.shape[1]
     count = blocks.shape[0]
     return pl.pallas_call(
@@ -229,7 +229,7 @@
             + [ANY] * len(after),
             out_specs=pl.BlockSpec((rows, columns), lambda j, chosen: (0, j)),
         ),
-        compiler_params=PARAMS,
+        compiler_params=params,
         cost_estimate=COST,
         name="base",
     )(blocks, tokens, weight, *after)
@@ -242,7 +242,9 @@
         keep = keep + [p + bit for p in keep]
         bit //= 2
     keep = jnp.array(keep, jnp.int32)
-    sent = base_part(tokens, weight, piece ^ keep ^ 1, columns, slab, slabs, after)
+    sent = base_part(
+        tokens, weight, piece ^ keep ^ 1, columns, slab, slabs, after, PARAMS if slab else WIDE
+    )
     kept = base_part(tokens, weight, piece ^ keep, columns, slab, slabs, [sent])
     bit, first = 1, None
     while True:
@@ -337,7 +339,7 @@
             bit *= 2
         return value[:half] + lax.ppermute(value[half:], "tensor", [(i, i ^ bit) for i in range(pieces)])
 
-    slabs = 2
+    slabs = 3
     slab_sums = [
         reduce_base(tokens, key_value_weight, piece, pieces, columns, slab, slabs, [mark])
         for slab in range(slabs)
@@ -348,7 +350,7 @@
     early = order[:-2] + [0]
     totals = []
     for r in early:
-        (value,) = shrink([arrived[r]], begun if r else [packed], [])
+        (value,) = shrink([arrived[r]], [total[:8] for total, _ in slab_sums[:1]] + begun[1:] if r else [packed], [])
         totals.append(combine(value))
     value, *totals = shrink([arrived[r] for r in late], [base[:8], base[-8:]], totals)
     last = combine(value)

time: 124 us -> 121 us (0.976)
  waiting for transfers between devices: 51.2 us -> 42.2 us
  Pallas kernels: 25.9 us -> 30.6 us
    ppermute x4 -> x6, waiting for transfers between devices: 8.8 us -> 0.02 us  [reduce_base(): lax.ppermute(sent, 'tensor', [(i, i ^ bit) for i in range(pieces)])]
    pallas_call x4 -> x6, Pallas kernels: 9.77 us -> 14.5 us  [base_part(): pl.pallas_call(functools.partial(base_kernel, len(after)), out_shape=jax....]
    ppermute x3, waiting for transfers between devices: 14.1 us -> 10.5 us  [combine(): lax.ppermute(value[half:], 'tensor', [(i, i ^ bit) for i in range(pieces)])]
    ppermute x3, waiting for transfers between devices: 0.35 us -> 2.52 us  [combine(): lax.ppermute(value, 'tensor', [(i, i ^ bit) for i in range(pieces)])]
    add x4 -> x6, other arithmetic: 2.7 us -> 4.61 us  [reduce_base(): kept + lax.ppermute(sent, 'tensor', [(i, i ^ bit) for i in range(pieces)])]
    ppermute x3, waiting for transfers between devices: 3.1 us -> 4.66 us  [give_back(): lax.ppermute(total, 'batch', [(i, (i - r) % homes) for i in range(homes)])]
    ppermute x4 -> x6, starting transfers between devices: 3.56 us -> 5.05 us  [reduce_base(): lax.ppermute(sent, 'tensor', [(i, i ^ bit) for i in range(pieces)])]
    unnamed x30 -> x52, local copies, waits for them, and re-layouts: 9.4 us -> 9.32 us
  transfers between devices with their start and end apart: 20 -> 22, of which waited for: 8 -> 10; matrix products, arithmetic and copies ran while one was open for 7% -> 8% of each run, Pallas kernels for 19% -> 20%
where the time goes in v10:
time: 121 us
  waiting for transfers between devices  42.2 us (35%)
  Pallas kernels  30.6 us (25%)
  starting transfers between devices  24.9 us (21%)
  local copies, waits for them, and re-layouts  12.4 us (10%)
  other arithmetic  6.54 us (5%)
  between operations  3.97 us (3%)
    ppermute x3, waiting for transfers between devices, send(): lax.ppermute(block, 'batch', [(i, (i + r) % homes) for i in range(homes)])  23 us
    pallas_call x6, Pallas kernels, base_part(): pl.pallas_call(functools.partial(base_kernel, len(after)), out_shape=jax....  14.5 us
    ppermute x3, waiting for transfers between devices, combine(): lax.ppermute(value[half:], 'tensor', [(i, i ^ bit) for i in range(pieces)])  10.5 us
    unnamed x52, local copies, waits for them, and re-layouts  9.32 us
    pallas_call x1, Pallas kernels, pack(): pl.pallas_call(functools.partial(pack_kernel, span, shifts), out_shape=[j...  6.47 us
    ppermute x3, starting transfers between devices, send(): lax.ppermute(block, 'batch', [(i, (i + r) % homes) for i in range(homes)])  6.35 us
    ppermute x3, starting transfers between devices, gather_up(): lax.ppermute(own, 'batch', [(i, (i - r) % homes) for i in range(homes)])  6.11 us
    ppermute x6, starting transfers between devices, reduce_base(): lax.ppermute(sent, 'tensor', [(i, i ^ bit) for i in range(pieces)])  5.05 us
  transfers between devices with their start and end apart: 22, of which 10 were waited for; matrix products, arithmetic and copies ran while one was open for 8% of the time, Pallas kernels for 20%

profile of v10, /device:TPU:0, one launch (start us, length us, event | category | flops | bytes accessed | tf_op | source)
XLA Modules:
  0.0 120.6 jit_solution(5040313959444167966)
XLA Ops:
  0.0 0.9 copy-done
  1.0 5.1 %collective-permute-start = (bf16[8,32,256]{2,1,0:T(8,128)(2,1)S(1)}, bf16[8,32,256]{2,1,0:T(8,128)(2,1)S(1)}, u32[]{:S(2)}, u32[]{:S(2)}) collective-permute-start(bf16[8,32,256]{2,1,0:T(8,128)(2,1)S(1)} %constant_dynamic-slice_fusion), channel_id=1, source_target_pairs={{0,12},{4,0},{8,4},{12,8},{1,13},{5,1},{9,5},{13,9},{2,14},{6,2},{... | collective-permute-start | bytes 393224 | tf_op jit(solution)/shard_map/ppermute | solution.py:192
  6.1 1.0 collective-permute-start.2
  7.1 1.7 %route.1 = (s32[1,768]{1,0:T(1,128)}, s32[8,128]{1,0:T(8,128)}) custom-call(s32[1]{0:T(128)} %bitcast.place_ref, s32[32]{0:T(128)} %entry_hbm.1, s32[768]{0:T(1024)} %request_hbm.1), custom_call_target="tpu_custom_call" | custom-call | flops 1 | bytes 1 | tf_op jit(solution)/shard_map/route/pallas_call | solution.py:275
  8.8 6.5 %pack.1 = (s32[8,128]{1,0:T(8,128)}, bf16[216,2048]{1,0:T(8,128)(2,1)}, bf16[216,2048]{1,0:T(8,128)(2,1)}, bf16[216,2048]{1,0:T(8,128)(2,1)}, bf16[216,2048]{1,0:T(8,128)(2,1)}) custom-call(s32[1,768]{1,0:T(1,128)} %get-tuple-element.20.index_ref, bf16[768,2048]{1,0:T(8,128)(2,1)} %tokens_ref.13), custom_call_target="tpu_custom_call" | custom-call | flops 1 | bytes 1 | tf_op jit(solution)/shard_map/pack/pallas_call | solution.py:293
  15.8 1.4 %collective-permute-done.1.refs_4_ = bf16[8,32,256]{2,1,0:T(8,128)(2,1)S(1)} collective-permute-done((bf16[8,32,256]{2,1,0:T(8,128)(2,1)S(1)}, bf16[8,32,256]{2,1,0:T(8,128)(2,1)S(1)}, u32[]{:S(2)}, u32[]{:S(2)}) %collective-permute-start.1) | collective-permute-done | bytes 131104 | tf_op jit(solution)/shard_map/ppermute | solution.py:192
  17.3 0.6 copy-done.17
  18.6 4.1 %base.6.refs_0_ = f32[256,512]{1,0:T(8,128)} custom-call(s32[2]{0:T(128)} %broadcast_xor_fusion.block_ref, bf16[768,2048]{1,0:T(8,128)(2,1)} %tokens_ref.13, bf16[2048,1024]{1,0:T(8,128)(2,1)} %weight_ref.11, s32[8,128]{1,0:T(8,128)} %get-tuple-element.24.refs_0_), custom_call_target="tpu_custom_call" | custom-call | flops 1 | bytes 1 | tf_op jit(solution)/shard_map/base/pallas_call | solution.py:219
  22.7 2.6 %collective-permute-start.12 = (bf16[216,2048]{1,0:T(8,128)(2,1)}, bf16[216,2048]{1,0:T(8,128)(2,1)}, u32[]{:S(2)}, u32[]{:S(2)}) collective-permute-start(bf16[216,2048]{1,0:T(8,128)(2,1)} %get-tuple-element.27), channel_id=1, source_target_pairs={{0,8},{4,12},{8,0},{12,4},{1,9},{5,13},{9,1},{13,5},{2,10},{6,14},... | collective-permute-start | bytes 2654216 | tf_op jit(solution)/shard_map/ppermute | solution.py:308
  25.3 2.2 %copy-done.2 = bf16[2048,1024]{1,0:T(8,128)(2,1)S(1)} copy-done((bf16[2048,1024]{1,0:T(8,128)(2,1)S(1)}, bf16[2048,1024]{1,0:T(8,128)(2,1)}, u32[]{:S(2)}) %copy-start.2) | copy-done | bytes 4194328
  27.5 2.5 %base.10.refs_0_ = f32[256,512]{1,0:T(8,128)} custom-call(s32[2]{0:T(128)S(1)} %copy-done.11, bf16[768,2048]{1,0:T(8,128)(2,1)S(1)} %copy-done.1, bf16[2048,1024]{1,0:T(8,128)(2,1)S(1)} %copy-done.2, s32[8,128]{1,0:T(8,128)S(1)} %copy-done.10), custom_call_target="tpu_custom_call" | custom-call | flops 1 | bytes 1 | tf_op jit(solution)/shard_map/base/pallas_call | solution.py:219
  30.2 2.5 %base.8.refs_0_ = f32[256,512]{1,0:T(8,128)} custom-call(s32[2]{0:T(128)S(1)} %copy-done.11, bf16[768,2048]{1,0:T(8,128)(2,1)S(1)} %copy-done.1, bf16[2048,1024]{1,0:T(8,128)(2,1)S(1)} %copy-done.2, s32[8,128]{1,0:T(8,128)S(1)} %copy-done.10), custom_call_target="tpu_custom_call" | custom-call | flops 1 | bytes 1 | tf_op jit(solution)/shard_map/base/pallas_call | solution.py:219
  33.0 1.3 %slice.58 = s32[1,1]{1,0:T(1,128)} slice(s32[8,128]{1,0:T(8,128)} %get-tuple-element.19), slice={[0:1], [0:1]} | slice | bytes 8 | tf_op jit(solution)/shard_map/slice | solution.py:316
  37.1 2.2 %copy-done.3 = bf16[2048,1024]{1,0:T(8,128)(2,1)S(1)} copy-done((bf16[2048,1024]{1,0:T(8,128)(2,1)S(1)}, bf16[2048,1024]{1,0:T(8,128)(2,1)}, u32[]{:S(2)}) %copy-start.3) | copy-done | bytes 4194328
  39.3 1.0 copy-done.8
  40.3 1.8 %base.7 = f32[256,512]{1,0:T(8,128)S(1)} custom-call(s32[2]{0:T(128)S(1)} %multiply_xor_fusion.block_ref, bf16[768,2048]{1,0:T(8,128)(2,1)S(1)} %copy-done.1, bf16[2048,1024]{1,0:T(8,128)(2,1)S(1)} %copy-done.3, f32[256,512]{1,0:T(8,128)S(1)} %copy-done.8), custom_call_target="tpu_custom_call" | custom-call | flops 1 | bytes 1 | tf_op jit(solution)/shard_map/base/pallas_call | solution.py:219
  42.1 1.1 add.50
  43.3 0.8 slice.78
  44.1 1.5 %collective-permute-start.4 = (f32[256,256]{1,0:T(8,128)}, f32[256,256]{1,0:T(8,128)}, u32[]{:S(2)}, u32[]{:S(2)}) collective-permute-start(f32[256,256]{1,0:T(8,128)} %slice.78), channel_id=1, source_target_pairs={{0,2},{1,3},{2,0},{3,1},{4,6},{5,7},{6,4},{7,5},{8,10},{9,11},{10,... | collective-permute-start | bytes 786440 | tf_op jit(solution)/shard_map/ppermute | solution.py:251
  45.6 1.4 %shrink.4 = f32[240,128]{1,0:T(8,128)S(1)} custom-call(s32[3]{0:T(128)S(1)} %pad_add_fusion.scalar_ref, bf16[216,2048]{1,0:T(8,128)(2,1)S(1)} %copy-done.9, bf16[8,2048,128]{2,1,0:T(8,128)(2,1)S(1)} %copy-done.5, s32[8,128]{1,0:T(8,128)S(1)} %copy-done.12), custom_call_target="tpu_custom_call" | custom-call | flops 1 | bytes 1 | tf_op jit(solution)/shard_map/shrink/pallas_call | solution.py:322
  47.8 0.9 copy.14.index_ref
  48.7 0.9 add.58
  49.7 0.6 collective-permute-start.16
  50.3 2.2 %copy-done.4 = bf16[2048,1024]{1,0:T(8,128)(2,1)S(1)} copy-done((bf16[2048,1024]{1,0:T(8,128)(2,1)S(1)}, bf16[2048,1024]{1,0:T(8,128)(2,1)}, u32[]{:S(2)}) %copy-start.4) | copy-done | bytes 4194328
  52.5 1.8 %base.9 = f32[256,512]{1,0:T(8,128)S(1)} custom-call(s32[2]{0:T(128)S(1)} %multiply_xor_fusion.block_ref, bf16[768,2048]{1,0:T(8,128)(2,1)S(1)} %copy-done.1, bf16[2048,1024]{1,0:T(8,128)(2,1)S(1)} %copy-done.4, f32[256,512]{1,0:T(8,128)} %base.8.refs_0_), custom_call_target="tpu_custom_call" | custom-call | flops 1 | bytes 1 | tf_op jit(solution)/shard_map/base/pallas_call | solution.py:219
  54.3 1.8 %base.11 = f32[256,512]{1,0:T(8,128)S(1)} custom-call(s32[2]{0:T(128)S(1)} %multiply_xor_fusion.block_ref, bf16[768,2048]{1,0:T(8,128)(2,1)S(1)} %copy-done.1, bf16[2048,1024]{1,0:T(8,128)(2,1)S(1)} %copy-done.4, f32[256,512]{1,0:T(8,128)} %base.10.refs_0_), custom_call_target="tpu_custom_call" | custom-call | flops 1 | bytes 1 | tf_op jit(solution)/shard_map/base/pallas_call | solution.py:219
  56.3 1.3 %add.54 = f32[256,512]{1,0:T(8,128)S(1)} add(f32[256,512]{1,0:T(8,128)S(1)} %base.11, f32[256,512]{1,0:T(8,128)} %collective-permute-done.7) | non-fusion elementwise | flops 131072 | bytes 1572864 | tf_op jit(solution)/shard_map/add | solution.py:251
  57.7 3.7 %collective-permute-start.11 = (bf16[216,2048]{1,0:T(8,128)(2,1)S(1)}, bf16[216,2048]{1,0:T(8,128)(2,1)S(1)}, u32[]{:S(2)}, u32[]{:S(2)}) collective-permute-start(bf16[216,2048]{1,0:T(8,128)(2,1)S(1)} %copy-done.24), channel_id=1, source_target_pairs={{0,12},{4,0},{8,4},{12,8},{1,13},{5,1},{9,5},{13,9},{2,14},{6,2},{... | collective-permute-start | bytes 2654216 | tf_op jit(solution)/shard_map/ppermute | solution.py:308
  61.4 1.1 add.52
  62.5 1.6 %collective-permute-start.8 = (f32[256,256]{1,0:T(8,128)S(1)}, f32[256,256]{1,0:T(8,128)S(1)}, u32[]{:S(2)}, u32[]{:S(2)}) collective-permute-start(f32[256,256]{1,0:T(8,128)S(1)} %slice.82), channel_id=1, source_target_pairs={{0,2},{1,3},{2,0},{3,1},{4,6},{5,7},{6,4},{7,5},{8,10},{9,11},{10,... | collective-permute-start | bytes 786440 | tf_op jit(solution)/shard_map/ppermute | solution.py:251
  64.1 1.0 slice_add_fusion.2
  65.1 19.3 %collective-permute-done.12.refs_0_ = bf16[216,2048]{1,0:T(8,128)(2,1)} collective-permute-done((bf16[216,2048]{1,0:T(8,128)(2,1)}, bf16[216,2048]{1,0:T(8,128)(2,1)}, u32[]{:S(2)}, u32[]{:S(2)}) %collective-permute-start.12) | collective-permute-done | bytes 884768 | tf_op jit(solution)/shard_map/ppermute | solution.py:308
  84.3 1.5 %collective-permute-start.9 = (bf16[32,32,256]{2,1,0:T(8,128)(2,1)S(1)}, bf16[32,32,256]{2,1,0:T(8,128)(2,1)S(1)}, u32[]{:S(2)}, u32[]{:S(2)}) collective-permute-start(bf16[32,32,256]{2,1,0:T(8,128)(2,1)S(1)} %pad_maximum_fusion.2), channel_id=1, source_target_pairs={{0,16},{16,0},{1,17},{17,1},{2,18},{18,2},{3,19},{19,3},{4,20},{20... | collective-permute-start | bytes 1572872 | tf_op jit(solution)/shard_map/ppermute | solution.py:196
  85.9 2.0 %shrink.3 = f32[240,128]{1,0:T(8,128)S(1)} custom-call(s32[3]{0:T(128)S(1)} %pad_add_fusion.scalar_ref, bf16[216,2048]{1,0:T(8,128)(2,1)} %collective-permute-done.12.refs_0_, bf16[8,2048,128]{2,1,0:T(8,128)(2,1)S(1)} %copy-done.6, f32[8,256]{1,0:T(8,128)S(1)} %slice.83.refs_2_.refs_3_, f32[8,512]{1,0:T(8,128)S(1)} %slice.85.refs_3_, f32[8,512]{1,0:T(8,128)S(1)} %slice.86.refs_4_), custom_call_target="tpu_custom_call" | custom-call | flops 1 | bytes 1 | tf_op jit(solution)/shard_map/shrink/pallas_call | solution.py:322
  88.0 1.3 %collective-permute-done.13 = f32[240,128]{1,0:T(8,128)S(1)} collective-permute-done((f32[240,128]{1,0:T(8,128)S(1)}, f32[240,128]{1,0:T(8,128)S(1)}, u32[]{:S(2)}, u32[]{:S(2)}) %collective-permute-start.13) | collective-permute-done | bytes 122912 | tf_op jit(solution)/shard_map/ppermute | solution.py:338
  89.3 1.5 %collective-permute-start.6 = (f32[256,256]{1,0:T(8,128)S(1)}, f32[256,256]{1,0:T(8,128)S(1)}, u32[]{:S(2)}, u32[]{:S(2)}) collective-permute-start(f32[256,256]{1,0:T(8,128)S(1)} %slice.80), channel_id=1, source_target_pairs={{0,2},{1,3},{2,0},{3,1},{4,6},{5,7},{6,4},{7,5},{8,10},{9,11},{10,... | collective-permute-start | bytes 786440 | tf_op jit(solution)/shard_map/ppermute | solution.py:251
  91.5 7.5 %collective-permute-done.14 = f32[120,128]{1,0:T(8,128)S(1)} collective-permute-done((f32[120,128]{1,0:T(8,128)S(1)}, f32[120,128]{1,0:T(8,128)S(1)}, u32[]{:S(2)}, u32[]{:S(2)}) %collective-permute-start.14) | collective-permute-done | bytes 61472 | tf_op jit(solution)/shard_map/ppermute | solution.py:340
  99.0 3.8 %collective-permute-done.11.refs_1_ = bf16[216,2048]{1,0:T(8,128)(2,1)S(1)} collective-permute-done((bf16[216,2048]{1,0:T(8,128)(2,1)S(1)}, bf16[216,2048]{1,0:T(8,128)(2,1)S(1)}, u32[]{:S(2)}, u32[]{:S(2)}) %collective-permute-start.11) | collective-permute-done | bytes 884768 | tf_op jit(solution)/shard_map/ppermute | solution.py:308
  102.8 1.4 %shrink.5 = (f32[480,128]{1,0:T(8,128)S(1)}, f32[120,128]{1,0:T(8,128)S(1)}, f32[120,128]{1,0:T(8,128)S(1)}) custom-call(s32[3]{0:T(128)S(1)} %pad_add_fusion.scalar_ref, bf16[216,2048]{1,0:T(8,128)(2,1)S(1)} %collective-permute-done.10.refs_0_, bf16[216,2048]{1,0:T(8,128)(2,1)S(1)} %collective-permute-done.11.refs_1_, bf16[8,2048,128]{2,1,0:T(8,128)(2,1)S(1)} %copy-done.6, ...), custom_call_target="tpu_custom_call" | custom-call | flops 1 | bytes 1 | tf_op jit(solution)/shard_map/shrink/pallas_call | solution.py:322
  104.6 1.2 %collective-permute-done.18 = f32[480,128]{1,0:T(8,128)S(1)} collective-permute-done((f32[480,128]{1,0:T(8,128)S(1)}, f32[480,128]{1,0:T(8,128)S(1)}, u32[]{:S(2)}, u32[]{:S(2)}) %collective-permute-start.18) | collective-permute-done | bytes 245792 | tf_op jit(solution)/shard_map/ppermute | solution.py:338
  105.9 1.6 %collective-permute-start.19 = (f32[240,128]{1,0:T(8,128)S(1)}, f32[240,128]{1,0:T(8,128)S(1)}, u32[]{:S(2)}, u32[]{:S(2)}) collective-permute-start(f32[240,128]{1,0:T(8,128)S(1)} %slice.92), channel_id=1, source_target_pairs={{0,2},{1,3},{2,0},{3,1},{4,6},{5,7},{6,4},{7,5},{8,10},{9,11},{10,... | collective-permute-start | bytes 368648 | tf_op jit(solution)/shard_map/ppermute | solution.py:340
  107.5 0.8 collective-permute-start.17
  108.3 3.0 %collective-permute-done.19 = f32[240,128]{1,0:T(8,128)S(1)} collective-permute-done((f32[240,128]{1,0:T(8,128)S(1)}, f32[240,128]{1,0:T(8,128)S(1)}, u32[]{:S(2)}, u32[]{:S(2)}) %collective-permute-start.19) | collective-permute-done | bytes 122912 | tf_op jit(solution)/shard_map/ppermute | solution.py:340
  111.3 1.7 %collective-permute-start.20 = (f32[120,128]{1,0:T(8,128)S(1)}, f32[120,128]{1,0:T(8,128)S(1)}, u32[]{:S(2)}, u32[]{:S(2)}) collective-permute-start(f32[120,128]{1,0:T(8,128)S(1)} %get-tuple-element.36), channel_id=1, source_target_pairs={{0,12},{4,0},{8,4},{12,8},{1,13},{5,1},{9,5},{13,9},{2,14},{6,2},{... | collective-permute-start | bytes 184328 | tf_op jit(solution)/shard_map/ppermute | solution.py:359
  113.7 0.9 finish.2.base_ref
  114.6 1.0 collective-permute-done.20.refs_0_
  115.6 3.4 %collective-permute-done.21.refs_1_ = f32[120,128]{1,0:T(8,128)S(1)} collective-permute-done((f32[120,128]{1,0:T(8,128)S(1)}, f32[120,128]{1,0:T(8,128)S(1)}, u32[]{:S(2)}, u32[]{:S(2)}) %collective-permute-start.21) | collective-permute-done | bytes 61472 | tf_op jit(solution)/shard_map/ppermute | solution.py:359
  119.0 1.6 %finish.3 = bf16[768,256]{1,0:T(8,128)(2,1)} custom-call(s32[1]{0:T(128)} %bitcast.2.place_ref, s32[768,1]{1,0:T(8,128)S(1)} %copy-done.7, f32[768,256]{1,0:T(8,128)S(1)} %finish.2.base_ref, bf16[32,64,256]{2,1,0:T(8,128)(2,1)S(1)} %pad_maximum_fusion.up_ref, f32[120,128]{1,0:T(8,128)S(1)} %collective-permute-done.20.refs_0_, ...), custom_call_target="tpu_custom_call" | custom-call | flops 1 | bytes 1 | tf_op jit(solution)/shard_map/finish/pallas_call | solution.py:156
  (95 shorter events, 4.0 us)
Async XLA Ops:
  0.0 1.0 copy-start
  1.0 17.6 %copy-start.21 = (bf16[8,32,256]{2,1,0:T(8,128)(2,1)}, bf16[8,32,256]{2,1,0:T(8,128)(2,1)S(1)}, u32[]{:S(2)}) copy-start(bf16[8,32,256]{2,1,0:T(8,128)(2,1)S(1)} %constant_dynamic-slice_fusion) | copy-start | bytes 393220
  1.0 14.9 %collective-permute-start = (bf16[8,32,256]{2,1,0:T(8,128)(2,1)S(1)}, bf16[8,32,256]{2,1,0:T(8,128)(2,1)S(1)}, u32[]{:S(2)}, u32[]{:S(2)}) collective-permute-start(bf16[8,32,256]{2,1,0:T(8,128)(2,1)S(1)} %constant_dynamic-slice_fusion), channel_id=1, source_target_pairs={{0,12},{4,0},{8,4},{12,8},{1,13},{5,1},{9,5},{13,9},{2,14},{6,2},{... | collective-permute-start | bytes 393224 | tf_op jit(solution)/shard_map/ppermute | solution.py:192
  6.1 11.2 %collective-permute-start.1 = (bf16[8,32,256]{2,1,0:T(8,128)(2,1)S(1)}, bf16[8,32,256]{2,1,0:T(8,128)(2,1)S(1)}, u32[]{:S(2)}, u32[]{:S(2)}) collective-permute-start(bf16[8,32,256]{2,1,0:T(8,128)(2,1)S(1)} %constant_dynamic-slice_fusion), channel_id=1, source_target_pairs={{0,8},{4,12},{8,0},{12,4},{1,9},{5,13},{9,1},{13,5},{2,10},{6,14},... | collective-permute-start | bytes 393224 | tf_op jit(solution)/shard_map/ppermute | solution.py:192
  6.1 11.2 %collective-permute-start.2 = (bf16[8,32,256]{2,1,0:T(8,128)(2,1)S(1)}, bf16[8,32,256]{2,1,0:T(8,128)(2,1)S(1)}, u32[]{:S(2)}, u32[]{:S(2)}) collective-permute-start(bf16[8,32,256]{2,1,0:T(8,128)(2,1)S(1)} %constant_dynamic-slice_fusion), channel_id=1, source_target_pairs={{0,4},{4,8},{8,12},{12,0},{1,5},{5,9},{9,13},{13,1},{2,6},{6,10},{... | collective-permute-start | bytes 393224 | tf_op jit(solution)/shard_map/ppermute | solution.py:192
  15.8 1.5 %copy-start.15 = (bf16[8,32,256]{2,1,0:T(8,128)(2,1)}, bf16[8,32,256]{2,1,0:T(8,128)(2,1)S(1)}, u32[]{:S(2)}) copy-start(bf16[8,32,256]{2,1,0:T(8,128)(2,1)S(1)} %collective-permute-done.refs_3_) | copy-start | bytes 393220
  17.3 0.6 copy-start.17
  17.3 0.7 copy-start.19
  18.6 6.7 %copy-start.1 = (bf16[768,2048]{1,0:T(8,128)(2,1)S(1)}, bf16[768,2048]{1,0:T(8,128)(2,1)}, u32[]{:S(2)}) copy-start(bf16[768,2048]{1,0:T(8,128)(2,1)} %tokens_ref.13) | copy-start | bytes 9437188
  18.6 6.7 %copy-start.10 = (s32[8,128]{1,0:T(8,128)S(1)}, s32[8,128]{1,0:T(8,128)}, u32[]{:S(2)}) copy-start(s32[8,128]{1,0:T(8,128)} %get-tuple-element.24.refs_0_) | copy-start | bytes 12292
  18.6 6.7 %copy-start.11 = (s32[2]{0:T(128)S(1)}, s32[2]{0:T(128)}, u32[]{:S(2)}) copy-start(s32[2]{0:T(128)} %broadcast_xor_fusion.block_ref) | copy-start | bytes 28
  22.7 19.4 %collective-permute-start.3 = (f32[256,512]{1,0:T(8,128)}, f32[256,512]{1,0:T(8,128)}, u32[]{:S(2)}, u32[]{:S(2)}) collective-permute-start(f32[256,512]{1,0:T(8,128)} %base.6.refs_0_), channel_id=1, source_target_pairs={{0,1},{1,0},{2,3},{3,2},{4,5},{5,4},{6,7},{7,6},{8,9},{9,8},{10,11... | collective-permute-start | bytes 1572872 | tf_op jit(solution)/shard_map/ppermute | solution.py:251
  22.7 61.6 %collective-permute-start.12 = (bf16[216,2048]{1,0:T(8,128)(2,1)}, bf16[216,2048]{1,0:T(8,128)(2,1)}, u32[]{:S(2)}, u32[]{:S(2)}) collective-permute-start(bf16[216,2048]{1,0:T(8,128)(2,1)} %get-tuple-element.27), channel_id=1, source_target_pairs={{0,8},{4,12},{8,0},{12,4},{1,9},{5,13},{9,1},{13,5},{2,10},{6,14},... | collective-permute-start | bytes 2654216 | tf_op jit(solution)/shard_map/ppermute | solution.py:308
  25.3 2.2 %copy-start.2 = (bf16[2048,1024]{1,0:T(8,128)(2,1)S(1)}, bf16[2048,1024]{1,0:T(8,128)(2,1)}, u32[]{:S(2)}) copy-start(bf16[2048,1024]{1,0:T(8,128)(2,1)} %weight_ref.11) | copy-start | bytes 12582916
  30.0 26.3 %collective-permute-start.7 = (f32[256,512]{1,0:T(8,128)}, f32[256,512]{1,0:T(8,128)}, u32[]{:S(2)}, u32[]{:S(2)}) collective-permute-start(f32[256,512]{1,0:T(8,128)} %base.10.refs_0_), channel_id=1, source_target_pairs={{0,1},{1,0},{2,3},{3,2},{4,5},{5,4},{6,7},{7,6},{8,9},{9,8},{10,11... | collective-permute-start | bytes 1572872 | tf_op jit(solution)/shard_map/ppermute | solution.py:251
  32.7 24.9 %collective-permute-start.5 = (f32[256,512]{1,0:T(8,128)}, f32[256,512]{1,0:T(8,128)}, u32[]{:S(2)}, u32[]{:S(2)}) collective-permute-start(f32[256,512]{1,0:T(8,128)} %base.8.refs_0_), channel_id=1, source_target_pairs={{0,1},{1,0},{2,3},{3,2},{4,5},{5,4},{6,7},{7,6},{8,9},{9,8},{10,11... | collective-permute-start | bytes 1572872 | tf_op jit(solution)/shard_map/ppermute | solution.py:251
  37.1 2.2 %copy-start.3 = (bf16[2048,1024]{1,0:T(8,128)(2,1)S(1)}, bf16[2048,1024]{1,0:T(8,128)(2,1)}, u32[]{:S(2)}) copy-start(bf16[2048,1024]{1,0:T(8,128)(2,1)} %weight_ref.11) | copy-start | bytes 12582916
  39.2 1.0 copy-start.8
  40.3 5.3 %copy-start.5 = (bf16[8,2048,128]{2,1,0:T(8,128)(2,1)S(1)}, bf16[8,2048,128]{2,1,0:T(8,128)(2,1)}, u32[]{:S(2)}) copy-start(bf16[8,2048,128]{2,1,0:T(8,128)(2,1)} %refs_2_.1) | copy-start | bytes 12582916
  40.3 5.3 %copy-start.9 = (bf16[216,2048]{1,0:T(8,128)(2,1)S(1)}, bf16[216,2048]{1,0:T(8,128)(2,1)}, u32[]{:S(2)}) copy-start(bf16[216,2048]{1,0:T(8,128)(2,1)} %get-tuple-element.28.refs_0_) | copy-start | bytes 2654212
  40.3 5.3 %copy-start.12 = (s32[8,128]{1,0:T(8,128)S(1)}, s32[8,128]{1,0:T(8,128)}, u32[]{:S(2)}) copy-start(s32[8,128]{1,0:T(8,128)} %get-tuple-element.29.refs_2_) | copy-start | bytes 12292
  43.2 3.8 %copy-start.13 = (f32[256,512]{1,0:T(8,128)}, f32[256,512]{1,0:T(8,128)S(1)}, u32[]{:S(2)}) copy-start(f32[256,512]{1,0:T(8,128)S(1)} %add.50) | copy-start | bytes 1572868
  43.3 4.5 %copy-start.25 = (s32[1,768]{1,0:T(1,128)S(1)}, s32[1,768]{1,0:T(1,128)}, u32[]{:S(2)}) copy-start(s32[1,768]{1,0:T(1,128)} %get-tuple-element.20.index_ref) | copy-start | bytes 9220
  44.1 18.4 %collective-permute-start.4 = (f32[256,256]{1,0:T(8,128)}, f32[256,256]{1,0:T(8,128)}, u32[]{:S(2)}, u32[]{:S(2)}) collective-permute-start(f32[256,256]{1,0:T(8,128)} %slice.78), channel_id=1, source_target_pairs={{0,2},{1,3},{2,0},{3,1},{4,6},{5,7},{6,4},{7,5},{8,10},{9,11},{10,... | collective-permute-start | bytes 786440 | tf_op jit(solution)/shard_map/ppermute | solution.py:251
  47.0 1.7 %collective-permute-start.15 = (f32[240,128]{1,0:T(8,128)S(1)}, f32[240,128]{1,0:T(8,128)}, u32[]{:S(2)}, u32[]{:S(2)}) collective-permute-start(f32[240,128]{1,0:T(8,128)S(1)} %shrink.4), channel_id=1, source_target_pairs={{0,1},{1,0},{2,3},{3,2},{4,5},{5,4},{6,7},{7,6},{8,9},{9,8},{10,11... | collective-permute-start | bytes 368648 | tf_op jit(solution)/shard_map/ppermute | solution.py:338
  49.7 38.2 %collective-permute-start.16 = (f32[120,128]{1,0:T(8,128)S(1)}, f32[120,128]{1,0:T(8,128)S(1)}, u32[]{:S(2)}, u32[]{:S(2)}) collective-permute-start(f32[120,128]{1,0:T(8,128)S(1)} %slice.90), channel_id=1, source_target_pairs={{0,2},{1,3},{2,0},{3,1},{4,6},{5,7},{6,4},{7,5},{8,10},{9,11},{10,... | collective-permute-start | bytes 184328 | tf_op jit(solution)/shard_map/ppermute | solution.py:340
  50.3 2.2 %copy-start.4 = (bf16[2048,1024]{1,0:T(8,128)(2,1)S(1)}, bf16[2048,1024]{1,0:T(8,128)(2,1)}, u32[]{:S(2)}) copy-start(bf16[2048,1024]{1,0:T(8,128)(2,1)} %weight_ref.11) | copy-start | bytes 12582916
  54.2 1.9 %copy-start.16 = (bf16[8,32,256]{2,1,0:T(8,128)(2,1)S(1)}, bf16[8,32,256]{2,1,0:T(8,128)(2,1)}, u32[]{:S(2)}) copy-start(bf16[8,32,256]{2,1,0:T(8,128)(2,1)} %copy-done.15) | copy-start | bytes 393220
  54.3 1.9 %copy-start.18 = (bf16[8,32,256]{2,1,0:T(8,128)(2,1)S(1)}, bf16[8,32,256]{2,1,0:T(8,128)(2,1)}, u32[]{:S(2)}) copy-start(bf16[8,32,256]{2,1,0:T(8,128)(2,1)} %copy-done.17) | copy-start | bytes 393220
  54.3 1.9 %copy-start.20 = (bf16[8,32,256]{2,1,0:T(8,128)(2,1)S(1)}, bf16[8,32,256]{2,1,0:T(8,128)(2,1)}, u32[]{:S(2)}) copy-start(bf16[8,32,256]{2,1,0:T(8,128)(2,1)} %copy-done.19) | copy-start | bytes 393220
  54.3 1.9 %copy-start.22 = (bf16[8,32,256]{2,1,0:T(8,128)(2,1)S(1)}, bf16[8,32,256]{2,1,0:T(8,128)(2,1)}, u32[]{:S(2)}) copy-start(bf16[8,32,256]{2,1,0:T(8,128)(2,1)} %copy-done.21) | copy-start | bytes 393220
  54.3 2.0 %copy-start.23 = (bf16[216,2048]{1,0:T(8,128)(2,1)S(1)}, bf16[216,2048]{1,0:T(8,128)(2,1)}, u32[]{:S(2)}) copy-start(bf16[216,2048]{1,0:T(8,128)(2,1)} %get-tuple-element.25) | copy-start | bytes 2654212
  54.3 3.4 %copy-start.24 = (bf16[216,2048]{1,0:T(8,128)(2,1)S(1)}, bf16[216,2048]{1,0:T(8,128)(2,1)}, u32[]{:S(2)}) copy-start(bf16[216,2048]{1,0:T(8,128)(2,1)} %get-tuple-element.26) | copy-start | bytes 2654212
  56.1 7.9 %copy-start.14 = (f32[256,512]{1,0:T(8,128)S(1)}, f32[256,512]{1,0:T(8,128)}, u32[]{:S(2)}) copy-start(f32[256,512]{1,0:T(8,128)} %copy-done.13) | copy-start | bytes 1572868
  56.2 29.7 %copy-start.6 = (bf16[8,2048,128]{2,1,0:T(8,128)(2,1)S(1)}, bf16[8,2048,128]{2,1,0:T(8,128)(2,1)}, u32[]{:S(2)}) copy-start(bf16[8,2048,128]{2,1,0:T(8,128)(2,1)} %refs_2_.1) | copy-start | bytes 12582916
  56.3 42.7 %collective-permute-start.10 = (bf16[216,2048]{1,0:T(8,128)(2,1)S(1)}, bf16[216,2048]{1,0:T(8,128)(2,1)S(1)}, u32[]{:S(2)}, u32[]{:S(2)}) collective-permute-start(bf16[216,2048]{1,0:T(8,128)(2,1)S(1)} %copy-done.23), channel_id=1, source_target_pairs={{0,4},{4,8},{8,12},{12,0},{1,5},{5,9},{9,13},{13,1},{2,6},{6,10},{... | collective-permute-start | bytes 2654216 | tf_op jit(solution)/shard_map/ppermute | solution.py:308
  57.7 45.1 %collective-permute-start.11 = (bf16[216,2048]{1,0:T(8,128)(2,1)S(1)}, bf16[216,2048]{1,0:T(8,128)(2,1)S(1)}, u32[]{:S(2)}, u32[]{:S(2)}) collective-permute-start(bf16[216,2048]{1,0:T(8,128)(2,1)S(1)} %copy-done.24), channel_id=1, source_target_pairs={{0,12},{4,0},{8,4},{12,8},{1,13},{5,1},{9,5},{13,9},{2,14},{6,2},{... | collective-permute-start | bytes 2654216 | tf_op jit(solution)/shard_map/ppermute | solution.py:308
  62.5 28.3 %collective-permute-start.8 = (f32[256,256]{1,0:T(8,128)S(1)}, f32[256,256]{1,0:T(8,128)S(1)}, u32[]{:S(2)}, u32[]{:S(2)}) collective-permute-start(f32[256,256]{1,0:T(8,128)S(1)} %slice.82), channel_id=1, source_target_pairs={{0,2},{1,3},{2,0},{3,1},{4,6},{5,7},{6,4},{7,5},{8,10},{9,11},{10,... | collective-permute-start | bytes 786440 | tf_op jit(solution)/shard_map/ppermute | solution.py:251
  84.3 20.0 %collective-permute-start.9 = (bf16[32,32,256]{2,1,0:T(8,128)(2,1)S(1)}, bf16[32,32,256]{2,1,0:T(8,128)(2,1)S(1)}, u32[]{:S(2)}, u32[]{:S(2)}) collective-permute-start(bf16[32,32,256]{2,1,0:T(8,128)(2,1)S(1)} %pad_maximum_fusion.2), channel_id=1, source_target_pairs={{0,16},{16,0},{1,17},{17,1},{2,18},{18,2},{3,19},{19,3},{4,20},{20... | collective-permute-start | bytes 1572872 | tf_op jit(solution)/shard_map/ppermute | solution.py:196
  87.9 1.4 %collective-permute-start.13 = (f32[240,128]{1,0:T(8,128)S(1)}, f32[240,128]{1,0:T(8,128)S(1)}, u32[]{:S(2)}, u32[]{:S(2)}) collective-permute-start(f32[240,128]{1,0:T(8,128)S(1)} %shrink.3), channel_id=1, source_target_pairs={{0,1},{1,0},{2,3},{3,2},{4,5},{5,4},{6,7},{7,6},{8,9},{9,8},{10,11... | collective-permute-start | bytes 368648 | tf_op jit(solution)/shard_map/ppermute | solution.py:338
  89.3 18.1 %collective-permute-start.6 = (f32[256,256]{1,0:T(8,128)S(1)}, f32[256,256]{1,0:T(8,128)S(1)}, u32[]{:S(2)}, u32[]{:S(2)}) collective-permute-start(f32[256,256]{1,0:T(8,128)S(1)} %slice.80), channel_id=1, source_target_pairs={{0,2},{1,3},{2,0},{3,1},{4,6},{5,7},{6,4},{7,5},{8,10},{9,11},{10,... | collective-permute-start | bytes 786440 | tf_op jit(solution)/shard_map/ppermute | solution.py:251
  90.8 8.1 %collective-permute-start.14 = (f32[120,128]{1,0:T(8,128)S(1)}, f32[120,128]{1,0:T(8,128)S(1)}, u32[]{:S(2)}, u32[]{:S(2)}) collective-permute-start(f32[120,128]{1,0:T(8,128)S(1)} %slice.88), channel_id=1, source_target_pairs={{0,2},{1,3},{2,0},{3,1},{4,6},{5,7},{6,4},{7,5},{8,10},{9,11},{10,... | collective-permute-start | bytes 184328 | tf_op jit(solution)/shard_map/ppermute | solution.py:340
  104.2 1.6 %collective-permute-start.18 = (f32[480,128]{1,0:T(8,128)S(1)}, f32[480,128]{1,0:T(8,128)S(1)}, u32[]{:S(2)}, u32[]{:S(2)}) collective-permute-start(f32[480,128]{1,0:T(8,128)S(1)} %get-tuple-element.32), channel_id=1, source_target_pairs={{0,1},{1,0},{2,3},{3,2},{4,5},{5,4},{6,7},{7,6},{8,9},{9,8},{10,11... | collective-permute-start | bytes 737288 | tf_op jit(solution)/shard_map/ppermute | solution.py:338
  104.5 9.2 %copy-start.7 = (s32[768,1]{1,0:T(8,128)S(1)}, s32[768,1]{1,0:T(8,128)}, u32[]{:S(2)}) copy-start(s32[768,1]{1,0:T(8,128)} %copy.14.index_ref) | copy-start | bytes 9220
  105.9 5.4 %collective-permute-start.19 = (f32[240,128]{1,0:T(8,128)S(1)}, f32[240,128]{1,0:T(8,128)S(1)}, u32[]{:S(2)}, u32[]{:S(2)}) collective-permute-start(f32[240,128]{1,0:T(8,128)S(1)} %slice.92), channel_id=1, source_target_pairs={{0,2},{1,3},{2,0},{3,1},{4,6},{5,7},{6,4},{7,5},{8,10},{9,11},{10,... | collective-permute-start | bytes 368648 | tf_op jit(solution)/shard_map/ppermute | solution.py:340
  107.5 6.2 %collective-permute-start.17 = (f32[120,128]{1,0:T(8,128)S(1)}, f32[120,128]{1,0:T(8,128)S(1)}, u32[]{:S(2)}, u32[]{:S(2)}) collective-permute-start(f32[120,128]{1,0:T(8,128)S(1)} %get-tuple-element.30), channel_id=1, source_target_pairs={{0,8},{4,12},{8,0},{12,4},{1,9},{5,13},{9,1},{13,5},{2,10},{6,14},... | collective-permute-start | bytes 184328 | tf_op jit(solution)/shard_map/ppermute | solution.py:359
  111.3 4.3 %collective-permute-start.20 = (f32[120,128]{1,0:T(8,128)S(1)}, f32[120,128]{1,0:T(8,128)S(1)}, u32[]{:S(2)}, u32[]{:S(2)}) collective-permute-start(f32[120,128]{1,0:T(8,128)S(1)} %get-tuple-element.36), channel_id=1, source_target_pairs={{0,12},{4,0},{8,4},{12,8},{1,13},{5,1},{9,5},{13,9},{2,14},{6,2},{... | collective-permute-start | bytes 184328 | tf_op jit(solution)/shard_map/ppermute | solution.py:359
  113.0 6.0 %collective-permute-start.21 = (f32[120,128]{1,0:T(8,128)S(1)}, f32[120,128]{1,0:T(8,128)S(1)}, u32[]{:S(2)}, u32[]{:S(2)}) collective-permute-start(f32[120,128]{1,0:T(8,128)S(1)} %get-tuple-element.35), channel_id=1, source_target_pairs={{0,4},{4,8},{8,12},{12,0},{1,5},{5,9},{9,13},{13,1},{2,6},{6,10},{... | collective-permute-start | bytes 184328 | tf_op jit(solution)/shard_map/ppermute | solution.py:359

commit v11 on v10

--- a/solution.py
+++ b/solution.py
@@ -110,6 +110,10 @@
         target[...] = source[...]
 
 
+def hold_kernel(value_ref, *refs):
+    refs[-1][...] = value_ref[...]
+
+
 def split_pair(value):
     high = value.astype(jnp.bfloat16)
     low = (value - high.astype(jnp.float32)).astype(jnp.bfloat16)
@@ -332,11 +336,24 @@
             name="shrink",
         )(scalars, *blocks, adapter_down, *after, *passed)
 
-    def combine(value):
+    def hold(value, after):
+        return pl.pallas_call(
+            hold_kernel,
+            out_shape=jax.ShapeDtypeStruct(value.shape, value.dtype),
+            in_specs=[VMEM] + [ANY] * len(after),
+            out_specs=VMEM,
+            compiler_params=PARAMS,
+            cost_estimate=COST,
+            name="hold",
+        )(value, *after)
+
+    def combine(value, after=()):
         bit, half = 1, value.shape[0] // 2
         while bit < pieces // 2:
             value = value + lax.ppermute(value, "tensor", [(i, i ^ bit) for i in range(pieces)])
             bit *= 2
+        if after:
+            value = hold(value, after)
         return value[:half] + lax.ppermute(value[half:], "tensor", [(i, i ^ bit) for i in range(pieces)])
 
     slabs = 3
@@ -346,12 +363,13 @@
     ]
     base = jnp.concatenate([total for total, _ in slab_sums], axis=0)
     begun = [first for _, first in slab_sums]
+    whole = [total[:8] for total, _ in slab_sums[:1]]
     late = order[-2:]
     early = order[:-2] + [0]
     totals = []
     for r in early:
-        (value,) = shrink([arrived[r]], [total[:8] for total, _ in slab_sums[:1]] + begun[1:] if r else [packed], [])
-        totals.append(combine(value))
+        (value,) = shrink([arrived[r]], begun if r else [packed], [])
+        totals.append(combine(value, whole if r else ()))
     value, *totals = shrink([arrived[r] for r in late], [base[:8], base[-8:]], totals)
     last = combine(value)
 

time: 121 us -> 116 us (0.959)
  waiting for transfers between devices: 42.2 us -> 37.3 us
    ppermute x3, waiting for transfers between devices: 23 us -> 18.8 us  [send(): lax.ppermute(block, 'batch', [(i, (i + r) % homes) for i in range(homes)])]
    ppermute x3, starting transfers between devices: 2.76 us -> 4.7 us  [combine(): lax.ppermute(value[half:], 'tensor', [(i, i ^ bit) for i in range(pieces)])]
    ppermute x6, starting transfers between devices: 5.05 us -> 3.18 us  [reduce_base(): lax.ppermute(sent, 'tensor', [(i, i ^ bit) for i in range(pieces)])]
    unnamed x52 -> x46, local copies, waits for them, and re-layouts: 9.32 us -> 10.5 us
  transfers between devices with their start and end apart: 22 -> 22, of which waited for: 10 -> 10; matrix products, arithmetic and copies ran while one was open for 8% -> 7% of each run, Pallas kernels for 20% -> 25%
where the time goes in v11:
time: 116 us; the launch traced here: 115 us
  waiting for transfers between devices  37.3 us (32%)
  Pallas kernels  30.6 us (26%)
  starting transfers between devices  25.8 us (22%)
  local copies, waits for them, and re-layouts  12.7 us (11%)
  other arithmetic  5.61 us (5%)
  between operations  3.23 us (3%)
    ppermute x3, waiting for transfers between devices, send(): lax.ppermute(block, 'batch', [(i, (i + r) % homes) for i in range(homes)])  18.8 us
    pallas_call x6, Pallas kernels, base_part(): pl.pallas_call(functools.partial(base_kernel, len(after)), out_shape=jax....  14.5 us
    unnamed x46, local copies, waits for them, and re-layouts  10.5 us
    ppermute x3, waiting for transfers between devices, combine(): lax.ppermute(value[half:], 'tensor', [(i, i ^ bit) for i in range(pieces)])  10.2 us
    pallas_call x1, Pallas kernels, pack(): pl.pallas_call(functools.partial(pack_kernel, span, shifts), out_shape=[j...  6.46 us
    ppermute x3, starting transfers between devices, send(): lax.ppermute(block, 'batch', [(i, (i + r) % homes) for i in range(homes)])  6.35 us
    ppermute x3, starting transfers between devices, gather_up(): lax.ppermute(own, 'batch', [(i, (i - r) % homes) for i in range(homes)])  6.11 us
    pallas_call x3, Pallas kernels, shrink(): pl.pallas_call(functools.partial(shrink_kernel, held, light, rank, value_...  4.86 us
  transfers between devices with their start and end apart: 22, of which 10 were waited for; matrix products, arithmetic and copies ran while one was open for 7% of the time, Pallas kernels for 25%

profile of v11, /device:TPU:0, one launch (start us, length us, event | category | flops | bytes accessed | tf_op | source)
XLA Modules:
  0.0 115.2 jit_solution(879083462927335331)
XLA Ops:
  0.0 0.9 copy-done
  1.0 5.1 %collective-permute-start = (bf16[8,32,256]{2,1,0:T(8,128)(2,1)S(1)}, bf16[8,32,256]{2,1,0:T(8,128)(2,1)S(1)}, u32[]{:S(2)}, u32[]{:S(2)}) collective-permute-start(bf16[8,32,256]{2,1,0:T(8,128)(2,1)S(1)} %constant_dynamic-slice_fusion), channel_id=1, source_target_pairs={{0,12},{4,0},{8,4},{12,8},{1,13},{5,1},{9,5},{13,9},{2,14},{6,2},{... | collective-permute-start | bytes 393224 | tf_op jit(solution)/shard_map/ppermute | solution.py:196
  6.1 1.0 collective-permute-start.2
  7.1 1.7 %route.1 = (s32[1,768]{1,0:T(1,128)}, s32[8,128]{1,0:T(8,128)}) custom-call(s32[1]{0:T(128)} %bitcast.place_ref, s32[32]{0:T(128)} %entry_hbm.1, s32[768]{0:T(1024)} %request_hbm.1), custom_call_target="tpu_custom_call" | custom-call | flops 1 | bytes 1 | tf_op jit(solution)/shard_map/route/pallas_call | solution.py:279
  8.8 6.5 %pack.1 = (s32[8,128]{1,0:T(8,128)}, bf16[216,2048]{1,0:T(8,128)(2,1)}, bf16[216,2048]{1,0:T(8,128)(2,1)}, bf16[216,2048]{1,0:T(8,128)(2,1)}, bf16[216,2048]{1,0:T(8,128)(2,1)}) custom-call(s32[1,768]{1,0:T(1,128)} %get-tuple-element.20.index_ref, bf16[768,2048]{1,0:T(8,128)(2,1)} %tokens_ref.13), custom_call_target="tpu_custom_call" | custom-call | flops 1 | bytes 1 | tf_op jit(solution)/shard_map/pack/pallas_call | solution.py:297
  15.3 2.0 %collective-permute-done.1.refs_4_ = bf16[8,32,256]{2,1,0:T(8,128)(2,1)S(1)} collective-permute-done((bf16[8,32,256]{2,1,0:T(8,128)(2,1)S(1)}, bf16[8,32,256]{2,1,0:T(8,128)(2,1)S(1)}, u32[]{:S(2)}, u32[]{:S(2)}) %collective-permute-start.1) | collective-permute-done | bytes 131104 | tf_op jit(solution)/shard_map/ppermute | solution.py:196
  17.3 0.6 copy-done.14
  18.0 0.6 gate.1
  18.6 2.6 %collective-permute-start.12 = (bf16[216,2048]{1,0:T(8,128)(2,1)}, bf16[216,2048]{1,0:T(8,128)(2,1)}, u32[]{:S(2)}, u32[]{:S(2)}) collective-permute-start(bf16[216,2048]{1,0:T(8,128)(2,1)} %get-tuple-element.27), channel_id=1, source_target_pairs={{0,8},{4,12},{8,0},{12,4},{1,9},{5,13},{9,1},{13,5},{2,10},{6,14},... | collective-permute-start | bytes 2654216 | tf_op jit(solution)/shard_map/ppermute | solution.py:312
  21.8 4.1 %base.6.refs_0_ = f32[256,512]{1,0:T(8,128)} custom-call(s32[2]{0:T(128)} %broadcast_xor_fusion.block_ref, bf16[768,2048]{1,0:T(8,128)(2,1)} %tokens_ref.13, bf16[2048,1024]{1,0:T(8,128)(2,1)} %weight_ref.11, s32[8,128]{1,0:T(8,128)} %get-tuple-element.24.refs_0_), custom_call_target="tpu_custom_call" | custom-call | flops 1 | bytes 1 | tf_op jit(solution)/shard_map/base/pallas_call | solution.py:223
  25.9 2.2 %copy-done.2 = bf16[2048,1024]{1,0:T(8,128)(2,1)S(1)} copy-done((bf16[2048,1024]{1,0:T(8,128)(2,1)S(1)}, bf16[2048,1024]{1,0:T(8,128)(2,1)}, u32[]{:S(2)}) %copy-start.2) | copy-done | bytes 4194328
  28.1 2.5 %base.10.refs_0_ = f32[256,512]{1,0:T(8,128)} custom-call(s32[2]{0:T(128)S(1)} %copy-done.10, bf16[768,2048]{1,0:T(8,128)(2,1)S(1)} %copy-done.1, bf16[2048,1024]{1,0:T(8,128)(2,1)S(1)} %copy-done.2, s32[8,128]{1,0:T(8,128)S(1)} %copy-done.9), custom_call_target="tpu_custom_call" | custom-call | flops 1 | bytes 1 | tf_op jit(solution)/shard_map/base/pallas_call | solution.py:223
  31.1 2.5 %base.8.refs_0_ = f32[256,512]{1,0:T(8,128)} custom-call(s32[2]{0:T(128)S(1)} %copy-done.10, bf16[768,2048]{1,0:T(8,128)(2,1)S(1)} %copy-done.1, bf16[2048,1024]{1,0:T(8,128)(2,1)S(1)} %copy-done.2, s32[8,128]{1,0:T(8,128)S(1)} %copy-done.9), custom_call_target="tpu_custom_call" | custom-call | flops 1 | bytes 1 | tf_op jit(solution)/shard_map/base/pallas_call | solution.py:223
  33.6 1.2 %slice.61 = s32[1,1]{1,0:T(1,128)} slice(s32[8,128]{1,0:T(8,128)} %get-tuple-element.19), slice={[0:1], [0:1]} | slice | bytes 8 | tf_op jit(solution)/shard_map/slice | solution.py:320
  37.1 2.2 %copy-done.4 = bf16[8,2048,128]{2,1,0:T(8,128)(2,1)S(1)} copy-done((bf16[8,2048,128]{2,1,0:T(8,128)(2,1)S(1)}, bf16[8,2048,128]{2,1,0:T(8,128)(2,1)}, u32[]{:S(2)}) %copy-start.4) | copy-done | bytes 4194328
  39.3 1.2 %copy-done.8 = bf16[216,2048]{1,0:T(8,128)(2,1)S(1)} copy-done((bf16[216,2048]{1,0:T(8,128)(2,1)S(1)}, bf16[216,2048]{1,0:T(8,128)(2,1)}, u32[]{:S(2)}) %copy-start.8) | copy-done | bytes 884760
  40.4 1.4 %shrink.4 = f32[240,128]{1,0:T(8,128)S(1)} custom-call(s32[3]{0:T(128)S(1)} %pad_add_fusion.scalar_ref, bf16[216,2048]{1,0:T(8,128)(2,1)S(1)} %copy-done.8, bf16[8,2048,128]{2,1,0:T(8,128)(2,1)S(1)} %copy-done.4, s32[8,128]{1,0:T(8,128)S(1)} %copy-done.11), custom_call_target="tpu_custom_call" | custom-call | flops 1 | bytes 1 | tf_op jit(solution)/shard_map/shrink/pallas_call | solution.py:326
  42.9 0.9 copy.14.index_ref
  43.8 0.9 add.58
  44.8 1.6 %collective-permute-start.16 = (f32[120,128]{1,0:T(8,128)S(1)}, f32[120,128]{1,0:T(8,128)S(1)}, u32[]{:S(2)}, u32[]{:S(2)}) collective-permute-start(f32[120,128]{1,0:T(8,128)S(1)} %slice.95), channel_id=1, source_target_pairs={{0,2},{1,3},{2,0},{3,1},{4,6},{5,7},{6,4},{7,5},{8,10},{9,11},{10,... | collective-permute-start | bytes 184328 | tf_op jit(solution)/shard_map/ppermute | solution.py:357
  46.3 2.2 %copy-done.3 = bf16[2048,1024]{1,0:T(8,128)(2,1)S(1)} copy-done((bf16[2048,1024]{1,0:T(8,128)(2,1)S(1)}, bf16[2048,1024]{1,0:T(8,128)(2,1)}, u32[]{:S(2)}) %copy-start.3) | copy-done | bytes 4194328
  48.5 1.0 copy-done.7
  49.6 1.8 %base.7 = f32[256,512]{1,0:T(8,128)S(1)} custom-call(s32[2]{0:T(128)S(1)} %multiply_xor_fusion.block_ref, bf16[768,2048]{1,0:T(8,128)(2,1)S(1)} %copy-done.1, bf16[2048,1024]{1,0:T(8,128)(2,1)S(1)} %copy-done.3, f32[256,512]{1,0:T(8,128)S(1)} %copy-done.7), custom_call_target="tpu_custom_call" | custom-call | flops 1 | bytes 1 | tf_op jit(solution)/shard_map/base/pallas_call | solution.py:223
  51.4 1.1 add.50
  53.2 1.8 %base.9 = f32[256,512]{1,0:T(8,128)S(1)} custom-call(s32[2]{0:T(128)S(1)} %multiply_xor_fusion.block_ref, bf16[768,2048]{1,0:T(8,128)(2,1)S(1)} %copy-done.1, bf16[2048,1024]{1,0:T(8,128)(2,1)S(1)} %copy-done.3, f32[256,512]{1,0:T(8,128)} %base.8.refs_0_), custom_call_target="tpu_custom_call" | custom-call | flops 1 | bytes 1 | tf_op jit(solution)/shard_map/base/pallas_call | solution.py:223
  55.0 1.8 %base.11 = f32[256,512]{1,0:T(8,128)S(1)} custom-call(s32[2]{0:T(128)S(1)} %multiply_xor_fusion.block_ref, bf16[768,2048]{1,0:T(8,128)(2,1)S(1)} %copy-done.1, bf16[2048,1024]{1,0:T(8,128)(2,1)S(1)} %copy-done.3, f32[256,512]{1,0:T(8,128)} %base.10.refs_0_), custom_call_target="tpu_custom_call" | custom-call | flops 1 | bytes 1 | tf_op jit(solution)/shard_map/base/pallas_call | solution.py:223
  56.9 1.3 %add.54 = f32[256,512]{1,0:T(8,128)S(1)} add(f32[256,512]{1,0:T(8,128)S(1)} %base.11, f32[256,512]{1,0:T(8,128)} %collective-permute-done.7) | non-fusion elementwise | flops 131072 | bytes 1572864 | tf_op jit(solution)/shard_map/add | solution.py:255
  58.3 3.7 %collective-permute-start.11 = (bf16[216,2048]{1,0:T(8,128)(2,1)S(1)}, bf16[216,2048]{1,0:T(8,128)(2,1)S(1)}, u32[]{:S(2)}, u32[]{:S(2)}) collective-permute-start(bf16[216,2048]{1,0:T(8,128)(2,1)S(1)} %copy-done.21), channel_id=1, source_target_pairs={{0,12},{4,0},{8,4},{12,8},{1,13},{5,1},{9,5},{13,9},{2,14},{6,2},{... | collective-permute-start | bytes 2654216 | tf_op jit(solution)/shard_map/ppermute | solution.py:312
  62.0 1.5 %collective-permute-start.8 = (f32[256,256]{1,0:T(8,128)S(1)}, f32[256,256]{1,0:T(8,128)S(1)}, u32[]{:S(2)}, u32[]{:S(2)}) collective-permute-start(f32[256,256]{1,0:T(8,128)S(1)} %slice.86), channel_id=1, source_target_pairs={{0,2},{1,3},{2,0},{3,1},{4,6},{5,7},{6,4},{7,5},{8,10},{9,11},{10,... | collective-permute-start | bytes 786440 | tf_op jit(solution)/shard_map/ppermute | solution.py:255
  63.5 1.1 add.52
  64.7 1.6 %collective-permute-start.9 = (bf16[32,32,256]{2,1,0:T(8,128)(2,1)S(1)}, bf16[32,32,256]{2,1,0:T(8,128)(2,1)S(1)}, u32[]{:S(2)}, u32[]{:S(2)}) collective-permute-start(bf16[32,32,256]{2,1,0:T(8,128)(2,1)S(1)} %pad_maximum_fusion.2), channel_id=1, source_target_pairs={{0,16},{16,0},{1,17},{17,1},{2,18},{18,2},{3,19},{19,3},{4,20},{20... | collective-permute-start | bytes 1572872 | tf_op jit(solution)/shard_map/ppermute | solution.py:200
  66.3 2.0 %shrink.3 = f32[240,128]{1,0:T(8,128)S(1)} custom-call(s32[3]{0:T(128)S(1)} %pad_add_fusion.scalar_ref, bf16[216,2048]{1,0:T(8,128)(2,1)} %collective-permute-done.12.refs_0_, bf16[8,2048,128]{2,1,0:T(8,128)(2,1)S(1)} %copy-done.5, f32[8,512]{1,0:T(8,128)S(1)} %slice.89.refs_2_, f32[8,512]{1,0:T(8,128)S(1)} %slice.90.refs_3_, f32[8,512]{1,0:T(8,128)S(1)} %slice.91.refs_4_), custom_call_target="tpu_custom_call" | custom-call | flops 1 | bytes 1 | tf_op jit(solution)/shard_map/shrink/pallas_call | solution.py:326
  68.4 1.3 %collective-permute-done.13 = f32[240,128]{1,0:T(8,128)S(1)} collective-permute-done((f32[240,128]{1,0:T(8,128)S(1)}, f32[240,128]{1,0:T(8,128)S(1)}, u32[]{:S(2)}, u32[]{:S(2)}) %collective-permute-start.13) | collective-permute-done | bytes 122912 | tf_op jit(solution)/shard_map/ppermute | solution.py:353
  70.3 1.6 %collective-permute-start.14 = (f32[120,128]{1,0:T(8,128)S(1)}, f32[120,128]{1,0:T(8,128)S(1)}, u32[]{:S(2)}, u32[]{:S(2)}) collective-permute-start(f32[120,128]{1,0:T(8,128)S(1)} %slice.93), channel_id=1, source_target_pairs={{0,2},{1,3},{2,0},{3,1},{4,6},{5,7},{6,4},{7,5},{8,10},{9,11},{10,... | collective-permute-start | bytes 184328 | tf_op jit(solution)/shard_map/ppermute | solution.py:357
  71.9 7.5 %collective-permute-done.14 = f32[120,128]{1,0:T(8,128)S(1)} collective-permute-done((f32[120,128]{1,0:T(8,128)S(1)}, f32[120,128]{1,0:T(8,128)S(1)}, u32[]{:S(2)}, u32[]{:S(2)}) %collective-permute-start.14) | collective-permute-done | bytes 61472 | tf_op jit(solution)/shard_map/ppermute | solution.py:357
  79.4 1.9 %collective-permute-done.10.refs_0_ = bf16[216,2048]{1,0:T(8,128)(2,1)S(1)} collective-permute-done((bf16[216,2048]{1,0:T(8,128)(2,1)S(1)}, bf16[216,2048]{1,0:T(8,128)(2,1)S(1)}, u32[]{:S(2)}, u32[]{:S(2)}) %collective-permute-start.10) | collective-permute-done | bytes 884768 | tf_op jit(solution)/shard_map/ppermute | solution.py:312
  81.3 16.9 %collective-permute-done.11.refs_1_ = bf16[216,2048]{1,0:T(8,128)(2,1)S(1)} collective-permute-done((bf16[216,2048]{1,0:T(8,128)(2,1)S(1)}, bf16[216,2048]{1,0:T(8,128)(2,1)S(1)}, u32[]{:S(2)}, u32[]{:S(2)}) %collective-permute-start.11) | collective-permute-done | bytes 884768 | tf_op jit(solution)/shard_map/ppermute | solution.py:312
  98.3 1.5 %shrink.5 = (f32[480,128]{1,0:T(8,128)S(1)}, f32[120,128]{1,0:T(8,128)S(1)}, f32[120,128]{1,0:T(8,128)S(1)}) custom-call(s32[3]{0:T(128)S(1)} %pad_add_fusion.scalar_ref, bf16[216,2048]{1,0:T(8,128)(2,1)S(1)} %collective-permute-done.10.refs_0_, bf16[216,2048]{1,0:T(8,128)(2,1)S(1)} %collective-permute-done.11.refs_1_, bf16[8,2048,128]{2,1,0:T(8,128)(2,1)S(1)} %copy-done.5, ...), custom_call_target="tpu_custom_call" | custom-call | flops 1 | bytes 1 | tf_op jit(solution)/shard_map/shrink/pallas_call | solution.py:326
  100.0 1.3 %collective-permute-done.18 = f32[480,128]{1,0:T(8,128)S(1)} collective-permute-done((f32[480,128]{1,0:T(8,128)S(1)}, f32[480,128]{1,0:T(8,128)S(1)}, u32[]{:S(2)}, u32[]{:S(2)}) %collective-permute-start.18) | collective-permute-done | bytes 245792 | tf_op jit(solution)/shard_map/ppermute | solution.py:353
  101.4 1.6 %collective-permute-start.19 = (f32[240,128]{1,0:T(8,128)S(1)}, f32[240,128]{1,0:T(8,128)S(1)}, u32[]{:S(2)}, u32[]{:S(2)}) collective-permute-start(f32[240,128]{1,0:T(8,128)S(1)} %slice.97), channel_id=1, source_target_pairs={{0,2},{1,3},{2,0},{3,1},{4,6},{5,7},{6,4},{7,5},{8,10},{9,11},{10,... | collective-permute-start | bytes 368648 | tf_op jit(solution)/shard_map/ppermute | solution.py:357
  103.0 1.1 collective-permute-start.17
  104.1 2.7 %collective-permute-done.19 = f32[240,128]{1,0:T(8,128)S(1)} collective-permute-done((f32[240,128]{1,0:T(8,128)S(1)}, f32[240,128]{1,0:T(8,128)S(1)}, u32[]{:S(2)}, u32[]{:S(2)}) %collective-permute-start.19) | collective-permute-done | bytes 122912 | tf_op jit(solution)/shard_map/ppermute | solution.py:357
  106.8 0.7 collective-permute-start.20
  107.6 1.3 %collective-permute-start.21 = (f32[120,128]{1,0:T(8,128)S(1)}, f32[120,128]{1,0:T(8,128)S(1)}, u32[]{:S(2)}, u32[]{:S(2)}) collective-permute-start(f32[120,128]{1,0:T(8,128)S(1)} %get-tuple-element.35), channel_id=1, source_target_pairs={{0,4},{4,8},{8,12},{12,0},{1,5},{5,9},{9,13},{13,1},{2,6},{6,10},{... | collective-permute-start | bytes 184328 | tf_op jit(solution)/shard_map/ppermute | solution.py:377
  109.2 0.9 finish.2.base_ref
  110.0 1.2 %collective-permute-done.20.refs_0_ = f32[120,128]{1,0:T(8,128)S(1)} collective-permute-done((f32[120,128]{1,0:T(8,128)S(1)}, f32[120,128]{1,0:T(8,128)S(1)}, u32[]{:S(2)}, u32[]{:S(2)}) %collective-permute-start.20) | collective-permute-done | bytes 61472 | tf_op jit(solution)/shard_map/ppermute | solution.py:377
  111.2 2.4 %collective-permute-done.21.refs_1_ = f32[120,128]{1,0:T(8,128)S(1)} collective-permute-done((f32[120,128]{1,0:T(8,128)S(1)}, f32[120,128]{1,0:T(8,128)S(1)}, u32[]{:S(2)}, u32[]{:S(2)}) %collective-permute-start.21) | collective-permute-done | bytes 61472 | tf_op jit(solution)/shard_map/ppermute | solution.py:377
  113.6 1.6 %finish.3 = bf16[768,256]{1,0:T(8,128)(2,1)} custom-call(s32[1]{0:T(128)} %bitcast.2.place_ref, s32[768,1]{1,0:T(8,128)S(1)} %copy-done.6, f32[768,256]{1,0:T(8,128)S(1)} %finish.2.base_ref, bf16[32,64,256]{2,1,0:T(8,128)(2,1)S(1)} %pad_maximum_fusion.up_ref, f32[120,128]{1,0:T(8,128)S(1)} %collective-permute-done.20.refs_0_, ...), custom_call_target="tpu_custom_call" | custom-call | flops 1 | bytes 1 | tf_op jit(solution)/shard_map/finish/pallas_call | solution.py:160
  (91 shorter events, 4.1 us)
Async XLA Ops:
  0.0 1.0 copy-start
  1.0 20.8 %copy-start.18 = (bf16[8,32,256]{2,1,0:T(8,128)(2,1)}, bf16[8,32,256]{2,1,0:T(8,128)(2,1)S(1)}, u32[]{:S(2)}) copy-start(bf16[8,32,256]{2,1,0:T(8,128)(2,1)S(1)} %constant_dynamic-slice_fusion) | copy-start | bytes 393220
  1.0 14.3 %collective-permute-start = (bf16[8,32,256]{2,1,0:T(8,128)(2,1)S(1)}, bf16[8,32,256]{2,1,0:T(8,128)(2,1)S(1)}, u32[]{:S(2)}, u32[]{:S(2)}) collective-permute-start(bf16[8,32,256]{2,1,0:T(8,128)(2,1)S(1)} %constant_dynamic-slice_fusion), channel_id=1, source_target_pairs={{0,12},{4,0},{8,4},{12,8},{1,13},{5,1},{9,5},{13,9},{2,14},{6,2},{... | collective-permute-start | bytes 393224 | tf_op jit(solution)/shard_map/ppermute | solution.py:196
  6.1 11.2 %collective-permute-start.1 = (bf16[8,32,256]{2,1,0:T(8,128)(2,1)S(1)}, bf16[8,32,256]{2,1,0:T(8,128)(2,1)S(1)}, u32[]{:S(2)}, u32[]{:S(2)}) collective-permute-start(bf16[8,32,256]{2,1,0:T(8,128)(2,1)S(1)} %constant_dynamic-slice_fusion), channel_id=1, source_target_pairs={{0,8},{4,12},{8,0},{12,4},{1,9},{5,13},{9,1},{13,5},{2,10},{6,14},... | collective-permute-start | bytes 393224 | tf_op jit(solution)/shard_map/ppermute | solution.py:196
  6.1 11.2 %collective-permute-start.2 = (bf16[8,32,256]{2,1,0:T(8,128)(2,1)S(1)}, bf16[8,32,256]{2,1,0:T(8,128)(2,1)S(1)}, u32[]{:S(2)}, u32[]{:S(2)}) collective-permute-start(bf16[8,32,256]{2,1,0:T(8,128)(2,1)S(1)} %constant_dynamic-slice_fusion), channel_id=1, source_target_pairs={{0,4},{4,8},{8,12},{12,0},{1,5},{5,9},{9,13},{13,1},{2,6},{6,10},{... | collective-permute-start | bytes 393224 | tf_op jit(solution)/shard_map/ppermute | solution.py:196
  15.3 2.0 %copy-start.12 = (bf16[8,32,256]{2,1,0:T(8,128)(2,1)}, bf16[8,32,256]{2,1,0:T(8,128)(2,1)S(1)}, u32[]{:S(2)}) copy-start(bf16[8,32,256]{2,1,0:T(8,128)(2,1)S(1)} %collective-permute-done.refs_3_) | copy-start | bytes 393220
  17.3 0.6 copy-start.14
  17.3 0.7 copy-start.16
  18.6 46.1 %collective-permute-start.12 = (bf16[216,2048]{1,0:T(8,128)(2,1)}, bf16[216,2048]{1,0:T(8,128)(2,1)}, u32[]{:S(2)}, u32[]{:S(2)}) collective-permute-start(bf16[216,2048]{1,0:T(8,128)(2,1)} %get-tuple-element.27), channel_id=1, source_target_pairs={{0,8},{4,12},{8,0},{12,4},{1,9},{5,13},{9,1},{13,5},{2,10},{6,14},... | collective-permute-start | bytes 2654216 | tf_op jit(solution)/shard_map/ppermute | solution.py:312
  21.8 4.2 %copy-start.1 = (bf16[768,2048]{1,0:T(8,128)(2,1)S(1)}, bf16[768,2048]{1,0:T(8,128)(2,1)}, u32[]{:S(2)}) copy-start(bf16[768,2048]{1,0:T(8,128)(2,1)} %tokens_ref.13) | copy-start | bytes 9437188
  21.8 4.2 %copy-start.9 = (s32[8,128]{1,0:T(8,128)S(1)}, s32[8,128]{1,0:T(8,128)}, u32[]{:S(2)}) copy-start(s32[8,128]{1,0:T(8,128)} %get-tuple-element.24.refs_0_) | copy-start | bytes 12292
  21.8 4.2 %copy-start.10 = (s32[2]{0:T(128)S(1)}, s32[2]{0:T(128)}, u32[]{:S(2)}) copy-start(s32[2]{0:T(128)} %broadcast_xor_fusion.block_ref) | copy-start | bytes 28
  25.9 25.5 %collective-permute-start.3 = (f32[256,512]{1,0:T(8,128)}, f32[256,512]{1,0:T(8,128)}, u32[]{:S(2)}, u32[]{:S(2)}) collective-permute-start(f32[256,512]{1,0:T(8,128)} %base.6.refs_0_), channel_id=1, source_target_pairs={{0,1},{1,0},{2,3},{3,2},{4,5},{5,4},{6,7},{7,6},{8,9},{9,8},{10,11... | collective-permute-start | bytes 1572872 | tf_op jit(solution)/shard_map/ppermute | solution.py:255
  25.9 2.2 %copy-start.2 = (bf16[2048,1024]{1,0:T(8,128)(2,1)S(1)}, bf16[2048,1024]{1,0:T(8,128)(2,1)}, u32[]{:S(2)}) copy-start(bf16[2048,1024]{1,0:T(8,128)(2,1)} %weight_ref.11) | copy-start | bytes 12582916
  30.6 6.5 %copy-start.11 = (s32[8,128]{1,0:T(8,128)S(1)}, s32[8,128]{1,0:T(8,128)}, u32[]{:S(2)}) copy-start(s32[8,128]{1,0:T(8,128)} %get-tuple-element.29.refs_2_) | copy-start | bytes 12292
  30.6 26.3 %collective-permute-start.7 = (f32[256,512]{1,0:T(8,128)}, f32[256,512]{1,0:T(8,128)}, u32[]{:S(2)}, u32[]{:S(2)}) collective-permute-start(f32[256,512]{1,0:T(8,128)} %base.10.refs_0_), channel_id=1, source_target_pairs={{0,1},{1,0},{2,3},{3,2},{4,5},{5,4},{6,7},{7,6},{8,9},{9,8},{10,11... | collective-permute-start | bytes 1572872 | tf_op jit(solution)/shard_map/ppermute | solution.py:255
  33.6 9.3 %copy-start.22 = (s32[1,768]{1,0:T(1,128)S(1)}, s32[1,768]{1,0:T(1,128)}, u32[]{:S(2)}) copy-start(s32[1,768]{1,0:T(1,128)} %get-tuple-element.20.index_ref) | copy-start | bytes 9220
  33.6 28.4 %collective-permute-start.5 = (f32[256,512]{1,0:T(8,128)}, f32[256,512]{1,0:T(8,128)}, u32[]{:S(2)}, u32[]{:S(2)}) collective-permute-start(f32[256,512]{1,0:T(8,128)} %base.8.refs_0_), channel_id=1, source_target_pairs={{0,1},{1,0},{2,3},{3,2},{4,5},{5,4},{6,7},{7,6},{8,9},{9,8},{10,11... | collective-permute-start | bytes 1572872 | tf_op jit(solution)/shard_map/ppermute | solution.py:255
  37.1 2.2 %copy-start.4 = (bf16[8,2048,128]{2,1,0:T(8,128)(2,1)S(1)}, bf16[8,2048,128]{2,1,0:T(8,128)(2,1)}, u32[]{:S(2)}) copy-start(bf16[8,2048,128]{2,1,0:T(8,128)(2,1)} %refs_2_.1) | copy-start | bytes 12582916
  39.3 1.2 %copy-start.8 = (bf16[216,2048]{1,0:T(8,128)(2,1)S(1)}, bf16[216,2048]{1,0:T(8,128)(2,1)}, u32[]{:S(2)}) copy-start(bf16[216,2048]{1,0:T(8,128)(2,1)} %get-tuple-element.28.refs_0_) | copy-start | bytes 2654212
  41.8 2.0 %collective-permute-start.15 = (f32[240,128]{1,0:T(8,128)S(1)}, f32[240,128]{1,0:T(8,128)}, u32[]{:S(2)}, u32[]{:S(2)}) collective-permute-start(f32[240,128]{1,0:T(8,128)S(1)} %shrink.4), channel_id=1, source_target_pairs={{0,1},{1,0},{2,3},{3,2},{4,5},{5,4},{6,7},{7,6},{8,9},{9,8},{10,11... | collective-permute-start | bytes 368648 | tf_op jit(solution)/shard_map/ppermute | solution.py:353
  44.8 13.5 %collective-permute-start.16 = (f32[120,128]{1,0:T(8,128)S(1)}, f32[120,128]{1,0:T(8,128)S(1)}, u32[]{:S(2)}, u32[]{:S(2)}) collective-permute-start(f32[120,128]{1,0:T(8,128)S(1)} %slice.95), channel_id=1, source_target_pairs={{0,2},{1,3},{2,0},{3,1},{4,6},{5,7},{6,4},{7,5},{8,10},{9,11},{10,... | collective-permute-start | bytes 184328 | tf_op jit(solution)/shard_map/ppermute | solution.py:357
  46.3 2.2 %copy-start.3 = (bf16[2048,1024]{1,0:T(8,128)(2,1)S(1)}, bf16[2048,1024]{1,0:T(8,128)(2,1)}, u32[]{:S(2)}) copy-start(bf16[2048,1024]{1,0:T(8,128)(2,1)} %weight_ref.11) | copy-start | bytes 12582916
  48.5 1.0 copy-start.7
  49.6 3.6 %copy-start.13 = (bf16[8,32,256]{2,1,0:T(8,128)(2,1)S(1)}, bf16[8,32,256]{2,1,0:T(8,128)(2,1)}, u32[]{:S(2)}) copy-start(bf16[8,32,256]{2,1,0:T(8,128)(2,1)} %copy-done.12) | copy-start | bytes 393220
  49.6 3.6 %copy-start.15 = (bf16[8,32,256]{2,1,0:T(8,128)(2,1)S(1)}, bf16[8,32,256]{2,1,0:T(8,128)(2,1)}, u32[]{:S(2)}) copy-start(bf16[8,32,256]{2,1,0:T(8,128)(2,1)} %copy-done.14) | copy-start | bytes 393220
  49.6 3.6 %copy-start.17 = (bf16[8,32,256]{2,1,0:T(8,128)(2,1)S(1)}, bf16[8,32,256]{2,1,0:T(8,128)(2,1)}, u32[]{:S(2)}) copy-start(bf16[8,32,256]{2,1,0:T(8,128)(2,1)} %copy-done.16) | copy-start | bytes 393220
  49.6 3.6 %copy-start.19 = (bf16[8,32,256]{2,1,0:T(8,128)(2,1)S(1)}, bf16[8,32,256]{2,1,0:T(8,128)(2,1)}, u32[]{:S(2)}) copy-start(bf16[8,32,256]{2,1,0:T(8,128)(2,1)} %copy-done.18) | copy-start | bytes 393220
  52.5 15.7 %collective-permute-start.4 = (f32[256,256]{1,0:T(8,128)S(1)}, f32[256,256]{1,0:T(8,128)S(1)}, u32[]{:S(2)}, u32[]{:S(2)}) collective-permute-start(f32[256,256]{1,0:T(8,128)S(1)} %slice.82), channel_id=1, source_target_pairs={{0,2},{1,3},{2,0},{3,1},{4,6},{5,7},{6,4},{7,5},{8,10},{9,11},{10,... | collective-permute-start | bytes 786440 | tf_op jit(solution)/shard_map/ppermute | solution.py:255
  55.0 1.8 %copy-start.20 = (bf16[216,2048]{1,0:T(8,128)(2,1)S(1)}, bf16[216,2048]{1,0:T(8,128)(2,1)}, u32[]{:S(2)}) copy-start(bf16[216,2048]{1,0:T(8,128)(2,1)} %get-tuple-element.25) | copy-start | bytes 2654212
  55.0 3.2 %copy-start.21 = (bf16[216,2048]{1,0:T(8,128)(2,1)S(1)}, bf16[216,2048]{1,0:T(8,128)(2,1)}, u32[]{:S(2)}) copy-start(bf16[216,2048]{1,0:T(8,128)(2,1)} %get-tuple-element.26) | copy-start | bytes 2654212
  56.8 9.4 %copy-start.5 = (bf16[8,2048,128]{2,1,0:T(8,128)(2,1)S(1)}, bf16[8,2048,128]{2,1,0:T(8,128)(2,1)}, u32[]{:S(2)}) copy-start(bf16[8,2048,128]{2,1,0:T(8,128)(2,1)} %refs_2_.1) | copy-start | bytes 12582916
  56.9 24.4 %collective-permute-start.10 = (bf16[216,2048]{1,0:T(8,128)(2,1)S(1)}, bf16[216,2048]{1,0:T(8,128)(2,1)S(1)}, u32[]{:S(2)}, u32[]{:S(2)}) collective-permute-start(bf16[216,2048]{1,0:T(8,128)(2,1)S(1)} %copy-done.20), channel_id=1, source_target_pairs={{0,4},{4,8},{8,12},{12,0},{1,5},{5,9},{9,13},{13,1},{2,6},{6,10},{... | collective-permute-start | bytes 2654216 | tf_op jit(solution)/shard_map/ppermute | solution.py:312
  58.3 40.0 %collective-permute-start.11 = (bf16[216,2048]{1,0:T(8,128)(2,1)S(1)}, bf16[216,2048]{1,0:T(8,128)(2,1)S(1)}, u32[]{:S(2)}, u32[]{:S(2)}) collective-permute-start(bf16[216,2048]{1,0:T(8,128)(2,1)S(1)} %copy-done.21), channel_id=1, source_target_pairs={{0,12},{4,0},{8,4},{12,8},{1,13},{5,1},{9,5},{13,9},{2,14},{6,2},{... | collective-permute-start | bytes 2654216 | tf_op jit(solution)/shard_map/ppermute | solution.py:312
  62.0 8.3 %collective-permute-start.8 = (f32[256,256]{1,0:T(8,128)S(1)}, f32[256,256]{1,0:T(8,128)S(1)}, u32[]{:S(2)}, u32[]{:S(2)}) collective-permute-start(f32[256,256]{1,0:T(8,128)S(1)} %slice.86), channel_id=1, source_target_pairs={{0,2},{1,3},{2,0},{3,1},{4,6},{5,7},{6,4},{7,5},{8,10},{9,11},{10,... | collective-permute-start | bytes 786440 | tf_op jit(solution)/shard_map/ppermute | solution.py:255
  64.7 35.2 %collective-permute-start.9 = (bf16[32,32,256]{2,1,0:T(8,128)(2,1)S(1)}, bf16[32,32,256]{2,1,0:T(8,128)(2,1)S(1)}, u32[]{:S(2)}, u32[]{:S(2)}) collective-permute-start(bf16[32,32,256]{2,1,0:T(8,128)(2,1)S(1)} %pad_maximum_fusion.2), channel_id=1, source_target_pairs={{0,16},{16,0},{1,17},{17,1},{2,18},{18,2},{3,19},{19,3},{4,20},{20... | collective-permute-start | bytes 1572872 | tf_op jit(solution)/shard_map/ppermute | solution.py:200
  68.3 1.4 %collective-permute-start.13 = (f32[240,128]{1,0:T(8,128)S(1)}, f32[240,128]{1,0:T(8,128)S(1)}, u32[]{:S(2)}, u32[]{:S(2)}) collective-permute-start(f32[240,128]{1,0:T(8,128)S(1)} %shrink.3), channel_id=1, source_target_pairs={{0,1},{1,0},{2,3},{3,2},{4,5},{5,4},{6,7},{7,6},{8,9},{9,8},{10,11... | collective-permute-start | bytes 368648 | tf_op jit(solution)/shard_map/ppermute | solution.py:353
  69.7 33.2 %collective-permute-start.6 = (f32[256,256]{1,0:T(8,128)S(1)}, f32[256,256]{1,0:T(8,128)S(1)}, u32[]{:S(2)}, u32[]{:S(2)}) collective-permute-start(f32[256,256]{1,0:T(8,128)S(1)} %slice.84), channel_id=1, source_target_pairs={{0,2},{1,3},{2,0},{3,1},{4,6},{5,7},{6,4},{7,5},{8,10},{9,11},{10,... | collective-permute-start | bytes 786440 | tf_op jit(solution)/shard_map/ppermute | solution.py:255
  70.3 9.1 %collective-permute-start.14 = (f32[120,128]{1,0:T(8,128)S(1)}, f32[120,128]{1,0:T(8,128)S(1)}, u32[]{:S(2)}, u32[]{:S(2)}) collective-permute-start(f32[120,128]{1,0:T(8,128)S(1)} %slice.93), channel_id=1, source_target_pairs={{0,2},{1,3},{2,0},{3,1},{4,6},{5,7},{6,4},{7,5},{8,10},{9,11},{10,... | collective-permute-start | bytes 184328 | tf_op jit(solution)/shard_map/ppermute | solution.py:357
  99.7 1.6 %collective-permute-start.18 = (f32[480,128]{1,0:T(8,128)S(1)}, f32[480,128]{1,0:T(8,128)S(1)}, u32[]{:S(2)}, u32[]{:S(2)}) collective-permute-start(f32[480,128]{1,0:T(8,128)S(1)} %get-tuple-element.32), channel_id=1, source_target_pairs={{0,1},{1,0},{2,3},{3,2},{4,5},{5,4},{6,7},{7,6},{8,9},{9,8},{10,11... | collective-permute-start | bytes 737288 | tf_op jit(solution)/shard_map/ppermute | solution.py:353
  99.9 9.2 %copy-start.6 = (s32[768,1]{1,0:T(8,128)S(1)}, s32[768,1]{1,0:T(8,128)}, u32[]{:S(2)}) copy-start(s32[768,1]{1,0:T(8,128)} %copy.14.index_ref) | copy-start | bytes 9220
  101.4 5.4 %collective-permute-start.19 = (f32[240,128]{1,0:T(8,128)S(1)}, f32[240,128]{1,0:T(8,128)S(1)}, u32[]{:S(2)}, u32[]{:S(2)}) collective-permute-start(f32[240,128]{1,0:T(8,128)S(1)} %slice.97), channel_id=1, source_target_pairs={{0,2},{1,3},{2,0},{3,1},{4,6},{5,7},{6,4},{7,5},{8,10},{9,11},{10,... | collective-permute-start | bytes 368648 | tf_op jit(solution)/shard_map/ppermute | solution.py:357
  103.0 6.2 %collective-permute-start.17 = (f32[120,128]{1,0:T(8,128)S(1)}, f32[120,128]{1,0:T(8,128)S(1)}, u32[]{:S(2)}, u32[]{:S(2)}) collective-permute-start(f32[120,128]{1,0:T(8,128)S(1)} %get-tuple-element.30), channel_id=1, source_target_pairs={{0,8},{4,12},{8,0},{12,4},{1,9},{5,13},{9,1},{13,5},{2,10},{6,14},... | collective-permute-start | bytes 184328 | tf_op jit(solution)/shard_map/ppermute | solution.py:377
  106.8 4.4 %collective-permute-start.20 = (f32[120,128]{1,0:T(8,128)S(1)}, f32[120,128]{1,0:T(8,128)S(1)}, u32[]{:S(2)}, u32[]{:S(2)}) collective-permute-start(f32[120,128]{1,0:T(8,128)S(1)} %get-tuple-element.36), channel_id=1, source_target_pairs={{0,12},{4,0},{8,4},{12,8},{1,13},{5,1},{9,5},{13,9},{2,14},{6,2},{... | collective-permute-start | bytes 184328 | tf_op jit(solution)/shard_map/ppermute | solution.py:377
  107.6 6.0 %collective-permute-start.21 = (f32[120,128]{1,0:T(8,128)S(1)}, f32[120,128]{1,0:T(8,128)S(1)}, u32[]{:S(2)}, u32[]{:S(2)}) collective-permute-start(f32[120,128]{1,0:T(8,128)S(1)} %get-tuple-element.35), channel_id=1, source_target_pairs={{0,4},{4,8},{8,12},{12,0},{1,5},{5,9},{9,13},{13,1},{2,6},{6,10},{... | collective-permute-start | bytes 184328 | tf_op jit(solution)/shard_map/ppermute | solution.py:377

commit v12 on v11

--- a/solution.py
+++ b/solution.py
@@ -313,7 +313,7 @@
 
     packed, own_block, *blocks = pack([0] + order)
     arrived = {0: own_block}
-    mark, *blocks = gate(blocks, found)
+    mark, *blocks = gate(blocks, [packed])
     for r, block in zip(order, blocks):
         arrived[r] = send(block, r)
 
@@ -358,7 +358,7 @@
 
     slabs = 3
     slab_sums = [
-        reduce_base(tokens, key_value_weight, piece, pieces, columns, slab, slabs, [mark])
+        reduce_base(tokens, key_value_weight, piece, pieces, columns, slab, slabs, [mark] + found)
         for slab in range(slabs)
     ]
     base = jnp.concatenate([total for total, _ in slab_sums], axis=0)

time: 116 us -> 117 us (level)
  local copies, waits for them, and re-layouts: 12.7 us -> 14.3 us
    ppermute x3, waiting for transfers between devices: 1.96 us -> 0.01 us  [gather_up(): lax.ppermute(own, 'batch', [(i, (i - r) % homes) for i in range(homes)])]
    unnamed x46 -> x52, local copies, waits for them, and re-layouts: 10.5 us -> 12 us
  transfers between devices with their start and end apart: 22 -> 22, of which waited for: 10 -> 9; matrix products, arithmetic and copies ran while one was open for 7% -> 7% of each run, Pallas kernels for 25% -> 25%
where the time goes in v12:
time: 117 us; the launch traced here: 116 us
  waiting for transfers between devices  36.7 us (31%)
  Pallas kernels  30.7 us (26%)
  starting transfers between devices  25.1 us (21%)
  local copies, waits for them, and re-layouts  14.3 us (12%)
  other arithmetic  5.41 us (5%)
  between operations  3.94 us (3%)
    ppermute x3, waiting for transfers between devices, send(): lax.ppermute(block, 'batch', [(i, (i + r) % homes) for i in range(homes)])  19 us
    pallas_call x6, Pallas kernels, base_part(): pl.pallas_call(functools.partial(base_kernel, len(after)), out_shape=jax....  14.5 us
    unnamed x52, local copies, waits for them, and re-layouts  12 us
    ppermute x3, waiting for transfers between devices, combine(): lax.ppermute(value[half:], 'tensor', [(i, i ^ bit) for i in range(pieces)])  10.6 us
    pallas_call x1, Pallas kernels, pack(): pl.pallas_call(functools.partial(pack_kernel, span, shifts), out_shape=[j...  6.47 us
    ppermute x3, starting transfers between devices, gather_up(): lax.ppermute(own, 'batch', [(i, (i - r) % homes) for i in range(homes)])  6.11 us
    ppermute x3, starting transfers between devices, send(): lax.ppermute(block, 'batch', [(i, (i + r) % homes) for i in range(homes)])  6.1 us
    pallas_call x3, Pallas kernels, shrink(): pl.pallas_call(functools.partial(shrink_kernel, held, light, rank, value_...  4.86 us
  transfers between devices with their start and end apart: 22, of which 9 were waited for; matrix products, arithmetic and copies ran while one was open for 7% of the time, Pallas kernels for 25%

profile of v12, /device:TPU:0, one launch (start us, length us, event | category | flops | bytes accessed | tf_op | source)
XLA Modules:
  0.0 116.2 jit_solution(16871701500100453517)
XLA Ops:
  0.0 0.9 copy-done
  1.0 5.1 %collective-permute-start = (bf16[8,32,256]{2,1,0:T(8,128)(2,1)S(1)}, bf16[8,32,256]{2,1,0:T(8,128)(2,1)S(1)}, u32[]{:S(2)}, u32[]{:S(2)}) collective-permute-start(bf16[8,32,256]{2,1,0:T(8,128)(2,1)S(1)} %constant_dynamic-slice_fusion), channel_id=1, source_target_pairs={{0,12},{4,0},{8,4},{12,8},{1,13},{5,1},{9,5},{13,9},{2,14},{6,2},{... | collective-permute-start | bytes 393224 | tf_op jit(solution)/shard_map/ppermute | solution.py:196
  6.1 1.0 collective-permute-start.2
  7.1 1.7 %route.1 = (s32[1,768]{1,0:T(1,128)}, s32[8,128]{1,0:T(8,128)}) custom-call(s32[1]{0:T(128)} %bitcast.place_ref, s32[32]{0:T(128)} %entry_hbm.1, s32[768]{0:T(1024)} %request_hbm.1), custom_call_target="tpu_custom_call" | custom-call | flops 1 | bytes 1 | tf_op jit(solution)/shard_map/route/pallas_call | solution.py:279
  8.8 6.5 %pack.1 = (s32[8,128]{1,0:T(8,128)}, bf16[216,2048]{1,0:T(8,128)(2,1)}, bf16[216,2048]{1,0:T(8,128)(2,1)}, bf16[216,2048]{1,0:T(8,128)(2,1)}, bf16[216,2048]{1,0:T(8,128)(2,1)}) custom-call(s32[1,768]{1,0:T(1,128)} %get-tuple-element.20.index_ref, bf16[768,2048]{1,0:T(8,128)(2,1)} %tokens_ref.13), custom_call_target="tpu_custom_call" | custom-call | flops 1 | bytes 1 | tf_op jit(solution)/shard_map/pack/pallas_call | solution.py:297
  15.9 1.9 %collective-permute-start.12 = (bf16[216,2048]{1,0:T(8,128)(2,1)}, bf16[216,2048]{1,0:T(8,128)(2,1)}, u32[]{:S(2)}, u32[]{:S(2)}) collective-permute-start(bf16[216,2048]{1,0:T(8,128)(2,1)} %get-tuple-element.28), channel_id=1, source_target_pairs={{0,8},{4,12},{8,0},{12,4},{1,9},{5,13},{9,1},{13,5},{2,10},{6,14},... | collective-permute-start | bytes 2654216 | tf_op jit(solution)/shard_map/ppermute | solution.py:312
  18.4 0.7 copy-done.10
  19.1 0.6 copy-done.13
  19.7 4.2 %base.6.refs_0_ = f32[256,512]{1,0:T(8,128)} custom-call(s32[2]{0:T(128)} %broadcast_xor_fusion.block_ref, bf16[768,2048]{1,0:T(8,128)(2,1)} %tokens_ref.13, bf16[2048,1024]{1,0:T(8,128)(2,1)} %weight_ref.11, s32[8,128]{1,0:T(8,128)} %get-tuple-element.25.refs_0_, bf16[8,32,256]{2,1,0:T(8,128)(2,1)} %copy-done.7, bf16[8,32,256]{2,1,0:T(8,128)(2,1)} %copy-done.10, ...), custom_call_target="tpu_custom_call" | custom-call | flops 1 | bytes 1 | tf_op jit(solution)/shard_map/base/pallas_call | solution.py:223
  24.0 2.2 %copy-done.2 = bf16[2048,1024]{1,0:T(8,128)(2,1)S(1)} copy-done((bf16[2048,1024]{1,0:T(8,128)(2,1)S(1)}, bf16[2048,1024]{1,0:T(8,128)(2,1)}, u32[]{:S(2)}) %copy-start.2) | copy-done | bytes 4194328
  26.1 0.9 copy-done.8
  27.0 2.5 %base.10.refs_0_ = f32[256,512]{1,0:T(8,128)} custom-call(s32[2]{0:T(128)S(1)} %copy-done.20, bf16[768,2048]{1,0:T(8,128)(2,1)S(1)} %copy-done.1, bf16[2048,1024]{1,0:T(8,128)(2,1)S(1)} %copy-done.2, s32[8,128]{1,0:T(8,128)S(1)} %copy-done.18, bf16[8,32,256]{2,1,0:T(8,128)(2,1)S(1)} %copy-done.8, bf16[8,32,256]{2,1,0:T(8,128)(2,1)S(1)} %copy-done.11, ...), custom_call_target="tpu_custom_call" | custom-call | flops 1 | bytes 1 | tf_op jit(solution)/shard_map/base/pallas_call | solution.py:223
  30.0 2.5 %base.8.refs_0_ = f32[256,512]{1,0:T(8,128)} custom-call(s32[2]{0:T(128)S(1)} %copy-done.20, bf16[768,2048]{1,0:T(8,128)(2,1)S(1)} %copy-done.1, bf16[2048,1024]{1,0:T(8,128)(2,1)S(1)} %copy-done.2, s32[8,128]{1,0:T(8,128)S(1)} %copy-done.18, bf16[8,32,256]{2,1,0:T(8,128)(2,1)S(1)} %copy-done.8, bf16[8,32,256]{2,1,0:T(8,128)(2,1)S(1)} %copy-done.11, ...), custom_call_target="tpu_custom_call" | custom-call | flops 1 | bytes 1 | tf_op jit(solution)/shard_map/base/pallas_call | solution.py:223
  32.5 1.3 %slice.61 = s32[1,1]{1,0:T(1,128)} slice(s32[8,128]{1,0:T(8,128)} %get-tuple-element.19), slice={[0:1], [0:1]} | slice | bytes 8 | tf_op jit(solution)/shard_map/slice | solution.py:320
  36.7 2.2 %copy-done.4 = bf16[8,2048,128]{2,1,0:T(8,128)(2,1)S(1)} copy-done((bf16[8,2048,128]{2,1,0:T(8,128)(2,1)S(1)}, bf16[8,2048,128]{2,1,0:T(8,128)(2,1)}, u32[]{:S(2)}) %copy-start.4) | copy-done | bytes 4194328
  38.9 1.2 %copy-done.17 = bf16[216,2048]{1,0:T(8,128)(2,1)S(1)} copy-done((bf16[216,2048]{1,0:T(8,128)(2,1)S(1)}, bf16[216,2048]{1,0:T(8,128)(2,1)}, u32[]{:S(2)}) %copy-start.17) | copy-done | bytes 884760
  40.0 1.4 %shrink.4 = f32[240,128]{1,0:T(8,128)S(1)} custom-call(s32[3]{0:T(128)S(1)} %pad_add_fusion.scalar_ref, bf16[216,2048]{1,0:T(8,128)(2,1)S(1)} %copy-done.17, bf16[8,2048,128]{2,1,0:T(8,128)(2,1)S(1)} %copy-done.4, s32[8,128]{1,0:T(8,128)S(1)} %copy-done.19), custom_call_target="tpu_custom_call" | custom-call | flops 1 | bytes 1 | tf_op jit(solution)/shard_map/shrink/pallas_call | solution.py:326
  42.6 0.9 copy.14.index_ref
  43.6 0.9 add.58
  44.5 1.6 %collective-permute-start.16 = (f32[120,128]{1,0:T(8,128)S(1)}, f32[120,128]{1,0:T(8,128)S(1)}, u32[]{:S(2)}, u32[]{:S(2)}) collective-permute-start(f32[120,128]{1,0:T(8,128)S(1)} %slice.95), channel_id=1, source_target_pairs={{0,2},{1,3},{2,0},{3,1},{4,6},{5,7},{6,4},{7,5},{8,10},{9,11},{10,... | collective-permute-start | bytes 184328 | tf_op jit(solution)/shard_map/ppermute | solution.py:357
  46.1 2.2 %copy-done.3 = bf16[2048,1024]{1,0:T(8,128)(2,1)S(1)} copy-done((bf16[2048,1024]{1,0:T(8,128)(2,1)S(1)}, bf16[2048,1024]{1,0:T(8,128)(2,1)}, u32[]{:S(2)}) %copy-start.3) | copy-done | bytes 4194328
  48.3 1.0 copy-done.16
  49.3 1.8 %base.7 = f32[256,512]{1,0:T(8,128)S(1)} custom-call(s32[2]{0:T(128)S(1)} %multiply_xor_fusion.block_ref, bf16[768,2048]{1,0:T(8,128)(2,1)S(1)} %copy-done.1, bf16[2048,1024]{1,0:T(8,128)(2,1)S(1)} %copy-done.3, f32[256,512]{1,0:T(8,128)S(1)} %copy-done.16), custom_call_target="tpu_custom_call" | custom-call | flops 1 | bytes 1 | tf_op jit(solution)/shard_map/base/pallas_call | solution.py:223
  51.1 1.1 add.50
  53.0 1.8 %base.9 = f32[256,512]{1,0:T(8,128)S(1)} custom-call(s32[2]{0:T(128)S(1)} %multiply_xor_fusion.block_ref, bf16[768,2048]{1,0:T(8,128)(2,1)S(1)} %copy-done.1, bf16[2048,1024]{1,0:T(8,128)(2,1)S(1)} %copy-done.3, f32[256,512]{1,0:T(8,128)} %base.8.refs_0_), custom_call_target="tpu_custom_call" | custom-call | flops 1 | bytes 1 | tf_op jit(solution)/shard_map/base/pallas_call | solution.py:223
  54.8 1.8 %base.11 = f32[256,512]{1,0:T(8,128)S(1)} custom-call(s32[2]{0:T(128)S(1)} %multiply_xor_fusion.block_ref, bf16[768,2048]{1,0:T(8,128)(2,1)S(1)} %copy-done.1, bf16[2048,1024]{1,0:T(8,128)(2,1)S(1)} %copy-done.3, f32[256,512]{1,0:T(8,128)} %base.10.refs_0_), custom_call_target="tpu_custom_call" | custom-call | flops 1 | bytes 1 | tf_op jit(solution)/shard_map/base/pallas_call | solution.py:223
  56.6 1.5 %collective-permute-start.10 = (bf16[216,2048]{1,0:T(8,128)(2,1)S(1)}, bf16[216,2048]{1,0:T(8,128)(2,1)S(1)}, u32[]{:S(2)}, u32[]{:S(2)}) collective-permute-start(bf16[216,2048]{1,0:T(8,128)(2,1)S(1)} %copy-done.23), channel_id=1, source_target_pairs={{0,4},{4,8},{8,12},{12,0},{1,5},{5,9},{9,13},{13,1},{2,6},{6,10},{... | collective-permute-start | bytes 2654216 | tf_op jit(solution)/shard_map/ppermute | solution.py:312
  58.1 1.1 add.54
  59.3 2.7 %collective-permute-start.11 = (bf16[216,2048]{1,0:T(8,128)(2,1)S(1)}, bf16[216,2048]{1,0:T(8,128)(2,1)S(1)}, u32[]{:S(2)}, u32[]{:S(2)}) collective-permute-start(bf16[216,2048]{1,0:T(8,128)(2,1)S(1)} %copy-done.24), channel_id=1, source_target_pairs={{0,12},{4,0},{8,4},{12,8},{1,13},{5,1},{9,5},{13,9},{2,14},{6,2},{... | collective-permute-start | bytes 2654216 | tf_op jit(solution)/shard_map/ppermute | solution.py:312
  62.0 1.5 %collective-permute-start.8 = (f32[256,256]{1,0:T(8,128)S(1)}, f32[256,256]{1,0:T(8,128)S(1)}, u32[]{:S(2)}, u32[]{:S(2)}) collective-permute-start(f32[256,256]{1,0:T(8,128)S(1)} %slice.86), channel_id=1, source_target_pairs={{0,2},{1,3},{2,0},{3,1},{4,6},{5,7},{6,4},{7,5},{8,10},{9,11},{10,... | collective-permute-start | bytes 786440 | tf_op jit(solution)/shard_map/ppermute | solution.py:255
  63.5 1.1 add.52
  64.7 1.5 %collective-permute-start.9 = (bf16[32,32,256]{2,1,0:T(8,128)(2,1)S(1)}, bf16[32,32,256]{2,1,0:T(8,128)(2,1)S(1)}, u32[]{:S(2)}, u32[]{:S(2)}) collective-permute-start(bf16[32,32,256]{2,1,0:T(8,128)(2,1)S(1)} %pad_maximum_fusion.2), channel_id=1, source_target_pairs={{0,16},{16,0},{1,17},{17,1},{2,18},{18,2},{3,19},{19,3},{4,20},{20... | collective-permute-start | bytes 1572872 | tf_op jit(solution)/shard_map/ppermute | solution.py:200
  66.2 2.0 %shrink.3 = f32[240,128]{1,0:T(8,128)S(1)} custom-call(s32[3]{0:T(128)S(1)} %pad_add_fusion.scalar_ref, bf16[216,2048]{1,0:T(8,128)(2,1)} %collective-permute-done.12.refs_0_, bf16[8,2048,128]{2,1,0:T(8,128)(2,1)S(1)} %copy-done.5, f32[8,512]{1,0:T(8,128)S(1)} %slice.89.refs_2_, f32[8,512]{1,0:T(8,128)S(1)} %slice.90.refs_3_, f32[8,512]{1,0:T(8,128)S(1)} %slice.91.refs_4_), custom_call_target="tpu_custom_call" | custom-call | flops 1 | bytes 1 | tf_op jit(solution)/shard_map/shrink/pallas_call | solution.py:326
  68.4 1.3 %collective-permute-done.13 = f32[240,128]{1,0:T(8,128)S(1)} collective-permute-done((f32[240,128]{1,0:T(8,128)S(1)}, f32[240,128]{1,0:T(8,128)S(1)}, u32[]{:S(2)}, u32[]{:S(2)}) %collective-permute-start.13) | collective-permute-done | bytes 122912 | tf_op jit(solution)/shard_map/ppermute | solution.py:353
  70.3 1.5 %collective-permute-start.14 = (f32[120,128]{1,0:T(8,128)S(1)}, f32[120,128]{1,0:T(8,128)S(1)}, u32[]{:S(2)}, u32[]{:S(2)}) collective-permute-start(f32[120,128]{1,0:T(8,128)S(1)} %slice.93), channel_id=1, source_target_pairs={{0,2},{1,3},{2,0},{3,1},{4,6},{5,7},{6,4},{7,5},{8,10},{9,11},{10,... | collective-permute-start | bytes 184328 | tf_op jit(solution)/shard_map/ppermute | solution.py:357
  71.9 7.5 %collective-permute-done.14 = f32[120,128]{1,0:T(8,128)S(1)} collective-permute-done((f32[120,128]{1,0:T(8,128)S(1)}, f32[120,128]{1,0:T(8,128)S(1)}, u32[]{:S(2)}, u32[]{:S(2)}) %collective-permute-start.14) | collective-permute-done | bytes 61472 | tf_op jit(solution)/shard_map/ppermute | solution.py:357
  79.4 1.7 %collective-permute-done.10.refs_0_ = bf16[216,2048]{1,0:T(8,128)(2,1)S(1)} collective-permute-done((bf16[216,2048]{1,0:T(8,128)(2,1)S(1)}, bf16[216,2048]{1,0:T(8,128)(2,1)S(1)}, u32[]{:S(2)}, u32[]{:S(2)}) %collective-permute-start.10) | collective-permute-done | bytes 884768 | tf_op jit(solution)/shard_map/ppermute | solution.py:312
  81.1 17.3 %collective-permute-done.11.refs_1_ = bf16[216,2048]{1,0:T(8,128)(2,1)S(1)} collective-permute-done((bf16[216,2048]{1,0:T(8,128)(2,1)S(1)}, bf16[216,2048]{1,0:T(8,128)(2,1)S(1)}, u32[]{:S(2)}, u32[]{:S(2)}) %collective-permute-start.11) | collective-permute-done | bytes 884768 | tf_op jit(solution)/shard_map/ppermute | solution.py:312
  98.4 1.5 %shrink.5 = (f32[480,128]{1,0:T(8,128)S(1)}, f32[120,128]{1,0:T(8,128)S(1)}, f32[120,128]{1,0:T(8,128)S(1)}) custom-call(s32[3]{0:T(128)S(1)} %pad_add_fusion.scalar_ref, bf16[216,2048]{1,0:T(8,128)(2,1)S(1)} %collective-permute-done.10.refs_0_, bf16[216,2048]{1,0:T(8,128)(2,1)S(1)} %collective-permute-done.11.refs_1_, bf16[8,2048,128]{2,1,0:T(8,128)(2,1)S(1)} %copy-done.5, ...), custom_call_target="tpu_custom_call" | custom-call | flops 1 | bytes 1 | tf_op jit(solution)/shard_map/shrink/pallas_call | solution.py:326
  100.2 1.3 %collective-permute-done.18 = f32[480,128]{1,0:T(8,128)S(1)} collective-permute-done((f32[480,128]{1,0:T(8,128)S(1)}, f32[480,128]{1,0:T(8,128)S(1)}, u32[]{:S(2)}, u32[]{:S(2)}) %collective-permute-start.18) | collective-permute-done | bytes 245792 | tf_op jit(solution)/shard_map/ppermute | solution.py:353
  101.5 1.6 %collective-permute-start.19 = (f32[240,128]{1,0:T(8,128)S(1)}, f32[240,128]{1,0:T(8,128)S(1)}, u32[]{:S(2)}, u32[]{:S(2)}) collective-permute-start(f32[240,128]{1,0:T(8,128)S(1)} %slice.97), channel_id=1, source_target_pairs={{0,2},{1,3},{2,0},{3,1},{4,6},{5,7},{6,4},{7,5},{8,10},{9,11},{10,... | collective-permute-start | bytes 368648 | tf_op jit(solution)/shard_map/ppermute | solution.py:357
  103.2 0.7 collective-permute-start.17
  103.8 3.1 %collective-permute-done.19 = f32[240,128]{1,0:T(8,128)S(1)} collective-permute-done((f32[240,128]{1,0:T(8,128)S(1)}, f32[240,128]{1,0:T(8,128)S(1)}, u32[]{:S(2)}, u32[]{:S(2)}) %collective-permute-start.19) | collective-permute-done | bytes 122912 | tf_op jit(solution)/shard_map/ppermute | solution.py:357
  107.0 1.5 %collective-permute-start.20 = (f32[120,128]{1,0:T(8,128)S(1)}, f32[120,128]{1,0:T(8,128)S(1)}, u32[]{:S(2)}, u32[]{:S(2)}) collective-permute-start(f32[120,128]{1,0:T(8,128)S(1)} %get-tuple-element.36), channel_id=1, source_target_pairs={{0,12},{4,0},{8,4},{12,8},{1,13},{5,1},{9,5},{13,9},{2,14},{6,2},{... | collective-permute-start | bytes 184328 | tf_op jit(solution)/shard_map/ppermute | solution.py:377
  109.4 0.9 finish.2.base_ref
  110.3 0.9 collective-permute-done.20.refs_0_
  111.3 3.3 %collective-permute-done.21.refs_1_ = f32[120,128]{1,0:T(8,128)S(1)} collective-permute-done((f32[120,128]{1,0:T(8,128)S(1)}, f32[120,128]{1,0:T(8,128)S(1)}, u32[]{:S(2)}, u32[]{:S(2)}) %collective-permute-start.21) | collective-permute-done | bytes 61472 | tf_op jit(solution)/shard_map/ppermute | solution.py:377
  114.5 1.6 %finish.3 = bf16[768,256]{1,0:T(8,128)(2,1)} custom-call(s32[1]{0:T(128)} %bitcast.2.place_ref, s32[768,1]{1,0:T(8,128)S(1)} %copy-done.6, f32[768,256]{1,0:T(8,128)S(1)} %finish.2.base_ref, bf16[32,64,256]{2,1,0:T(8,128)(2,1)S(1)} %pad_maximum_fusion.up_ref, f32[120,128]{1,0:T(8,128)S(1)} %collective-permute-done.20.refs_0_, ...), custom_call_target="tpu_custom_call" | custom-call | flops 1 | bytes 1 | tf_op jit(solution)/shard_map/finish/pallas_call | solution.py:160
  (97 shorter events, 5.2 us)
Async XLA Ops:
  0.0 1.0 copy-start
  1.0 17.4 %copy-start.21 = (bf16[8,32,256]{2,1,0:T(8,128)(2,1)}, bf16[8,32,256]{2,1,0:T(8,128)(2,1)S(1)}, u32[]{:S(2)}) copy-start(bf16[8,32,256]{2,1,0:T(8,128)(2,1)S(1)} %constant_dynamic-slice_fusion) | copy-start | bytes 393220
  1.0 17.4 %collective-permute-start = (bf16[8,32,256]{2,1,0:T(8,128)(2,1)S(1)}, bf16[8,32,256]{2,1,0:T(8,128)(2,1)S(1)}, u32[]{:S(2)}, u32[]{:S(2)}) collective-permute-start(bf16[8,32,256]{2,1,0:T(8,128)(2,1)S(1)} %constant_dynamic-slice_fusion), channel_id=1, source_target_pairs={{0,12},{4,0},{8,4},{12,8},{1,13},{5,1},{9,5},{13,9},{2,14},{6,2},{... | collective-permute-start | bytes 393224 | tf_op jit(solution)/shard_map/ppermute | solution.py:196
  6.1 12.3 %collective-permute-start.1 = (bf16[8,32,256]{2,1,0:T(8,128)(2,1)S(1)}, bf16[8,32,256]{2,1,0:T(8,128)(2,1)S(1)}, u32[]{:S(2)}, u32[]{:S(2)}) collective-permute-start(bf16[8,32,256]{2,1,0:T(8,128)(2,1)S(1)} %constant_dynamic-slice_fusion), channel_id=1, source_target_pairs={{0,8},{4,12},{8,0},{12,4},{1,9},{5,13},{9,1},{13,5},{2,10},{6,14},... | collective-permute-start | bytes 393224 | tf_op jit(solution)/shard_map/ppermute | solution.py:196
  6.1 12.3 %collective-permute-start.2 = (bf16[8,32,256]{2,1,0:T(8,128)(2,1)S(1)}, bf16[8,32,256]{2,1,0:T(8,128)(2,1)S(1)}, u32[]{:S(2)}, u32[]{:S(2)}) collective-permute-start(bf16[8,32,256]{2,1,0:T(8,128)(2,1)S(1)} %constant_dynamic-slice_fusion), channel_id=1, source_target_pairs={{0,4},{4,8},{8,12},{12,0},{1,5},{5,9},{9,13},{13,1},{2,6},{6,10},{... | collective-permute-start | bytes 393224 | tf_op jit(solution)/shard_map/ppermute | solution.py:196
  15.9 48.8 %collective-permute-start.12 = (bf16[216,2048]{1,0:T(8,128)(2,1)}, bf16[216,2048]{1,0:T(8,128)(2,1)}, u32[]{:S(2)}, u32[]{:S(2)}) collective-permute-start(bf16[216,2048]{1,0:T(8,128)(2,1)} %get-tuple-element.28), channel_id=1, source_target_pairs={{0,8},{4,12},{8,0},{12,4},{1,9},{5,13},{9,1},{13,5},{2,10},{6,14},... | collective-permute-start | bytes 2654216 | tf_op jit(solution)/shard_map/ppermute | solution.py:312
  18.3 1.4 %copy-start.7 = (bf16[8,32,256]{2,1,0:T(8,128)(2,1)}, bf16[8,32,256]{2,1,0:T(8,128)(2,1)S(1)}, u32[]{:S(2)}) copy-start(bf16[8,32,256]{2,1,0:T(8,128)(2,1)S(1)} %collective-permute-done.refs_1_) | copy-start | bytes 393220
  18.3 0.7 copy-start.10
  19.0 0.7 copy-start.13
  19.7 4.2 %copy-start.1 = (bf16[768,2048]{1,0:T(8,128)(2,1)S(1)}, bf16[768,2048]{1,0:T(8,128)(2,1)}, u32[]{:S(2)}) copy-start(bf16[768,2048]{1,0:T(8,128)(2,1)} %tokens_ref.13) | copy-start | bytes 9437188
  19.7 4.2 %copy-start.11 = (bf16[8,32,256]{2,1,0:T(8,128)(2,1)S(1)}, bf16[8,32,256]{2,1,0:T(8,128)(2,1)}, u32[]{:S(2)}) copy-start(bf16[8,32,256]{2,1,0:T(8,128)(2,1)} %copy-done.10) | copy-start | bytes 393220
  19.7 4.2 %copy-start.14 = (bf16[8,32,256]{2,1,0:T(8,128)(2,1)S(1)}, bf16[8,32,256]{2,1,0:T(8,128)(2,1)}, u32[]{:S(2)}) copy-start(bf16[8,32,256]{2,1,0:T(8,128)(2,1)} %copy-done.13) | copy-start | bytes 393220
  19.7 4.2 %copy-start.18 = (s32[8,128]{1,0:T(8,128)S(1)}, s32[8,128]{1,0:T(8,128)}, u32[]{:S(2)}) copy-start(s32[8,128]{1,0:T(8,128)} %get-tuple-element.25.refs_0_) | copy-start | bytes 12292
  19.7 4.2 %copy-start.20 = (s32[2]{0:T(128)S(1)}, s32[2]{0:T(128)}, u32[]{:S(2)}) copy-start(s32[2]{0:T(128)} %broadcast_xor_fusion.block_ref) | copy-start | bytes 28
  23.9 27.2 %collective-permute-start.3 = (f32[256,512]{1,0:T(8,128)}, f32[256,512]{1,0:T(8,128)}, u32[]{:S(2)}, u32[]{:S(2)}) collective-permute-start(f32[256,512]{1,0:T(8,128)} %base.6.refs_0_), channel_id=1, source_target_pairs={{0,1},{1,0},{2,3},{3,2},{4,5},{5,4},{6,7},{7,6},{8,9},{9,8},{10,11... | collective-permute-start | bytes 1572872 | tf_op jit(solution)/shard_map/ppermute | solution.py:255
  24.0 2.2 %copy-start.2 = (bf16[2048,1024]{1,0:T(8,128)(2,1)S(1)}, bf16[2048,1024]{1,0:T(8,128)(2,1)}, u32[]{:S(2)}) copy-start(bf16[2048,1024]{1,0:T(8,128)(2,1)} %weight_ref.11) | copy-start | bytes 12582916
  26.1 0.9 copy-start.8
  29.5 7.1 %copy-start.19 = (s32[8,128]{1,0:T(8,128)S(1)}, s32[8,128]{1,0:T(8,128)}, u32[]{:S(2)}) copy-start(s32[8,128]{1,0:T(8,128)} %get-tuple-element.24.refs_3_.refs_2_) | copy-start | bytes 12292
  29.5 27.1 %collective-permute-start.7 = (f32[256,512]{1,0:T(8,128)}, f32[256,512]{1,0:T(8,128)}, u32[]{:S(2)}, u32[]{:S(2)}) collective-permute-start(f32[256,512]{1,0:T(8,128)} %base.10.refs_0_), channel_id=1, source_target_pairs={{0,1},{1,0},{2,3},{3,2},{4,5},{5,4},{6,7},{7,6},{8,9},{9,8},{10,11... | collective-permute-start | bytes 1572872 | tf_op jit(solution)/shard_map/ppermute | solution.py:255
  32.5 10.1 %copy-start.25 = (s32[1,768]{1,0:T(1,128)S(1)}, s32[1,768]{1,0:T(1,128)}, u32[]{:S(2)}) copy-start(s32[1,768]{1,0:T(1,128)} %get-tuple-element.20.index_ref) | copy-start | bytes 9220
  32.5 29.4 %collective-permute-start.5 = (f32[256,512]{1,0:T(8,128)}, f32[256,512]{1,0:T(8,128)}, u32[]{:S(2)}, u32[]{:S(2)}) collective-permute-start(f32[256,512]{1,0:T(8,128)} %base.8.refs_0_), channel_id=1, source_target_pairs={{0,1},{1,0},{2,3},{3,2},{4,5},{5,4},{6,7},{7,6},{8,9},{9,8},{10,11... | collective-permute-start | bytes 1572872 | tf_op jit(solution)/shard_map/ppermute | solution.py:255
  36.7 2.2 %copy-start.4 = (bf16[8,2048,128]{2,1,0:T(8,128)(2,1)S(1)}, bf16[8,2048,128]{2,1,0:T(8,128)(2,1)}, u32[]{:S(2)}) copy-start(bf16[8,2048,128]{2,1,0:T(8,128)(2,1)} %refs_2_.1) | copy-start | bytes 12582916
  38.9 1.2 %copy-start.17 = (bf16[216,2048]{1,0:T(8,128)(2,1)S(1)}, bf16[216,2048]{1,0:T(8,128)(2,1)}, u32[]{:S(2)}) copy-start(bf16[216,2048]{1,0:T(8,128)(2,1)} %get-tuple-element.29.refs_0_) | copy-start | bytes 2654212
  41.4 2.2 %collective-permute-start.15 = (f32[240,128]{1,0:T(8,128)S(1)}, f32[240,128]{1,0:T(8,128)}, u32[]{:S(2)}, u32[]{:S(2)}) collective-permute-start(f32[240,128]{1,0:T(8,128)S(1)} %shrink.4), channel_id=1, source_target_pairs={{0,1},{1,0},{2,3},{3,2},{4,5},{5,4},{6,7},{7,6},{8,9},{9,8},{10,11... | collective-permute-start | bytes 368648 | tf_op jit(solution)/shard_map/ppermute | solution.py:353
  44.5 14.7 %collective-permute-start.16 = (f32[120,128]{1,0:T(8,128)S(1)}, f32[120,128]{1,0:T(8,128)S(1)}, u32[]{:S(2)}, u32[]{:S(2)}) collective-permute-start(f32[120,128]{1,0:T(8,128)S(1)} %slice.95), channel_id=1, source_target_pairs={{0,2},{1,3},{2,0},{3,1},{4,6},{5,7},{6,4},{7,5},{8,10},{9,11},{10,... | collective-permute-start | bytes 184328 | tf_op jit(solution)/shard_map/ppermute | solution.py:357
  46.1 2.2 %copy-start.3 = (bf16[2048,1024]{1,0:T(8,128)(2,1)S(1)}, bf16[2048,1024]{1,0:T(8,128)(2,1)}, u32[]{:S(2)}) copy-start(bf16[2048,1024]{1,0:T(8,128)(2,1)} %weight_ref.11) | copy-start | bytes 12582916
  48.3 1.0 copy-start.16
  49.3 3.6 %copy-start.9 = (bf16[8,32,256]{2,1,0:T(8,128)(2,1)S(1)}, bf16[8,32,256]{2,1,0:T(8,128)(2,1)}, u32[]{:S(2)}) copy-start(bf16[8,32,256]{2,1,0:T(8,128)(2,1)} %copy-done.7) | copy-start | bytes 393220
  49.3 3.6 %copy-start.12 = (bf16[8,32,256]{2,1,0:T(8,128)(2,1)S(1)}, bf16[8,32,256]{2,1,0:T(8,128)(2,1)}, u32[]{:S(2)}) copy-start(bf16[8,32,256]{2,1,0:T(8,128)(2,1)} %copy-done.10) | copy-start | bytes 393220
  49.3 3.6 %copy-start.15 = (bf16[8,32,256]{2,1,0:T(8,128)(2,1)S(1)}, bf16[8,32,256]{2,1,0:T(8,128)(2,1)}, u32[]{:S(2)}) copy-start(bf16[8,32,256]{2,1,0:T(8,128)(2,1)} %copy-done.13) | copy-start | bytes 393220
  49.3 3.6 %copy-start.22 = (bf16[8,32,256]{2,1,0:T(8,128)(2,1)S(1)}, bf16[8,32,256]{2,1,0:T(8,128)(2,1)}, u32[]{:S(2)}) copy-start(bf16[8,32,256]{2,1,0:T(8,128)(2,1)} %copy-done.21) | copy-start | bytes 393220
  52.3 15.9 %collective-permute-start.4 = (f32[256,256]{1,0:T(8,128)S(1)}, f32[256,256]{1,0:T(8,128)S(1)}, u32[]{:S(2)}, u32[]{:S(2)}) collective-permute-start(f32[256,256]{1,0:T(8,128)S(1)} %slice.82), channel_id=1, source_target_pairs={{0,2},{1,3},{2,0},{3,1},{4,6},{5,7},{6,4},{7,5},{8,10},{9,11},{10,... | collective-permute-start | bytes 786440 | tf_op jit(solution)/shard_map/ppermute | solution.py:255
  54.8 1.8 %copy-start.23 = (bf16[216,2048]{1,0:T(8,128)(2,1)S(1)}, bf16[216,2048]{1,0:T(8,128)(2,1)}, u32[]{:S(2)}) copy-start(bf16[216,2048]{1,0:T(8,128)(2,1)} %get-tuple-element.26) | copy-start | bytes 2654212
  54.8 4.5 %copy-start.24 = (bf16[216,2048]{1,0:T(8,128)(2,1)S(1)}, bf16[216,2048]{1,0:T(8,128)(2,1)}, u32[]{:S(2)}) copy-start(bf16[216,2048]{1,0:T(8,128)(2,1)} %get-tuple-element.27) | copy-start | bytes 2654212
  56.6 9.7 %copy-start.5 = (bf16[8,2048,128]{2,1,0:T(8,128)(2,1)S(1)}, bf16[8,2048,128]{2,1,0:T(8,128)(2,1)}, u32[]{:S(2)}) copy-start(bf16[8,2048,128]{2,1,0:T(8,128)(2,1)} %refs_2_.1) | copy-start | bytes 12582916
  56.6 24.5 %collective-permute-start.10 = (bf16[216,2048]{1,0:T(8,128)(2,1)S(1)}, bf16[216,2048]{1,0:T(8,128)(2,1)S(1)}, u32[]{:S(2)}, u32[]{:S(2)}) collective-permute-start(bf16[216,2048]{1,0:T(8,128)(2,1)S(1)} %copy-done.23), channel_id=1, source_target_pairs={{0,4},{4,8},{8,12},{12,0},{1,5},{5,9},{9,13},{13,1},{2,6},{6,10},{... | collective-permute-start | bytes 2654216 | tf_op jit(solution)/shard_map/ppermute | solution.py:312
  59.3 39.1 %collective-permute-start.11 = (bf16[216,2048]{1,0:T(8,128)(2,1)S(1)}, bf16[216,2048]{1,0:T(8,128)(2,1)S(1)}, u32[]{:S(2)}, u32[]{:S(2)}) collective-permute-start(bf16[216,2048]{1,0:T(8,128)(2,1)S(1)} %copy-done.24), channel_id=1, source_target_pairs={{0,12},{4,0},{8,4},{12,8},{1,13},{5,1},{9,5},{13,9},{2,14},{6,2},{... | collective-permute-start | bytes 2654216 | tf_op jit(solution)/shard_map/ppermute | solution.py:312
  62.0 8.4 %collective-permute-start.8 = (f32[256,256]{1,0:T(8,128)S(1)}, f32[256,256]{1,0:T(8,128)S(1)}, u32[]{:S(2)}, u32[]{:S(2)}) collective-permute-start(f32[256,256]{1,0:T(8,128)S(1)} %slice.86), channel_id=1, source_target_pairs={{0,2},{1,3},{2,0},{3,1},{4,6},{5,7},{6,4},{7,5},{8,10},{9,11},{10,... | collective-permute-start | bytes 786440 | tf_op jit(solution)/shard_map/ppermute | solution.py:255
  64.7 35.3 %collective-permute-start.9 = (bf16[32,32,256]{2,1,0:T(8,128)(2,1)S(1)}, bf16[32,32,256]{2,1,0:T(8,128)(2,1)S(1)}, u32[]{:S(2)}, u32[]{:S(2)}) collective-permute-start(bf16[32,32,256]{2,1,0:T(8,128)(2,1)S(1)} %pad_maximum_fusion.2), channel_id=1, source_target_pairs={{0,16},{16,0},{1,17},{17,1},{2,18},{18,2},{3,19},{19,3},{4,20},{20... | collective-permute-start | bytes 1572872 | tf_op jit(solution)/shard_map/ppermute | solution.py:200
  68.2 1.4 %collective-permute-start.13 = (f32[240,128]{1,0:T(8,128)S(1)}, f32[240,128]{1,0:T(8,128)S(1)}, u32[]{:S(2)}, u32[]{:S(2)}) collective-permute-start(f32[240,128]{1,0:T(8,128)S(1)} %shrink.3), channel_id=1, source_target_pairs={{0,1},{1,0},{2,3},{3,2},{4,5},{5,4},{6,7},{7,6},{8,9},{9,8},{10,11... | collective-permute-start | bytes 368648 | tf_op jit(solution)/shard_map/ppermute | solution.py:353
  69.7 33.5 %collective-permute-start.6 = (f32[256,256]{1,0:T(8,128)S(1)}, f32[256,256]{1,0:T(8,128)S(1)}, u32[]{:S(2)}, u32[]{:S(2)}) collective-permute-start(f32[256,256]{1,0:T(8,128)S(1)} %slice.84), channel_id=1, source_target_pairs={{0,2},{1,3},{2,0},{3,1},{4,6},{5,7},{6,4},{7,5},{8,10},{9,11},{10,... | collective-permute-start | bytes 786440 | tf_op jit(solution)/shard_map/ppermute | solution.py:255
  70.3 9.1 %collective-permute-start.14 = (f32[120,128]{1,0:T(8,128)S(1)}, f32[120,128]{1,0:T(8,128)S(1)}, u32[]{:S(2)}, u32[]{:S(2)}) collective-permute-start(f32[120,128]{1,0:T(8,128)S(1)} %slice.93), channel_id=1, source_target_pairs={{0,2},{1,3},{2,0},{3,1},{4,6},{5,7},{6,4},{7,5},{8,10},{9,11},{10,... | collective-permute-start | bytes 184328 | tf_op jit(solution)/shard_map/ppermute | solution.py:357
  99.9 1.6 %collective-permute-start.18 = (f32[480,128]{1,0:T(8,128)S(1)}, f32[480,128]{1,0:T(8,128)S(1)}, u32[]{:S(2)}, u32[]{:S(2)}) collective-permute-start(f32[480,128]{1,0:T(8,128)S(1)} %get-tuple-element.32), channel_id=1, source_target_pairs={{0,1},{1,0},{2,3},{3,2},{4,5},{5,4},{6,7},{7,6},{8,9},{9,8},{10,11... | collective-permute-start | bytes 737288 | tf_op jit(solution)/shard_map/ppermute | solution.py:353
  100.1 9.3 %copy-start.6 = (s32[768,1]{1,0:T(8,128)S(1)}, s32[768,1]{1,0:T(8,128)}, u32[]{:S(2)}) copy-start(s32[768,1]{1,0:T(8,128)} %copy.14.index_ref) | copy-start | bytes 9220
  101.5 5.4 %collective-permute-start.19 = (f32[240,128]{1,0:T(8,128)S(1)}, f32[240,128]{1,0:T(8,128)S(1)}, u32[]{:S(2)}, u32[]{:S(2)}) collective-permute-start(f32[240,128]{1,0:T(8,128)S(1)} %slice.97), channel_id=1, source_target_pairs={{0,2},{1,3},{2,0},{3,1},{4,6},{5,7},{6,4},{7,5},{8,10},{9,11},{10,... | collective-permute-start | bytes 368648 | tf_op jit(solution)/shard_map/ppermute | solution.py:357
  103.2 6.3 %collective-permute-start.17 = (f32[120,128]{1,0:T(8,128)S(1)}, f32[120,128]{1,0:T(8,128)S(1)}, u32[]{:S(2)}, u32[]{:S(2)}) collective-permute-start(f32[120,128]{1,0:T(8,128)S(1)} %get-tuple-element.30), channel_id=1, source_target_pairs={{0,8},{4,12},{8,0},{12,4},{1,9},{5,13},{9,1},{13,5},{2,10},{6,14},... | collective-permute-start | bytes 184328 | tf_op jit(solution)/shard_map/ppermute | solution.py:377
  107.0 4.3 %collective-permute-start.20 = (f32[120,128]{1,0:T(8,128)S(1)}, f32[120,128]{1,0:T(8,128)S(1)}, u32[]{:S(2)}, u32[]{:S(2)}) collective-permute-start(f32[120,128]{1,0:T(8,128)S(1)} %get-tuple-element.36), channel_id=1, source_target_pairs={{0,12},{4,0},{8,4},{12,8},{1,13},{5,1},{9,5},{13,9},{2,14},{6,2},{... | collective-permute-start | bytes 184328 | tf_op jit(solution)/shard_map/ppermute | solution.py:377
  108.5 6.0 %collective-permute-start.21 = (f32[120,128]{1,0:T(8,128)S(1)}, f32[120,128]{1,0:T(8,128)S(1)}, u32[]{:S(2)}, u32[]{:S(2)}) collective-permute-start(f32[120,128]{1,0:T(8,128)S(1)} %get-tuple-element.35), channel_id=1, source_target_pairs={{0,4},{4,8},{8,12},{12,0},{1,5},{5,9},{9,13},{13,1},{2,6},{6,10},{... | collective-permute-start | bytes 184328 | tf_op jit(solution)/shard_map/ppermute | solution.py:377

commit v13 on v12

--- a/solution.py
+++ b/solution.py
@@ -366,9 +366,10 @@
     whole = [total[:8] for total, _ in slab_sums[:1]]
     late = order[-2:]
     early = order[:-2] + [0]
-    totals = []
+    totals, far = [], [packed]
     for r in early:
-        (value,) = shrink([arrived[r]], begun if r else [packed], [])
+        (value,) = shrink([arrived[r]], begun if r else far, [])
+        far = [value]
         totals.append(combine(value, whole if r else ()))
     value, *totals = shrink([arrived[r] for r in late], [base[:8], base[-8:]], totals)
     last = combine(value)

time: 117 us -> 115 us (0.983)
  local copies, waits for them, and re-layouts: 14.3 us -> 11.4 us
    unnamed x52, local copies, waits for them, and re-layouts: 12 us -> 8.4 us
    ppermute x3, waiting for transfers between devices: 19 us -> 21.6 us  [send(): lax.ppermute(block, 'batch', [(i, (i + r) % homes) for i in range(homes)])]
    ppermute x3, waiting for transfers between devices: 10.6 us -> 9.32 us  [combine(): lax.ppermute(value[half:], 'tensor', [(i, i ^ bit) for i in range(pieces)])]
  transfers between devices with their start and end apart: 22 -> 22, of which waited for: 9 -> 8; matrix products, arithmetic and copies ran while one was open for 7% -> 7% of each run, Pallas kernels for 25% -> 26%
where the time goes in v13:
time: 115 us
  waiting for transfers between devices  37.6 us (33%)
  Pallas kernels  31.3 us (27%)
  starting transfers between devices  25.7 us (22%)
  local copies, waits for them, and re-layouts  11.4 us (10%)
  other arithmetic  4.48 us (4%)
  between operations  4 us (3%)
    ppermute x3, waiting for transfers between devices, send(): lax.ppermute(block, 'batch', [(i, (i + r) % homes) for i in range(homes)])  21.6 us
    pallas_call x6, Pallas kernels, base_part(): pl.pallas_call(functools.partial(base_kernel, len(after)), out_shape=jax....  14.5 us
    ppermute x3, waiting for transfers between devices, combine(): lax.ppermute(value[half:], 'tensor', [(i, i ^ bit) for i in range(pieces)])  9.32 us
    unnamed x52, local copies, waits for them, and re-layouts  8.4 us
    pallas_call x1, Pallas kernels, pack(): pl.pallas_call(functools.partial(pack_kernel, span, shifts), out_shape=[j...  6.48 us
    ppermute x3, starting transfers between devices, gather_up(): lax.ppermute(own, 'batch', [(i, (i - r) % homes) for i in range(homes)])  6.11 us
    ppermute x3, starting transfers between devices, send(): lax.ppermute(block, 'batch', [(i, (i + r) % homes) for i in range(homes)])  5.78 us
    pallas_call x3, Pallas kernels, shrink(): pl.pallas_call(functools.partial(shrink_kernel, held, light, rank, value_...  5.5 us
  transfers between devices with their start and end apart: 22, of which 8 were waited for; matrix products, arithmetic and copies ran while one was open for 7% of the time, Pallas kernels for 26%

profile of v13, /device:TPU:0, one launch (start us, length us, event | category | flops | bytes accessed | tf_op | source)
XLA Modules:
  0.0 114.5 jit_solution(11675409757727706707)
XLA Ops:
  0.0 0.9 copy-done
  1.0 5.1 %collective-permute-start = (bf16[8,32,256]{2,1,0:T(8,128)(2,1)S(1)}, bf16[8,32,256]{2,1,0:T(8,128)(2,1)S(1)}, u32[]{:S(2)}, u32[]{:S(2)}) collective-permute-start(bf16[8,32,256]{2,1,0:T(8,128)(2,1)S(1)} %constant_dynamic-slice_fusion), channel_id=1, source_target_pairs={{0,12},{4,0},{8,4},{12,8},{1,13},{5,1},{9,5},{13,9},{2,14},{6,2},{... | collective-permute-start | bytes 393224 | tf_op jit(solution)/shard_map/ppermute | solution.py:196
  6.1 1.0 collective-permute-start.2
  7.1 1.7 %route.1 = (s32[1,768]{1,0:T(1,128)}, s32[8,128]{1,0:T(8,128)}) custom-call(s32[1]{0:T(128)} %bitcast.place_ref, s32[32]{0:T(128)} %entry_hbm.1, s32[768]{0:T(1024)} %request_hbm.1), custom_call_target="tpu_custom_call" | custom-call | flops 1 | bytes 1 | tf_op jit(solution)/shard_map/route/pallas_call | solution.py:279
  8.8 6.5 %pack.1 = (s32[8,128]{1,0:T(8,128)}, bf16[216,2048]{1,0:T(8,128)(2,1)}, bf16[216,2048]{1,0:T(8,128)(2,1)}, bf16[216,2048]{1,0:T(8,128)(2,1)}, bf16[216,2048]{1,0:T(8,128)(2,1)}) custom-call(s32[1,768]{1,0:T(1,128)} %get-tuple-element.20.index_ref, bf16[768,2048]{1,0:T(8,128)(2,1)} %tokens_ref.13), custom_call_target="tpu_custom_call" | custom-call | flops 1 | bytes 1 | tf_op jit(solution)/shard_map/pack/pallas_call | solution.py:297
  15.3 0.6 gate.1
  15.9 1.9 %collective-permute-start.12 = (bf16[216,2048]{1,0:T(8,128)(2,1)}, bf16[216,2048]{1,0:T(8,128)(2,1)}, u32[]{:S(2)}, u32[]{:S(2)}) collective-permute-start(bf16[216,2048]{1,0:T(8,128)(2,1)} %get-tuple-element.28), channel_id=1, source_target_pairs={{0,8},{4,12},{8,0},{12,4},{1,9},{5,13},{9,1},{13,5},{2,10},{6,14},... | collective-permute-start | bytes 2654216 | tf_op jit(solution)/shard_map/ppermute | solution.py:312
  18.4 0.6 copy-done.10
  19.1 0.7 copy-done.13
  19.8 4.2 %base.6.refs_0_ = f32[256,512]{1,0:T(8,128)} custom-call(s32[2]{0:T(128)} %broadcast_xor_fusion.block_ref, bf16[768,2048]{1,0:T(8,128)(2,1)} %tokens_ref.13, bf16[2048,1024]{1,0:T(8,128)(2,1)} %weight_ref.11, s32[8,128]{1,0:T(8,128)} %get-tuple-element.25.refs_0_, bf16[8,32,256]{2,1,0:T(8,128)(2,1)} %copy-done.7, bf16[8,32,256]{2,1,0:T(8,128)(2,1)} %copy-done.10, ...), custom_call_target="tpu_custom_call" | custom-call | flops 1 | bytes 1 | tf_op jit(solution)/shard_map/base/pallas_call | solution.py:223
  24.0 2.2 %copy-done.2 = bf16[2048,1024]{1,0:T(8,128)(2,1)S(1)} copy-done((bf16[2048,1024]{1,0:T(8,128)(2,1)S(1)}, bf16[2048,1024]{1,0:T(8,128)(2,1)}, u32[]{:S(2)}) %copy-start.2) | copy-done | bytes 4194328
  26.2 0.9 copy-done.8
  27.1 2.5 %base.10.refs_0_ = f32[256,512]{1,0:T(8,128)} custom-call(s32[2]{0:T(128)S(1)} %copy-done.19, bf16[768,2048]{1,0:T(8,128)(2,1)S(1)} %copy-done.1, bf16[2048,1024]{1,0:T(8,128)(2,1)S(1)} %copy-done.2, s32[8,128]{1,0:T(8,128)S(1)} %copy-done.18, bf16[8,32,256]{2,1,0:T(8,128)(2,1)S(1)} %copy-done.8, bf16[8,32,256]{2,1,0:T(8,128)(2,1)S(1)} %copy-done.11, ...), custom_call_target="tpu_custom_call" | custom-call | flops 1 | bytes 1 | tf_op jit(solution)/shard_map/base/pallas_call | solution.py:223
  30.1 2.5 %base.8.refs_0_ = f32[256,512]{1,0:T(8,128)} custom-call(s32[2]{0:T(128)S(1)} %copy-done.19, bf16[768,2048]{1,0:T(8,128)(2,1)S(1)} %copy-done.1, bf16[2048,1024]{1,0:T(8,128)(2,1)S(1)} %copy-done.2, s32[8,128]{1,0:T(8,128)S(1)} %copy-done.18, bf16[8,32,256]{2,1,0:T(8,128)(2,1)S(1)} %copy-done.8, bf16[8,32,256]{2,1,0:T(8,128)(2,1)S(1)} %copy-done.11, ...), custom_call_target="tpu_custom_call" | custom-call | flops 1 | bytes 1 | tf_op jit(solution)/shard_map/base/pallas_call | solution.py:223
  32.6 1.8 %base.7 = f32[256,512]{1,0:T(8,128)S(1)} custom-call(s32[2]{0:T(128)S(1)} %multiply_xor_fusion.block_ref, bf16[768,2048]{1,0:T(8,128)(2,1)S(1)} %copy-done.1, bf16[2048,1024]{1,0:T(8,128)(2,1)S(1)} %copy-done.3, f32[256,512]{1,0:T(8,128)S(1)} %copy-done.16), custom_call_target="tpu_custom_call" | custom-call | flops 1 | bytes 1 | tf_op jit(solution)/shard_map/base/pallas_call | solution.py:223
  34.5 0.8 copy-done.20
  35.3 0.7 slice.82
  36.0 1.5 %collective-permute-start.4 = (f32[256,256]{1,0:T(8,128)}, f32[256,256]{1,0:T(8,128)}, u32[]{:S(2)}, u32[]{:S(2)}) collective-permute-start(f32[256,256]{1,0:T(8,128)} %slice.82), channel_id=1, source_target_pairs={{0,2},{1,3},{2,0},{3,1},{4,6},{5,7},{6,4},{7,5},{8,10},{9,11},{10,... | collective-permute-start | bytes 786440 | tf_op jit(solution)/shard_map/ppermute | solution.py:255
  37.5 1.5 %collective-permute-start.10 = (bf16[216,2048]{1,0:T(8,128)(2,1)}, bf16[216,2048]{1,0:T(8,128)(2,1)}, u32[]{:S(2)}, u32[]{:S(2)}) collective-permute-start(bf16[216,2048]{1,0:T(8,128)(2,1)} %get-tuple-element.26), channel_id=1, source_target_pairs={{0,4},{4,8},{8,12},{12,0},{1,5},{5,9},{9,13},{13,1},{2,6},{6,10},{... | collective-permute-start | bytes 2654216 | tf_op jit(solution)/shard_map/ppermute | solution.py:312
  39.0 1.3 %slice.61 = s32[1,1]{1,0:T(1,128)} slice(s32[8,128]{1,0:T(8,128)} %get-tuple-element.19), slice={[0:1], [0:1]} | slice | bytes 8 | tf_op jit(solution)/shard_map/slice | solution.py:320
  43.7 0.9 copy.14.index_ref
  44.8 2.2 %copy-done.4 = bf16[2048,1024]{1,0:T(8,128)(2,1)S(1)} copy-done((bf16[2048,1024]{1,0:T(8,128)(2,1)S(1)}, bf16[2048,1024]{1,0:T(8,128)(2,1)}, u32[]{:S(2)}) %copy-start.4) | copy-done | bytes 4194328
  47.0 1.8 %base.11 = f32[256,512]{1,0:T(8,128)S(1)} custom-call(s32[2]{0:T(128)S(1)} %multiply_xor_fusion.block_ref, bf16[768,2048]{1,0:T(8,128)(2,1)S(1)} %copy-done.1, bf16[2048,1024]{1,0:T(8,128)(2,1)S(1)} %copy-done.4, f32[256,512]{1,0:T(8,128)} %base.10.refs_0_), custom_call_target="tpu_custom_call" | custom-call | flops 1 | bytes 1 | tf_op jit(solution)/shard_map/base/pallas_call | solution.py:223
  48.8 1.1 add.54
  49.9 0.6 collective-permute-start.8
  50.6 1.8 %base.9 = f32[256,512]{1,0:T(8,128)S(1)} custom-call(s32[2]{0:T(128)S(1)} %multiply_xor_fusion.block_ref, bf16[768,2048]{1,0:T(8,128)(2,1)S(1)} %copy-done.1, bf16[2048,1024]{1,0:T(8,128)(2,1)S(1)} %copy-done.4, f32[256,512]{1,0:T(8,128)} %base.8.refs_0_), custom_call_target="tpu_custom_call" | custom-call | flops 1 | bytes 1 | tf_op jit(solution)/shard_map/base/pallas_call | solution.py:223
  52.5 2.4 %collective-permute-start.11 = (bf16[216,2048]{1,0:T(8,128)(2,1)S(1)}, bf16[216,2048]{1,0:T(8,128)(2,1)S(1)}, u32[]{:S(2)}, u32[]{:S(2)}) collective-permute-start(bf16[216,2048]{1,0:T(8,128)(2,1)S(1)} %copy-done.24), channel_id=1, source_target_pairs={{0,12},{4,0},{8,4},{12,8},{1,13},{5,1},{9,5},{13,9},{2,14},{6,2},{... | collective-permute-start | bytes 2654216 | tf_op jit(solution)/shard_map/ppermute | solution.py:312
  54.9 1.1 add.52
  56.1 21.6 %collective-permute-done.12.refs_0_ = bf16[216,2048]{1,0:T(8,128)(2,1)} collective-permute-done((bf16[216,2048]{1,0:T(8,128)(2,1)}, bf16[216,2048]{1,0:T(8,128)(2,1)}, u32[]{:S(2)}, u32[]{:S(2)}) %collective-permute-start.12) | collective-permute-done | bytes 884768 | tf_op jit(solution)/shard_map/ppermute | solution.py:312
  77.7 1.5 %collective-permute-start.9 = (bf16[32,32,256]{2,1,0:T(8,128)(2,1)S(1)}, bf16[32,32,256]{2,1,0:T(8,128)(2,1)S(1)}, u32[]{:S(2)}, u32[]{:S(2)}) collective-permute-start(bf16[32,32,256]{2,1,0:T(8,128)(2,1)S(1)} %pad_maximum_fusion.2), channel_id=1, source_target_pairs={{0,16},{16,0},{1,17},{17,1},{2,18},{18,2},{3,19},{19,3},{4,20},{20... | collective-permute-start | bytes 1572872 | tf_op jit(solution)/shard_map/ppermute | solution.py:200
  79.2 2.0 %shrink.3.refs_2_ = f32[240,128]{1,0:T(8,128)S(1)} custom-call(s32[3]{0:T(128)S(1)} %pad_add_fusion.scalar_ref, bf16[216,2048]{1,0:T(8,128)(2,1)} %collective-permute-done.12.refs_0_, bf16[8,2048,128]{2,1,0:T(8,128)(2,1)S(1)} %copy-done.5, f32[8,512]{1,0:T(8,128)S(1)} %slice.89.refs_2_, f32[8,512]{1,0:T(8,128)S(1)} %slice.90.refs_3_, f32[8,512]{1,0:T(8,128)S(1)} %slice.91.refs_4_), custom_call_target="tpu_custom_call" | custom-call | flops 1 | bytes 1 | tf_op jit(solution)/shard_map/shrink/pallas_call | solution.py:326
  81.2 1.4 %shrink.4 = f32[240,128]{1,0:T(8,128)S(1)} custom-call(s32[3]{0:T(128)S(1)} %pad_add_fusion.scalar_ref, bf16[216,2048]{1,0:T(8,128)(2,1)S(1)} %copy-done.17, bf16[8,2048,128]{2,1,0:T(8,128)(2,1)S(1)} %copy-done.5, f32[240,128]{1,0:T(8,128)S(1)} %shrink.3.refs_2_), custom_call_target="tpu_custom_call" | custom-call | flops 1 | bytes 1 | tf_op jit(solution)/shard_map/shrink/pallas_call | solution.py:326
  82.7 1.0 slice_add_fusion.2
  84.3 1.6 %collective-permute-start.16 = (f32[120,128]{1,0:T(8,128)S(1)}, f32[120,128]{1,0:T(8,128)S(1)}, u32[]{:S(2)}, u32[]{:S(2)}) collective-permute-start(f32[120,128]{1,0:T(8,128)S(1)} %slice.95), channel_id=1, source_target_pairs={{0,2},{1,3},{2,0},{3,1},{4,6},{5,7},{6,4},{7,5},{8,10},{9,11},{10,... | collective-permute-start | bytes 184328 | tf_op jit(solution)/shard_map/ppermute | solution.py:357
  85.9 0.9 collective-permute-start.6
  86.9 1.8 %collective-permute-done.16 = f32[120,128]{1,0:T(8,128)S(1)} collective-permute-done((f32[120,128]{1,0:T(8,128)S(1)}, f32[120,128]{1,0:T(8,128)S(1)}, u32[]{:S(2)}, u32[]{:S(2)}) %collective-permute-start.16) | collective-permute-done | bytes 61472 | tf_op jit(solution)/shard_map/ppermute | solution.py:357
  88.7 1.8 %collective-permute-start.14 = (f32[120,128]{1,0:T(8,128)S(1)}, f32[120,128]{1,0:T(8,128)S(1)}, u32[]{:S(2)}, u32[]{:S(2)}) collective-permute-start(f32[120,128]{1,0:T(8,128)S(1)} %slice.93), channel_id=1, source_target_pairs={{0,2},{1,3},{2,0},{3,1},{4,6},{5,7},{6,4},{7,5},{8,10},{9,11},{10,... | collective-permute-start | bytes 184328 | tf_op jit(solution)/shard_map/ppermute | solution.py:357
  90.5 5.0 %collective-permute-done.14 = f32[120,128]{1,0:T(8,128)S(1)} collective-permute-done((f32[120,128]{1,0:T(8,128)S(1)}, f32[120,128]{1,0:T(8,128)S(1)}, u32[]{:S(2)}, u32[]{:S(2)}) %collective-permute-start.14) | collective-permute-done | bytes 61472 | tf_op jit(solution)/shard_map/ppermute | solution.py:357
  95.5 2.1 %shrink.5 = (f32[480,128]{1,0:T(8,128)S(1)}, f32[120,128]{1,0:T(8,128)S(1)}, f32[120,128]{1,0:T(8,128)S(1)}) custom-call(s32[3]{0:T(128)S(1)} %pad_add_fusion.scalar_ref, bf16[216,2048]{1,0:T(8,128)(2,1)} %collective-permute-done.10.refs_0_, bf16[216,2048]{1,0:T(8,128)(2,1)S(1)} %collective-permute-done.11.refs_1_, bf16[8,2048,128]{2,1,0:T(8,128)(2,1)S(1)} %copy-done.5, ...), custom_call_target="tpu_custom_call" | custom-call | flops 1 | bytes 1 | tf_op jit(solution)/shard_map/shrink/pallas_call | solution.py:326
  98.0 1.3 %collective-permute-done.18 = f32[480,128]{1,0:T(8,128)S(1)} collective-permute-done((f32[480,128]{1,0:T(8,128)S(1)}, f32[480,128]{1,0:T(8,128)S(1)}, u32[]{:S(2)}, u32[]{:S(2)}) %collective-permute-start.18) | collective-permute-done | bytes 245792 | tf_op jit(solution)/shard_map/ppermute | solution.py:353
  99.3 1.6 %collective-permute-start.19 = (f32[240,128]{1,0:T(8,128)S(1)}, f32[240,128]{1,0:T(8,128)S(1)}, u32[]{:S(2)}, u32[]{:S(2)}) collective-permute-start(f32[240,128]{1,0:T(8,128)S(1)} %slice.97), channel_id=1, source_target_pairs={{0,2},{1,3},{2,0},{3,1},{4,6},{5,7},{6,4},{7,5},{8,10},{9,11},{10,... | collective-permute-start | bytes 368648 | tf_op jit(solution)/shard_map/ppermute | solution.py:357
  100.9 1.3 %collective-permute-start.17 = (f32[120,128]{1,0:T(8,128)S(1)}, f32[120,128]{1,0:T(8,128)S(1)}, u32[]{:S(2)}, u32[]{:S(2)}) collective-permute-start(f32[120,128]{1,0:T(8,128)S(1)} %get-tuple-element.30), channel_id=1, source_target_pairs={{0,8},{4,12},{8,0},{12,4},{1,9},{5,13},{9,1},{13,5},{2,10},{6,14},... | collective-permute-start | bytes 184328 | tf_op jit(solution)/shard_map/ppermute | solution.py:378
  102.2 2.5 %collective-permute-done.19 = f32[240,128]{1,0:T(8,128)S(1)} collective-permute-done((f32[240,128]{1,0:T(8,128)S(1)}, f32[240,128]{1,0:T(8,128)S(1)}, u32[]{:S(2)}, u32[]{:S(2)}) %collective-permute-start.19) | collective-permute-done | bytes 122912 | tf_op jit(solution)/shard_map/ppermute | solution.py:357
  104.7 2.2 %collective-permute-start.20 = (f32[120,128]{1,0:T(8,128)S(1)}, f32[120,128]{1,0:T(8,128)S(1)}, u32[]{:S(2)}, u32[]{:S(2)}) collective-permute-start(f32[120,128]{1,0:T(8,128)S(1)} %get-tuple-element.36), channel_id=1, source_target_pairs={{0,12},{4,0},{8,4},{12,8},{1,13},{5,1},{9,5},{13,9},{2,14},{6,2},{... | collective-permute-start | bytes 184328 | tf_op jit(solution)/shard_map/ppermute | solution.py:378
  107.0 0.9 finish.2.base_ref
  107.9 1.2 %collective-permute-done.20.refs_0_ = f32[120,128]{1,0:T(8,128)S(1)} collective-permute-done((f32[120,128]{1,0:T(8,128)S(1)}, f32[120,128]{1,0:T(8,128)S(1)}, u32[]{:S(2)}, u32[]{:S(2)}) %collective-permute-start.20) | collective-permute-done | bytes 61472 | tf_op jit(solution)/shard_map/ppermute | solution.py:378
  109.0 3.9 %collective-permute-done.21.refs_1_ = f32[120,128]{1,0:T(8,128)S(1)} collective-permute-done((f32[120,128]{1,0:T(8,128)S(1)}, f32[120,128]{1,0:T(8,128)S(1)}, u32[]{:S(2)}, u32[]{:S(2)}) %collective-permute-start.21) | collective-permute-done | bytes 61472 | tf_op jit(solution)/shard_map/ppermute | solution.py:378
  112.9 1.6 %finish.3 = bf16[768,256]{1,0:T(8,128)(2,1)} custom-call(s32[1]{0:T(128)} %bitcast.2.place_ref, s32[768,1]{1,0:T(8,128)S(1)} %copy-done.6, f32[768,256]{1,0:T(8,128)S(1)} %finish.2.base_ref, bf16[32,64,256]{2,1,0:T(8,128)(2,1)S(1)} %pad_maximum_fusion.up_ref, f32[120,128]{1,0:T(8,128)S(1)} %collective-permute-done.20.refs_0_, ...), custom_call_target="tpu_custom_call" | custom-call | flops 1 | bytes 1 | tf_op jit(solution)/shard_map/finish/pallas_call | solution.py:160
  (97 shorter events, 2.7 us)
Async XLA Ops:
  0.0 1.0 copy-start
  1.0 17.5 %copy-start.22 = (bf16[8,32,256]{2,1,0:T(8,128)(2,1)}, bf16[8,32,256]{2,1,0:T(8,128)(2,1)S(1)}, u32[]{:S(2)}) copy-start(bf16[8,32,256]{2,1,0:T(8,128)(2,1)S(1)} %constant_dynamic-slice_fusion) | copy-start | bytes 393220
  1.0 17.4 %collective-permute-start = (bf16[8,32,256]{2,1,0:T(8,128)(2,1)S(1)}, bf16[8,32,256]{2,1,0:T(8,128)(2,1)S(1)}, u32[]{:S(2)}, u32[]{:S(2)}) collective-permute-start(bf16[8,32,256]{2,1,0:T(8,128)(2,1)S(1)} %constant_dynamic-slice_fusion), channel_id=1, source_target_pairs={{0,12},{4,0},{8,4},{12,8},{1,13},{5,1},{9,5},{13,9},{2,14},{6,2},{... | collective-permute-start | bytes 393224 | tf_op jit(solution)/shard_map/ppermute | solution.py:196
  6.1 12.3 %collective-permute-start.1 = (bf16[8,32,256]{2,1,0:T(8,128)(2,1)S(1)}, bf16[8,32,256]{2,1,0:T(8,128)(2,1)S(1)}, u32[]{:S(2)}, u32[]{:S(2)}) collective-permute-start(bf16[8,32,256]{2,1,0:T(8,128)(2,1)S(1)} %constant_dynamic-slice_fusion), channel_id=1, source_target_pairs={{0,8},{4,12},{8,0},{12,4},{1,9},{5,13},{9,1},{13,5},{2,10},{6,14},... | collective-permute-start | bytes 393224 | tf_op jit(solution)/shard_map/ppermute | solution.py:196
  6.1 12.4 %collective-permute-start.2 = (bf16[8,32,256]{2,1,0:T(8,128)(2,1)S(1)}, bf16[8,32,256]{2,1,0:T(8,128)(2,1)S(1)}, u32[]{:S(2)}, u32[]{:S(2)}) collective-permute-start(bf16[8,32,256]{2,1,0:T(8,128)(2,1)S(1)} %constant_dynamic-slice_fusion), channel_id=1, source_target_pairs={{0,4},{4,8},{8,12},{12,0},{1,5},{5,9},{9,13},{13,1},{2,6},{6,10},{... | collective-permute-start | bytes 393224 | tf_op jit(solution)/shard_map/ppermute | solution.py:196
  15.9 61.8 %collective-permute-start.12 = (bf16[216,2048]{1,0:T(8,128)(2,1)}, bf16[216,2048]{1,0:T(8,128)(2,1)}, u32[]{:S(2)}, u32[]{:S(2)}) collective-permute-start(bf16[216,2048]{1,0:T(8,128)(2,1)} %get-tuple-element.28), channel_id=1, source_target_pairs={{0,8},{4,12},{8,0},{12,4},{1,9},{5,13},{9,1},{13,5},{2,10},{6,14},... | collective-permute-start | bytes 2654216 | tf_op jit(solution)/shard_map/ppermute | solution.py:312
  18.4 1.3 %copy-start.7 = (bf16[8,32,256]{2,1,0:T(8,128)(2,1)}, bf16[8,32,256]{2,1,0:T(8,128)(2,1)S(1)}, u32[]{:S(2)}) copy-start(bf16[8,32,256]{2,1,0:T(8,128)(2,1)S(1)} %collective-permute-done.refs_1_) | copy-start | bytes 393220
  18.4 0.7 copy-start.10
  19.1 0.7 copy-start.13
  19.8 4.2 %copy-start.1 = (bf16[768,2048]{1,0:T(8,128)(2,1)S(1)}, bf16[768,2048]{1,0:T(8,128)(2,1)}, u32[]{:S(2)}) copy-start(bf16[768,2048]{1,0:T(8,128)(2,1)} %tokens_ref.13) | copy-start | bytes 9437188
  19.8 4.2 %copy-start.11 = (bf16[8,32,256]{2,1,0:T(8,128)(2,1)S(1)}, bf16[8,32,256]{2,1,0:T(8,128)(2,1)}, u32[]{:S(2)}) copy-start(bf16[8,32,256]{2,1,0:T(8,128)(2,1)} %copy-done.10) | copy-start | bytes 393220
  19.8 4.2 %copy-start.14 = (bf16[8,32,256]{2,1,0:T(8,128)(2,1)S(1)}, bf16[8,32,256]{2,1,0:T(8,128)(2,1)}, u32[]{:S(2)}) copy-start(bf16[8,32,256]{2,1,0:T(8,128)(2,1)} %copy-done.13) | copy-start | bytes 393220
  19.8 4.2 %copy-start.18 = (s32[8,128]{1,0:T(8,128)S(1)}, s32[8,128]{1,0:T(8,128)}, u32[]{:S(2)}) copy-start(s32[8,128]{1,0:T(8,128)} %get-tuple-element.25.refs_0_) | copy-start | bytes 12292
  19.8 4.2 %copy-start.19 = (s32[2]{0:T(128)S(1)}, s32[2]{0:T(128)}, u32[]{:S(2)}) copy-start(s32[2]{0:T(128)} %broadcast_xor_fusion.block_ref) | copy-start | bytes 28
  24.0 10.4 %collective-permute-start.3 = (f32[256,512]{1,0:T(8,128)}, f32[256,512]{1,0:T(8,128)S(1)}, u32[]{:S(2)}, u32[]{:S(2)}) collective-permute-start(f32[256,512]{1,0:T(8,128)} %base.6.refs_0_), channel_id=1, source_target_pairs={{0,1},{1,0},{2,3},{3,2},{4,5},{5,4},{6,7},{7,6},{8,9},{9,8},{10,11... | collective-permute-start | bytes 1572872 | tf_op jit(solution)/shard_map/ppermute | solution.py:255
  24.0 2.2 %copy-start.2 = (bf16[2048,1024]{1,0:T(8,128)(2,1)S(1)}, bf16[2048,1024]{1,0:T(8,128)(2,1)}, u32[]{:S(2)}) copy-start(bf16[2048,1024]{1,0:T(8,128)(2,1)} %weight_ref.11) | copy-start | bytes 12582916
  26.2 0.9 copy-start.8
  29.6 3.0 %copy-start.3 = (bf16[2048,1024]{1,0:T(8,128)(2,1)S(1)}, bf16[2048,1024]{1,0:T(8,128)(2,1)}, u32[]{:S(2)}) copy-start(bf16[2048,1024]{1,0:T(8,128)(2,1)} %weight_ref.11) | copy-start | bytes 12582916
  29.6 3.0 %copy-start.16 = (f32[256,512]{1,0:T(8,128)S(1)}, f32[256,512]{1,0:T(8,128)}, u32[]{:S(2)}) copy-start(f32[256,512]{1,0:T(8,128)} %base.6.refs_0_) | copy-start | bytes 1572868
  29.6 19.2 %collective-permute-start.7 = (f32[256,512]{1,0:T(8,128)}, f32[256,512]{1,0:T(8,128)}, u32[]{:S(2)}, u32[]{:S(2)}) collective-permute-start(f32[256,512]{1,0:T(8,128)} %base.10.refs_0_), channel_id=1, source_target_pairs={{0,1},{1,0},{2,3},{3,2},{4,5},{5,4},{6,7},{7,6},{8,9},{9,8},{10,11... | collective-permute-start | bytes 1572872 | tf_op jit(solution)/shard_map/ppermute | solution.py:255
  32.6 19.9 %collective-permute-start.5 = (f32[256,512]{1,0:T(8,128)}, f32[256,512]{1,0:T(8,128)}, u32[]{:S(2)}, u32[]{:S(2)}) collective-permute-start(f32[256,512]{1,0:T(8,128)} %base.8.refs_0_), channel_id=1, source_target_pairs={{0,1},{1,0},{2,3},{3,2},{4,5},{5,4},{6,7},{7,6},{8,9},{9,8},{10,11... | collective-permute-start | bytes 1572872 | tf_op jit(solution)/shard_map/ppermute | solution.py:255
  32.6 11.1 %copy-start.25 = (s32[1,768]{1,0:T(1,128)S(1)}, s32[1,768]{1,0:T(1,128)}, u32[]{:S(2)}) copy-start(s32[1,768]{1,0:T(1,128)} %get-tuple-element.20.index_ref) | copy-start | bytes 9220
  34.5 0.8 copy-start.20
  36.0 46.6 %collective-permute-start.4 = (f32[256,256]{1,0:T(8,128)}, f32[256,256]{1,0:T(8,128)}, u32[]{:S(2)}, u32[]{:S(2)}) collective-permute-start(f32[256,256]{1,0:T(8,128)} %slice.82), channel_id=1, source_target_pairs={{0,2},{1,3},{2,0},{3,1},{4,6},{5,7},{6,4},{7,5},{8,10},{9,11},{10,... | collective-permute-start | bytes 786440 | tf_op jit(solution)/shard_map/ppermute | solution.py:255
  37.5 58.0 %collective-permute-start.10 = (bf16[216,2048]{1,0:T(8,128)(2,1)}, bf16[216,2048]{1,0:T(8,128)(2,1)}, u32[]{:S(2)}, u32[]{:S(2)}) collective-permute-start(bf16[216,2048]{1,0:T(8,128)(2,1)} %get-tuple-element.26), channel_id=1, source_target_pairs={{0,4},{4,8},{8,12},{12,0},{1,5},{5,9},{9,13},{13,1},{2,6},{6,10},{... | collective-permute-start | bytes 2654216 | tf_op jit(solution)/shard_map/ppermute | solution.py:312
  44.8 2.2 %copy-start.4 = (bf16[2048,1024]{1,0:T(8,128)(2,1)S(1)}, bf16[2048,1024]{1,0:T(8,128)(2,1)}, u32[]{:S(2)}) copy-start(bf16[2048,1024]{1,0:T(8,128)(2,1)} %weight_ref.11) | copy-start | bytes 12582916
  46.9 3.6 %copy-start.9 = (bf16[8,32,256]{2,1,0:T(8,128)(2,1)S(1)}, bf16[8,32,256]{2,1,0:T(8,128)(2,1)}, u32[]{:S(2)}) copy-start(bf16[8,32,256]{2,1,0:T(8,128)(2,1)} %copy-done.7) | copy-start | bytes 393220
  46.9 3.6 %copy-start.12 = (bf16[8,32,256]{2,1,0:T(8,128)(2,1)S(1)}, bf16[8,32,256]{2,1,0:T(8,128)(2,1)}, u32[]{:S(2)}) copy-start(bf16[8,32,256]{2,1,0:T(8,128)(2,1)} %copy-done.10) | copy-start | bytes 393220
  46.9 3.6 %copy-start.15 = (bf16[8,32,256]{2,1,0:T(8,128)(2,1)S(1)}, bf16[8,32,256]{2,1,0:T(8,128)(2,1)}, u32[]{:S(2)}) copy-start(bf16[8,32,256]{2,1,0:T(8,128)(2,1)} %copy-done.13) | copy-start | bytes 393220
  47.0 3.6 %copy-start.23 = (bf16[8,32,256]{2,1,0:T(8,128)(2,1)S(1)}, bf16[8,32,256]{2,1,0:T(8,128)(2,1)}, u32[]{:S(2)}) copy-start(bf16[8,32,256]{2,1,0:T(8,128)(2,1)} %copy-done.22) | copy-start | bytes 393220
  49.9 34.4 %collective-permute-start.8 = (f32[256,256]{1,0:T(8,128)S(1)}, f32[256,256]{1,0:T(8,128)S(1)}, u32[]{:S(2)}, u32[]{:S(2)}) collective-permute-start(f32[256,256]{1,0:T(8,128)S(1)} %slice.86), channel_id=1, source_target_pairs={{0,2},{1,3},{2,0},{3,1},{4,6},{5,7},{6,4},{7,5},{8,10},{9,11},{10,... | collective-permute-start | bytes 786440 | tf_op jit(solution)/shard_map/ppermute | solution.py:255
  50.6 1.8 %copy-start.21 = (f32[256,512]{1,0:T(8,128)S(1)}, f32[256,512]{1,0:T(8,128)}, u32[]{:S(2)}) copy-start(f32[256,512]{1,0:T(8,128)} %copy-done.20) | copy-start | bytes 1572868
  50.6 1.9 %copy-start.24 = (bf16[216,2048]{1,0:T(8,128)(2,1)S(1)}, bf16[216,2048]{1,0:T(8,128)(2,1)}, u32[]{:S(2)}) copy-start(bf16[216,2048]{1,0:T(8,128)(2,1)} %get-tuple-element.27) | copy-start | bytes 2654212
  50.6 28.6 %copy-start.5 = (bf16[8,2048,128]{2,1,0:T(8,128)(2,1)S(1)}, bf16[8,2048,128]{2,1,0:T(8,128)(2,1)}, u32[]{:S(2)}) copy-start(bf16[8,2048,128]{2,1,0:T(8,128)(2,1)} %refs_2_.1) | copy-start | bytes 12582916
  52.5 43.0 %collective-permute-start.11 = (bf16[216,2048]{1,0:T(8,128)(2,1)S(1)}, bf16[216,2048]{1,0:T(8,128)(2,1)S(1)}, u32[]{:S(2)}, u32[]{:S(2)}) collective-permute-start(bf16[216,2048]{1,0:T(8,128)(2,1)S(1)} %copy-done.24), channel_id=1, source_target_pairs={{0,12},{4,0},{8,4},{12,8},{1,13},{5,1},{9,5},{13,9},{2,14},{6,2},{... | collective-permute-start | bytes 2654216 | tf_op jit(solution)/shard_map/ppermute | solution.py:312
  56.0 25.2 %copy-start.17 = (bf16[216,2048]{1,0:T(8,128)(2,1)S(1)}, bf16[216,2048]{1,0:T(8,128)(2,1)}, u32[]{:S(2)}) copy-start(bf16[216,2048]{1,0:T(8,128)(2,1)} %get-tuple-element.29.refs_0_) | copy-start | bytes 2654212
  77.7 20.1 %collective-permute-start.9 = (bf16[32,32,256]{2,1,0:T(8,128)(2,1)S(1)}, bf16[32,32,256]{2,1,0:T(8,128)(2,1)S(1)}, u32[]{:S(2)}, u32[]{:S(2)}) collective-permute-start(bf16[32,32,256]{2,1,0:T(8,128)(2,1)S(1)} %pad_maximum_fusion.2), channel_id=1, source_target_pairs={{0,16},{16,0},{1,17},{17,1},{2,18},{18,2},{3,19},{19,3},{4,20},{20... | collective-permute-start | bytes 1572872 | tf_op jit(solution)/shard_map/ppermute | solution.py:200
  82.6 1.4 %collective-permute-start.15 = (f32[240,128]{1,0:T(8,128)S(1)}, f32[240,128]{1,0:T(8,128)S(1)}, u32[]{:S(2)}, u32[]{:S(2)}) collective-permute-start(f32[240,128]{1,0:T(8,128)S(1)} %shrink.4), channel_id=1, source_target_pairs={{0,1},{1,0},{2,3},{3,2},{4,5},{5,4},{6,7},{7,6},{8,9},{9,8},{10,11... | collective-permute-start | bytes 368648 | tf_op jit(solution)/shard_map/ppermute | solution.py:353
  84.0 1.9 %collective-permute-start.13 = (f32[240,128]{1,0:T(8,128)S(1)}, f32[240,128]{1,0:T(8,128)S(1)}, u32[]{:S(2)}, u32[]{:S(2)}) collective-permute-start(f32[240,128]{1,0:T(8,128)S(1)} %shrink.3.refs_2_), channel_id=1, source_target_pairs={{0,1},{1,0},{2,3},{3,2},{4,5},{5,4},{6,7},{7,6},{8,9},{9,8},{10,11... | collective-permute-start | bytes 368648 | tf_op jit(solution)/shard_map/ppermute | solution.py:353
  84.3 4.4 %collective-permute-start.16 = (f32[120,128]{1,0:T(8,128)S(1)}, f32[120,128]{1,0:T(8,128)S(1)}, u32[]{:S(2)}, u32[]{:S(2)}) collective-permute-start(f32[120,128]{1,0:T(8,128)S(1)} %slice.95), channel_id=1, source_target_pairs={{0,2},{1,3},{2,0},{3,1},{4,6},{5,7},{6,4},{7,5},{8,10},{9,11},{10,... | collective-permute-start | bytes 184328 | tf_op jit(solution)/shard_map/ppermute | solution.py:357
  85.9 14.9 %collective-permute-start.6 = (f32[256,256]{1,0:T(8,128)S(1)}, f32[256,256]{1,0:T(8,128)S(1)}, u32[]{:S(2)}, u32[]{:S(2)}) collective-permute-start(f32[256,256]{1,0:T(8,128)S(1)} %slice.84), channel_id=1, source_target_pairs={{0,2},{1,3},{2,0},{3,1},{4,6},{5,7},{6,4},{7,5},{8,10},{9,11},{10,... | collective-permute-start | bytes 786440 | tf_op jit(solution)/shard_map/ppermute | solution.py:255
  88.7 6.8 %collective-permute-start.14 = (f32[120,128]{1,0:T(8,128)S(1)}, f32[120,128]{1,0:T(8,128)S(1)}, u32[]{:S(2)}, u32[]{:S(2)}) collective-permute-start(f32[120,128]{1,0:T(8,128)S(1)} %slice.93), channel_id=1, source_target_pairs={{0,2},{1,3},{2,0},{3,1},{4,6},{5,7},{6,4},{7,5},{8,10},{9,11},{10,... | collective-permute-start | bytes 184328 | tf_op jit(solution)/shard_map/ppermute | solution.py:357
  97.6 1.6 %collective-permute-start.18 = (f32[480,128]{1,0:T(8,128)S(1)}, f32[480,128]{1,0:T(8,128)S(1)}, u32[]{:S(2)}, u32[]{:S(2)}) collective-permute-start(f32[480,128]{1,0:T(8,128)S(1)} %get-tuple-element.32), channel_id=1, source_target_pairs={{0,1},{1,0},{2,3},{3,2},{4,5},{5,4},{6,7},{7,6},{8,9},{9,8},{10,11... | collective-permute-start | bytes 737288 | tf_op jit(solution)/shard_map/ppermute | solution.py:353
  97.9 9.1 %copy-start.6 = (s32[768,1]{1,0:T(8,128)S(1)}, s32[768,1]{1,0:T(8,128)}, u32[]{:S(2)}) copy-start(s32[768,1]{1,0:T(8,128)} %copy.14.index_ref) | copy-start | bytes 9220
  99.3 5.4 %collective-permute-start.19 = (f32[240,128]{1,0:T(8,128)S(1)}, f32[240,128]{1,0:T(8,128)S(1)}, u32[]{:S(2)}, u32[]{:S(2)}) collective-permute-start(f32[240,128]{1,0:T(8,128)S(1)} %slice.97), channel_id=1, source_target_pairs={{0,2},{1,3},{2,0},{3,1},{4,6},{5,7},{6,4},{7,5},{8,10},{9,11},{10,... | collective-permute-start | bytes 368648 | tf_op jit(solution)/shard_map/ppermute | solution.py:357
  100.9 6.1 %collective-permute-start.17 = (f32[120,128]{1,0:T(8,128)S(1)}, f32[120,128]{1,0:T(8,128)S(1)}, u32[]{:S(2)}, u32[]{:S(2)}) collective-permute-start(f32[120,128]{1,0:T(8,128)S(1)} %get-tuple-element.30), channel_id=1, source_target_pairs={{0,8},{4,12},{8,0},{12,4},{1,9},{5,13},{9,1},{13,5},{2,10},{6,14},... | collective-permute-start | bytes 184328 | tf_op jit(solution)/shard_map/ppermute | solution.py:378
  104.7 4.3 %collective-permute-start.20 = (f32[120,128]{1,0:T(8,128)S(1)}, f32[120,128]{1,0:T(8,128)S(1)}, u32[]{:S(2)}, u32[]{:S(2)}) collective-permute-start(f32[120,128]{1,0:T(8,128)S(1)} %get-tuple-element.36), channel_id=1, source_target_pairs={{0,12},{4,0},{8,4},{12,8},{1,13},{5,1},{9,5},{13,9},{2,14},{6,2},{... | collective-permute-start | bytes 184328 | tf_op jit(solution)/shard_map/ppermute | solution.py:378
  106.9 6.0 %collective-permute-start.21 = (f32[120,128]{1,0:T(8,128)S(1)}, f32[120,128]{1,0:T(8,128)S(1)}, u32[]{:S(2)}, u32[]{:S(2)}) collective-permute-start(f32[120,128]{1,0:T(8,128)S(1)} %get-tuple-element.35), channel_id=1, source_target_pairs={{0,4},{4,8},{8,12},{12,0},{1,5},{5,9},{9,13},{13,1},{2,6},{6,10},{... | collective-permute-start | bytes 184328 | tf_op jit(solution)/shard_map/ppermute | solution.py:378

commit v14 on v13

--- a/solution.py
+++ b/solution.py
@@ -313,7 +313,7 @@
 
     packed, own_block, *blocks = pack([0] + order)
     arrived = {0: own_block}
-    mark, *blocks = gate(blocks, [packed])
+    mark, *blocks = gate(blocks, found)
     for r, block in zip(order, blocks):
         arrived[r] = send(block, r)
 
@@ -358,7 +358,7 @@
 
     slabs = 3
     slab_sums = [
-        reduce_base(tokens, key_value_weight, piece, pieces, columns, slab, slabs, [mark] + found)
+        reduce_base(tokens, key_value_weight, piece, pieces, columns, slab, slabs, [mark])
         for slab in range(slabs)
     ]
     base = jnp.concatenate([total for total, _ in slab_sums], axis=0)

time: 115 us -> 115 us (level)
  waiting for transfers between devices: 37.6 us -> 41.3 us
  local copies, waits for them, and re-layouts: 11.4 us -> 9.79 us
    ppermute x3, waiting for transfers between devices: 0.01 us -> 1.96 us  [gather_up(): lax.ppermute(own, 'batch', [(i, (i - r) % homes) for i in range(homes)])]
    ppermute x3, waiting for transfers between devices: 21.6 us -> 23.3 us  [send(): lax.ppermute(block, 'batch', [(i, (i + r) % homes) for i in range(homes)])]
    unnamed x52 -> x48, local copies, waits for them, and re-layouts: 8.4 us -> 6.87 us
    ppermute x3, starting transfers between devices: 3.47 us -> 2.17 us  [give_back(): lax.ppermute(total, 'batch', [(i, (i - r) % homes) for i in range(homes)])]
    ppermute x3, waiting for transfers between devices: 9.32 us -> 10.5 us  [combine(): lax.ppermute(value[half:], 'tensor', [(i, i ^ bit) for i in range(pieces)])]
  transfers between devices with their start and end apart: 22 -> 22, of which waited for: 8 -> 11; matrix products, arithmetic and copies ran while one was open for 7% -> 6% of each run, Pallas kernels for 26% -> 25%
where the time goes in v14:
time: 115 us
  waiting for transfers between devices  41.3 us (36%)
  Pallas kernels  30.7 us (27%)
  starting transfers between devices  25.1 us (22%)
  local copies, waits for them, and re-layouts  9.79 us (9%)
  other arithmetic  4.39 us (4%)
  between operations  3.26 us (3%)
    ppermute x3, waiting for transfers between devices, send(): lax.ppermute(block, 'batch', [(i, (i + r) % homes) for i in range(homes)])  23.3 us
    pallas_call x6, Pallas kernels, base_part(): pl.pallas_call(functools.partial(base_kernel, len(after)), out_shape=jax....  14.5 us
    ppermute x3, waiting for transfers between devices, combine(): lax.ppermute(value[half:], 'tensor', [(i, i ^ bit) for i in range(pieces)])  10.5 us
    unnamed x48, local copies, waits for them, and re-layouts  6.87 us
    ppermute x3, starting transfers between devices, send(): lax.ppermute(block, 'batch', [(i, (i + r) % homes) for i in range(homes)])  6.48 us
    pallas_call x1, Pallas kernels, pack(): pl.pallas_call(functools.partial(pack_kernel, span, shifts), out_shape=[j...  6.46 us
    ppermute x3, starting transfers between devices, gather_up(): lax.ppermute(own, 'batch', [(i, (i - r) % homes) for i in range(homes)])  6.11 us
    ppermute x3, starting transfers between devices, combine(): lax.ppermute(value[half:], 'tensor', [(i, i ^ bit) for i in range(pieces)])  4.91 us
  transfers between devices with their start and end apart: 22, of which 11 were waited for; matrix products, arithmetic and copies ran while one was open for 6% of the time, Pallas kernels for 25%

profile of v14, /device:TPU:0, one launch (start us, length us, event | category | flops | bytes accessed | tf_op | source)
XLA Modules:
  0.0 114.6 jit_solution(17031914107615276336)
XLA Ops:
  0.0 0.9 copy-done
  1.0 5.1 %collective-permute-start = (bf16[8,32,256]{2,1,0:T(8,128)(2,1)S(1)}, bf16[8,32,256]{2,1,0:T(8,128)(2,1)S(1)}, u32[]{:S(2)}, u32[]{:S(2)}) collective-permute-start(bf16[8,32,256]{2,1,0:T(8,128)(2,1)S(1)} %constant_dynamic-slice_fusion), channel_id=1, source_target_pairs={{0,12},{4,0},{8,4},{12,8},{1,13},{5,1},{9,5},{13,9},{2,14},{6,2},{... | collective-permute-start | bytes 393224 | tf_op jit(solution)/shard_map/ppermute | solution.py:196
  6.1 1.0 collective-permute-start.2
  7.1 1.7 %route.1 = (s32[1,768]{1,0:T(1,128)}, s32[8,128]{1,0:T(8,128)}) custom-call(s32[1]{0:T(128)} %bitcast.place_ref, s32[32]{0:T(128)} %entry_hbm.1, s32[768]{0:T(1024)} %request_hbm.1), custom_call_target="tpu_custom_call" | custom-call | flops 1 | bytes 1 | tf_op jit(solution)/shard_map/route/pallas_call | solution.py:279
  8.8 6.5 %pack.1 = (s32[8,128]{1,0:T(8,128)}, bf16[216,2048]{1,0:T(8,128)(2,1)}, bf16[216,2048]{1,0:T(8,128)(2,1)}, bf16[216,2048]{1,0:T(8,128)(2,1)}, bf16[216,2048]{1,0:T(8,128)(2,1)}) custom-call(s32[1,768]{1,0:T(1,128)} %get-tuple-element.19.index_ref, bf16[768,2048]{1,0:T(8,128)(2,1)} %tokens_ref.13), custom_call_target="tpu_custom_call" | custom-call | flops 1 | bytes 1 | tf_op jit(solution)/shard_map/pack/pallas_call | solution.py:297
  15.3 2.0 %collective-permute-done.1.refs_4_ = bf16[8,32,256]{2,1,0:T(8,128)(2,1)S(1)} collective-permute-done((bf16[8,32,256]{2,1,0:T(8,128)(2,1)S(1)}, bf16[8,32,256]{2,1,0:T(8,128)(2,1)S(1)}, u32[]{:S(2)}, u32[]{:S(2)}) %collective-permute-start.1) | collective-permute-done | bytes 131104 | tf_op jit(solution)/shard_map/ppermute | solution.py:196
  17.3 0.6 copy-done.15
  18.0 0.6 gate.1
  18.6 2.6 %collective-permute-start.12 = (bf16[216,2048]{1,0:T(8,128)(2,1)}, bf16[216,2048]{1,0:T(8,128)(2,1)}, u32[]{:S(2)}, u32[]{:S(2)}) collective-permute-start(bf16[216,2048]{1,0:T(8,128)(2,1)} %get-tuple-element.26), channel_id=1, source_target_pairs={{0,8},{4,12},{8,0},{12,4},{1,9},{5,13},{9,1},{13,5},{2,10},{6,14},... | collective-permute-start | bytes 2654216 | tf_op jit(solution)/shard_map/ppermute | solution.py:312
  21.7 4.2 %base.6.refs_0_ = f32[256,512]{1,0:T(8,128)} custom-call(s32[2]{0:T(128)} %broadcast_xor_fusion.block_ref, bf16[768,2048]{1,0:T(8,128)(2,1)} %tokens_ref.13, bf16[2048,1024]{1,0:T(8,128)(2,1)} %weight_ref.11, s32[8,128]{1,0:T(8,128)} %get-tuple-element.23.refs_0_), custom_call_target="tpu_custom_call" | custom-call | flops 1 | bytes 1 | tf_op jit(solution)/shard_map/base/pallas_call | solution.py:223
  25.9 2.2 %copy-done.2 = bf16[2048,1024]{1,0:T(8,128)(2,1)S(1)} copy-done((bf16[2048,1024]{1,0:T(8,128)(2,1)S(1)}, bf16[2048,1024]{1,0:T(8,128)(2,1)}, u32[]{:S(2)}) %copy-start.2) | copy-done | bytes 4194328
  28.0 2.5 %base.10.refs_0_ = f32[256,512]{1,0:T(8,128)} custom-call(s32[2]{0:T(128)S(1)} %copy-done.10, bf16[768,2048]{1,0:T(8,128)(2,1)S(1)} %copy-done.1, bf16[2048,1024]{1,0:T(8,128)(2,1)S(1)} %copy-done.2, s32[8,128]{1,0:T(8,128)S(1)} %copy-done.9), custom_call_target="tpu_custom_call" | custom-call | flops 1 | bytes 1 | tf_op jit(solution)/shard_map/base/pallas_call | solution.py:223
  30.5 0.5 collective-permute-start.7
  31.0 2.5 %base.8.refs_0_ = f32[256,512]{1,0:T(8,128)} custom-call(s32[2]{0:T(128)S(1)} %copy-done.10, bf16[768,2048]{1,0:T(8,128)(2,1)S(1)} %copy-done.1, bf16[2048,1024]{1,0:T(8,128)(2,1)S(1)} %copy-done.2, s32[8,128]{1,0:T(8,128)S(1)} %copy-done.9), custom_call_target="tpu_custom_call" | custom-call | flops 1 | bytes 1 | tf_op jit(solution)/shard_map/base/pallas_call | solution.py:223
  33.6 1.8 %base.7 = f32[256,512]{1,0:T(8,128)S(1)} custom-call(s32[2]{0:T(128)S(1)} %multiply_xor_fusion.block_ref, bf16[768,2048]{1,0:T(8,128)(2,1)S(1)} %copy-done.1, bf16[2048,1024]{1,0:T(8,128)(2,1)S(1)} %copy-done.3, f32[256,512]{1,0:T(8,128)S(1)} %copy-done.7), custom_call_target="tpu_custom_call" | custom-call | flops 1 | bytes 1 | tf_op jit(solution)/shard_map/base/pallas_call | solution.py:223
  35.5 0.8 copy-done.11
  36.2 0.7 slice.82
  37.0 1.5 %collective-permute-start.4 = (f32[256,256]{1,0:T(8,128)}, f32[256,256]{1,0:T(8,128)}, u32[]{:S(2)}, u32[]{:S(2)}) collective-permute-start(f32[256,256]{1,0:T(8,128)} %slice.82), channel_id=1, source_target_pairs={{0,2},{1,3},{2,0},{3,1},{4,6},{5,7},{6,4},{7,5},{8,10},{9,11},{10,... | collective-permute-start | bytes 786440 | tf_op jit(solution)/shard_map/ppermute | solution.py:255
  38.5 1.2 %slice.61 = s32[1,1]{1,0:T(1,128)} slice(s32[8,128]{1,0:T(8,128)} %get-tuple-element.18), slice={[0:1], [0:1]} | slice | bytes 8 | tf_op jit(solution)/shard_map/slice | solution.py:320
  42.4 0.9 copy.14.index_ref
  43.5 2.2 %copy-done.4 = bf16[2048,1024]{1,0:T(8,128)(2,1)S(1)} copy-done((bf16[2048,1024]{1,0:T(8,128)(2,1)S(1)}, bf16[2048,1024]{1,0:T(8,128)(2,1)}, u32[]{:S(2)}) %copy-start.4) | copy-done | bytes 4194328
  45.7 1.8 %base.11 = f32[256,512]{1,0:T(8,128)S(1)} custom-call(s32[2]{0:T(128)S(1)} %multiply_xor_fusion.block_ref, bf16[768,2048]{1,0:T(8,128)(2,1)S(1)} %copy-done.1, bf16[2048,1024]{1,0:T(8,128)(2,1)S(1)} %copy-done.4, f32[256,512]{1,0:T(8,128)} %base.10.refs_0_), custom_call_target="tpu_custom_call" | custom-call | flops 1 | bytes 1 | tf_op jit(solution)/shard_map/base/pallas_call | solution.py:223
  47.6 1.1 add.54
  48.7 0.6 collective-permute-start.8
  49.4 1.8 %base.9 = f32[256,512]{1,0:T(8,128)S(1)} custom-call(s32[2]{0:T(128)S(1)} %multiply_xor_fusion.block_ref, bf16[768,2048]{1,0:T(8,128)(2,1)S(1)} %copy-done.1, bf16[2048,1024]{1,0:T(8,128)(2,1)S(1)} %copy-done.4, f32[256,512]{1,0:T(8,128)} %base.8.refs_0_), custom_call_target="tpu_custom_call" | custom-call | flops 1 | bytes 1 | tf_op jit(solution)/shard_map/base/pallas_call | solution.py:223
  51.3 3.8 %collective-permute-start.11 = (bf16[216,2048]{1,0:T(8,128)(2,1)S(1)}, bf16[216,2048]{1,0:T(8,128)(2,1)S(1)}, u32[]{:S(2)}, u32[]{:S(2)}) collective-permute-start(bf16[216,2048]{1,0:T(8,128)(2,1)S(1)} %copy-done.22), channel_id=1, source_target_pairs={{0,12},{4,0},{8,4},{12,8},{1,13},{5,1},{9,5},{13,9},{2,14},{6,2},{... | collective-permute-start | bytes 2654216 | tf_op jit(solution)/shard_map/ppermute | solution.py:312
  55.1 1.1 add.52
  56.3 22.4 %collective-permute-done.12.refs_0_ = bf16[216,2048]{1,0:T(8,128)(2,1)} collective-permute-done((bf16[216,2048]{1,0:T(8,128)(2,1)}, bf16[216,2048]{1,0:T(8,128)(2,1)}, u32[]{:S(2)}, u32[]{:S(2)}) %collective-permute-start.12) | collective-permute-done | bytes 884768 | tf_op jit(solution)/shard_map/ppermute | solution.py:312
  78.7 1.5 %collective-permute-start.9 = (bf16[32,32,256]{2,1,0:T(8,128)(2,1)S(1)}, bf16[32,32,256]{2,1,0:T(8,128)(2,1)S(1)}, u32[]{:S(2)}, u32[]{:S(2)}) collective-permute-start(bf16[32,32,256]{2,1,0:T(8,128)(2,1)S(1)} %pad_maximum_fusion.2), channel_id=1, source_target_pairs={{0,16},{16,0},{1,17},{17,1},{2,18},{18,2},{3,19},{19,3},{4,20},{20... | collective-permute-start | bytes 1572872 | tf_op jit(solution)/shard_map/ppermute | solution.py:200
  80.3 2.0 %shrink.3.refs_2_ = f32[240,128]{1,0:T(8,128)S(1)} custom-call(s32[3]{0:T(128)S(1)} %pad_add_fusion.scalar_ref, bf16[216,2048]{1,0:T(8,128)(2,1)} %collective-permute-done.12.refs_0_, bf16[8,2048,128]{2,1,0:T(8,128)(2,1)S(1)} %copy-done.5, f32[8,512]{1,0:T(8,128)S(1)} %slice.89.refs_2_, f32[8,512]{1,0:T(8,128)S(1)} %slice.90.refs_3_, f32[8,512]{1,0:T(8,128)S(1)} %slice.91.refs_4_), custom_call_target="tpu_custom_call" | custom-call | flops 1 | bytes 1 | tf_op jit(solution)/shard_map/shrink/pallas_call | solution.py:326
  82.3 1.4 %shrink.4 = f32[240,128]{1,0:T(8,128)S(1)} custom-call(s32[3]{0:T(128)S(1)} %pad_add_fusion.scalar_ref, bf16[216,2048]{1,0:T(8,128)(2,1)S(1)} %copy-done.8, bf16[8,2048,128]{2,1,0:T(8,128)(2,1)S(1)} %copy-done.5, f32[240,128]{1,0:T(8,128)S(1)} %shrink.3.refs_2_), custom_call_target="tpu_custom_call" | custom-call | flops 1 | bytes 1 | tf_op jit(solution)/shard_map/shrink/pallas_call | solution.py:326
  83.7 1.0 slice_add_fusion.2
  85.3 1.6 %collective-permute-start.16 = (f32[120,128]{1,0:T(8,128)S(1)}, f32[120,128]{1,0:T(8,128)S(1)}, u32[]{:S(2)}, u32[]{:S(2)}) collective-permute-start(f32[120,128]{1,0:T(8,128)S(1)} %slice.95), channel_id=1, source_target_pairs={{0,2},{1,3},{2,0},{3,1},{4,6},{5,7},{6,4},{7,5},{8,10},{9,11},{10,... | collective-permute-start | bytes 184328 | tf_op jit(solution)/shard_map/ppermute | solution.py:357
  87.0 0.9 collective-permute-start.6
  87.9 1.8 %collective-permute-done.16 = f32[120,128]{1,0:T(8,128)S(1)} collective-permute-done((f32[120,128]{1,0:T(8,128)S(1)}, f32[120,128]{1,0:T(8,128)S(1)}, u32[]{:S(2)}, u32[]{:S(2)}) %collective-permute-start.16) | collective-permute-done | bytes 61472 | tf_op jit(solution)/shard_map/ppermute | solution.py:357
  89.7 1.8 %collective-permute-start.14 = (f32[120,128]{1,0:T(8,128)S(1)}, f32[120,128]{1,0:T(8,128)S(1)}, u32[]{:S(2)}, u32[]{:S(2)}) collective-permute-start(f32[120,128]{1,0:T(8,128)S(1)} %slice.93), channel_id=1, source_target_pairs={{0,2},{1,3},{2,0},{3,1},{4,6},{5,7},{6,4},{7,5},{8,10},{9,11},{10,... | collective-permute-start | bytes 184328 | tf_op jit(solution)/shard_map/ppermute | solution.py:357
  91.5 5.0 %collective-permute-done.14 = f32[120,128]{1,0:T(8,128)S(1)} collective-permute-done((f32[120,128]{1,0:T(8,128)S(1)}, f32[120,128]{1,0:T(8,128)S(1)}, u32[]{:S(2)}, u32[]{:S(2)}) %collective-permute-start.14) | collective-permute-done | bytes 61472 | tf_op jit(solution)/shard_map/ppermute | solution.py:357
  96.6 0.9 collective-permute-done.11.refs_1_
  97.4 1.5 %shrink.5 = (f32[480,128]{1,0:T(8,128)S(1)}, f32[120,128]{1,0:T(8,128)S(1)}, f32[120,128]{1,0:T(8,128)S(1)}) custom-call(s32[3]{0:T(128)S(1)} %pad_add_fusion.scalar_ref, bf16[216,2048]{1,0:T(8,128)(2,1)S(1)} %collective-permute-done.10.refs_0_, bf16[216,2048]{1,0:T(8,128)(2,1)S(1)} %collective-permute-done.11.refs_1_, bf16[8,2048,128]{2,1,0:T(8,128)(2,1)S(1)} %copy-done.5, ...), custom_call_target="tpu_custom_call" | custom-call | flops 1 | bytes 1 | tf_op jit(solution)/shard_map/shrink/pallas_call | solution.py:326
  99.2 1.3 %collective-permute-done.18 = f32[480,128]{1,0:T(8,128)S(1)} collective-permute-done((f32[480,128]{1,0:T(8,128)S(1)}, f32[480,128]{1,0:T(8,128)S(1)}, u32[]{:S(2)}, u32[]{:S(2)}) %collective-permute-start.18) | collective-permute-done | bytes 245792 | tf_op jit(solution)/shard_map/ppermute | solution.py:353
  100.6 1.6 %collective-permute-start.19 = (f32[240,128]{1,0:T(8,128)S(1)}, f32[240,128]{1,0:T(8,128)S(1)}, u32[]{:S(2)}, u32[]{:S(2)}) collective-permute-start(f32[240,128]{1,0:T(8,128)S(1)} %slice.97), channel_id=1, source_target_pairs={{0,2},{1,3},{2,0},{3,1},{4,6},{5,7},{6,4},{7,5},{8,10},{9,11},{10,... | collective-permute-start | bytes 368648 | tf_op jit(solution)/shard_map/ppermute | solution.py:357
  102.3 3.7 %collective-permute-done.19 = f32[240,128]{1,0:T(8,128)S(1)} collective-permute-done((f32[240,128]{1,0:T(8,128)S(1)}, f32[240,128]{1,0:T(8,128)S(1)}, u32[]{:S(2)}, u32[]{:S(2)}) %collective-permute-start.19) | collective-permute-done | bytes 122912 | tf_op jit(solution)/shard_map/ppermute | solution.py:357
  106.0 0.9 collective-permute-start.20
  107.0 1.1 collective-permute-start.21
  108.4 0.9 finish.2.base_ref
  109.3 1.0 collective-permute-done.20.refs_0_
  110.3 2.7 %collective-permute-done.21.refs_1_ = f32[120,128]{1,0:T(8,128)S(1)} collective-permute-done((f32[120,128]{1,0:T(8,128)S(1)}, f32[120,128]{1,0:T(8,128)S(1)}, u32[]{:S(2)}, u32[]{:S(2)}) %collective-permute-start.21) | collective-permute-done | bytes 61472 | tf_op jit(solution)/shard_map/ppermute | solution.py:378
  113.0 1.6 %finish.3 = bf16[768,256]{1,0:T(8,128)(2,1)} custom-call(s32[1]{0:T(128)} %bitcast.2.place_ref, s32[768,1]{1,0:T(8,128)S(1)} %copy-done.6, f32[768,256]{1,0:T(8,128)S(1)} %finish.2.base_ref, bf16[32,64,256]{2,1,0:T(8,128)(2,1)S(1)} %pad_maximum_fusion.up_ref, f32[120,128]{1,0:T(8,128)S(1)} %collective-permute-done.20.refs_0_, ...), custom_call_target="tpu_custom_call" | custom-call | flops 1 | bytes 1 | tf_op jit(solution)/shard_map/finish/pallas_call | solution.py:160
  (93 shorter events, 2.5 us)
Async XLA Ops:
  0.0 1.0 copy-start
  1.0 20.7 %copy-start.19 = (bf16[8,32,256]{2,1,0:T(8,128)(2,1)}, bf16[8,32,256]{2,1,0:T(8,128)(2,1)S(1)}, u32[]{:S(2)}) copy-start(bf16[8,32,256]{2,1,0:T(8,128)(2,1)S(1)} %constant_dynamic-slice_fusion) | copy-start | bytes 393220
  1.0 14.3 %collective-permute-start = (bf16[8,32,256]{2,1,0:T(8,128)(2,1)S(1)}, bf16[8,32,256]{2,1,0:T(8,128)(2,1)S(1)}, u32[]{:S(2)}, u32[]{:S(2)}) collective-permute-start(bf16[8,32,256]{2,1,0:T(8,128)(2,1)S(1)} %constant_dynamic-slice_fusion), channel_id=1, source_target_pairs={{0,12},{4,0},{8,4},{12,8},{1,13},{5,1},{9,5},{13,9},{2,14},{6,2},{... | collective-permute-start | bytes 393224 | tf_op jit(solution)/shard_map/ppermute | solution.py:196
  6.1 11.2 %collective-permute-start.1 = (bf16[8,32,256]{2,1,0:T(8,128)(2,1)S(1)}, bf16[8,32,256]{2,1,0:T(8,128)(2,1)S(1)}, u32[]{:S(2)}, u32[]{:S(2)}) collective-permute-start(bf16[8,32,256]{2,1,0:T(8,128)(2,1)S(1)} %constant_dynamic-slice_fusion), channel_id=1, source_target_pairs={{0,8},{4,12},{8,0},{12,4},{1,9},{5,13},{9,1},{13,5},{2,10},{6,14},... | collective-permute-start | bytes 393224 | tf_op jit(solution)/shard_map/ppermute | solution.py:196
  6.1 11.2 %collective-permute-start.2 = (bf16[8,32,256]{2,1,0:T(8,128)(2,1)S(1)}, bf16[8,32,256]{2,1,0:T(8,128)(2,1)S(1)}, u32[]{:S(2)}, u32[]{:S(2)}) collective-permute-start(bf16[8,32,256]{2,1,0:T(8,128)(2,1)S(1)} %constant_dynamic-slice_fusion), channel_id=1, source_target_pairs={{0,4},{4,8},{8,12},{12,0},{1,5},{5,9},{9,13},{13,1},{2,6},{6,10},{... | collective-permute-start | bytes 393224 | tf_op jit(solution)/shard_map/ppermute | solution.py:196
  15.3 2.0 %copy-start.13 = (bf16[8,32,256]{2,1,0:T(8,128)(2,1)}, bf16[8,32,256]{2,1,0:T(8,128)(2,1)S(1)}, u32[]{:S(2)}) copy-start(bf16[8,32,256]{2,1,0:T(8,128)(2,1)S(1)} %collective-permute-done.refs_3_) | copy-start | bytes 393220
  17.3 0.7 copy-start.15
  17.3 0.7 copy-start.17
  18.6 60.2 %collective-permute-start.12 = (bf16[216,2048]{1,0:T(8,128)(2,1)}, bf16[216,2048]{1,0:T(8,128)(2,1)}, u32[]{:S(2)}, u32[]{:S(2)}) collective-permute-start(bf16[216,2048]{1,0:T(8,128)(2,1)} %get-tuple-element.26), channel_id=1, source_target_pairs={{0,8},{4,12},{8,0},{12,4},{1,9},{5,13},{9,1},{13,5},{2,10},{6,14},... | collective-permute-start | bytes 2654216 | tf_op jit(solution)/shard_map/ppermute | solution.py:312
  21.7 4.2 %copy-start.1 = (bf16[768,2048]{1,0:T(8,128)(2,1)S(1)}, bf16[768,2048]{1,0:T(8,128)(2,1)}, u32[]{:S(2)}) copy-start(bf16[768,2048]{1,0:T(8,128)(2,1)} %tokens_ref.13) | copy-start | bytes 9437188
  21.7 4.2 %copy-start.9 = (s32[8,128]{1,0:T(8,128)S(1)}, s32[8,128]{1,0:T(8,128)}, u32[]{:S(2)}) copy-start(s32[8,128]{1,0:T(8,128)} %get-tuple-element.23.refs_0_) | copy-start | bytes 12292
  21.7 4.2 %copy-start.10 = (s32[2]{0:T(128)S(1)}, s32[2]{0:T(128)}, u32[]{:S(2)}) copy-start(s32[2]{0:T(128)} %broadcast_xor_fusion.block_ref) | copy-start | bytes 28
  25.8 9.5 %collective-permute-start.3 = (f32[256,512]{1,0:T(8,128)}, f32[256,512]{1,0:T(8,128)S(1)}, u32[]{:S(2)}, u32[]{:S(2)}) collective-permute-start(f32[256,512]{1,0:T(8,128)} %base.6.refs_0_), channel_id=1, source_target_pairs={{0,1},{1,0},{2,3},{3,2},{4,5},{5,4},{6,7},{7,6},{8,9},{9,8},{10,11... | collective-permute-start | bytes 1572872 | tf_op jit(solution)/shard_map/ppermute | solution.py:255
  25.9 2.2 %copy-start.2 = (bf16[2048,1024]{1,0:T(8,128)(2,1)S(1)}, bf16[2048,1024]{1,0:T(8,128)(2,1)}, u32[]{:S(2)}) copy-start(bf16[2048,1024]{1,0:T(8,128)(2,1)} %weight_ref.11) | copy-start | bytes 12582916
  30.5 3.0 %copy-start.3 = (bf16[2048,1024]{1,0:T(8,128)(2,1)S(1)}, bf16[2048,1024]{1,0:T(8,128)(2,1)}, u32[]{:S(2)}) copy-start(bf16[2048,1024]{1,0:T(8,128)(2,1)} %weight_ref.11) | copy-start | bytes 12582916
  30.5 3.0 %copy-start.7 = (f32[256,512]{1,0:T(8,128)S(1)}, f32[256,512]{1,0:T(8,128)}, u32[]{:S(2)}) copy-start(f32[256,512]{1,0:T(8,128)} %base.6.refs_0_) | copy-start | bytes 1572868
  30.5 17.0 %collective-permute-start.7 = (f32[256,512]{1,0:T(8,128)}, f32[256,512]{1,0:T(8,128)}, u32[]{:S(2)}, u32[]{:S(2)}) collective-permute-start(f32[256,512]{1,0:T(8,128)} %base.10.refs_0_), channel_id=1, source_target_pairs={{0,1},{1,0},{2,3},{3,2},{4,5},{5,4},{6,7},{7,6},{8,9},{9,8},{10,11... | collective-permute-start | bytes 1572872 | tf_op jit(solution)/shard_map/ppermute | solution.py:255
  33.5 17.7 %collective-permute-start.5 = (f32[256,512]{1,0:T(8,128)}, f32[256,512]{1,0:T(8,128)}, u32[]{:S(2)}, u32[]{:S(2)}) collective-permute-start(f32[256,512]{1,0:T(8,128)} %base.8.refs_0_), channel_id=1, source_target_pairs={{0,1},{1,0},{2,3},{3,2},{4,5},{5,4},{6,7},{7,6},{8,9},{9,8},{10,11... | collective-permute-start | bytes 1572872 | tf_op jit(solution)/shard_map/ppermute | solution.py:255
  33.6 8.9 %copy-start.23 = (s32[1,768]{1,0:T(1,128)S(1)}, s32[1,768]{1,0:T(1,128)}, u32[]{:S(2)}) copy-start(s32[1,768]{1,0:T(1,128)} %get-tuple-element.19.index_ref) | copy-start | bytes 9220
  35.4 0.8 copy-start.11
  37.0 46.7 %collective-permute-start.4 = (f32[256,256]{1,0:T(8,128)}, f32[256,256]{1,0:T(8,128)}, u32[]{:S(2)}, u32[]{:S(2)}) collective-permute-start(f32[256,256]{1,0:T(8,128)} %slice.82), channel_id=1, source_target_pairs={{0,2},{1,3},{2,0},{3,1},{4,6},{5,7},{6,4},{7,5},{8,10},{9,11},{10,... | collective-permute-start | bytes 786440 | tf_op jit(solution)/shard_map/ppermute | solution.py:255
  43.5 2.2 %copy-start.4 = (bf16[2048,1024]{1,0:T(8,128)(2,1)S(1)}, bf16[2048,1024]{1,0:T(8,128)(2,1)}, u32[]{:S(2)}) copy-start(bf16[2048,1024]{1,0:T(8,128)(2,1)} %weight_ref.11) | copy-start | bytes 12582916
  45.6 1.8 %copy-start.21 = (bf16[216,2048]{1,0:T(8,128)(2,1)S(1)}, bf16[216,2048]{1,0:T(8,128)(2,1)}, u32[]{:S(2)}) copy-start(bf16[216,2048]{1,0:T(8,128)(2,1)} %get-tuple-element.24) | copy-start | bytes 2654212
  45.6 3.7 %copy-start.14 = (bf16[8,32,256]{2,1,0:T(8,128)(2,1)S(1)}, bf16[8,32,256]{2,1,0:T(8,128)(2,1)}, u32[]{:S(2)}) copy-start(bf16[8,32,256]{2,1,0:T(8,128)(2,1)} %copy-done.13) | copy-start | bytes 393220
  45.6 3.7 %copy-start.16 = (bf16[8,32,256]{2,1,0:T(8,128)(2,1)S(1)}, bf16[8,32,256]{2,1,0:T(8,128)(2,1)}, u32[]{:S(2)}) copy-start(bf16[8,32,256]{2,1,0:T(8,128)(2,1)} %copy-done.15) | copy-start | bytes 393220
  45.6 3.7 %copy-start.18 = (bf16[8,32,256]{2,1,0:T(8,128)(2,1)S(1)}, bf16[8,32,256]{2,1,0:T(8,128)(2,1)}, u32[]{:S(2)}) copy-start(bf16[8,32,256]{2,1,0:T(8,128)(2,1)} %copy-done.17) | copy-start | bytes 393220
  45.7 3.7 %copy-start.20 = (bf16[8,32,256]{2,1,0:T(8,128)(2,1)S(1)}, bf16[8,32,256]{2,1,0:T(8,128)(2,1)}, u32[]{:S(2)}) copy-start(bf16[8,32,256]{2,1,0:T(8,128)(2,1)} %copy-done.19) | copy-start | bytes 393220
  47.5 49.1 %collective-permute-start.10 = (bf16[216,2048]{1,0:T(8,128)(2,1)S(1)}, bf16[216,2048]{1,0:T(8,128)(2,1)S(1)}, u32[]{:S(2)}, u32[]{:S(2)}) collective-permute-start(bf16[216,2048]{1,0:T(8,128)(2,1)S(1)} %copy-done.21), channel_id=1, source_target_pairs={{0,4},{4,8},{8,12},{12,0},{1,5},{5,9},{9,13},{13,1},{2,6},{6,10},{... | collective-permute-start | bytes 2654216 | tf_op jit(solution)/shard_map/ppermute | solution.py:312
  48.7 36.6 %collective-permute-start.8 = (f32[256,256]{1,0:T(8,128)S(1)}, f32[256,256]{1,0:T(8,128)S(1)}, u32[]{:S(2)}, u32[]{:S(2)}) collective-permute-start(f32[256,256]{1,0:T(8,128)S(1)} %slice.86), channel_id=1, source_target_pairs={{0,2},{1,3},{2,0},{3,1},{4,6},{5,7},{6,4},{7,5},{8,10},{9,11},{10,... | collective-permute-start | bytes 786440 | tf_op jit(solution)/shard_map/ppermute | solution.py:255
  49.4 1.8 %copy-start.12 = (f32[256,512]{1,0:T(8,128)S(1)}, f32[256,512]{1,0:T(8,128)}, u32[]{:S(2)}) copy-start(f32[256,512]{1,0:T(8,128)} %copy-done.11) | copy-start | bytes 1572868
  49.4 1.9 %copy-start.22 = (bf16[216,2048]{1,0:T(8,128)(2,1)S(1)}, bf16[216,2048]{1,0:T(8,128)(2,1)}, u32[]{:S(2)}) copy-start(bf16[216,2048]{1,0:T(8,128)(2,1)} %get-tuple-element.25) | copy-start | bytes 2654212
  49.4 30.8 %copy-start.5 = (bf16[8,2048,128]{2,1,0:T(8,128)(2,1)S(1)}, bf16[8,2048,128]{2,1,0:T(8,128)(2,1)}, u32[]{:S(2)}) copy-start(bf16[8,2048,128]{2,1,0:T(8,128)(2,1)} %refs_2_.1) | copy-start | bytes 12582916
  51.3 46.2 %collective-permute-start.11 = (bf16[216,2048]{1,0:T(8,128)(2,1)S(1)}, bf16[216,2048]{1,0:T(8,128)(2,1)S(1)}, u32[]{:S(2)}, u32[]{:S(2)}) collective-permute-start(bf16[216,2048]{1,0:T(8,128)(2,1)S(1)} %copy-done.22), channel_id=1, source_target_pairs={{0,12},{4,0},{8,4},{12,8},{1,13},{5,1},{9,5},{13,9},{2,14},{6,2},{... | collective-permute-start | bytes 2654216 | tf_op jit(solution)/shard_map/ppermute | solution.py:312
  56.3 26.0 %copy-start.8 = (bf16[216,2048]{1,0:T(8,128)(2,1)S(1)}, bf16[216,2048]{1,0:T(8,128)(2,1)}, u32[]{:S(2)}) copy-start(bf16[216,2048]{1,0:T(8,128)(2,1)} %get-tuple-element.27.refs_0_) | copy-start | bytes 2654212
  78.7 20.3 %collective-permute-start.9 = (bf16[32,32,256]{2,1,0:T(8,128)(2,1)S(1)}, bf16[32,32,256]{2,1,0:T(8,128)(2,1)S(1)}, u32[]{:S(2)}, u32[]{:S(2)}) collective-permute-start(bf16[32,32,256]{2,1,0:T(8,128)(2,1)S(1)} %pad_maximum_fusion.2), channel_id=1, source_target_pairs={{0,16},{16,0},{1,17},{17,1},{2,18},{18,2},{3,19},{19,3},{4,20},{20... | collective-permute-start | bytes 1572872 | tf_op jit(solution)/shard_map/ppermute | solution.py:200
  83.7 1.4 %collective-permute-start.15 = (f32[240,128]{1,0:T(8,128)S(1)}, f32[240,128]{1,0:T(8,128)S(1)}, u32[]{:S(2)}, u32[]{:S(2)}) collective-permute-start(f32[240,128]{1,0:T(8,128)S(1)} %shrink.4), channel_id=1, source_target_pairs={{0,1},{1,0},{2,3},{3,2},{4,5},{5,4},{6,7},{7,6},{8,9},{9,8},{10,11... | collective-permute-start | bytes 368648 | tf_op jit(solution)/shard_map/ppermute | solution.py:353
  85.1 1.9 %collective-permute-start.13 = (f32[240,128]{1,0:T(8,128)S(1)}, f32[240,128]{1,0:T(8,128)S(1)}, u32[]{:S(2)}, u32[]{:S(2)}) collective-permute-start(f32[240,128]{1,0:T(8,128)S(1)} %shrink.3.refs_2_), channel_id=1, source_target_pairs={{0,1},{1,0},{2,3},{3,2},{4,5},{5,4},{6,7},{7,6},{8,9},{9,8},{10,11... | collective-permute-start | bytes 368648 | tf_op jit(solution)/shard_map/ppermute | solution.py:353
  85.3 4.4 %collective-permute-start.16 = (f32[120,128]{1,0:T(8,128)S(1)}, f32[120,128]{1,0:T(8,128)S(1)}, u32[]{:S(2)}, u32[]{:S(2)}) collective-permute-start(f32[120,128]{1,0:T(8,128)S(1)} %slice.95), channel_id=1, source_target_pairs={{0,2},{1,3},{2,0},{3,1},{4,6},{5,7},{6,4},{7,5},{8,10},{9,11},{10,... | collective-permute-start | bytes 184328 | tf_op jit(solution)/shard_map/ppermute | solution.py:357
  87.0 15.2 %collective-permute-start.6 = (f32[256,256]{1,0:T(8,128)S(1)}, f32[256,256]{1,0:T(8,128)S(1)}, u32[]{:S(2)}, u32[]{:S(2)}) collective-permute-start(f32[256,256]{1,0:T(8,128)S(1)} %slice.84), channel_id=1, source_target_pairs={{0,2},{1,3},{2,0},{3,1},{4,6},{5,7},{6,4},{7,5},{8,10},{9,11},{10,... | collective-permute-start | bytes 786440 | tf_op jit(solution)/shard_map/ppermute | solution.py:255
  89.7 6.9 %collective-permute-start.14 = (f32[120,128]{1,0:T(8,128)S(1)}, f32[120,128]{1,0:T(8,128)S(1)}, u32[]{:S(2)}, u32[]{:S(2)}) collective-permute-start(f32[120,128]{1,0:T(8,128)S(1)} %slice.93), channel_id=1, source_target_pairs={{0,2},{1,3},{2,0},{3,1},{4,6},{5,7},{6,4},{7,5},{8,10},{9,11},{10,... | collective-permute-start | bytes 184328 | tf_op jit(solution)/shard_map/ppermute | solution.py:357
  98.9 1.6 %collective-permute-start.18 = (f32[480,128]{1,0:T(8,128)S(1)}, f32[480,128]{1,0:T(8,128)S(1)}, u32[]{:S(2)}, u32[]{:S(2)}) collective-permute-start(f32[480,128]{1,0:T(8,128)S(1)} %get-tuple-element.30), channel_id=1, source_target_pairs={{0,1},{1,0},{2,3},{3,2},{4,5},{5,4},{6,7},{7,6},{8,9},{9,8},{10,11... | collective-permute-start | bytes 737288 | tf_op jit(solution)/shard_map/ppermute | solution.py:353
  99.1 9.2 %copy-start.6 = (s32[768,1]{1,0:T(8,128)S(1)}, s32[768,1]{1,0:T(8,128)}, u32[]{:S(2)}) copy-start(s32[768,1]{1,0:T(8,128)} %copy.14.index_ref) | copy-start | bytes 9220
  100.6 5.4 %collective-permute-start.19 = (f32[240,128]{1,0:T(8,128)S(1)}, f32[240,128]{1,0:T(8,128)S(1)}, u32[]{:S(2)}, u32[]{:S(2)}) collective-permute-start(f32[240,128]{1,0:T(8,128)S(1)} %slice.97), channel_id=1, source_target_pairs={{0,2},{1,3},{2,0},{3,1},{4,6},{5,7},{6,4},{7,5},{8,10},{9,11},{10,... | collective-permute-start | bytes 368648 | tf_op jit(solution)/shard_map/ppermute | solution.py:357
  102.2 6.2 %collective-permute-start.17 = (f32[120,128]{1,0:T(8,128)S(1)}, f32[120,128]{1,0:T(8,128)S(1)}, u32[]{:S(2)}, u32[]{:S(2)}) collective-permute-start(f32[120,128]{1,0:T(8,128)S(1)} %get-tuple-element.28), channel_id=1, source_target_pairs={{0,8},{4,12},{8,0},{12,4},{1,9},{5,13},{9,1},{13,5},{2,10},{6,14},... | collective-permute-start | bytes 184328 | tf_op jit(solution)/shard_map/ppermute | solution.py:378
  106.0 4.3 %collective-permute-start.20 = (f32[120,128]{1,0:T(8,128)S(1)}, f32[120,128]{1,0:T(8,128)S(1)}, u32[]{:S(2)}, u32[]{:S(2)}) collective-permute-start(f32[120,128]{1,0:T(8,128)S(1)} %get-tuple-element.34), channel_id=1, source_target_pairs={{0,12},{4,0},{8,4},{12,8},{1,13},{5,1},{9,5},{13,9},{2,14},{6,2},{... | collective-permute-start | bytes 184328 | tf_op jit(solution)/shard_map/ppermute | solution.py:378
  107.0 6.0 %collective-permute-start.21 = (f32[120,128]{1,0:T(8,128)S(1)}, f32[120,128]{1,0:T(8,128)S(1)}, u32[]{:S(2)}, u32[]{:S(2)}) collective-permute-start(f32[120,128]{1,0:T(8,128)S(1)} %get-tuple-element.33), channel_id=1, source_target_pairs={{0,4},{4,8},{8,12},{12,0},{1,5},{5,9},{9,13},{13,1},{2,6},{6,10},{... | collective-permute-start | bytes 184328 | tf_op jit(solution)/shard_map/ppermute | solution.py:378

commit v15 on v13

--- a/solution.py
+++ b/solution.py
@@ -63,7 +63,8 @@
     heavy_ref[...] = jnp.broadcast_to(heavy, heavy_ref.shape)
 
 
-def pack_kernel(span, shifts, index_ref, tokens_ref, mark_ref, *refs):
+def pack_kernel(span, shifts, waited, index_ref, tokens_ref, *refs):
+    mark_ref, *refs = refs[waited:]
     count = len(shifts)
     block_refs, buffer, sems = refs[:count], refs[count], refs[count + 1]
     mark_ref[...] = jnp.zeros_like(mark_ref)
@@ -293,11 +294,11 @@
         cost_estimate=COST,
         name="route",
     )(place.reshape(1), adapter_entry, request_adapter)
-    def pack(shifts):
+    def pack(shifts, after):
         return pl.pallas_call(
-            functools.partial(pack_kernel, span, shifts),
+            functools.partial(pack_kernel, span, shifts, len(after)),
             out_shape=[jax.ShapeDtypeStruct((8, 128), jnp.int32)] + [block_shape] * len(shifts),
-            in_specs=[VMEM] * 2,
+            in_specs=[VMEM] * 2 + [ANY] * len(after),
             out_specs=[VMEM] + [HBM] * len(shifts),
             scratch_shapes=[
                 pltpu.VMEM((len(shifts), span, width), jnp.bfloat16),
@@ -306,14 +307,15 @@
             compiler_params=WIDE,
             cost_estimate=COST,
             name="pack",
-        )(index, tokens)
+        )(index, tokens, *after)
 
     def send(block, r):
         return lax.ppermute(block, "batch", [(i, (i + r) % homes) for i in range(homes)])
 
-    packed, own_block, *blocks = pack([0] + order)
+    packed, *blocks = pack(order, [])
+    mark, *blocks = gate(blocks, [packed])
+    _, own_block = pack([0], [mark])
     arrived = {0: own_block}
-    mark, *blocks = gate(blocks, [packed])
     for r, block in zip(order, blocks):
         arrived[r] = send(block, r)
 

time: 115 us -> 114 us (level)
  waiting for transfers between devices: 37.6 us -> 33.9 us
  Pallas kernels: 31.3 us -> 34.9 us
    ppermute x3, waiting for transfers between devices: 21.6 us -> 17.9 us  [send(): lax.ppermute(block, 'batch', [(i, (i + r) % homes) for i in range(homes)])]
    pallas_call x1 -> x2, Pallas kernels: 6.48 us -> 10.1 us  [pack(): pl.pallas_call(functools.partial(pack_kernel, span, shifts, len(after)),...]
    unnamed x52 -> x54, local copies, waits for them, and re-layouts: 8.4 us -> 8.37 us
  transfers between devices with their start and end apart: 22 -> 22, of which waited for: 8 -> 8; matrix products, arithmetic and copies ran while one was open for 7% -> 7% of each run, Pallas kernels for 26% -> 29%
where the time goes in v15:
time: 114 us
  Pallas kernels  34.9 us (31%)
  waiting for transfers between devices  33.9 us (30%)
  starting transfers between devices  25.8 us (23%)
  local copies, waits for them, and re-layouts  11.4 us (10%)
  other arithmetic  4.51 us (4%)
  between operations  3.44 us (3%)
    ppermute x3, waiting for transfers between devices, send(): lax.ppermute(block, 'batch', [(i, (i + r) % homes) for i in range(homes)])  17.9 us
    pallas_call x6, Pallas kernels, base_part(): pl.pallas_call(functools.partial(base_kernel, len(after)), out_shape=jax....  14.5 us
    pallas_call x2, Pallas kernels, pack(): pl.pallas_call(functools.partial(pack_kernel, span, shifts, len(after)),...  10.1 us
    ppermute x3, waiting for transfers between devices, combine(): lax.ppermute(value[half:], 'tensor', [(i, i ^ bit) for i in range(pieces)])  9.27 us
    unnamed x54, local copies, waits for them, and re-layouts  8.37 us
    ppermute x3, starting transfers between devices, gather_up(): lax.ppermute(own, 'batch', [(i, (i - r) % homes) for i in range(homes)])  6.11 us
    ppermute x3, starting transfers between devices, send(): lax.ppermute(block, 'batch', [(i, (i + r) % homes) for i in range(homes)])  5.8 us
    pallas_call x3, Pallas kernels, shrink(): pl.pallas_call(functools.partial(shrink_kernel, held, light, rank, value_...  5.49 us
  transfers between devices with their start and end apart: 22, of which 8 were waited for; matrix products, arithmetic and copies ran while one was open for 7% of the time, Pallas kernels for 29%

profile of v15, /device:TPU:0, one launch (start us, length us, event | category | flops | bytes accessed | tf_op | source)
XLA Modules:
  0.0 113.8 jit_solution(14571340008576156606)
XLA Ops:
  0.0 0.9 copy-done
  1.0 5.1 %collective-permute-start = (bf16[8,32,256]{2,1,0:T(8,128)(2,1)S(1)}, bf16[8,32,256]{2,1,0:T(8,128)(2,1)S(1)}, u32[]{:S(2)}, u32[]{:S(2)}) collective-permute-start(bf16[8,32,256]{2,1,0:T(8,128)(2,1)S(1)} %constant_dynamic-slice_fusion), channel_id=1, source_target_pairs={{0,12},{4,0},{8,4},{12,8},{1,13},{5,1},{9,5},{13,9},{2,14},{6,2},{... | collective-permute-start | bytes 393224 | tf_op jit(solution)/shard_map/ppermute | solution.py:197
  6.1 1.0 collective-permute-start.2
  7.1 1.7 %route.1 = (s32[1,768]{1,0:T(1,128)}, s32[8,128]{1,0:T(8,128)}) custom-call(s32[1]{0:T(128)} %bitcast.place_ref, s32[32]{0:T(128)} %entry_hbm.1, s32[768]{0:T(1024)} %request_hbm.1), custom_call_target="tpu_custom_call" | custom-call | flops 1 | bytes 1 | tf_op jit(solution)/shard_map/route/pallas_call | solution.py:280
  8.8 5.8 %pack.2 = (s32[8,128]{1,0:T(8,128)}, bf16[216,2048]{1,0:T(8,128)(2,1)}, bf16[216,2048]{1,0:T(8,128)(2,1)}, bf16[216,2048]{1,0:T(8,128)(2,1)}) custom-call(s32[1,768]{1,0:T(1,128)} %get-tuple-element.20.index_ref, bf16[768,2048]{1,0:T(8,128)(2,1)} %tokens_ref.15), custom_call_target="tpu_custom_call" | custom-call | flops 1 | bytes 1 | tf_op jit(solution)/shard_map/pack/pallas_call | solution.py:298
  15.2 1.9 %collective-permute-start.12 = (bf16[216,2048]{1,0:T(8,128)(2,1)}, bf16[216,2048]{1,0:T(8,128)(2,1)}, u32[]{:S(2)}, u32[]{:S(2)}) collective-permute-start(bf16[216,2048]{1,0:T(8,128)(2,1)} %get-tuple-element.28), channel_id=1, source_target_pairs={{0,8},{4,12},{8,0},{12,4},{1,9},{5,13},{9,1},{13,5},{2,10},{6,14},... | collective-permute-start | bytes 2654216 | tf_op jit(solution)/shard_map/ppermute | solution.py:313
  17.1 0.6 broadcast_xor_fusion.block_ref
  17.8 0.6 copy-done.11
  18.4 0.6 copy-done.14
  19.1 4.2 %base.6.refs_0_ = f32[256,512]{1,0:T(8,128)} custom-call(s32[2]{0:T(128)} %broadcast_xor_fusion.block_ref, bf16[768,2048]{1,0:T(8,128)(2,1)} %tokens_ref.15, bf16[2048,1024]{1,0:T(8,128)(2,1)} %weight_ref.11, s32[8,128]{1,0:T(8,128)} %get-tuple-element.25.refs_0_, bf16[8,32,256]{2,1,0:T(8,128)(2,1)} %copy-done.8, bf16[8,32,256]{2,1,0:T(8,128)(2,1)} %copy-done.11, ...), custom_call_target="tpu_custom_call" | custom-call | flops 1 | bytes 1 | tf_op jit(solution)/shard_map/base/pallas_call | solution.py:224
  23.3 2.2 %copy-done.3 = bf16[2048,1024]{1,0:T(8,128)(2,1)S(1)} copy-done((bf16[2048,1024]{1,0:T(8,128)(2,1)S(1)}, bf16[2048,1024]{1,0:T(8,128)(2,1)}, u32[]{:S(2)}) %copy-start.3) | copy-done | bytes 4194328
  25.5 0.9 copy-done.9
  26.4 2.5 %base.10.refs_0_ = f32[256,512]{1,0:T(8,128)} custom-call(s32[2]{0:T(128)S(1)} %copy-done.20, bf16[768,2048]{1,0:T(8,128)(2,1)S(1)} %copy-done.1, bf16[2048,1024]{1,0:T(8,128)(2,1)S(1)} %copy-done.3, s32[8,128]{1,0:T(8,128)S(1)} %copy-done.19, bf16[8,32,256]{2,1,0:T(8,128)(2,1)S(1)} %copy-done.9, bf16[8,32,256]{2,1,0:T(8,128)(2,1)S(1)} %copy-done.12, ...), custom_call_target="tpu_custom_call" | custom-call | flops 1 | bytes 1 | tf_op jit(solution)/shard_map/base/pallas_call | solution.py:224
  29.3 2.5 %base.8.refs_0_ = f32[256,512]{1,0:T(8,128)} custom-call(s32[2]{0:T(128)S(1)} %copy-done.20, bf16[768,2048]{1,0:T(8,128)(2,1)S(1)} %copy-done.1, bf16[2048,1024]{1,0:T(8,128)(2,1)S(1)} %copy-done.3, s32[8,128]{1,0:T(8,128)S(1)} %copy-done.19, bf16[8,32,256]{2,1,0:T(8,128)(2,1)S(1)} %copy-done.9, bf16[8,32,256]{2,1,0:T(8,128)(2,1)S(1)} %copy-done.12, ...), custom_call_target="tpu_custom_call" | custom-call | flops 1 | bytes 1 | tf_op jit(solution)/shard_map/base/pallas_call | solution.py:224
  31.9 1.8 %base.7 = f32[256,512]{1,0:T(8,128)S(1)} custom-call(s32[2]{0:T(128)S(1)} %multiply_xor_fusion.block_ref, bf16[768,2048]{1,0:T(8,128)(2,1)S(1)} %copy-done.1, bf16[2048,1024]{1,0:T(8,128)(2,1)S(1)} %copy-done.4, f32[256,512]{1,0:T(8,128)S(1)} %copy-done.17), custom_call_target="tpu_custom_call" | custom-call | flops 1 | bytes 1 | tf_op jit(solution)/shard_map/base/pallas_call | solution.py:224
  33.8 0.8 copy-done.21
  34.6 0.7 slice.82
  35.3 1.5 %collective-permute-start.4 = (f32[256,256]{1,0:T(8,128)}, f32[256,256]{1,0:T(8,128)}, u32[]{:S(2)}, u32[]{:S(2)}) collective-permute-start(f32[256,256]{1,0:T(8,128)} %slice.82), channel_id=1, source_target_pairs={{0,2},{1,3},{2,0},{3,1},{4,6},{5,7},{6,4},{7,5},{8,10},{9,11},{10,... | collective-permute-start | bytes 786440 | tf_op jit(solution)/shard_map/ppermute | solution.py:256
  36.8 1.5 %collective-permute-start.10 = (bf16[216,2048]{1,0:T(8,128)(2,1)}, bf16[216,2048]{1,0:T(8,128)(2,1)}, u32[]{:S(2)}, u32[]{:S(2)}) collective-permute-start(bf16[216,2048]{1,0:T(8,128)(2,1)} %get-tuple-element.26), channel_id=1, source_target_pairs={{0,4},{4,8},{8,12},{12,0},{1,5},{5,9},{9,13},{13,1},{2,6},{6,10},{... | collective-permute-start | bytes 2654216 | tf_op jit(solution)/shard_map/ppermute | solution.py:313
  38.3 4.3 %pack.3 = (s32[8,128]{1,0:T(8,128)}, bf16[216,2048]{1,0:T(8,128)(2,1)}) custom-call(s32[1,768]{1,0:T(1,128)} %get-tuple-element.20.index_ref, bf16[768,2048]{1,0:T(8,128)(2,1)} %tokens_ref.15, s32[8,128]{1,0:T(8,128)} %get-tuple-element.25.refs_0_), custom_call_target="tpu_custom_call" | custom-call | flops 1 | bytes 1 | tf_op jit(solution)/shard_map/pack/pallas_call | solution.py:298
  42.6 1.2 %slice.61 = s32[1,1]{1,0:T(1,128)} slice(s32[8,128]{1,0:T(8,128)} %get-tuple-element.19), slice={[0:1], [0:1]} | slice | bytes 8 | tf_op jit(solution)/shard_map/slice | solution.py:322
  46.7 0.9 copy.14.index_ref
  47.7 2.2 %copy-done.5 = bf16[2048,1024]{1,0:T(8,128)(2,1)S(1)} copy-done((bf16[2048,1024]{1,0:T(8,128)(2,1)S(1)}, bf16[2048,1024]{1,0:T(8,128)(2,1)}, u32[]{:S(2)}) %copy-start.5) | copy-done | bytes 4194328
  49.9 1.8 %base.11 = f32[256,512]{1,0:T(8,128)S(1)} custom-call(s32[2]{0:T(128)S(1)} %multiply_xor_fusion.block_ref, bf16[768,2048]{1,0:T(8,128)(2,1)S(1)} %copy-done.2, bf16[2048,1024]{1,0:T(8,128)(2,1)S(1)} %copy-done.5, f32[256,512]{1,0:T(8,128)} %base.10.refs_0_), custom_call_target="tpu_custom_call" | custom-call | flops 1 | bytes 1 | tf_op jit(solution)/shard_map/base/pallas_call | solution.py:224
  51.7 1.1 add.54
  53.6 1.8 %base.9 = f32[256,512]{1,0:T(8,128)S(1)} custom-call(s32[2]{0:T(128)S(1)} %multiply_xor_fusion.block_ref, bf16[768,2048]{1,0:T(8,128)(2,1)S(1)} %copy-done.2, bf16[2048,1024]{1,0:T(8,128)(2,1)S(1)} %copy-done.5, f32[256,512]{1,0:T(8,128)} %base.8.refs_0_), custom_call_target="tpu_custom_call" | custom-call | flops 1 | bytes 1 | tf_op jit(solution)/shard_map/base/pallas_call | solution.py:224
  55.4 2.4 %collective-permute-start.11 = (bf16[216,2048]{1,0:T(8,128)(2,1)S(1)}, bf16[216,2048]{1,0:T(8,128)(2,1)S(1)}, u32[]{:S(2)}, u32[]{:S(2)}) collective-permute-start(bf16[216,2048]{1,0:T(8,128)(2,1)S(1)} %copy-done.25), channel_id=1, source_target_pairs={{0,12},{4,0},{8,4},{12,8},{1,13},{5,1},{9,5},{13,9},{2,14},{6,2},{... | collective-permute-start | bytes 2654216 | tf_op jit(solution)/shard_map/ppermute | solution.py:313
  57.8 1.1 add.52
  59.0 17.9 %collective-permute-done.12.refs_0_ = bf16[216,2048]{1,0:T(8,128)(2,1)} collective-permute-done((bf16[216,2048]{1,0:T(8,128)(2,1)}, bf16[216,2048]{1,0:T(8,128)(2,1)}, u32[]{:S(2)}, u32[]{:S(2)}) %collective-permute-start.12) | collective-permute-done | bytes 884768 | tf_op jit(solution)/shard_map/ppermute | solution.py:313
  77.0 1.5 %collective-permute-start.9 = (bf16[32,32,256]{2,1,0:T(8,128)(2,1)S(1)}, bf16[32,32,256]{2,1,0:T(8,128)(2,1)S(1)}, u32[]{:S(2)}, u32[]{:S(2)}) collective-permute-start(bf16[32,32,256]{2,1,0:T(8,128)(2,1)S(1)} %pad_maximum_fusion.2), channel_id=1, source_target_pairs={{0,16},{16,0},{1,17},{17,1},{2,18},{18,2},{3,19},{19,3},{4,20},{20... | collective-permute-start | bytes 1572872 | tf_op jit(solution)/shard_map/ppermute | solution.py:201
  78.5 2.0 %shrink.3.refs_2_ = f32[240,128]{1,0:T(8,128)S(1)} custom-call(s32[3]{0:T(128)S(1)} %pad_add_fusion.scalar_ref, bf16[216,2048]{1,0:T(8,128)(2,1)} %collective-permute-done.12.refs_0_, bf16[8,2048,128]{2,1,0:T(8,128)(2,1)S(1)} %copy-done.6, f32[8,512]{1,0:T(8,128)S(1)} %slice.89.refs_2_, f32[8,512]{1,0:T(8,128)S(1)} %slice.90.refs_3_, f32[8,512]{1,0:T(8,128)S(1)} %slice.91.refs_4_), custom_call_target="tpu_custom_call" | custom-call | flops 1 | bytes 1 | tf_op jit(solution)/shard_map/shrink/pallas_call | solution.py:328
  80.5 1.4 %shrink.4 = f32[240,128]{1,0:T(8,128)S(1)} custom-call(s32[3]{0:T(128)S(1)} %pad_add_fusion.scalar_ref, bf16[216,2048]{1,0:T(8,128)(2,1)S(1)} %copy-done.18, bf16[8,2048,128]{2,1,0:T(8,128)(2,1)S(1)} %copy-done.6, f32[240,128]{1,0:T(8,128)S(1)} %shrink.3.refs_2_), custom_call_target="tpu_custom_call" | custom-call | flops 1 | bytes 1 | tf_op jit(solution)/shard_map/shrink/pallas_call | solution.py:328
  82.0 1.0 slice_add_fusion.2
  83.6 1.6 %collective-permute-start.16 = (f32[120,128]{1,0:T(8,128)S(1)}, f32[120,128]{1,0:T(8,128)S(1)}, u32[]{:S(2)}, u32[]{:S(2)}) collective-permute-start(f32[120,128]{1,0:T(8,128)S(1)} %slice.95), channel_id=1, source_target_pairs={{0,2},{1,3},{2,0},{3,1},{4,6},{5,7},{6,4},{7,5},{8,10},{9,11},{10,... | collective-permute-start | bytes 184328 | tf_op jit(solution)/shard_map/ppermute | solution.py:359
  85.2 0.9 collective-permute-start.6
  86.2 1.8 %collective-permute-done.16 = f32[120,128]{1,0:T(8,128)S(1)} collective-permute-done((f32[120,128]{1,0:T(8,128)S(1)}, f32[120,128]{1,0:T(8,128)S(1)}, u32[]{:S(2)}, u32[]{:S(2)}) %collective-permute-start.16) | collective-permute-done | bytes 61472 | tf_op jit(solution)/shard_map/ppermute | solution.py:359
  87.9 1.8 %collective-permute-start.14 = (f32[120,128]{1,0:T(8,128)S(1)}, f32[120,128]{1,0:T(8,128)S(1)}, u32[]{:S(2)}, u32[]{:S(2)}) collective-permute-start(f32[120,128]{1,0:T(8,128)S(1)} %slice.93), channel_id=1, source_target_pairs={{0,2},{1,3},{2,0},{3,1},{4,6},{5,7},{6,4},{7,5},{8,10},{9,11},{10,... | collective-permute-start | bytes 184328 | tf_op jit(solution)/shard_map/ppermute | solution.py:359
  89.8 5.0 %collective-permute-done.14 = f32[120,128]{1,0:T(8,128)S(1)} collective-permute-done((f32[120,128]{1,0:T(8,128)S(1)}, f32[120,128]{1,0:T(8,128)S(1)}, u32[]{:S(2)}, u32[]{:S(2)}) %collective-permute-start.14) | collective-permute-done | bytes 61472 | tf_op jit(solution)/shard_map/ppermute | solution.py:359
  94.8 2.1 %shrink.5 = (f32[480,128]{1,0:T(8,128)S(1)}, f32[120,128]{1,0:T(8,128)S(1)}, f32[120,128]{1,0:T(8,128)S(1)}) custom-call(s32[3]{0:T(128)S(1)} %pad_add_fusion.scalar_ref, bf16[216,2048]{1,0:T(8,128)(2,1)} %collective-permute-done.10.refs_0_, bf16[216,2048]{1,0:T(8,128)(2,1)S(1)} %collective-permute-done.11.refs_1_, bf16[8,2048,128]{2,1,0:T(8,128)(2,1)S(1)} %copy-done.6, ...), custom_call_target="tpu_custom_call" | custom-call | flops 1 | bytes 1 | tf_op jit(solution)/shard_map/shrink/pallas_call | solution.py:328
  97.2 1.3 %collective-permute-done.18 = f32[480,128]{1,0:T(8,128)S(1)} collective-permute-done((f32[480,128]{1,0:T(8,128)S(1)}, f32[480,128]{1,0:T(8,128)S(1)}, u32[]{:S(2)}, u32[]{:S(2)}) %collective-permute-start.18) | collective-permute-done | bytes 245792 | tf_op jit(solution)/shard_map/ppermute | solution.py:355
  98.6 1.6 %collective-permute-start.19 = (f32[240,128]{1,0:T(8,128)S(1)}, f32[240,128]{1,0:T(8,128)S(1)}, u32[]{:S(2)}, u32[]{:S(2)}) collective-permute-start(f32[240,128]{1,0:T(8,128)S(1)} %slice.97), channel_id=1, source_target_pairs={{0,2},{1,3},{2,0},{3,1},{4,6},{5,7},{6,4},{7,5},{8,10},{9,11},{10,... | collective-permute-start | bytes 368648 | tf_op jit(solution)/shard_map/ppermute | solution.py:359
  100.2 1.3 %collective-permute-start.17 = (f32[120,128]{1,0:T(8,128)S(1)}, f32[120,128]{1,0:T(8,128)S(1)}, u32[]{:S(2)}, u32[]{:S(2)}) collective-permute-start(f32[120,128]{1,0:T(8,128)S(1)} %get-tuple-element.30), channel_id=1, source_target_pairs={{0,8},{4,12},{8,0},{12,4},{1,9},{5,13},{9,1},{13,5},{2,10},{6,14},... | collective-permute-start | bytes 184328 | tf_op jit(solution)/shard_map/ppermute | solution.py:380
  101.5 2.5 %collective-permute-done.19 = f32[240,128]{1,0:T(8,128)S(1)} collective-permute-done((f32[240,128]{1,0:T(8,128)S(1)}, f32[240,128]{1,0:T(8,128)S(1)}, u32[]{:S(2)}, u32[]{:S(2)}) %collective-permute-start.19) | collective-permute-done | bytes 122912 | tf_op jit(solution)/shard_map/ppermute | solution.py:359
  104.0 2.2 %collective-permute-start.20 = (f32[120,128]{1,0:T(8,128)S(1)}, f32[120,128]{1,0:T(8,128)S(1)}, u32[]{:S(2)}, u32[]{:S(2)}) collective-permute-start(f32[120,128]{1,0:T(8,128)S(1)} %get-tuple-element.36), channel_id=1, source_target_pairs={{0,12},{4,0},{8,4},{12,8},{1,13},{5,1},{9,5},{13,9},{2,14},{6,2},{... | collective-permute-start | bytes 184328 | tf_op jit(solution)/shard_map/ppermute | solution.py:380
  106.3 0.9 finish.2.base_ref
  107.1 1.1 %collective-permute-done.20.refs_0_ = f32[120,128]{1,0:T(8,128)S(1)} collective-permute-done((f32[120,128]{1,0:T(8,128)S(1)}, f32[120,128]{1,0:T(8,128)S(1)}, u32[]{:S(2)}, u32[]{:S(2)}) %collective-permute-start.20) | collective-permute-done | bytes 61472 | tf_op jit(solution)/shard_map/ppermute | solution.py:380
  108.3 3.9 %collective-permute-done.21.refs_1_ = f32[120,128]{1,0:T(8,128)S(1)} collective-permute-done((f32[120,128]{1,0:T(8,128)S(1)}, f32[120,128]{1,0:T(8,128)S(1)}, u32[]{:S(2)}, u32[]{:S(2)}) %collective-permute-start.21) | collective-permute-done | bytes 61472 | tf_op jit(solution)/shard_map/ppermute | solution.py:380
  112.2 1.6 %finish.3 = bf16[768,256]{1,0:T(8,128)(2,1)} custom-call(s32[1]{0:T(128)} %bitcast.2.place_ref, s32[768,1]{1,0:T(8,128)S(1)} %copy-done.7, f32[768,256]{1,0:T(8,128)S(1)} %finish.2.base_ref, bf16[32,64,256]{2,1,0:T(8,128)(2,1)S(1)} %pad_maximum_fusion.up_ref, f32[120,128]{1,0:T(8,128)S(1)} %collective-permute-done.20.refs_0_, ...), custom_call_target="tpu_custom_call" | custom-call | flops 1 | bytes 1 | tf_op jit(solution)/shard_map/finish/pallas_call | solution.py:161
  (100 shorter events, 3.3 us)
Async XLA Ops:
  0.0 1.0 copy-start
  1.0 16.8 %copy-start.23 = (bf16[8,32,256]{2,1,0:T(8,128)(2,1)}, bf16[8,32,256]{2,1,0:T(8,128)(2,1)S(1)}, u32[]{:S(2)}) copy-start(bf16[8,32,256]{2,1,0:T(8,128)(2,1)S(1)} %constant_dynamic-slice_fusion) | copy-start | bytes 393220
  1.0 16.7 %collective-permute-start = (bf16[8,32,256]{2,1,0:T(8,128)(2,1)S(1)}, bf16[8,32,256]{2,1,0:T(8,128)(2,1)S(1)}, u32[]{:S(2)}, u32[]{:S(2)}) collective-permute-start(bf16[8,32,256]{2,1,0:T(8,128)(2,1)S(1)} %constant_dynamic-slice_fusion), channel_id=1, source_target_pairs={{0,12},{4,0},{8,4},{12,8},{1,13},{5,1},{9,5},{13,9},{2,14},{6,2},{... | collective-permute-start | bytes 393224 | tf_op jit(solution)/shard_map/ppermute | solution.py:197
  6.1 11.6 %collective-permute-start.1 = (bf16[8,32,256]{2,1,0:T(8,128)(2,1)S(1)}, bf16[8,32,256]{2,1,0:T(8,128)(2,1)S(1)}, u32[]{:S(2)}, u32[]{:S(2)}) collective-permute-start(bf16[8,32,256]{2,1,0:T(8,128)(2,1)S(1)} %constant_dynamic-slice_fusion), channel_id=1, source_target_pairs={{0,8},{4,12},{8,0},{12,4},{1,9},{5,13},{9,1},{13,5},{2,10},{6,14},... | collective-permute-start | bytes 393224 | tf_op jit(solution)/shard_map/ppermute | solution.py:197
  6.1 11.7 %collective-permute-start.2 = (bf16[8,32,256]{2,1,0:T(8,128)(2,1)S(1)}, bf16[8,32,256]{2,1,0:T(8,128)(2,1)S(1)}, u32[]{:S(2)}, u32[]{:S(2)}) collective-permute-start(bf16[8,32,256]{2,1,0:T(8,128)(2,1)S(1)} %constant_dynamic-slice_fusion), channel_id=1, source_target_pairs={{0,4},{4,8},{8,12},{12,0},{1,5},{5,9},{9,13},{13,1},{2,6},{6,10},{... | collective-permute-start | bytes 393224 | tf_op jit(solution)/shard_map/ppermute | solution.py:197
  15.2 61.8 %collective-permute-start.12 = (bf16[216,2048]{1,0:T(8,128)(2,1)}, bf16[216,2048]{1,0:T(8,128)(2,1)}, u32[]{:S(2)}, u32[]{:S(2)}) collective-permute-start(bf16[216,2048]{1,0:T(8,128)(2,1)} %get-tuple-element.28), channel_id=1, source_target_pairs={{0,8},{4,12},{8,0},{12,4},{1,9},{5,13},{9,1},{13,5},{2,10},{6,14},... | collective-permute-start | bytes 2654216 | tf_op jit(solution)/shard_map/ppermute | solution.py:313
  17.7 1.3 %copy-start.8 = (bf16[8,32,256]{2,1,0:T(8,128)(2,1)}, bf16[8,32,256]{2,1,0:T(8,128)(2,1)S(1)}, u32[]{:S(2)}) copy-start(bf16[8,32,256]{2,1,0:T(8,128)(2,1)S(1)} %collective-permute-done.refs_1_) | copy-start | bytes 393220
  17.7 0.7 copy-start.11
  19.0 4.2 %copy-start.1 = (bf16[768,2048]{1,0:T(8,128)(2,1)S(1)}, bf16[768,2048]{1,0:T(8,128)(2,1)}, u32[]{:S(2)}) copy-start(bf16[768,2048]{1,0:T(8,128)(2,1)} %tokens_ref.15) | copy-start | bytes 9437188
  19.0 4.2 %copy-start.12 = (bf16[8,32,256]{2,1,0:T(8,128)(2,1)S(1)}, bf16[8,32,256]{2,1,0:T(8,128)(2,1)}, u32[]{:S(2)}) copy-start(bf16[8,32,256]{2,1,0:T(8,128)(2,1)} %copy-done.11) | copy-start | bytes 393220
  19.0 4.2 %copy-start.15 = (bf16[8,32,256]{2,1,0:T(8,128)(2,1)S(1)}, bf16[8,32,256]{2,1,0:T(8,128)(2,1)}, u32[]{:S(2)}) copy-start(bf16[8,32,256]{2,1,0:T(8,128)(2,1)} %copy-done.14) | copy-start | bytes 393220
  19.0 4.2 %copy-start.19 = (s32[8,128]{1,0:T(8,128)S(1)}, s32[8,128]{1,0:T(8,128)}, u32[]{:S(2)}) copy-start(s32[8,128]{1,0:T(8,128)} %get-tuple-element.25.refs_0_) | copy-start | bytes 12292
  19.1 4.2 %copy-start.20 = (s32[2]{0:T(128)S(1)}, s32[2]{0:T(128)}, u32[]{:S(2)}) copy-start(s32[2]{0:T(128)} %broadcast_xor_fusion.block_ref) | copy-start | bytes 28
  23.2 10.4 %collective-permute-start.3 = (f32[256,512]{1,0:T(8,128)}, f32[256,512]{1,0:T(8,128)S(1)}, u32[]{:S(2)}, u32[]{:S(2)}) collective-permute-start(f32[256,512]{1,0:T(8,128)} %base.6.refs_0_), channel_id=1, source_target_pairs={{0,1},{1,0},{2,3},{3,2},{4,5},{5,4},{6,7},{7,6},{8,9},{9,8},{10,11... | collective-permute-start | bytes 1572872 | tf_op jit(solution)/shard_map/ppermute | solution.py:256
  23.3 2.2 %copy-start.3 = (bf16[2048,1024]{1,0:T(8,128)(2,1)S(1)}, bf16[2048,1024]{1,0:T(8,128)(2,1)}, u32[]{:S(2)}) copy-start(bf16[2048,1024]{1,0:T(8,128)(2,1)} %weight_ref.11) | copy-start | bytes 12582916
  25.5 0.9 copy-start.9
  28.8 3.0 %copy-start.4 = (bf16[2048,1024]{1,0:T(8,128)(2,1)S(1)}, bf16[2048,1024]{1,0:T(8,128)(2,1)}, u32[]{:S(2)}) copy-start(bf16[2048,1024]{1,0:T(8,128)(2,1)} %weight_ref.11) | copy-start | bytes 12582916
  28.8 3.0 %copy-start.17 = (f32[256,512]{1,0:T(8,128)S(1)}, f32[256,512]{1,0:T(8,128)}, u32[]{:S(2)}) copy-start(f32[256,512]{1,0:T(8,128)} %base.6.refs_0_) | copy-start | bytes 1572868
  28.8 22.9 %collective-permute-start.7 = (f32[256,512]{1,0:T(8,128)}, f32[256,512]{1,0:T(8,128)}, u32[]{:S(2)}, u32[]{:S(2)}) collective-permute-start(f32[256,512]{1,0:T(8,128)} %base.10.refs_0_), channel_id=1, source_target_pairs={{0,1},{1,0},{2,3},{3,2},{4,5},{5,4},{6,7},{7,6},{8,9},{9,8},{10,11... | collective-permute-start | bytes 1572872 | tf_op jit(solution)/shard_map/ppermute | solution.py:256
  31.8 23.6 %collective-permute-start.5 = (f32[256,512]{1,0:T(8,128)}, f32[256,512]{1,0:T(8,128)}, u32[]{:S(2)}, u32[]{:S(2)}) collective-permute-start(f32[256,512]{1,0:T(8,128)} %base.8.refs_0_), channel_id=1, source_target_pairs={{0,1},{1,0},{2,3},{3,2},{4,5},{5,4},{6,7},{7,6},{8,9},{9,8},{10,11... | collective-permute-start | bytes 1572872 | tf_op jit(solution)/shard_map/ppermute | solution.py:256
  33.6 13.0 %copy-start.26 = (s32[1,768]{1,0:T(1,128)S(1)}, s32[1,768]{1,0:T(1,128)}, u32[]{:S(2)}) copy-start(s32[1,768]{1,0:T(1,128)} %get-tuple-element.20.index_ref) | copy-start | bytes 9220
  33.7 14.1 %copy-start.2 = (bf16[768,2048]{1,0:T(8,128)(2,1)S(1)}, bf16[768,2048]{1,0:T(8,128)(2,1)}, u32[]{:S(2)}) copy-start(bf16[768,2048]{1,0:T(8,128)(2,1)} %tokens_ref.15) | copy-start | bytes 9437188
  33.8 0.8 copy-start.21
  35.3 46.6 %collective-permute-start.4 = (f32[256,256]{1,0:T(8,128)}, f32[256,256]{1,0:T(8,128)}, u32[]{:S(2)}, u32[]{:S(2)}) collective-permute-start(f32[256,256]{1,0:T(8,128)} %slice.82), channel_id=1, source_target_pairs={{0,2},{1,3},{2,0},{3,1},{4,6},{5,7},{6,4},{7,5},{8,10},{9,11},{10,... | collective-permute-start | bytes 786440 | tf_op jit(solution)/shard_map/ppermute | solution.py:256
  36.8 58.0 %collective-permute-start.10 = (bf16[216,2048]{1,0:T(8,128)(2,1)}, bf16[216,2048]{1,0:T(8,128)(2,1)}, u32[]{:S(2)}, u32[]{:S(2)}) collective-permute-start(bf16[216,2048]{1,0:T(8,128)(2,1)} %get-tuple-element.26), channel_id=1, source_target_pairs={{0,4},{4,8},{8,12},{12,0},{1,5},{5,9},{9,13},{13,1},{2,6},{6,10},{... | collective-permute-start | bytes 2654216 | tf_op jit(solution)/shard_map/ppermute | solution.py:313
  47.7 2.2 %copy-start.5 = (bf16[2048,1024]{1,0:T(8,128)(2,1)S(1)}, bf16[2048,1024]{1,0:T(8,128)(2,1)}, u32[]{:S(2)}) copy-start(bf16[2048,1024]{1,0:T(8,128)(2,1)} %weight_ref.11) | copy-start | bytes 12582916
  49.9 3.5 %copy-start.10 = (bf16[8,32,256]{2,1,0:T(8,128)(2,1)S(1)}, bf16[8,32,256]{2,1,0:T(8,128)(2,1)}, u32[]{:S(2)}) copy-start(bf16[8,32,256]{2,1,0:T(8,128)(2,1)} %copy-done.8) | copy-start | bytes 393220
  49.9 3.5 %copy-start.13 = (bf16[8,32,256]{2,1,0:T(8,128)(2,1)S(1)}, bf16[8,32,256]{2,1,0:T(8,128)(2,1)}, u32[]{:S(2)}) copy-start(bf16[8,32,256]{2,1,0:T(8,128)(2,1)} %copy-done.11) | copy-start | bytes 393220
  49.9 3.5 %copy-start.16 = (bf16[8,32,256]{2,1,0:T(8,128)(2,1)S(1)}, bf16[8,32,256]{2,1,0:T(8,128)(2,1)}, u32[]{:S(2)}) copy-start(bf16[8,32,256]{2,1,0:T(8,128)(2,1)} %copy-done.14) | copy-start | bytes 393220
  49.9 3.5 %copy-start.24 = (bf16[8,32,256]{2,1,0:T(8,128)(2,1)S(1)}, bf16[8,32,256]{2,1,0:T(8,128)(2,1)}, u32[]{:S(2)}) copy-start(bf16[8,32,256]{2,1,0:T(8,128)(2,1)} %copy-done.23) | copy-start | bytes 393220
  52.9 30.7 %collective-permute-start.8 = (f32[256,256]{1,0:T(8,128)S(1)}, f32[256,256]{1,0:T(8,128)S(1)}, u32[]{:S(2)}, u32[]{:S(2)}) collective-permute-start(f32[256,256]{1,0:T(8,128)S(1)} %slice.86), channel_id=1, source_target_pairs={{0,2},{1,3},{2,0},{3,1},{4,6},{5,7},{6,4},{7,5},{8,10},{9,11},{10,... | collective-permute-start | bytes 786440 | tf_op jit(solution)/shard_map/ppermute | solution.py:256
  53.5 1.8 %copy-start.22 = (f32[256,512]{1,0:T(8,128)S(1)}, f32[256,512]{1,0:T(8,128)}, u32[]{:S(2)}) copy-start(f32[256,512]{1,0:T(8,128)} %copy-done.21) | copy-start | bytes 1572868
  53.5 1.9 %copy-start.25 = (bf16[216,2048]{1,0:T(8,128)(2,1)S(1)}, bf16[216,2048]{1,0:T(8,128)(2,1)}, u32[]{:S(2)}) copy-start(bf16[216,2048]{1,0:T(8,128)(2,1)} %get-tuple-element.27) | copy-start | bytes 2654212
  53.6 24.9 %copy-start.6 = (bf16[8,2048,128]{2,1,0:T(8,128)(2,1)S(1)}, bf16[8,2048,128]{2,1,0:T(8,128)(2,1)}, u32[]{:S(2)}) copy-start(bf16[8,2048,128]{2,1,0:T(8,128)(2,1)} %refs_2_.1) | copy-start | bytes 12582916
  55.4 39.4 %collective-permute-start.11 = (bf16[216,2048]{1,0:T(8,128)(2,1)S(1)}, bf16[216,2048]{1,0:T(8,128)(2,1)S(1)}, u32[]{:S(2)}, u32[]{:S(2)}) collective-permute-start(bf16[216,2048]{1,0:T(8,128)(2,1)S(1)} %copy-done.25), channel_id=1, source_target_pairs={{0,12},{4,0},{8,4},{12,8},{1,13},{5,1},{9,5},{13,9},{2,14},{6,2},{... | collective-permute-start | bytes 2654216 | tf_op jit(solution)/shard_map/ppermute | solution.py:313
  59.0 21.5 %copy-start.18 = (bf16[216,2048]{1,0:T(8,128)(2,1)S(1)}, bf16[216,2048]{1,0:T(8,128)(2,1)}, u32[]{:S(2)}) copy-start(bf16[216,2048]{1,0:T(8,128)(2,1)} %get-tuple-element.29.refs_0_) | copy-start | bytes 2654212
  77.0 20.1 %collective-permute-start.9 = (bf16[32,32,256]{2,1,0:T(8,128)(2,1)S(1)}, bf16[32,32,256]{2,1,0:T(8,128)(2,1)S(1)}, u32[]{:S(2)}, u32[]{:S(2)}) collective-permute-start(bf16[32,32,256]{2,1,0:T(8,128)(2,1)S(1)} %pad_maximum_fusion.2), channel_id=1, source_target_pairs={{0,16},{16,0},{1,17},{17,1},{2,18},{18,2},{3,19},{19,3},{4,20},{20... | collective-permute-start | bytes 1572872 | tf_op jit(solution)/shard_map/ppermute | solution.py:201
  81.9 1.4 %collective-permute-start.15 = (f32[240,128]{1,0:T(8,128)S(1)}, f32[240,128]{1,0:T(8,128)S(1)}, u32[]{:S(2)}, u32[]{:S(2)}) collective-permute-start(f32[240,128]{1,0:T(8,128)S(1)} %shrink.4), channel_id=1, source_target_pairs={{0,1},{1,0},{2,3},{3,2},{4,5},{5,4},{6,7},{7,6},{8,9},{9,8},{10,11... | collective-permute-start | bytes 368648 | tf_op jit(solution)/shard_map/ppermute | solution.py:355
  83.3 1.9 %collective-permute-start.13 = (f32[240,128]{1,0:T(8,128)S(1)}, f32[240,128]{1,0:T(8,128)S(1)}, u32[]{:S(2)}, u32[]{:S(2)}) collective-permute-start(f32[240,128]{1,0:T(8,128)S(1)} %shrink.3.refs_2_), channel_id=1, source_target_pairs={{0,1},{1,0},{2,3},{3,2},{4,5},{5,4},{6,7},{7,6},{8,9},{9,8},{10,11... | collective-permute-start | bytes 368648 | tf_op jit(solution)/shard_map/ppermute | solution.py:355
  83.6 4.4 %collective-permute-start.16 = (f32[120,128]{1,0:T(8,128)S(1)}, f32[120,128]{1,0:T(8,128)S(1)}, u32[]{:S(2)}, u32[]{:S(2)}) collective-permute-start(f32[120,128]{1,0:T(8,128)S(1)} %slice.95), channel_id=1, source_target_pairs={{0,2},{1,3},{2,0},{3,1},{4,6},{5,7},{6,4},{7,5},{8,10},{9,11},{10,... | collective-permute-start | bytes 184328 | tf_op jit(solution)/shard_map/ppermute | solution.py:359
  85.2 14.9 %collective-permute-start.6 = (f32[256,256]{1,0:T(8,128)S(1)}, f32[256,256]{1,0:T(8,128)S(1)}, u32[]{:S(2)}, u32[]{:S(2)}) collective-permute-start(f32[256,256]{1,0:T(8,128)S(1)} %slice.84), channel_id=1, source_target_pairs={{0,2},{1,3},{2,0},{3,1},{4,6},{5,7},{6,4},{7,5},{8,10},{9,11},{10,... | collective-permute-start | bytes 786440 | tf_op jit(solution)/shard_map/ppermute | solution.py:256
  87.9 6.9 %collective-permute-start.14 = (f32[120,128]{1,0:T(8,128)S(1)}, f32[120,128]{1,0:T(8,128)S(1)}, u32[]{:S(2)}, u32[]{:S(2)}) collective-permute-start(f32[120,128]{1,0:T(8,128)S(1)} %slice.93), channel_id=1, source_target_pairs={{0,2},{1,3},{2,0},{3,1},{4,6},{5,7},{6,4},{7,5},{8,10},{9,11},{10,... | collective-permute-start | bytes 184328 | tf_op jit(solution)/shard_map/ppermute | solution.py:359
  96.9 1.6 %collective-permute-start.18 = (f32[480,128]{1,0:T(8,128)S(1)}, f32[480,128]{1,0:T(8,128)S(1)}, u32[]{:S(2)}, u32[]{:S(2)}) collective-permute-start(f32[480,128]{1,0:T(8,128)S(1)} %get-tuple-element.32), channel_id=1, source_target_pairs={{0,1},{1,0},{2,3},{3,2},{4,5},{5,4},{6,7},{7,6},{8,9},{9,8},{10,11... | collective-permute-start | bytes 737288 | tf_op jit(solution)/shard_map/ppermute | solution.py:355
  97.1 9.1 %copy-start.7 = (s32[768,1]{1,0:T(8,128)S(1)}, s32[768,1]{1,0:T(8,128)}, u32[]{:S(2)}) copy-start(s32[768,1]{1,0:T(8,128)} %copy.14.index_ref) | copy-start | bytes 9220
  98.6 5.4 %collective-permute-start.19 = (f32[240,128]{1,0:T(8,128)S(1)}, f32[240,128]{1,0:T(8,128)S(1)}, u32[]{:S(2)}, u32[]{:S(2)}) collective-permute-start(f32[240,128]{1,0:T(8,128)S(1)} %slice.97), channel_id=1, source_target_pairs={{0,2},{1,3},{2,0},{3,1},{4,6},{5,7},{6,4},{7,5},{8,10},{9,11},{10,... | collective-permute-start | bytes 368648 | tf_op jit(solution)/shard_map/ppermute | solution.py:359
  100.2 6.1 %collective-permute-start.17 = (f32[120,128]{1,0:T(8,128)S(1)}, f32[120,128]{1,0:T(8,128)S(1)}, u32[]{:S(2)}, u32[]{:S(2)}) collective-permute-start(f32[120,128]{1,0:T(8,128)S(1)} %get-tuple-element.30), channel_id=1, source_target_pairs={{0,8},{4,12},{8,0},{12,4},{1,9},{5,13},{9,1},{13,5},{2,10},{6,14},... | collective-permute-start | bytes 184328 | tf_op jit(solution)/shard_map/ppermute | solution.py:380
  104.0 4.3 %collective-permute-start.20 = (f32[120,128]{1,0:T(8,128)S(1)}, f32[120,128]{1,0:T(8,128)S(1)}, u32[]{:S(2)}, u32[]{:S(2)}) collective-permute-start(f32[120,128]{1,0:T(8,128)S(1)} %get-tuple-element.36), channel_id=1, source_target_pairs={{0,12},{4,0},{8,4},{12,8},{1,13},{5,1},{9,5},{13,9},{2,14},{6,2},{... | collective-permute-start | bytes 184328 | tf_op jit(solution)/shard_map/ppermute | solution.py:380
  106.2 6.0 %collective-permute-start.21 = (f32[120,128]{1,0:T(8,128)S(1)}, f32[120,128]{1,0:T(8,128)S(1)}, u32[]{:S(2)}, u32[]{:S(2)}) collective-permute-start(f32[120,128]{1,0:T(8,128)S(1)} %get-tuple-element.35), channel_id=1, source_target_pairs={{0,4},{4,8},{8,12},{12,0},{1,5},{5,9},{9,13},{13,1},{2,6},{6,10},{... | collective-permute-start | bytes 184328 | tf_op jit(solution)/shard_map/ppermute | solution.py:380
  (1 other events, 0.6 us)

commit v16 on v15

--- a/solution.py
+++ b/solution.py
@@ -313,7 +313,7 @@
         return lax.ppermute(block, "batch", [(i, (i + r) % homes) for i in range(homes)])
 
     packed, *blocks = pack(order, [])
-    mark, *blocks = gate(blocks, [packed])
+    mark, *blocks = gate(blocks, found)
     _, own_block = pack([0], [mark])
     arrived = {0: own_block}
     for r, block in zip(order, blocks):
@@ -360,7 +360,7 @@
 
     slabs = 3
     slab_sums = [
-        reduce_base(tokens, key_value_weight, piece, pieces, columns, slab, slabs, [mark] + found)
+        reduce_base(tokens, key_value_weight, piece, pieces, columns, slab, slabs, [mark])
         for slab in range(slabs)
     ]
     base = jnp.concatenate([total for total, _ in slab_sums], axis=0)

time: 114 us -> 118 us (1.035)
  local copies, waits for them, and re-layouts: 11.4 us -> 13.9 us
  starting transfers between devices: 25.8 us -> 23.6 us
  other arithmetic: 4.51 us -> 6.34 us
    ppermute x3, waiting for transfers between devices: 9.27 us -> 12 us  [combine(): lax.ppermute(value[half:], 'tensor', [(i, i ^ bit) for i in range(pieces)])]
    ppermute x3, waiting for transfers between devices: 0.01 us -> 2.69 us  [gather_up(): lax.ppermute(own, 'batch', [(i, (i - r) % homes) for i in range(homes)])]
    ppermute x3, waiting for transfers between devices: 17.9 us -> 15.4 us  [send(): lax.ppermute(block, 'batch', [(i, (i + r) % homes) for i in range(homes)])]
    ppermute x3, waiting for transfers between devices: 5.05 us -> 3.1 us  [give_back(): lax.ppermute(total, 'batch', [(i, (i - r) % homes) for i in range(homes)])]
    unnamed x54 -> x60, local copies, waits for them, and re-layouts: 8.37 us -> 10.2 us
    ppermute x3, starting transfers between devices: 3.46 us -> 2.14 us  [give_back(): lax.ppermute(total, 'batch', [(i, (i - r) % homes) for i in range(homes)])]
    ppermute x3, starting transfers between devices: 4.97 us -> 3.75 us  [combine(): lax.ppermute(value[half:], 'tensor', [(i, i ^ bit) for i in range(pieces)])]
  transfers between devices with their start and end apart: 22 -> 22, of which waited for: 8 -> 9; matrix products, arithmetic and copies ran while one was open for 7% -> 9% of each run, Pallas kernels for 29% -> 28%
where the time goes in v16:
time: 118 us; the launch traced here: 117 us
  Pallas kernels  35.1 us (30%)
  waiting for transfers between devices  34.7 us (29%)
  starting transfers between devices  23.6 us (20%)
  local copies, waits for them, and re-layouts  13.9 us (12%)
  other arithmetic  6.34 us (5%)
  between operations  3.43 us (3%)
    ppermute x3, waiting for transfers between devices, send(): lax.ppermute(block, 'batch', [(i, (i + r) % homes) for i in range(homes)])  15.4 us
    pallas_call x6, Pallas kernels, base_part(): pl.pallas_call(functools.partial(base_kernel, len(after)), out_shape=jax....  14.5 us
    ppermute x3, waiting for transfers between devices, combine(): lax.ppermute(value[half:], 'tensor', [(i, i ^ bit) for i in range(pieces)])  12 us
    pallas_call x2, Pallas kernels, pack(): pl.pallas_call(functools.partial(pack_kernel, span, shifts, len(after)),...  10.2 us
    unnamed x60, local copies, waits for them, and re-layouts  10.2 us
    ppermute x3, starting transfers between devices, send(): lax.ppermute(block, 'batch', [(i, (i + r) % homes) for i in range(homes)])  6.5 us
    ppermute x3, starting transfers between devices, gather_up(): lax.ppermute(own, 'batch', [(i, (i - r) % homes) for i in range(homes)])  6.11 us
    pallas_call x3, Pallas kernels, shrink(): pl.pallas_call(functools.partial(shrink_kernel, held, light, rank, value_...  5.62 us
  transfers between devices with their start and end apart: 22, of which 9 were waited for; matrix products, arithmetic and copies ran while one was open for 9% of the time, Pallas kernels for 28%

profile of v16, /device:TPU:0, one launch (start us, length us, event | category | flops | bytes accessed | tf_op | source)
XLA Modules:
  0.0 117.1 jit_solution(7344554270007673261)
XLA Ops:
  0.0 0.9 copy-done
  1.0 5.1 %collective-permute-start = (bf16[8,32,256]{2,1,0:T(8,128)(2,1)S(1)}, bf16[8,32,256]{2,1,0:T(8,128)(2,1)S(1)}, u32[]{:S(2)}, u32[]{:S(2)}) collective-permute-start(bf16[8,32,256]{2,1,0:T(8,128)(2,1)S(1)} %constant_dynamic-slice_fusion), channel_id=1, source_target_pairs={{0,12},{4,0},{8,4},{12,8},{1,13},{5,1},{9,5},{13,9},{2,14},{6,2},{... | collective-permute-start | bytes 393224 | tf_op jit(solution)/shard_map/ppermute | solution.py:197
  6.1 1.0 collective-permute-start.2
  7.1 1.7 %route.1 = (s32[1,768]{1,0:T(1,128)}, s32[8,128]{1,0:T(8,128)}) custom-call(s32[1]{0:T(128)} %bitcast.place_ref, s32[32]{0:T(128)} %entry_hbm.1, s32[768]{0:T(1024)} %request_hbm.1), custom_call_target="tpu_custom_call" | custom-call | flops 1 | bytes 1 | tf_op jit(solution)/shard_map/route/pallas_call | solution.py:280
  8.8 5.7 %pack.2 = (s32[8,128]{1,0:T(8,128)}, bf16[216,2048]{1,0:T(8,128)(2,1)}, bf16[216,2048]{1,0:T(8,128)(2,1)}, bf16[216,2048]{1,0:T(8,128)(2,1)}) custom-call(s32[1,768]{1,0:T(1,128)} %get-tuple-element.19.index_ref, bf16[768,2048]{1,0:T(8,128)(2,1)} %tokens_ref.15), custom_call_target="tpu_custom_call" | custom-call | flops 1 | bytes 1 | tf_op jit(solution)/shard_map/pack/pallas_call | solution.py:298
  14.6 2.7 %collective-permute-done.1.refs_4_ = bf16[8,32,256]{2,1,0:T(8,128)(2,1)S(1)} collective-permute-done((bf16[8,32,256]{2,1,0:T(8,128)(2,1)S(1)}, bf16[8,32,256]{2,1,0:T(8,128)(2,1)S(1)}, u32[]{:S(2)}, u32[]{:S(2)}) %collective-permute-start.1) | collective-permute-done | bytes 131104 | tf_op jit(solution)/shard_map/ppermute | solution.py:197
  17.3 0.6 copy-done.18
  18.6 2.6 %collective-permute-start.12 = (bf16[216,2048]{1,0:T(8,128)(2,1)}, bf16[216,2048]{1,0:T(8,128)(2,1)}, u32[]{:S(2)}, u32[]{:S(2)}) collective-permute-start(bf16[216,2048]{1,0:T(8,128)(2,1)} %get-tuple-element.26), channel_id=1, source_target_pairs={{0,8},{4,12},{8,0},{12,4},{1,9},{5,13},{9,1},{13,5},{2,10},{6,14},... | collective-permute-start | bytes 2654216 | tf_op jit(solution)/shard_map/ppermute | solution.py:313
  21.8 4.1 %base.6.refs_0_ = f32[256,512]{1,0:T(8,128)} custom-call(s32[2]{0:T(128)} %broadcast_xor_fusion.block_ref, bf16[768,2048]{1,0:T(8,128)(2,1)} %tokens_ref.15, bf16[2048,1024]{1,0:T(8,128)(2,1)} %weight_ref.11, s32[8,128]{1,0:T(8,128)} %get-tuple-element.23.refs_0_), custom_call_target="tpu_custom_call" | custom-call | flops 1 | bytes 1 | tf_op jit(solution)/shard_map/base/pallas_call | solution.py:224
  25.9 2.2 %copy-done.2 = bf16[2048,1024]{1,0:T(8,128)(2,1)S(1)} copy-done((bf16[2048,1024]{1,0:T(8,128)(2,1)S(1)}, bf16[2048,1024]{1,0:T(8,128)(2,1)}, u32[]{:S(2)}) %copy-start.2) | copy-done | bytes 4194328
  28.1 2.5 %base.10.refs_0_ = f32[256,512]{1,0:T(8,128)} custom-call(s32[2]{0:T(128)S(1)} %copy-done.11, bf16[768,2048]{1,0:T(8,128)(2,1)S(1)} %copy-done.1, bf16[2048,1024]{1,0:T(8,128)(2,1)S(1)} %copy-done.2, s32[8,128]{1,0:T(8,128)S(1)} %copy-done.10), custom_call_target="tpu_custom_call" | custom-call | flops 1 | bytes 1 | tf_op jit(solution)/shard_map/base/pallas_call | solution.py:224
  31.1 2.5 %base.8.refs_0_ = f32[256,512]{1,0:T(8,128)} custom-call(s32[2]{0:T(128)S(1)} %copy-done.11, bf16[768,2048]{1,0:T(8,128)(2,1)S(1)} %copy-done.1, bf16[2048,1024]{1,0:T(8,128)(2,1)S(1)} %copy-done.2, s32[8,128]{1,0:T(8,128)S(1)} %copy-done.10), custom_call_target="tpu_custom_call" | custom-call | flops 1 | bytes 1 | tf_op jit(solution)/shard_map/base/pallas_call | solution.py:224
  33.6 1.8 %base.7 = f32[256,512]{1,0:T(8,128)S(1)} custom-call(s32[2]{0:T(128)S(1)} %multiply_xor_fusion.block_ref, bf16[768,2048]{1,0:T(8,128)(2,1)S(1)} %copy-done.1, bf16[2048,1024]{1,0:T(8,128)(2,1)S(1)} %copy-done.3, f32[256,512]{1,0:T(8,128)S(1)} %copy-done.8), custom_call_target="tpu_custom_call" | custom-call | flops 1 | bytes 1 | tf_op jit(solution)/shard_map/base/pallas_call | solution.py:224
  35.6 0.8 copy-done.12
  36.3 0.7 slice.82
  37.1 1.5 %collective-permute-start.4 = (f32[256,256]{1,0:T(8,128)}, f32[256,256]{1,0:T(8,128)}, u32[]{:S(2)}, u32[]{:S(2)}) collective-permute-start(f32[256,256]{1,0:T(8,128)} %slice.82), channel_id=1, source_target_pairs={{0,2},{1,3},{2,0},{3,1},{4,6},{5,7},{6,4},{7,5},{8,10},{9,11},{10,... | collective-permute-start | bytes 786440 | tf_op jit(solution)/shard_map/ppermute | solution.py:256
  38.6 1.2 %slice.61 = s32[1,1]{1,0:T(1,128)} slice(s32[8,128]{1,0:T(8,128)} %get-tuple-element.18), slice={[0:1], [0:1]} | slice | bytes 8 | tf_op jit(solution)/shard_map/slice | solution.py:322
  42.6 0.9 copy.14.index_ref
  43.6 2.2 %copy-done.4 = bf16[2048,1024]{1,0:T(8,128)(2,1)S(1)} copy-done((bf16[2048,1024]{1,0:T(8,128)(2,1)S(1)}, bf16[2048,1024]{1,0:T(8,128)(2,1)}, u32[]{:S(2)}) %copy-start.4) | copy-done | bytes 4194328
  45.8 1.8 %base.11 = f32[256,512]{1,0:T(8,128)S(1)} custom-call(s32[2]{0:T(128)S(1)} %multiply_xor_fusion.block_ref, bf16[768,2048]{1,0:T(8,128)(2,1)S(1)} %copy-done.1, bf16[2048,1024]{1,0:T(8,128)(2,1)S(1)} %copy-done.4, f32[256,512]{1,0:T(8,128)} %base.10.refs_0_), custom_call_target="tpu_custom_call" | custom-call | flops 1 | bytes 1 | tf_op jit(solution)/shard_map/base/pallas_call | solution.py:224
  47.7 1.1 add.54
  48.8 0.8 copy-done.14
  49.7 0.7 slice.86
  51.0 0.9 pad_maximum_fusion.2
  51.9 1.8 %base.9 = f32[256,512]{1,0:T(8,128)S(1)} custom-call(s32[2]{0:T(128)S(1)} %multiply_xor_fusion.block_ref, bf16[768,2048]{1,0:T(8,128)(2,1)S(1)} %copy-done.1, bf16[2048,1024]{1,0:T(8,128)(2,1)S(1)} %copy-done.4, f32[256,512]{1,0:T(8,128)} %base.8.refs_0_), custom_call_target="tpu_custom_call" | custom-call | flops 1 | bytes 1 | tf_op jit(solution)/shard_map/base/pallas_call | solution.py:224
  53.7 4.5 %pack.3 = (s32[8,128]{1,0:T(8,128)}, bf16[216,2048]{1,0:T(8,128)(2,1)}) custom-call(s32[1,768]{1,0:T(1,128)} %get-tuple-element.19.index_ref, bf16[768,2048]{1,0:T(8,128)(2,1)} %tokens_ref.15, s32[8,128]{1,0:T(8,128)} %get-tuple-element.23.refs_0_), custom_call_target="tpu_custom_call" | custom-call | flops 1 | bytes 1 | tf_op jit(solution)/shard_map/pack/pallas_call | solution.py:298
  58.2 3.9 %collective-permute-start.11 = (bf16[216,2048]{1,0:T(8,128)(2,1)S(1)}, bf16[216,2048]{1,0:T(8,128)(2,1)S(1)}, u32[]{:S(2)}, u32[]{:S(2)}) collective-permute-start(bf16[216,2048]{1,0:T(8,128)(2,1)S(1)} %copy-done.27), channel_id=1, source_target_pairs={{0,12},{4,0},{8,4},{12,8},{1,13},{5,1},{9,5},{13,9},{2,14},{6,2},{... | collective-permute-start | bytes 2654216 | tf_op jit(solution)/shard_map/ppermute | solution.py:313
  62.1 1.2 %add.52 = f32[256,512]{1,0:T(8,128)S(1)} add(f32[256,512]{1,0:T(8,128)S(1)} %base.9, f32[256,512]{1,0:T(8,128)} %collective-permute-done.5) | non-fusion elementwise | flops 131072 | bytes 1572864 | tf_op jit(solution)/shard_map/add | solution.py:256
  63.3 15.4 %collective-permute-done.12.refs_0_ = bf16[216,2048]{1,0:T(8,128)(2,1)} collective-permute-done((bf16[216,2048]{1,0:T(8,128)(2,1)}, bf16[216,2048]{1,0:T(8,128)(2,1)}, u32[]{:S(2)}, u32[]{:S(2)}) %collective-permute-start.12) | collective-permute-done | bytes 884768 | tf_op jit(solution)/shard_map/ppermute | solution.py:313
  78.7 1.5 %collective-permute-start.9 = (bf16[32,32,256]{2,1,0:T(8,128)(2,1)S(1)}, bf16[32,32,256]{2,1,0:T(8,128)(2,1)S(1)}, u32[]{:S(2)}, u32[]{:S(2)}) collective-permute-start(bf16[32,32,256]{2,1,0:T(8,128)(2,1)S(1)} %copy-done.28), channel_id=1, source_target_pairs={{0,16},{16,0},{1,17},{17,1},{2,18},{18,2},{3,19},{19,3},{4,20},{20... | collective-permute-start | bytes 1572872 | tf_op jit(solution)/shard_map/ppermute | solution.py:201
  80.3 2.2 %copy-done.5 = bf16[8,2048,128]{2,1,0:T(8,128)(2,1)S(1)} copy-done((bf16[8,2048,128]{2,1,0:T(8,128)(2,1)S(1)}, bf16[8,2048,128]{2,1,0:T(8,128)(2,1)}, u32[]{:S(2)}) %copy-start.5) | copy-done | bytes 4194328
  82.4 2.2 %shrink.3.refs_2_ = f32[240,128]{1,0:T(8,128)S(1)} custom-call(s32[3]{0:T(128)S(1)} %pad_add_fusion.scalar_ref, bf16[216,2048]{1,0:T(8,128)(2,1)} %collective-permute-done.12.refs_0_, bf16[8,2048,128]{2,1,0:T(8,128)(2,1)S(1)} %copy-done.5, f32[8,512]{1,0:T(8,128)S(1)} %slice.89.refs_2_, f32[8,512]{1,0:T(8,128)S(1)} %slice.90.refs_3_, f32[8,512]{1,0:T(8,128)S(1)} %slice.91.refs_4_), custom_call_target="tpu_custom_call" | custom-call | flops 1 | bytes 1 | tf_op jit(solution)/shard_map/shrink/pallas_call | solution.py:328
  84.9 1.4 %shrink.4 = f32[240,128]{1,0:T(8,128)S(1)} custom-call(s32[3]{0:T(128)S(1)} %pad_add_fusion.scalar_ref, bf16[216,2048]{1,0:T(8,128)(2,1)S(1)} %copy-done.9, bf16[8,2048,128]{2,1,0:T(8,128)(2,1)S(1)} %copy-done.6, f32[240,128]{1,0:T(8,128)S(1)} %shrink.3.refs_2_), custom_call_target="tpu_custom_call" | custom-call | flops 1 | bytes 1 | tf_op jit(solution)/shard_map/shrink/pallas_call | solution.py:328
  86.4 1.0 slice_add_fusion.2
  88.0 1.6 %collective-permute-start.16 = (f32[120,128]{1,0:T(8,128)S(1)}, f32[120,128]{1,0:T(8,128)S(1)}, u32[]{:S(2)}, u32[]{:S(2)}) collective-permute-start(f32[120,128]{1,0:T(8,128)S(1)} %slice.95), channel_id=1, source_target_pairs={{0,2},{1,3},{2,0},{3,1},{4,6},{5,7},{6,4},{7,5},{8,10},{9,11},{10,... | collective-permute-start | bytes 184328 | tf_op jit(solution)/shard_map/ppermute | solution.py:359
  89.5 1.0 slice_add_fusion
  91.2 1.0 collective-permute-done.16
  92.3 1.6 %collective-permute-start.14 = (f32[120,128]{1,0:T(8,128)S(1)}, f32[120,128]{1,0:T(8,128)S(1)}, u32[]{:S(2)}, u32[]{:S(2)}) collective-permute-start(f32[120,128]{1,0:T(8,128)S(1)} %slice.93), channel_id=1, source_target_pairs={{0,2},{1,3},{2,0},{3,1},{4,6},{5,7},{6,4},{7,5},{8,10},{9,11},{10,... | collective-permute-start | bytes 184328 | tf_op jit(solution)/shard_map/ppermute | solution.py:359
  93.9 6.3 %collective-permute-done.14 = f32[120,128]{1,0:T(8,128)S(1)} collective-permute-done((f32[120,128]{1,0:T(8,128)S(1)}, f32[120,128]{1,0:T(8,128)S(1)}, u32[]{:S(2)}, u32[]{:S(2)}) %collective-permute-start.14) | collective-permute-done | bytes 61472 | tf_op jit(solution)/shard_map/ppermute | solution.py:359
  100.2 2.1 %shrink.5 = (f32[480,128]{1,0:T(8,128)S(1)}, f32[120,128]{1,0:T(8,128)S(1)}, f32[120,128]{1,0:T(8,128)S(1)}) custom-call(s32[3]{0:T(128)S(1)} %pad_add_fusion.scalar_ref, bf16[216,2048]{1,0:T(8,128)(2,1)} %collective-permute-done.10.refs_0_, bf16[216,2048]{1,0:T(8,128)(2,1)S(1)} %collective-permute-done.11.refs_1_, bf16[8,2048,128]{2,1,0:T(8,128)(2,1)S(1)} %copy-done.6, ...), custom_call_target="tpu_custom_call" | custom-call | flops 1 | bytes 1 | tf_op jit(solution)/shard_map/shrink/pallas_call | solution.py:328
  102.6 1.2 %collective-permute-done.18 = f32[480,128]{1,0:T(8,128)S(1)} collective-permute-done((f32[480,128]{1,0:T(8,128)S(1)}, f32[480,128]{1,0:T(8,128)S(1)}, u32[]{:S(2)}, u32[]{:S(2)}) %collective-permute-start.18) | collective-permute-done | bytes 245792 | tf_op jit(solution)/shard_map/ppermute | solution.py:355
  103.9 0.6 collective-permute-start.19
  104.6 4.7 %collective-permute-done.19 = f32[240,128]{1,0:T(8,128)S(1)} collective-permute-done((f32[240,128]{1,0:T(8,128)S(1)}, f32[240,128]{1,0:T(8,128)S(1)}, u32[]{:S(2)}, u32[]{:S(2)}) %collective-permute-start.19) | collective-permute-done | bytes 122912 | tf_op jit(solution)/shard_map/ppermute | solution.py:359
  109.4 2.0 %collective-permute-start.21 = (f32[120,128]{1,0:T(8,128)S(1)}, f32[120,128]{1,0:T(8,128)S(1)}, u32[]{:S(2)}, u32[]{:S(2)}) collective-permute-start(f32[120,128]{1,0:T(8,128)S(1)} %get-tuple-element.33), channel_id=1, source_target_pairs={{0,4},{4,8},{8,12},{12,0},{1,5},{5,9},{9,13},{13,1},{2,6},{6,10},{... | collective-permute-start | bytes 184328 | tf_op jit(solution)/shard_map/ppermute | solution.py:380
  111.5 0.9 finish.2.base_ref
  112.4 1.9 %collective-permute-done.20.refs_0_ = f32[120,128]{1,0:T(8,128)S(1)} collective-permute-done((f32[120,128]{1,0:T(8,128)S(1)}, f32[120,128]{1,0:T(8,128)S(1)}, u32[]{:S(2)}, u32[]{:S(2)}) %collective-permute-start.20) | collective-permute-done | bytes 61472 | tf_op jit(solution)/shard_map/ppermute | solution.py:380
  114.3 1.2 %collective-permute-done.21.refs_1_ = f32[120,128]{1,0:T(8,128)S(1)} collective-permute-done((f32[120,128]{1,0:T(8,128)S(1)}, f32[120,128]{1,0:T(8,128)S(1)}, u32[]{:S(2)}, u32[]{:S(2)}) %collective-permute-start.21) | collective-permute-done | bytes 61472 | tf_op jit(solution)/shard_map/ppermute | solution.py:380
  115.5 1.6 %finish.3 = bf16[768,256]{1,0:T(8,128)(2,1)} custom-call(s32[1]{0:T(128)} %bitcast.2.place_ref, s32[768,1]{1,0:T(8,128)S(1)} %copy-done.7, f32[768,256]{1,0:T(8,128)S(1)} %finish.2.base_ref, bf16[32,64,256]{2,1,0:T(8,128)(2,1)S(1)} %pad_maximum_fusion.up_ref, f32[120,128]{1,0:T(8,128)S(1)} %collective-permute-done.20.refs_0_, ...), custom_call_target="tpu_custom_call" | custom-call | flops 1 | bytes 1 | tf_op jit(solution)/shard_map/finish/pallas_call | solution.py:161
  (106 shorter events, 4.9 us)
Async XLA Ops:
  0.0 1.0 copy-start
  1.0 20.8 %copy-start.24 = (bf16[8,32,256]{2,1,0:T(8,128)(2,1)}, bf16[8,32,256]{2,1,0:T(8,128)(2,1)S(1)}, u32[]{:S(2)}) copy-start(bf16[8,32,256]{2,1,0:T(8,128)(2,1)S(1)} %constant_dynamic-slice_fusion) | copy-start | bytes 393220
  1.0 13.6 %collective-permute-start = (bf16[8,32,256]{2,1,0:T(8,128)(2,1)S(1)}, bf16[8,32,256]{2,1,0:T(8,128)(2,1)S(1)}, u32[]{:S(2)}, u32[]{:S(2)}) collective-permute-start(bf16[8,32,256]{2,1,0:T(8,128)(2,1)S(1)} %constant_dynamic-slice_fusion), channel_id=1, source_target_pairs={{0,12},{4,0},{8,4},{12,8},{1,13},{5,1},{9,5},{13,9},{2,14},{6,2},{... | collective-permute-start | bytes 393224 | tf_op jit(solution)/shard_map/ppermute | solution.py:197
  6.1 11.2 %collective-permute-start.1 = (bf16[8,32,256]{2,1,0:T(8,128)(2,1)S(1)}, bf16[8,32,256]{2,1,0:T(8,128)(2,1)S(1)}, u32[]{:S(2)}, u32[]{:S(2)}) collective-permute-start(bf16[8,32,256]{2,1,0:T(8,128)(2,1)S(1)} %constant_dynamic-slice_fusion), channel_id=1, source_target_pairs={{0,8},{4,12},{8,0},{12,4},{1,9},{5,13},{9,1},{13,5},{2,10},{6,14},... | collective-permute-start | bytes 393224 | tf_op jit(solution)/shard_map/ppermute | solution.py:197
  6.1 11.2 %collective-permute-start.2 = (bf16[8,32,256]{2,1,0:T(8,128)(2,1)S(1)}, bf16[8,32,256]{2,1,0:T(8,128)(2,1)S(1)}, u32[]{:S(2)}, u32[]{:S(2)}) collective-permute-start(bf16[8,32,256]{2,1,0:T(8,128)(2,1)S(1)} %constant_dynamic-slice_fusion), channel_id=1, source_target_pairs={{0,4},{4,8},{8,12},{12,0},{1,5},{5,9},{9,13},{13,1},{2,6},{6,10},{... | collective-permute-start | bytes 393224 | tf_op jit(solution)/shard_map/ppermute | solution.py:197
  14.6 2.7 %copy-start.16 = (bf16[8,32,256]{2,1,0:T(8,128)(2,1)}, bf16[8,32,256]{2,1,0:T(8,128)(2,1)S(1)}, u32[]{:S(2)}) copy-start(bf16[8,32,256]{2,1,0:T(8,128)(2,1)S(1)} %collective-permute-done.refs_3_) | copy-start | bytes 393220
  18.6 60.2 %collective-permute-start.12 = (bf16[216,2048]{1,0:T(8,128)(2,1)}, bf16[216,2048]{1,0:T(8,128)(2,1)}, u32[]{:S(2)}, u32[]{:S(2)}) collective-permute-start(bf16[216,2048]{1,0:T(8,128)(2,1)} %get-tuple-element.26), channel_id=1, source_target_pairs={{0,8},{4,12},{8,0},{12,4},{1,9},{5,13},{9,1},{13,5},{2,10},{6,14},... | collective-permute-start | bytes 2654216 | tf_op jit(solution)/shard_map/ppermute | solution.py:313
  21.8 4.1 %copy-start.1 = (bf16[768,2048]{1,0:T(8,128)(2,1)S(1)}, bf16[768,2048]{1,0:T(8,128)(2,1)}, u32[]{:S(2)}) copy-start(bf16[768,2048]{1,0:T(8,128)(2,1)} %tokens_ref.15) | copy-start | bytes 9437188
  21.8 4.1 %copy-start.10 = (s32[8,128]{1,0:T(8,128)S(1)}, s32[8,128]{1,0:T(8,128)}, u32[]{:S(2)}) copy-start(s32[8,128]{1,0:T(8,128)} %get-tuple-element.23.refs_0_) | copy-start | bytes 12292
  21.8 4.1 %copy-start.11 = (s32[2]{0:T(128)S(1)}, s32[2]{0:T(128)}, u32[]{:S(2)}) copy-start(s32[2]{0:T(128)} %broadcast_xor_fusion.block_ref) | copy-start | bytes 28
  25.9 9.6 %collective-permute-start.3 = (f32[256,512]{1,0:T(8,128)}, f32[256,512]{1,0:T(8,128)S(1)}, u32[]{:S(2)}, u32[]{:S(2)}) collective-permute-start(f32[256,512]{1,0:T(8,128)} %base.6.refs_0_), channel_id=1, source_target_pairs={{0,1},{1,0},{2,3},{3,2},{4,5},{5,4},{6,7},{7,6},{8,9},{9,8},{10,11... | collective-permute-start | bytes 1572872 | tf_op jit(solution)/shard_map/ppermute | solution.py:256
  25.9 2.2 %copy-start.2 = (bf16[2048,1024]{1,0:T(8,128)(2,1)S(1)}, bf16[2048,1024]{1,0:T(8,128)(2,1)}, u32[]{:S(2)}) copy-start(bf16[2048,1024]{1,0:T(8,128)(2,1)} %weight_ref.11) | copy-start | bytes 12582916
  30.6 3.0 %copy-start.3 = (bf16[2048,1024]{1,0:T(8,128)(2,1)S(1)}, bf16[2048,1024]{1,0:T(8,128)(2,1)}, u32[]{:S(2)}) copy-start(bf16[2048,1024]{1,0:T(8,128)(2,1)} %weight_ref.11) | copy-start | bytes 12582916
  30.6 3.0 %copy-start.8 = (f32[256,512]{1,0:T(8,128)S(1)}, f32[256,512]{1,0:T(8,128)}, u32[]{:S(2)}) copy-start(f32[256,512]{1,0:T(8,128)} %base.6.refs_0_) | copy-start | bytes 1572868
  30.6 17.1 %collective-permute-start.7 = (f32[256,512]{1,0:T(8,128)}, f32[256,512]{1,0:T(8,128)}, u32[]{:S(2)}, u32[]{:S(2)}) collective-permute-start(f32[256,512]{1,0:T(8,128)} %base.10.refs_0_), channel_id=1, source_target_pairs={{0,1},{1,0},{2,3},{3,2},{4,5},{5,4},{6,7},{7,6},{8,9},{9,8},{10,11... | collective-permute-start | bytes 1572872 | tf_op jit(solution)/shard_map/ppermute | solution.py:256
  33.6 24.6 %collective-permute-start.5 = (f32[256,512]{1,0:T(8,128)}, f32[256,512]{1,0:T(8,128)}, u32[]{:S(2)}, u32[]{:S(2)}) collective-permute-start(f32[256,512]{1,0:T(8,128)} %base.8.refs_0_), channel_id=1, source_target_pairs={{0,1},{1,0},{2,3},{3,2},{4,5},{5,4},{6,7},{7,6},{8,9},{9,8},{10,11... | collective-permute-start | bytes 1572872 | tf_op jit(solution)/shard_map/ppermute | solution.py:256
  33.6 9.0 %copy-start.29 = (s32[1,768]{1,0:T(1,128)S(1)}, s32[1,768]{1,0:T(1,128)}, u32[]{:S(2)}) copy-start(s32[1,768]{1,0:T(1,128)} %get-tuple-element.19.index_ref) | copy-start | bytes 9220
  37.1 49.2 %collective-permute-start.4 = (f32[256,256]{1,0:T(8,128)}, f32[256,256]{1,0:T(8,128)}, u32[]{:S(2)}, u32[]{:S(2)}) collective-permute-start(f32[256,256]{1,0:T(8,128)} %slice.82), channel_id=1, source_target_pairs={{0,2},{1,3},{2,0},{3,1},{4,6},{5,7},{6,4},{7,5},{8,10},{9,11},{10,... | collective-permute-start | bytes 786440 | tf_op jit(solution)/shard_map/ppermute | solution.py:256
  43.6 2.2 %copy-start.4 = (bf16[2048,1024]{1,0:T(8,128)(2,1)S(1)}, bf16[2048,1024]{1,0:T(8,128)(2,1)}, u32[]{:S(2)}) copy-start(bf16[2048,1024]{1,0:T(8,128)(2,1)} %weight_ref.11) | copy-start | bytes 12582916
  45.8 5.1 %copy-start.17 = (bf16[8,32,256]{2,1,0:T(8,128)(2,1)S(1)}, bf16[8,32,256]{2,1,0:T(8,128)(2,1)}, u32[]{:S(2)}) copy-start(bf16[8,32,256]{2,1,0:T(8,128)(2,1)} %copy-done.16) | copy-start | bytes 393220
  45.8 5.1 %copy-start.19 = (bf16[8,32,256]{2,1,0:T(8,128)(2,1)S(1)}, bf16[8,32,256]{2,1,0:T(8,128)(2,1)}, u32[]{:S(2)}) copy-start(bf16[8,32,256]{2,1,0:T(8,128)(2,1)} %copy-done.18) | copy-start | bytes 393220
  45.8 5.1 %copy-start.22 = (bf16[8,32,256]{2,1,0:T(8,128)(2,1)S(1)}, bf16[8,32,256]{2,1,0:T(8,128)(2,1)}, u32[]{:S(2)}) copy-start(bf16[8,32,256]{2,1,0:T(8,128)(2,1)} %copy-done.21) | copy-start | bytes 393220
  45.8 5.1 %copy-start.25 = (bf16[8,32,256]{2,1,0:T(8,128)(2,1)S(1)}, bf16[8,32,256]{2,1,0:T(8,128)(2,1)}, u32[]{:S(2)}) copy-start(bf16[8,32,256]{2,1,0:T(8,128)(2,1)} %copy-done.24) | copy-start | bytes 393220
  47.6 52.5 %collective-permute-start.10 = (bf16[216,2048]{1,0:T(8,128)(2,1)}, bf16[216,2048]{1,0:T(8,128)(2,1)}, u32[]{:S(2)}, u32[]{:S(2)}) collective-permute-start(bf16[216,2048]{1,0:T(8,128)(2,1)} %get-tuple-element.24), channel_id=1, source_target_pairs={{0,4},{4,8},{8,12},{12,0},{1,5},{5,9},{9,13},{13,1},{2,6},{6,10},{... | collective-permute-start | bytes 2654216 | tf_op jit(solution)/shard_map/ppermute | solution.py:313
  50.4 37.6 %collective-permute-start.8 = (f32[256,256]{1,0:T(8,128)}, f32[256,256]{1,0:T(8,128)}, u32[]{:S(2)}, u32[]{:S(2)}) collective-permute-start(f32[256,256]{1,0:T(8,128)} %slice.86), channel_id=1, source_target_pairs={{0,2},{1,3},{2,0},{3,1},{4,6},{5,7},{6,4},{7,5},{8,10},{9,11},{10,... | collective-permute-start | bytes 786440 | tf_op jit(solution)/shard_map/ppermute | solution.py:256
  53.7 4.5 %copy-start.13 = (f32[256,512]{1,0:T(8,128)S(1)}, f32[256,512]{1,0:T(8,128)}, u32[]{:S(2)}) copy-start(f32[256,512]{1,0:T(8,128)} %copy-done.12) | copy-start | bytes 1572868
  53.7 4.5 %copy-start.15 = (f32[256,512]{1,0:T(8,128)S(1)}, f32[256,512]{1,0:T(8,128)}, u32[]{:S(2)}) copy-start(f32[256,512]{1,0:T(8,128)} %copy-done.14) | copy-start | bytes 1572868
  53.7 4.6 %copy-start.27 = (bf16[216,2048]{1,0:T(8,128)(2,1)S(1)}, bf16[216,2048]{1,0:T(8,128)(2,1)}, u32[]{:S(2)}) copy-start(bf16[216,2048]{1,0:T(8,128)(2,1)} %get-tuple-element.25) | copy-start | bytes 2654212
  53.7 25.1 %copy-start.28 = (bf16[32,32,256]{2,1,0:T(8,128)(2,1)S(1)}, bf16[32,32,256]{2,1,0:T(8,128)(2,1)}, u32[]{:S(2)}) copy-start(bf16[32,32,256]{2,1,0:T(8,128)(2,1)} %pad_maximum_fusion.2) | copy-start | bytes 1572868
  58.2 41.9 %collective-permute-start.11 = (bf16[216,2048]{1,0:T(8,128)(2,1)S(1)}, bf16[216,2048]{1,0:T(8,128)(2,1)S(1)}, u32[]{:S(2)}, u32[]{:S(2)}) collective-permute-start(bf16[216,2048]{1,0:T(8,128)(2,1)S(1)} %copy-done.27), channel_id=1, source_target_pairs={{0,12},{4,0},{8,4},{12,8},{1,13},{5,1},{9,5},{13,9},{2,14},{6,2},{... | collective-permute-start | bytes 2654216 | tf_op jit(solution)/shard_map/ppermute | solution.py:313
  62.1 22.5 %copy-start.9 = (bf16[216,2048]{1,0:T(8,128)(2,1)S(1)}, bf16[216,2048]{1,0:T(8,128)(2,1)}, u32[]{:S(2)}) copy-start(bf16[216,2048]{1,0:T(8,128)(2,1)} %get-tuple-element.27.refs_0_) | copy-start | bytes 2654212
  78.7 23.6 %collective-permute-start.9 = (bf16[32,32,256]{2,1,0:T(8,128)(2,1)S(1)}, bf16[32,32,256]{2,1,0:T(8,128)(2,1)S(1)}, u32[]{:S(2)}, u32[]{:S(2)}) collective-permute-start(bf16[32,32,256]{2,1,0:T(8,128)(2,1)S(1)} %copy-done.28), channel_id=1, source_target_pairs={{0,16},{16,0},{1,17},{17,1},{2,18},{18,2},{3,19},{19,3},{4,20},{20... | collective-permute-start | bytes 1572872 | tf_op jit(solution)/shard_map/ppermute | solution.py:201
  80.3 2.2 %copy-start.5 = (bf16[8,2048,128]{2,1,0:T(8,128)(2,1)S(1)}, bf16[8,2048,128]{2,1,0:T(8,128)(2,1)}, u32[]{:S(2)}) copy-start(bf16[8,2048,128]{2,1,0:T(8,128)(2,1)} %refs_2_.1) | copy-start | bytes 12582916
  82.4 2.5 %copy-start.6 = (bf16[8,2048,128]{2,1,0:T(8,128)(2,1)S(1)}, bf16[8,2048,128]{2,1,0:T(8,128)(2,1)}, u32[]{:S(2)}) copy-start(bf16[8,2048,128]{2,1,0:T(8,128)(2,1)} %refs_2_.1) | copy-start | bytes 12582916
  86.3 1.4 %collective-permute-start.15 = (f32[240,128]{1,0:T(8,128)S(1)}, f32[240,128]{1,0:T(8,128)S(1)}, u32[]{:S(2)}, u32[]{:S(2)}) collective-permute-start(f32[240,128]{1,0:T(8,128)S(1)} %shrink.4), channel_id=1, source_target_pairs={{0,1},{1,0},{2,3},{3,2},{4,5},{5,4},{6,7},{7,6},{8,9},{9,8},{10,11... | collective-permute-start | bytes 368648 | tf_op jit(solution)/shard_map/ppermute | solution.py:355
  87.7 2.9 %collective-permute-start.13 = (f32[240,128]{1,0:T(8,128)S(1)}, f32[240,128]{1,0:T(8,128)S(1)}, u32[]{:S(2)}, u32[]{:S(2)}) collective-permute-start(f32[240,128]{1,0:T(8,128)S(1)} %shrink.3.refs_2_), channel_id=1, source_target_pairs={{0,1},{1,0},{2,3},{3,2},{4,5},{5,4},{6,7},{7,6},{8,9},{9,8},{10,11... | collective-permute-start | bytes 368648 | tf_op jit(solution)/shard_map/ppermute | solution.py:355
  88.0 4.3 %collective-permute-start.16 = (f32[120,128]{1,0:T(8,128)S(1)}, f32[120,128]{1,0:T(8,128)S(1)}, u32[]{:S(2)}, u32[]{:S(2)}) collective-permute-start(f32[120,128]{1,0:T(8,128)S(1)} %slice.95), channel_id=1, source_target_pairs={{0,2},{1,3},{2,0},{3,1},{4,6},{5,7},{6,4},{7,5},{8,10},{9,11},{10,... | collective-permute-start | bytes 184328 | tf_op jit(solution)/shard_map/ppermute | solution.py:359
  90.6 14.0 %collective-permute-start.6 = (f32[256,256]{1,0:T(8,128)S(1)}, f32[256,256]{1,0:T(8,128)S(1)}, u32[]{:S(2)}, u32[]{:S(2)}) collective-permute-start(f32[256,256]{1,0:T(8,128)S(1)} %slice.84), channel_id=1, source_target_pairs={{0,2},{1,3},{2,0},{3,1},{4,6},{5,7},{6,4},{7,5},{8,10},{9,11},{10,... | collective-permute-start | bytes 786440 | tf_op jit(solution)/shard_map/ppermute | solution.py:256
  92.3 7.9 %collective-permute-start.14 = (f32[120,128]{1,0:T(8,128)S(1)}, f32[120,128]{1,0:T(8,128)S(1)}, u32[]{:S(2)}, u32[]{:S(2)}) collective-permute-start(f32[120,128]{1,0:T(8,128)S(1)} %slice.93), channel_id=1, source_target_pairs={{0,2},{1,3},{2,0},{3,1},{4,6},{5,7},{6,4},{7,5},{8,10},{9,11},{10,... | collective-permute-start | bytes 184328 | tf_op jit(solution)/shard_map/ppermute | solution.py:359
  93.8 8.5 %copy-start.20 = (bf16[8,32,256]{2,1,0:T(8,128)(2,1)S(1)}, bf16[8,32,256]{2,1,0:T(8,128)(2,1)}, u32[]{:S(2)}) copy-start(bf16[8,32,256]{2,1,0:T(8,128)(2,1)} %copy-done.18) | copy-start | bytes 393220
  93.9 8.5 %copy-start.23 = (bf16[8,32,256]{2,1,0:T(8,128)(2,1)S(1)}, bf16[8,32,256]{2,1,0:T(8,128)(2,1)}, u32[]{:S(2)}) copy-start(bf16[8,32,256]{2,1,0:T(8,128)(2,1)} %copy-done.21) | copy-start | bytes 393220
  93.9 8.5 %copy-start.26 = (bf16[8,32,256]{2,1,0:T(8,128)(2,1)S(1)}, bf16[8,32,256]{2,1,0:T(8,128)(2,1)}, u32[]{:S(2)}) copy-start(bf16[8,32,256]{2,1,0:T(8,128)(2,1)} %copy-done.24) | copy-start | bytes 393220
  102.3 1.6 %collective-permute-start.18 = (f32[480,128]{1,0:T(8,128)S(1)}, f32[480,128]{1,0:T(8,128)S(1)}, u32[]{:S(2)}, u32[]{:S(2)}) collective-permute-start(f32[480,128]{1,0:T(8,128)S(1)} %get-tuple-element.30), channel_id=1, source_target_pairs={{0,1},{1,0},{2,3},{3,2},{4,5},{5,4},{6,7},{7,6},{8,9},{9,8},{10,11... | collective-permute-start | bytes 737288 | tf_op jit(solution)/shard_map/ppermute | solution.py:355
  102.5 9.0 %copy-start.7 = (s32[768,1]{1,0:T(8,128)S(1)}, s32[768,1]{1,0:T(8,128)}, u32[]{:S(2)}) copy-start(s32[768,1]{1,0:T(8,128)} %copy.14.index_ref) | copy-start | bytes 9220
  103.9 5.4 %collective-permute-start.19 = (f32[240,128]{1,0:T(8,128)S(1)}, f32[240,128]{1,0:T(8,128)S(1)}, u32[]{:S(2)}, u32[]{:S(2)}) collective-permute-start(f32[240,128]{1,0:T(8,128)S(1)} %slice.97), channel_id=1, source_target_pairs={{0,2},{1,3},{2,0},{3,1},{4,6},{5,7},{6,4},{7,5},{8,10},{9,11},{10,... | collective-permute-start | bytes 368648 | tf_op jit(solution)/shard_map/ppermute | solution.py:359
  104.5 6.9 %collective-permute-start.17 = (f32[120,128]{1,0:T(8,128)S(1)}, f32[120,128]{1,0:T(8,128)S(1)}, u32[]{:S(2)}, u32[]{:S(2)}) collective-permute-start(f32[120,128]{1,0:T(8,128)S(1)} %get-tuple-element.28), channel_id=1, source_target_pairs={{0,8},{4,12},{8,0},{12,4},{1,9},{5,13},{9,1},{13,5},{2,10},{6,14},... | collective-permute-start | bytes 184328 | tf_op jit(solution)/shard_map/ppermute | solution.py:380
  109.3 4.9 %collective-permute-start.20 = (f32[120,128]{1,0:T(8,128)S(1)}, f32[120,128]{1,0:T(8,128)S(1)}, u32[]{:S(2)}, u32[]{:S(2)}) collective-permute-start(f32[120,128]{1,0:T(8,128)S(1)} %get-tuple-element.34), channel_id=1, source_target_pairs={{0,12},{4,0},{8,4},{12,8},{1,13},{5,1},{9,5},{13,9},{2,14},{6,2},{... | collective-permute-start | bytes 184328 | tf_op jit(solution)/shard_map/ppermute | solution.py:380
  109.4 6.1 %collective-permute-start.21 = (f32[120,128]{1,0:T(8,128)S(1)}, f32[120,128]{1,0:T(8,128)S(1)}, u32[]{:S(2)}, u32[]{:S(2)}) collective-permute-start(f32[120,128]{1,0:T(8,128)S(1)} %get-tuple-element.33), channel_id=1, source_target_pairs={{0,4},{4,8},{8,12},{12,0},{1,5},{5,9},{9,13},{13,1},{2,6},{6,10},{... | collective-permute-start | bytes 184328 | tf_op jit(solution)/shard_map/ppermute | solution.py:380
  (4 other events, 3.0 us)
